TPU v7x, 32 devices: a whole 2x2x4 slice. The times are simulated.
32 devices in a mesh: grp: 1, row: 16 (over z, y, x), col: 2 (over core).
Axes of the slice: x: 2, y: 2, z: 4, core: 2. Of those that a mesh axis runs over, the one named last changes fastest.
Arguments:
- pair: bfloat16 [192, 192, 128], P(('grp', 'row'), 'col'), may hold values from -6 to 6
- tile_mask: int32 [2, 2], P('grp'), may hold values 0 or 1
- chain_ids: int32 [192], P('grp'), may hold values from 0 to 5, never falling along the last dimension, each value on 1 to 64 neighbouring positions
- gain_in: float32 [128], replicated, may hold values from 0.1 to 1.9
- w_proj: bfloat16 [128, 640], replicated, may hold values from -0.5 to 0.5
- gain_mid: float32 [128], replicated, may hold values from 0.1 to 1.9
- w_out: bfloat16 [128, 128], replicated, may hold values from -0.5 to 0.5
Outputs:
- update: bfloat16 [192, 192, 128], P(('grp', 'row'), 'col')
Inputs may be any that keep to these rules, and one draw needn't show every extreme that they name: `chain_ids`: chains are runs of consecutive tokens with never falling ids, each at most 64 tokens long; one chain has exactly that many.
All inputs are finite; a program needn't handle non-finite values.
Results may differ from a plain program's by a relative error of at most 0.0079.
Values may be sent and summed in bfloat16 or wider, within the bound.
No kernel may reach another device: no remote copies, remote signals or barrier semaphores. Data moves between devices by JAX's collectives and lax.ppermute only.
A program may use at most 128 MiB of HBM per device.

v0:
```python
import jax
import jax.numpy as jnp
from jax import lax
from jax.sharding import PartitionSpec as P

TILE = 96


def layer_norm(values, gain):
    center = values - jnp.mean(values, axis=-1, keepdims=True)
    spread = jnp.mean(center * center, axis=-1, keepdims=True)
    return center * lax.rsqrt(spread + 1e-05) * gain


def on_device(pair, tile_mask, chain_ids, gain_in, w_proj, gain_mid, w_out):
    row_count, col_count, pair_width = pair.shape
    hidden = w_out.shape[0]
    row_at = lax.axis_index("row")
    col_at = lax.axis_index("col")
    row_tokens = row_at * row_count + lax.iota(jnp.int32, row_count)
    col_tokens = col_at * col_count + lax.iota(jnp.int32, col_count)
    tile_ids = lax.iota(jnp.int32, tile_mask.shape[0])
    row_onehot = (row_tokens[:, None] // TILE == tile_ids[None, :]).astype(jnp.float32)
    col_onehot = (col_tokens[:, None] // TILE == tile_ids[None, :]).astype(jnp.float32)
    tile_vals = jnp.dot(
        jnp.dot(row_onehot, tile_mask.astype(jnp.float32), precision=lax.Precision.HIGHEST),
        col_onehot.T,
        precision=lax.Precision.HIGHEST,
    )
    row_chain = lax.dynamic_slice_in_dim(chain_ids, row_at * row_count, row_count)
    col_chain = lax.dynamic_slice_in_dim(chain_ids, col_at * col_count, col_count)
    keep_mask = jnp.where(row_chain[:, None] == col_chain[None, :], jnp.float32(1.0), tile_vals)[
        ..., None
    ]
    normed = layer_norm(pair.astype(jnp.float32), gain_in).astype(jnp.bfloat16)
    projected = jnp.dot(
        normed.reshape(row_count * col_count, pair_width),
        w_proj,
        preferred_element_type=jnp.float32,
    )
    projected = projected.reshape(row_count, col_count, 4 * hidden + pair_width)
    left_terms = (
        jax.nn.sigmoid(projected[..., hidden : 2 * hidden]) * projected[..., :hidden] * keep_mask
    ).astype(jnp.bfloat16)
    right_terms = (
        jax.nn.sigmoid(projected[..., 3 * hidden : 4 * hidden])
        * projected[..., 2 * hidden : 3 * hidden]
        * keep_mask
    ).astype(jnp.bfloat16)
    left_all = lax.all_gather(left_terms, "col", axis=1, tiled=True)
    left_need = lax.all_to_all(left_all, "row", split_axis=1, concat_axis=0, tiled=True)
    mixed_sum = jnp.einsum(
        "kic,kjc->ijc",
        left_need,
        lax.all_gather(right_terms, "row", axis=0, tiled=True),
        preferred_element_type=jnp.float32,
    )
    mixed_norm = layer_norm(mixed_sum, gain_mid).astype(jnp.bfloat16)
    projected_out = jnp.dot(
        mixed_norm.reshape(row_count * col_count, hidden), w_out, preferred_element_type=jnp.float32
    )
    projected_out = projected_out.reshape(row_count, col_count, pair_width)
    return (jax.nn.sigmoid(projected[..., 4 * hidden :]) * projected_out).astype(jnp.bfloat16)


def solution(mesh):
    in_specs = (P(("grp", "row"), "col", None), P("grp", None), P("grp"), P(), P(), P(), P())
    out_specs = P(("grp", "row"), "col", None)
    return jax.shard_map(
        on_device, mesh=mesh, in_specs=in_specs, out_specs=out_specs, check_vma=False
    )
```

profile of v0, /device:TPU:0, one launch (start us, length us, event | category | flops | bytes accessed | tf_op | source)
XLA Modules:
  0.0 126.5 jit_solution(10985682529852240803)
XLA Ops:
  6.5 0.0 copy-start
  6.5 0.0 all-gather.2.cloned.1.call-start
  6.6 0.8 dynamic_slice.6
  7.4 0.8 dynamic_slice.7
  8.1 1.1 convert_reduce_fusion
  9.3 1.4 %fusion.3 = f32[12,96]{1,0:T(8,128)S(1)} fusion(bf16[12,96,128]{2,1,0:T(8,128)(2,1)} %param.7, f32[12,96]{1,0:T(8,128)S(1)} %broadcast_multiply_fusion.1), kind=kLoop, calls=%fused_computation.10 | loop fusion | flops 588672 | bytes 304128 | tf_op jit(solution)/shard_map/reduce_sum | solution.py:11
  10.7 0.9 fusion.28
  11.6 0.0 copy-done
  11.6 1.6 %fusion.20 = f32[12,96,640]{2,1,0:T(8,128)S(1)} fusion(bf16[12,96,128]{2,1,0:T(8,128)(2,1)} %param.7, f32[128]{0:T(128)} %param.10, f32[12,96]{1,0:T(8,128)S(1)} %add_rsqrt_fusion.1, f32[12,96]{1,0:T(8,128)S(1)} %broadcast_multiply_fusion.1, bf16[128,640]{1,0:T(8,128)(2,1)S(1)} %copy-done), kind=kOutput, calls=%fused_computation.32 | convolution fusion | flops 189480960 | bytes 3417600 | tf_op jit(solution)/shard_map/dot_general | solution.py:36
  13.2 0.2 convolution_select_fusion
  13.4 1.1 fusion.7
  14.6 0.0 all-gather.2.cloned.1.call-update
  14.6 2.3 %all_gather.7 = bf16[12,192,128]{2,1,0:T(8,128)(2,1)S(1)} all-gather(bf16[12,96,128]{2,1,0:T(8,128)(2,1)S(1)} %get-tuple-element.5), channel_id=1, replica_groups=mesh['grp'=1,'row'=16,'col'=2] {'col'}, dimensions={1}, use_global_device_ids=true | all-gather | bytes 884736 | tf_op jit(solution)/shard_map/all_gather | solution.py:50
  16.9 0.4 copy.15
  17.3 35.9 %all_to_all.18 = bf16[12,192,128]{2,0,1:T(8,128)(2,1)S(1)} all-to-all(bf16[12,192,128]{2,0,1:T(8,128)(2,1)S(1)} %copy.15), channel_id=1, replica_groups=mesh['grp'=1,'row'=16,'col'=2] {'row'}, dimensions={1} | all-to-all | bytes 1179648 | tf_op jit(solution)/shard_map/all_to_all | solution.py:51
  53.2 1.1 copy.17
  54.3 2.0 %all_to_all.16 = bf16[192,12,128]{2,0,1:T(8,128)(2,1)} reshape(bf16[16,12,12,128]{3,1,0,2:T(8,128)(2,1)} %copy.17) | data formatting | bytes 1179648 | tf_op jit(solution)/shard_map/all_to_all | solution.py:51
  56.3 2.6 %copy.19 = bf16[192,12,128]{0,1,2:T(8,128)(2,1)} copy(bf16[192,12,128]{2,0,1:T(8,128)(2,1)} %all_to_all.16) | data formatting | bytes 1179648 | tf_op jit(solution)/shard_map/all_to_all | solution.py:51
  58.9 46.0 %all-gather.2.cloned.1.call-done = bf16[192,96,128]{2,1,0:T(8,128)(2,1)} async-done(((bf16[12,96,128]{2,1,0:T(8,128)(2,1)}), bf16[192,96,128]{2,1,0:T(8,128)(2,1)}) %all-gather.2.cloned.1.call-update) | async-done | bytes 4718608 | tf_op jit(solution)/shard_map/all_gather | solution.py:55
  104.9 8.4 %copy.18 = bf16[192,96,128]{1,0,2:T(8,128)(2,1)} copy(bf16[192,96,128]{2,1,0:T(8,128)(2,1)} %all-gather.2.cloned.1.call-done) | data formatting | bytes 9437184 | tf_op jit(solution)/shard_map/all_gather | solution.py:55
  113.3 0.0 copy-start.1
  113.3 0.0 copy-start.2
  113.3 4.8 %fusion.31 = (f32[12,96]{1,0:T(8,128)S(1)}, f32[12,96,128]{1,0,2:T(8,128)S(1)}) fusion(bf16[192,96,128]{1,0,2:T(8,128)(2,1)} %copy.18, bf16[192,12,128]{0,1,2:T(8,128)(2,1)} %copy.19), kind=kOutput, calls=%fused_computation.50 | convolution fusion | flops 56769408 | bytes 5902848 | tf_op jit(solution)/shard_map/kic,kjc->ijc/dot_general | solution.py:52
  118.1 0.2 multiply_reduce_fusion
  118.4 0.0 copy-done.1
  118.4 0.2 multiply_convert_fusion
  118.6 0.0 copy-done.2
  118.6 1.0 fusion
  (6 shorter events, 0.1 us)
Async XLA Ops:
  6.5 5.1 %copy-start = (bf16[128,640]{1,0:T(8,128)(2,1)S(1)}, bf16[128,640]{1,0:T(8,128)(2,1)}, u32[]{:S(2)}) copy-start(bf16[128,640]{1,0:T(8,128)(2,1)} %param.11) | copy-start | bytes 491524
  6.5 98.4 %all-gather.2.cloned.1.call-start = ((), (), s32[]{:S(2)}) async-start(), calls=%async_computation.1 | async-start | bytes 5013504 | tf_op jit(solution)/shard_map/all_gather | solution.py:55
  113.3 5.0 %copy-start.1 = (f32[128]{0:T(128)S(1)}, f32[128]{0:T(128)}, u32[]{:S(2)}) copy-start(f32[128]{0:T(128)} %param.12) | copy-start | bytes 1540
  113.3 5.3 %copy-start.2 = (bf16[128,128]{1,0:T(8,128)(2,1)S(1)}, bf16[128,128]{1,0:T(8,128)(2,1)}, u32[]{:S(2)}) copy-start(bf16[128,128]{1,0:T(8,128)(2,1)} %param.13) | copy-start | bytes 98308
Sparse Core Ops, SparseCore 0:
  14.7 90.1 all-gather.1
where the time goes:
time: 127 us; the launch traced here: 126 us
  waiting for transfers between devices  46 us (36%)
  blocking collectives  38.2 us (30%)
  local copies, waits for them, and re-layouts  16.1 us (13%)
  between operations  13.5 us (11%)
  matrix products  8.52 us (7%)
  other arithmetic  4.15 us (3%)
    all_gather x1, waiting for transfers between devices, on_device(): lax.all_gather(right_terms, 'row', axis=0, tiled=True)  46 us
    all_to_all x1, blocking collectives, on_device(): lax.all_to_all(left_all, 'row', split_axis=1, concat_axis=0, tiled=True)  35.9 us
    all_gather x1, local copies, waits for them, and re-layouts, on_device(): lax.all_gather(right_terms, 'row', axis=0, tiled=True)  8.44 us
    all_to_all x3, local copies, waits for them, and re-layouts, on_device(): lax.all_to_all(left_all, 'row', split_axis=1, concat_axis=0, tiled=True)  5.68 us
    dot_general x1, matrix products, on_device(): jnp.einsum('kic,kjc->ijc', left_need, lax.all_gather(right_terms, 'row',...  4.79 us
  transfers between devices with their start and end apart: 1, of which 1 were waited for; matrix products, arithmetic and copies ran while one was open for 3% of the time, Pallas kernels for 0%

commit v1 on v0

v1 whole, which is shorter than its diff:
```python
import functools
import math

import jax
import jax.numpy as jnp
from jax import lax
from jax.experimental import pallas as pl
from jax.experimental.pallas import tpu as pltpu
from jax.sharding import PartitionSpec as P

TILE = 96
LANES = 128
EPS = 1e-05
VMEM = pl.BlockSpec(memory_space=pltpu.VMEM)
SMEM = pl.BlockSpec(memory_space=pltpu.SMEM)


def steps(at, width, count):
    total = jnp.zeros_like(at)
    for edge in range(1, count):
        total += (at >= edge * width).astype(jnp.int32)
    return total


def sigmoid(values):
    return 0.5 * jnp.tanh(0.5 * values) + 0.5


def keep_of(tile_ref, chain_ref, rows, cols):
    tokens = chain_ref.shape[1]
    tiles = tile_ref.shape[1]
    positions = rows * cols
    at = lax.broadcasted_iota(jnp.int32, (1, positions), 1)
    row = steps(at, cols, rows)
    k = lax.axis_index("row") * rows + row
    i = lax.axis_index("col") * cols + at - row * cols
    token = lax.broadcasted_iota(jnp.int32, (tokens, positions), 0)
    pick = (token == k).astype(jnp.float32) - (token == i).astype(jnp.float32)
    chains = jnp.broadcast_to(chain_ref[...].astype(jnp.bfloat16), (8, tokens))
    apart = jnp.dot(chains, pick.astype(jnp.bfloat16), preferred_element_type=jnp.float32)[:1]
    k_tile = steps(k, TILE, tiles)
    i_tile = steps(i, TILE, tiles)
    tile_vals = jnp.zeros((1, positions), jnp.float32)
    for a in range(tiles):
        for b in range(tiles):
            here = (k_tile == a) & (i_tile == b)
            tile_vals = jnp.where(here, tile_ref[a, b].astype(jnp.float32), tile_vals)
    return jnp.where(apart == 0.0, 1.0, tile_vals)


def project_kernel(
    rows, cols, shares, tile_ref, chain_ref, pair_ref, gain_ref, w_ref, left_ref, right_ref, gate_ref,
    w_t, left_f32, right_f32,
):
    hidden = (w_ref.shape[1] - w_ref.shape[0]) // 4
    own = hidden // shares
    keep = keep_of(tile_ref, chain_ref, rows, cols)
    w_t[...] = w_ref[...].T
    gain = gain_ref[...]
    for group in range(rows * cols // LANES):
        block = pair_ref[group * LANES : (group + 1) * LANES, :].astype(jnp.float32).T
        center = block - jnp.mean(block, axis=0, keepdims=True)
        spread = jnp.mean(center * center, axis=0, keepdims=True)
        normed = (center * lax.rsqrt(spread + EPS) * gain).astype(jnp.bfloat16)
        projected = jnp.dot(w_t[...], normed, preferred_element_type=jnp.float32)
        kept = keep[:, group * LANES : (group + 1) * LANES]
        left = sigmoid(projected[hidden : 2 * hidden]) * projected[:hidden] * kept
        right = sigmoid(projected[3 * hidden : 4 * hidden]) * projected[2 * hidden : 3 * hidden] * kept
        left_f32[:, group * own : (group + 1) * own, :] = left.reshape(shares, own, LANES)
        right_f32[:, group * own : (group + 1) * own, :] = right.reshape(shares, own, LANES)
        gate_ref[group] = sigmoid(projected[4 * hidden :])
    left_ref[...] = left_f32[...].astype(jnp.bfloat16)
    right_ref[...] = right_f32[...].astype(jnp.bfloat16)


def take_channel(ref, channel, own, cols):
    cycle = math.lcm(cols, LANES)
    groups, tokens = cycle // LANES, cycle // cols
    count = ref.shape[0] // (own * groups)
    lanes = [
        ref[pl.ds(group * own + channel, count, stride=own * groups), :] for group in range(groups)
    ]
    found = []
    for token in range(tokens):
        start, pieces = token * cols, []
        while start < (token + 1) * cols:
            group = start // LANES
            end = min((group + 1) * LANES, (token + 1) * cols)
            pieces.append(lanes[group][:, start - group * LANES : end - group * LANES])
            start = end
        found.append(jnp.concatenate(pieces, axis=1).astype(jnp.bfloat16))
    return jnp.concatenate(found, axis=0)


def put_channel(ref, first, held, channel, own, cols):
    cycle = math.lcm(cols, LANES)
    groups, tokens = cycle // LANES, cycle // cols
    count = cols // tokens
    lines = [
        jnp.concatenate(
            [held[piece, pl.ds(token, count, stride=tokens), :] for piece in range(held.shape[0])], axis=1
        )
        for token in range(tokens)
    ]
    for group in range(groups):
        start, pieces = group * LANES, []
        while start < (group + 1) * LANES:
            token = start // cols
            end = min((token + 1) * cols, (group + 1) * LANES)
            pieces.append(lines[token][:, start - token * cols : end - token * cols])
            start = end
        ref[pl.ds(first + group * own + channel, count, stride=own * groups), :] = jnp.concatenate(
            pieces, axis=1
        )


def triangle_kernel(own, cols, left_ref, other_ref, right_ref, mixed_ref, lefts, rights, held, mixed):
    lines = rights.shape[0]
    at = lax.axis_index("col")
    lefts[at] = left_ref[...].astype(jnp.float32).reshape(lines, LANES)
    lefts[1 - at] = other_ref[...].astype(jnp.float32).reshape(lines, LANES)
    rights[...] = right_ref[...].astype(jnp.float32).reshape(lines, LANES)
    for channel in range(own):
        right = take_channel(rights, channel, own, cols)
        for half in range(2):
            left = take_channel(lefts.at[half], channel, own, cols)
            total = lax.dot_general(
                left, right, (((0,), (0,)), ((), ())), preferred_element_type=jnp.float32
            )
            for start in range(0, cols, LANES):
                width = min(LANES, cols - start)
                held[half, start // LANES, :, :width] = total[:, start : start + width]
            put_channel(mixed, half * (lines // 2), held.at[half], channel, own, cols)
    mixed_ref[...] = mixed[...].astype(jnp.bfloat16).reshape(mixed_ref.shape)


def output_kernel(own, mixed_ref, gate_ref, gain_ref, w_ref, update_ref, mixed):
    shares = mixed_ref.shape[0]
    mixed[...] = mixed_ref[...].astype(jnp.float32)
    w_t = w_ref[...].T
    gain = gain_ref[...]
    for group in range(gate_ref.shape[0]):
        block = mixed[:, group * own : (group + 1) * own, :].reshape(shares * own, LANES)
        center = block - jnp.mean(block, axis=0, keepdims=True)
        spread = jnp.mean(center * center, axis=0, keepdims=True)
        normed = (center * lax.rsqrt(spread + EPS) * gain).astype(jnp.bfloat16)
        projected = jnp.dot(w_t, normed, preferred_element_type=jnp.float32)
        update = (gate_ref[group] * projected).T
        update_ref[group * LANES : (group + 1) * LANES, :] = update.astype(jnp.bfloat16)


def on_device(shares, pair, tile_mask, chain_ids, gain_in, w_proj, gain_mid, w_out):
    rows, cols, width = pair.shape
    hidden = w_out.shape[0]
    own = hidden // shares
    positions = rows * cols
    groups = positions // LANES
    lines = groups * own
    message = jax.ShapeDtypeStruct((shares, lines, LANES), jnp.bfloat16)
    params = pltpu.CompilerParams(vmem_limit_bytes=32 * 1024 * 1024)
    left, right, gate = pl.pallas_call(
        functools.partial(project_kernel, rows, cols, shares),
        out_shape=(message, message, jax.ShapeDtypeStruct((groups, width, LANES), jnp.float32)),
        in_specs=[SMEM, VMEM, VMEM, VMEM, VMEM],
        out_specs=(VMEM, VMEM, VMEM),
        scratch_shapes=[
            pltpu.VMEM((w_proj.shape[1], width), jnp.bfloat16),
            pltpu.VMEM((shares, lines, LANES), jnp.float32),
            pltpu.VMEM((shares, lines, LANES), jnp.float32),
        ],
        compiler_params=params,
        name="project",
    )(tile_mask, chain_ids[None, :], pair.reshape(positions, width), gain_in[:, None], w_proj)
    left = lax.all_to_all(left, "row", split_axis=0, concat_axis=0, tiled=True)
    other = lax.ppermute(left, "col", [(0, 1), (1, 0)])
    right = lax.all_to_all(right, "row", split_axis=0, concat_axis=0, tiled=True)
    mixed = pl.pallas_call(
        functools.partial(triangle_kernel, own, cols),
        out_shape=message,
        in_specs=[VMEM, VMEM, VMEM],
        out_specs=VMEM,
        scratch_shapes=[
            pltpu.VMEM((2, shares * lines, LANES), jnp.float32),
            pltpu.VMEM((shares * lines, LANES), jnp.float32),
            pltpu.VMEM((2, pl.cdiv(cols, LANES), cols, LANES), jnp.float32),
            pltpu.VMEM((shares * lines, LANES), jnp.float32),
        ],
        compiler_params=params,
        name="triangle",
    )(left, other, right)
    mixed = lax.all_to_all(mixed, "row", split_axis=0, concat_axis=0, tiled=True)
    update = pl.pallas_call(
        functools.partial(output_kernel, own),
        out_shape=jax.ShapeDtypeStruct((positions, width), jnp.bfloat16),
        in_specs=[VMEM, VMEM, VMEM, VMEM],
        out_specs=VMEM,
        scratch_shapes=[pltpu.VMEM((shares, lines, LANES), jnp.float32)],
        compiler_params=params,
        name="output",
    )(mixed, gate, gain_mid[:, None], w_out)
    return update.reshape(rows, cols, width)


def solution(mesh):
    in_specs = (P(("grp", "row"), "col", None), P("grp", None), P("grp"), P(), P(), P(), P())
    out_specs = P(("grp", "row"), "col", None)
    return jax.shard_map(
        functools.partial(on_device, mesh.shape["row"]),
        mesh=mesh,
        in_specs=in_specs,
        out_specs=out_specs,
        check_vma=False,
    )
```

time: 127 us -> 57.5 us (0.45)
  waiting for transfers between devices: 46 us -> 18.8 us
  blocking collectives: 38.2 us -> 18.8 us
  between operations: 13.5 us -> 0.05 us
  local copies, waits for them, and re-layouts: 16.1 us -> 4.09 us
  matrix products: 8.52 us -> 0 us
  Pallas kernels: 0 us -> 8.15 us
  starting transfers between devices: 0.01 us -> 7.15 us
  other arithmetic: 4.15 us -> 0 us
    all_gather x1 -> x0, waiting for transfers between devices: 46 us -> none  [on_device(): lax.all_gather(right_terms, 'row', axis=0, tiled=True)]
    all_to_all x0 -> x2, waiting for transfers between devices: none -> 18.8 us  [the longest x1 9.8 us: on_device(): lax.all_to_all(right, 'row', split_axis=0, concat_axis=0, tiled=True)]
    all_to_all x1, blocking collectives: 35.9 us -> 18.8 us  [on_device(): left = lax.all_to_all(left, 'row', split_axis=0, concat_axis=0, tiled=True)]
    all_gather x2 -> x0, local copies, waits for them, and re-layouts: 8.85 us -> none  [the longest x1 8.44 us: on_device(): lax.all_gather(right_terms, 'row', axis=0, tiled=True)]
    dot_general x5 -> x0, matrix products: 8.52 us -> none  [the longest x1 4.79 us: on_device(): jnp.einsum('kic,kjc->ijc', left_need, lax.all_gather(right_terms, 'row',...]
    pallas_call x0 -> x3, Pallas kernels: none -> 8.15 us  [the longest x1 4.83 us: on_device(): pl.pallas_call(functools.partial(triangle_kernel, own, cols), out_shape=m...]
    all_to_all x0 -> x2, starting transfers between devices: none -> 7.08 us  [the longest x1 3.54 us: on_device(): lax.all_to_all(right, 'row', split_axis=0, concat_axis=0, tiled=True)]
    all_to_all x3 -> x0, local copies, waits for them, and re-layouts: 5.68 us -> none  [on_device(): lax.all_to_all(left_all, 'row', split_axis=1, concat_axis=0, tiled=True)]
  transfers between devices with their start and end apart: 1 -> 3, of which waited for: 1 -> 2; matrix products, arithmetic and copies ran while one was open for 3% -> 0% of each run, Pallas kernels for 0% -> 0%
where the time goes in v1:
time: 57.5 us; the launch traced here: 57.1 us
  blocking collectives  18.8 us (33%)
  waiting for transfers between devices  18.8 us (33%)
  Pallas kernels  8.15 us (14%)
  starting transfers between devices  7.15 us (12%)
  local copies, waits for them, and re-layouts  4.09 us (7%)
    all_to_all x1, blocking collectives, on_device(): left = lax.all_to_all(left, 'row', split_axis=0, concat_axis=0, tiled=True)  18.8 us
    all_to_all x1, waiting for transfers between devices, on_device(): lax.all_to_all(right, 'row', split_axis=0, concat_axis=0, tiled=True)  9.8 us
    all_to_all x1, waiting for transfers between devices, on_device(): lax.all_to_all(mixed, 'row', split_axis=0, concat_axis=0, tiled=True)  9.03 us
    pallas_call x1, Pallas kernels, on_device(): pl.pallas_call(functools.partial(triangle_kernel, own, cols), out_shape=m...  4.83 us
    unnamed x14, local copies, waits for them, and re-layouts  3.87 us
    all_to_all x1, starting transfers between devices, on_device(): lax.all_to_all(right, 'row', split_axis=0, concat_axis=0, tiled=True)  3.54 us
    all_to_all x1, starting transfers between devices, on_device(): lax.all_to_all(mixed, 'row', split_axis=0, concat_axis=0, tiled=True)  3.54 us
    pallas_call x1, Pallas kernels, on_device(): pl.pallas_call(functools.partial(project_kernel, rows, cols, shares), out...  2.13 us
  transfers between devices with their start and end apart: 3, of which 2 were waited for; matrix products, arithmetic and copies ran while one was open for 0% of the time, Pallas kernels for 0%

profile of v1, /device:TPU:0, one launch (start us, length us, event | category | flops | bytes accessed | tf_op | source)
XLA Modules:
  0.0 57.1 jit_solution(1511295419876254982)
XLA Ops:
  0.0 0.0 copy-start.5
  0.0 0.7 %copy-done.5 = f32[128]{0:T(128)S(1)} copy-done((f32[128]{0:T(128)S(1)}, f32[128]{0:T(128)}, u32[]{:S(2)}) %copy-start.5) | copy-done | bytes 536
  0.7 0.1 copy.8.gain_ref
  0.8 0.0 copy-start.4
  0.8 0.0 copy-start.3
  0.8 0.7 %copy-done.4 = s32[192]{0:T(256)S(1)} copy-done((s32[192]{0:T(256)S(1)}, s32[192]{0:T(256)}, u32[]{:S(2)}) %copy-start.4) | copy-done | bytes 792
  1.4 0.0 copy-done.3
  1.5 0.0 copy-start
  1.5 1.0 %copy-done = bf16[12,96,128]{2,1,0:T(8,128)(2,1)S(1)} copy-done((bf16[12,96,128]{2,1,0:T(8,128)(2,1)S(1)}, bf16[12,96,128]{2,1,0:T(8,128)(2,1)}, u32[]{:S(2)}) %copy-start) | copy-done | bytes 294936
  2.4 0.0 copy-start.1
  2.4 0.9 %copy-done.1 = bf16[128,640]{1,0:T(8,128)(2,1)S(1)} copy-done((bf16[128,640]{1,0:T(8,128)(2,1)S(1)}, bf16[128,640]{1,0:T(8,128)(2,1)}, u32[]{:S(2)}) %copy-start.1) | copy-done | bytes 163864
  3.3 2.1 %project.1 = (bf16[16,72,128]{2,1,0:T(8,128)(2,1)S(1)}, bf16[16,72,128]{2,1,0:T(8,128)(2,1)}, f32[9,128,128]{2,1,0:T(8,128)S(1)}) custom-call(s32[2,2]{1,0:T(2,128)S(1)} %copy-done.3, s32[1,192]{1,0:T(1,128)S(1)} %bitcast.6, bf16[1152,128]{1,0:T(8,128)(2,1)S(1)} %bitcast.5, f32[128,1]{1,0:T(8,128)S(1)} %copy.8.gain_ref, bf16[128,640]{1,0:T(8,128)(2,1)S(1)} %copy-done.1), custom_call_target="tpu_custom_call" | custom-call | tf_op jit(solution)/shard_map/project/pallas_call | solution.py:161
  5.5 18.8 %all_to_all.15.left_ref = bf16[16,72,128]{2,1,0:T(8,128)(2,1)S(1)} all-to-all(bf16[16,72,128]{2,1,0:T(8,128)(2,1)S(1)} %get-tuple-element.8), channel_id=1, replica_groups=mesh['grp'=1,'row'=16,'col'=2] {'row'}, dimensions={0} | all-to-all | bytes 589824 | tf_op jit(solution)/shard_map/all_to_all | solution.py:174
  24.3 3.5 %all-to-all-start.1 = ((bf16[16,72,128]{2,1,0:T(8,128)(2,1)}), bf16[16,72,128]{2,1,0:T(8,128)(2,1)S(1)}, u32[]{:S(2)}, u32[]{:S(2)}) async-start(bf16[16,72,128]{2,1,0:T(8,128)(2,1)} %get-tuple-element.9), calls=%async_computation.1 | async-start | bytes 589824 | tf_op jit(solution)/shard_map/all_to_all | solution.py:176
  27.8 0.1 collective-permute-start
  27.9 9.8 %all-to-all-done.1.right_ref = bf16[16,72,128]{2,1,0:T(8,128)(2,1)S(1)} async-done(((bf16[16,72,128]{2,1,0:T(8,128)(2,1)}), bf16[16,72,128]{2,1,0:T(8,128)(2,1)S(1)}, u32[]{:S(2)}, u32[]{:S(2)}) %all-to-all-start.1) | async-done | bytes 294944 | tf_op jit(solution)/shard_map/all_to_all | solution.py:176
  37.7 0.0 collective-permute-done.other_ref
  37.7 4.8 %triangle.1 = bf16[16,72,128]{2,1,0:T(8,128)(2,1)} custom-call(bf16[16,72,128]{2,1,0:T(8,128)(2,1)S(1)} %all_to_all.15.left_ref, bf16[16,72,128]{2,1,0:T(8,128)(2,1)S(1)} %collective-permute-done.other_ref, bf16[16,72,128]{2,1,0:T(8,128)(2,1)S(1)} %all-to-all-done.1.right_ref), custom_call_target="tpu_custom_call" | custom-call | tf_op jit(solution)/shard_map/triangle/pallas_call | solution.py:177
  42.5 3.5 %all-to-all-start.2 = ((bf16[16,72,128]{2,1,0:T(8,128)(2,1)}), bf16[16,72,128]{2,1,0:T(8,128)(2,1)S(1)}, u32[]{:S(2)}, u32[]{:S(2)}) async-start(bf16[16,72,128]{2,1,0:T(8,128)(2,1)} %triangle.1), calls=%async_computation.2 | async-start | bytes 589824 | tf_op jit(solution)/shard_map/all_to_all | solution.py:191
  46.1 0.0 copy-start.6
  46.1 0.6 %copy-done.6 = f32[128]{0:T(128)S(1)} copy-done((f32[128]{0:T(128)S(1)}, f32[128]{0:T(128)}, u32[]{:S(2)}) %copy-start.6) | copy-done | bytes 536
  46.7 0.0 copy-start.2
  46.7 0.1 copy.9.gain_ref
  46.8 9.0 %all-to-all-done.2.mixed_ref = bf16[16,72,128]{2,1,0:T(8,128)(2,1)S(1)} async-done(((bf16[16,72,128]{2,1,0:T(8,128)(2,1)}), bf16[16,72,128]{2,1,0:T(8,128)(2,1)S(1)}, u32[]{:S(2)}, u32[]{:S(2)}) %all-to-all-start.2) | async-done | bytes 294944 | tf_op jit(solution)/shard_map/all_to_all | solution.py:191
  55.9 0.0 copy-done.2
  55.9 1.2 %output.1 = bf16[1152,128]{1,0:T(8,128)(2,1)} custom-call(bf16[16,72,128]{2,1,0:T(8,128)(2,1)S(1)} %all-to-all-done.2.mixed_ref, f32[9,128,128]{2,1,0:T(8,128)S(1)} %get-tuple-element.10.gate_ref, f32[128,1]{1,0:T(8,128)S(1)} %copy.9.gain_ref, bf16[128,128]{1,0:T(8,128)(2,1)S(1)} %copy-done.2), custom_call_target="tpu_custom_call" | custom-call | tf_op jit(solution)/shard_map/output/pallas_call | solution.py:192
Async XLA Ops:
  0.0 0.7 %copy-start.5 = (f32[128]{0:T(128)S(1)}, f32[128]{0:T(128)}, u32[]{:S(2)}) copy-start(f32[128]{0:T(128)} %param.10) | copy-start | bytes 1540
  0.8 0.7 %copy-start.4 = (s32[192]{0:T(256)S(1)}, s32[192]{0:T(256)}, u32[]{:S(2)}) copy-start(s32[192]{0:T(256)} %param.9) | copy-start | bytes 2308
  0.8 0.7 %copy-start.3 = (s32[2,2]{1,0:T(2,128)S(1)}, s32[2,2]{1,0:T(2,128)}, u32[]{:S(2)}) copy-start(s32[2,2]{1,0:T(2,128)} %tile_ref.1) | copy-start | bytes 52
  1.5 1.0 %copy-start = (bf16[12,96,128]{2,1,0:T(8,128)(2,1)S(1)}, bf16[12,96,128]{2,1,0:T(8,128)(2,1)}, u32[]{:S(2)}) copy-start(bf16[12,96,128]{2,1,0:T(8,128)(2,1)} %param.7) | copy-start | bytes 884740
  2.4 0.9 %copy-start.1 = (bf16[128,640]{1,0:T(8,128)(2,1)S(1)}, bf16[128,640]{1,0:T(8,128)(2,1)}, u32[]{:S(2)}) copy-start(bf16[128,640]{1,0:T(8,128)(2,1)} %w_ref.2) | copy-start | bytes 491524
  24.3 13.4 %all-to-all-start.1 = ((bf16[16,72,128]{2,1,0:T(8,128)(2,1)}), bf16[16,72,128]{2,1,0:T(8,128)(2,1)S(1)}, u32[]{:S(2)}, u32[]{:S(2)}) async-start(bf16[16,72,128]{2,1,0:T(8,128)(2,1)} %get-tuple-element.9), calls=%async_computation.1 | async-start | bytes 589824 | tf_op jit(solution)/shard_map/all_to_all | solution.py:176
  27.8 9.9 %collective-permute-start = (bf16[16,72,128]{2,1,0:T(8,128)(2,1)S(1)}, bf16[16,72,128]{2,1,0:T(8,128)(2,1)S(1)}, u32[]{:S(2)}, u32[]{:S(2)}) collective-permute-start(bf16[16,72,128]{2,1,0:T(8,128)(2,1)S(1)} %all_to_all.15.left_ref), channel_id=1, source_target_pairs={{0,1},{1,0},{2,3},{3,2},{4,5},{5,4},{6,7},{7,6},{8,9},{9,8},{10,11... | collective-permute-start | bytes 884744 | tf_op jit(solution)/shard_map/ppermute | solution.py:175
  42.5 13.4 %all-to-all-start.2 = ((bf16[16,72,128]{2,1,0:T(8,128)(2,1)}), bf16[16,72,128]{2,1,0:T(8,128)(2,1)S(1)}, u32[]{:S(2)}, u32[]{:S(2)}) async-start(bf16[16,72,128]{2,1,0:T(8,128)(2,1)} %triangle.1), calls=%async_computation.2 | async-start | bytes 589824 | tf_op jit(solution)/shard_map/all_to_all | solution.py:191
  46.1 0.7 %copy-start.6 = (f32[128]{0:T(128)S(1)}, f32[128]{0:T(128)}, u32[]{:S(2)}) copy-start(f32[128]{0:T(128)} %param.12) | copy-start | bytes 1540
  46.7 9.2 %copy-start.2 = (bf16[128,128]{1,0:T(8,128)(2,1)S(1)}, bf16[128,128]{1,0:T(8,128)(2,1)}, u32[]{:S(2)}) copy-start(bf16[128,128]{1,0:T(8,128)(2,1)} %w_ref.3) | copy-start | bytes 98308

commit v2 on v1

--- a/solution.py
+++ b/solution.py
@@ -12,6 +12,7 @@
 LANES = 128
 EPS = 1e-05
 VMEM = pl.BlockSpec(memory_space=pltpu.VMEM)
+HBM = pl.BlockSpec(memory_space=pltpu.HBM)
 SMEM = pl.BlockSpec(memory_space=pltpu.SMEM)
 
 
@@ -48,15 +49,27 @@
     return jnp.where(apart == 0.0, 1.0, tile_vals)
 
 
-def project_kernel(
-    rows, cols, shares, tile_ref, chain_ref, pair_ref, gain_ref, w_ref, left_ref, right_ref, gate_ref,
-    w_t, left_f32, right_f32,
-):
+def column(row):
+    return jnp.broadcast_to(row, (8, row.shape[1])).T[:, :1]
+
+
+def project_kernel(rows, cols, shares, *refs):
+    tile_ref, chain_ref, pair_hbm, gain_hbm, w_hbm = refs[:5]
+    left_refs, right_refs = refs[5 : 5 + shares], refs[5 + shares : 5 + 2 * shares]
+    gate_ref, pair_ref, gain_ref, w_ref, w_t, left_f32, right_f32, sems = refs[5 + 2 * shares :]
+    copies = [
+        pltpu.make_async_copy(src, dst, sems.at[at])
+        for at, (src, dst) in enumerate(((w_hbm, w_ref), (gain_hbm, gain_ref), (pair_hbm, pair_ref)))
+    ]
+    for copy in copies:
+        copy.start()
     hidden = (w_ref.shape[1] - w_ref.shape[0]) // 4
     own = hidden // shares
     keep = keep_of(tile_ref, chain_ref, rows, cols)
+    for copy in copies:
+        copy.wait()
     w_t[...] = w_ref[...].T
-    gain = gain_ref[...]
+    gain = column(gain_ref[...])
     for group in range(rows * cols // LANES):
         block = pair_ref[group * LANES : (group + 1) * LANES, :].astype(jnp.float32).T
         center = block - jnp.mean(block, axis=0, keepdims=True)
@@ -69,8 +82,10 @@
         left_f32[:, group * own : (group + 1) * own, :] = left.reshape(shares, own, LANES)
         right_f32[:, group * own : (group + 1) * own, :] = right.reshape(shares, own, LANES)
         gate_ref[group] = sigmoid(projected[4 * hidden :])
-    left_ref[...] = left_f32[...].astype(jnp.bfloat16)
-    right_ref[...] = right_f32[...].astype(jnp.bfloat16)
+    at = lax.axis_index("row")
+    for step in range(shares):
+        left_refs[step][...] = left_f32[at ^ step].astype(jnp.bfloat16)
+        right_refs[step][...] = right_f32[at ^ step].astype(jnp.bfloat16)
 
 
 def take_channel(ref, channel, own, cols):
@@ -114,12 +129,21 @@
         )
 
 
-def triangle_kernel(own, cols, left_ref, other_ref, right_ref, mixed_ref, lefts, rights, held, mixed):
+def collect_kernel(*refs):
+    for step, ref in enumerate(refs[:-1]):
+        refs[-1][step] = ref[...]
+
+
+def triangle_kernel(own, cols, shares, left_ref, other_ref, *refs):
+    right_refs, mixed_refs = refs[:shares], refs[shares : 2 * shares]
+    lefts, rights, held, mixed = refs[2 * shares :]
     lines = rights.shape[0]
     at = lax.axis_index("col")
     lefts[at] = left_ref[...].astype(jnp.float32).reshape(lines, LANES)
     lefts[1 - at] = other_ref[...].astype(jnp.float32).reshape(lines, LANES)
-    rights[...] = right_ref[...].astype(jnp.float32).reshape(lines, LANES)
+    each = lines // shares
+    for step in range(shares):
+        rights[step * each : (step + 1) * each, :] = right_refs[step][...].astype(jnp.float32)
     for channel in range(own):
         right = take_channel(rights, channel, own, cols)
         for half in range(2):
@@ -131,14 +155,19 @@
                 width = min(LANES, cols - start)
                 held[half, start // LANES, :, :width] = total[:, start : start + width]
             put_channel(mixed, half * (lines // 2), held.at[half], channel, own, cols)
-    mixed_ref[...] = mixed[...].astype(jnp.bfloat16).reshape(mixed_ref.shape)
-
-
-def output_kernel(own, mixed_ref, gate_ref, gain_ref, w_ref, update_ref, mixed):
-    shares = mixed_ref.shape[0]
-    mixed[...] = mixed_ref[...].astype(jnp.float32)
+    at = lax.axis_index("row")
+    for step in range(shares):
+        first = pl.multiple_of((at ^ step) * each, 8)
+        mixed_refs[step][...] = mixed[pl.ds(first, each), :].astype(jnp.bfloat16)
+
+
+def output_kernel(own, shares, *refs):
+    gate_ref, gain_ref, w_ref, update_ref, mixed = refs[shares:]
+    at = lax.axis_index("row")
+    for step in range(shares):
+        mixed[at ^ step] = refs[step][...].astype(jnp.float32)
     w_t = w_ref[...].T
-    gain = gain_ref[...]
+    gain = column(gain_ref[...])
     for group in range(gate_ref.shape[0]):
         block = mixed[:, group * own : (group + 1) * own, :].reshape(shares * own, LANES)
         center = block - jnp.mean(block, axis=0, keepdims=True)
@@ -149,6 +178,14 @@
         update_ref[group * LANES : (group + 1) * LANES, :] = update.astype(jnp.bfloat16)
 
 
+def exchange(blocks):
+    shares = len(blocks)
+    return [blocks[0]] + [
+        lax.ppermute(blocks[step], "row", [(src, src ^ step) for src in range(shares)])
+        for step in range(1, shares)
+    ]
+
+
 def on_device(shares, pair, tile_mask, chain_ids, gain_in, w_proj, gain_mid, w_out):
     rows, cols, width = pair.shape
     hidden = w_out.shape[0]
@@ -156,29 +193,42 @@
     positions = rows * cols
     groups = positions // LANES
     lines = groups * own
-    message = jax.ShapeDtypeStruct((shares, lines, LANES), jnp.bfloat16)
+    message = jax.ShapeDtypeStruct((lines, LANES), jnp.bfloat16)
     params = pltpu.CompilerParams(vmem_limit_bytes=32 * 1024 * 1024)
-    left, right, gate = pl.pallas_call(
+    outs = pl.pallas_call(
         functools.partial(project_kernel, rows, cols, shares),
-        out_shape=(message, message, jax.ShapeDtypeStruct((groups, width, LANES), jnp.float32)),
-        in_specs=[SMEM, VMEM, VMEM, VMEM, VMEM],
-        out_specs=(VMEM, VMEM, VMEM),
+        out_shape=[message] * (2 * shares)
+        + [jax.ShapeDtypeStruct((groups, width, LANES), jnp.float32)],
+        in_specs=[SMEM, VMEM, HBM, HBM, HBM],
+        out_specs=[VMEM] * (2 * shares + 1),
         scratch_shapes=[
+            pltpu.VMEM((positions, width), jnp.bfloat16),
+            pltpu.VMEM((1, width), jnp.float32),
+            pltpu.VMEM(w_proj.shape, jnp.bfloat16),
             pltpu.VMEM((w_proj.shape[1], width), jnp.bfloat16),
             pltpu.VMEM((shares, lines, LANES), jnp.float32),
             pltpu.VMEM((shares, lines, LANES), jnp.float32),
+            pltpu.SemaphoreType.DMA((3,)),
         ],
         compiler_params=params,
         name="project",
-    )(tile_mask, chain_ids[None, :], pair.reshape(positions, width), gain_in[:, None], w_proj)
-    left = lax.all_to_all(left, "row", split_axis=0, concat_axis=0, tiled=True)
+    )(tile_mask, chain_ids[None, :], pair.reshape(positions, width), gain_in[None, :], w_proj)
+    lefts, rights, gate = outs[:shares], outs[shares : 2 * shares], outs[2 * shares]
+    lefts, rights = exchange(lefts), exchange(rights)
+    left = pl.pallas_call(
+        collect_kernel,
+        out_shape=jax.ShapeDtypeStruct((shares, lines, LANES), jnp.bfloat16),
+        in_specs=[VMEM] * shares,
+        out_specs=VMEM,
+        compiler_params=params,
+        name="collect",
+    )(*lefts)
     other = lax.ppermute(left, "col", [(0, 1), (1, 0)])
-    right = lax.all_to_all(right, "row", split_axis=0, concat_axis=0, tiled=True)
     mixed = pl.pallas_call(
-        functools.partial(triangle_kernel, own, cols),
-        out_shape=message,
-        in_specs=[VMEM, VMEM, VMEM],
-        out_specs=VMEM,
+        functools.partial(triangle_kernel, own, cols, shares),
+        out_shape=[message] * shares,
+        in_specs=[VMEM] * (2 + shares),
+        out_specs=[VMEM] * shares,
         scratch_shapes=[
             pltpu.VMEM((2, shares * lines, LANES), jnp.float32),
             pltpu.VMEM((shares * lines, LANES), jnp.float32),
@@ -187,17 +237,17 @@
         ],
         compiler_params=params,
         name="triangle",
-    )(left, other, right)
-    mixed = lax.all_to_all(mixed, "row", split_axis=0, concat_axis=0, tiled=True)
+    )(left, other, *rights)
+    mixed = exchange(mixed)
     update = pl.pallas_call(
-        functools.partial(output_kernel, own),
+        functools.partial(output_kernel, own, shares),
         out_shape=jax.ShapeDtypeStruct((positions, width), jnp.bfloat16),
-        in_specs=[VMEM, VMEM, VMEM, VMEM],
+        in_specs=[VMEM] * (shares + 3),
         out_specs=VMEM,
         scratch_shapes=[pltpu.VMEM((shares, lines, LANES), jnp.float32)],
         compiler_params=params,
         name="output",
-    )(mixed, gate, gain_mid[:, None], w_out)
+    )(*mixed, gate, gain_mid[None, :], w_out)
     return update.reshape(rows, cols, width)
 
 

time: 57.5 us -> 108 us (1.88)
  starting transfers between devices: 7.15 us -> 80.7 us
  blocking collectives: 18.8 us -> 0 us
  waiting for transfers between devices: 18.8 us -> 16.8 us
    ppermute x0 -> x45, starting transfers between devices: none -> 80.6 us  [exchange(): lax.ppermute(blocks[step], 'row', [(src, src ^ step) for src in range(sha...]
    all_to_all x2 -> x0, waiting for transfers between devices: 18.8 us -> none  [the longest x1 9.8 us: on_device(): lax.all_to_all(right, 'row', split_axis=0, concat_axis=0, tiled=True)]
    all_to_all x1 -> x0, blocking collectives: 18.8 us -> none  [on_device(): left = lax.all_to_all(left, 'row', split_axis=0, concat_axis=0, tiled=True)]
    ppermute x0 -> x45, waiting for transfers between devices: none -> 16.8 us  [exchange(): lax.ppermute(blocks[step], 'row', [(src, src ^ step) for src in range(sha...]
    all_to_all x2 -> x0, starting transfers between devices: 7.08 us -> none  [the longest x1 3.54 us: on_device(): lax.all_to_all(right, 'row', split_axis=0, concat_axis=0, tiled=True)]
    pallas_call x2 -> x3, Pallas kernels: 6.02 us -> 5.41 us  [the longest x1 4.12 us: on_device(): pl.pallas_call(functools.partial(triangle_kernel, own, cols, shares), out...]
  transfers between devices with their start and end apart: 3 -> 46, of which waited for: 2 -> 9; matrix products, arithmetic and copies ran while one was open for 0% -> 0% of each run, Pallas kernels for 0% -> 0%
where the time goes in v2:
time: 108 us
  starting transfers between devices  80.7 us (75%)
  waiting for transfers between devices  16.8 us (16%)
  Pallas kernels  7.43 us (7%)
  local copies, waits for them, and re-layouts  3.23 us (3%)
    ppermute x45, starting transfers between devices, exchange(): lax.ppermute(blocks[step], 'row', [(src, src ^ step) for src in range(sha...  80.6 us
    ppermute x45, waiting for transfers between devices, exchange(): lax.ppermute(blocks[step], 'row', [(src, src ^ step) for src in range(sha...  16.8 us
    pallas_call x1, Pallas kernels, on_device(): pl.pallas_call(functools.partial(triangle_kernel, own, cols, shares), out...  4.12 us
    unnamed x14, local copies, waits for them, and re-layouts  3.23 us
  transfers between devices with their start and end apart: 46, of which 9 were waited for; matrix products, arithmetic and copies ran while one was open for 0% of the time, Pallas kernels for 0%

profile of v2, /device:TPU:0, one launch (start us, length us, event | category | flops | bytes accessed | tf_op | source)
XLA Modules:
  0.0 108.2 jit_solution(7837452741166377662)
XLA Ops:
  2.6 2.0 %project.1 = (bf16[72,128]{1,0:T(8,128)(2,1)S(1)}, bf16[72,128]{1,0:T(8,128)(2,1)S(1)}, bf16[72,128]{1,0:T(8,128)(2,1)S(1)}, bf16[72,128]{1,0:T(8,128)(2,1)S(1)}...) custom-call(s32[2,2]{1,0:T(2,128)S(1)} %copy-done.3, ...), custom_call_target="tpu_custom_call" | custom-call | tf_op jit(solution)/shard_map/project/pallas_call | solution.py:198
  4.6 3.0 %collective-permute-start = (bf16[72,128]{1,0:T(8,128)(2,1)S(1)}, bf16[72,128]{1,0:T(8,128)(2,1)S(1)}, u32[]{:S(2)}, u32[]{:S(2)}) collective-permute-start(bf16[72,128]{1,0:T(8,128)(2,1)S(1)} %get-tuple-element.55), channel_id=1, source_target_pairs={{0,2},{2,0},{4,6},{6,4},{8,10},{10,8},{12,14},{14,12},{16,18},{18,... | collective-permute-start | bytes 55304 | tf_op jit(solution)/shard_map/ppermute | solution.py:184
  7.6 1.5 %collective-permute-start.1 = (bf16[72,128]{1,0:T(8,128)(2,1)S(1)}, bf16[72,128]{1,0:T(8,128)(2,1)S(1)}, u32[]{:S(2)}, u32[]{:S(2)}) collective-permute-start(bf16[72,128]{1,0:T(8,128)(2,1)S(1)} %get-tuple-element.56), channel_id=1, source_target_pairs={{0,4},{2,6},{4,0},{6,2},{8,12},{10,14},{12,8},{14,10},{16,20},{18,... | collective-permute-start | bytes 55304 | tf_op jit(solution)/shard_map/ppermute | solution.py:184
  9.2 2.0 %collective-permute-start.3 = (bf16[72,128]{1,0:T(8,128)(2,1)S(1)}, bf16[72,128]{1,0:T(8,128)(2,1)S(1)}, u32[]{:S(2)}, u32[]{:S(2)}) collective-permute-start(bf16[72,128]{1,0:T(8,128)(2,1)S(1)} %get-tuple-element.58), channel_id=1, source_target_pairs={{0,8},{2,10},{4,12},{6,14},{8,0},{10,2},{12,4},{14,6},{16,24},{18,... | collective-permute-start | bytes 55304 | tf_op jit(solution)/shard_map/ppermute | solution.py:184
  11.2 1.4 %collective-permute-start.4 = (bf16[72,128]{1,0:T(8,128)(2,1)S(1)}, bf16[72,128]{1,0:T(8,128)(2,1)S(1)}, u32[]{:S(2)}, u32[]{:S(2)}) collective-permute-start(bf16[72,128]{1,0:T(8,128)(2,1)S(1)} %get-tuple-element.59), channel_id=1, source_target_pairs={{0,10},{2,8},{4,14},{6,12},{8,2},{10,0},{12,6},{14,4},{16,26},{18,... | collective-permute-start | bytes 55304 | tf_op jit(solution)/shard_map/ppermute | solution.py:184
  12.6 2.5 %collective-permute-start.5 = (bf16[72,128]{1,0:T(8,128)(2,1)S(1)}, bf16[72,128]{1,0:T(8,128)(2,1)S(1)}, u32[]{:S(2)}, u32[]{:S(2)}) collective-permute-start(bf16[72,128]{1,0:T(8,128)(2,1)S(1)} %get-tuple-element.60), channel_id=1, source_target_pairs={{0,12},{2,14},{4,8},{6,10},{8,4},{10,6},{12,0},{14,2},{16,28},{18,... | collective-permute-start | bytes 55304 | tf_op jit(solution)/shard_map/ppermute | solution.py:184
  15.2 2.9 %collective-permute-start.7 = (bf16[72,128]{1,0:T(8,128)(2,1)S(1)}, bf16[72,128]{1,0:T(8,128)(2,1)S(1)}, u32[]{:S(2)}, u32[]{:S(2)}) collective-permute-start(bf16[72,128]{1,0:T(8,128)(2,1)S(1)} %get-tuple-element.62), channel_id=1, source_target_pairs={{0,16},{2,18},{4,20},{6,22},{8,24},{10,26},{12,28},{14,30},{16,0},... | collective-permute-start | bytes 55304 | tf_op jit(solution)/shard_map/ppermute | solution.py:184
  18.1 1.3 %collective-permute-start.8 = (bf16[72,128]{1,0:T(8,128)(2,1)S(1)}, bf16[72,128]{1,0:T(8,128)(2,1)S(1)}, u32[]{:S(2)}, u32[]{:S(2)}) collective-permute-start(bf16[72,128]{1,0:T(8,128)(2,1)S(1)} %get-tuple-element.63), channel_id=1, source_target_pairs={{0,18},{2,16},{4,22},{6,20},{8,26},{10,24},{12,30},{14,28},{16,2},... | collective-permute-start | bytes 55304 | tf_op jit(solution)/shard_map/ppermute | solution.py:184
  19.3 3.5 %collective-permute-start.9 = (bf16[72,128]{1,0:T(8,128)(2,1)S(1)}, bf16[72,128]{1,0:T(8,128)(2,1)S(1)}, u32[]{:S(2)}, u32[]{:S(2)}) collective-permute-start(bf16[72,128]{1,0:T(8,128)(2,1)S(1)} %get-tuple-element.64), channel_id=1, source_target_pairs={{0,20},{2,22},{4,16},{6,18},{8,28},{10,30},{12,24},{14,26},{16,4},... | collective-permute-start | bytes 55304 | tf_op jit(solution)/shard_map/ppermute | solution.py:184
  22.9 3.8 %collective-permute-start.11 = (bf16[72,128]{1,0:T(8,128)(2,1)S(1)}, bf16[72,128]{1,0:T(8,128)(2,1)S(1)}, u32[]{:S(2)}, u32[]{:S(2)}) collective-permute-start(bf16[72,128]{1,0:T(8,128)(2,1)S(1)} %get-tuple-element.66), channel_id=1, source_target_pairs={{0,24},{2,26},{4,28},{6,30},{8,16},{10,18},{12,20},{14,22},{16,8},... | collective-permute-start | bytes 55304 | tf_op jit(solution)/shard_map/ppermute | solution.py:184
  27.9 4.6 %collective-permute-start.13 = (bf16[72,128]{1,0:T(8,128)(2,1)S(1)}, bf16[72,128]{1,0:T(8,128)(2,1)S(1)}, u32[]{:S(2)}, u32[]{:S(2)}) collective-permute-start(bf16[72,128]{1,0:T(8,128)(2,1)S(1)} %get-tuple-element.68), channel_id=1, source_target_pairs={{0,28},{2,30},{4,24},{6,26},{8,20},{10,22},{12,16},{14,18},{16,12}... | collective-permute-start | bytes 55304 | tf_op jit(solution)/shard_map/ppermute | solution.py:184
  34.4 5.4 %collective-permute-done.14.refs_15_ = bf16[72,128]{1,0:T(8,128)(2,1)S(1)} collective-permute-done((bf16[72,128]{1,0:T(8,128)(2,1)S(1)}, bf16[72,128]{1,0:T(8,128)(2,1)S(1)}, u32[]{:S(2)}, u32[]{:S(2)}) %collective-permute-start.14) | collective-permute-done | bytes 18464 | tf_op jit(solution)/shard_map/ppermute | solution.py:184
  41.0 2.5 %collective-permute-start.18 = (bf16[72,128]{1,0:T(8,128)(2,1)S(1)}, bf16[72,128]{1,0:T(8,128)(2,1)S(1)}, u32[]{:S(2)}, u32[]{:S(2)}) collective-permute-start(bf16[72,128]{1,0:T(8,128)(2,1)S(1)} %get-tuple-element.73), channel_id=1, source_target_pairs={{0,6},{2,4},{4,2},{6,0},{8,14},{10,12},{12,10},{14,8},{16,22},{18,... | collective-permute-start | bytes 55304 | tf_op jit(solution)/shard_map/ppermute | solution.py:184
  43.8 1.7 %collective-permute-start.20 = (bf16[72,128]{1,0:T(8,128)(2,1)S(1)}, bf16[72,128]{1,0:T(8,128)(2,1)S(1)}, u32[]{:S(2)}, u32[]{:S(2)}) collective-permute-start(bf16[72,128]{1,0:T(8,128)(2,1)S(1)} %get-tuple-element.75), channel_id=1, source_target_pairs={{0,10},{2,8},{4,14},{6,12},{8,2},{10,0},{12,6},{14,4},{16,26},{18,... | collective-permute-start | bytes 55304 | tf_op jit(solution)/shard_map/ppermute | solution.py:184
  45.7 3.7 %collective-permute-start.22 = (bf16[72,128]{1,0:T(8,128)(2,1)S(1)}, bf16[72,128]{1,0:T(8,128)(2,1)S(1)}, u32[]{:S(2)}, u32[]{:S(2)}) collective-permute-start(bf16[72,128]{1,0:T(8,128)(2,1)S(1)} %get-tuple-element.77), channel_id=1, source_target_pairs={{0,14},{2,12},{4,10},{6,8},{8,6},{10,4},{12,2},{14,0},{16,30},{18,... | collective-permute-start | bytes 55304 | tf_op jit(solution)/shard_map/ppermute | solution.py:184
  49.4 2.9 %collective-permute-start.24 = (bf16[72,128]{1,0:T(8,128)(2,1)S(1)}, bf16[72,128]{1,0:T(8,128)(2,1)S(1)}, u32[]{:S(2)}, u32[]{:S(2)}) collective-permute-start(bf16[72,128]{1,0:T(8,128)(2,1)S(1)} %get-tuple-element.79), channel_id=1, source_target_pairs={{0,18},{2,16},{4,22},{6,20},{8,26},{10,24},{12,30},{14,28},{16,2},... | collective-permute-start | bytes 55304 | tf_op jit(solution)/shard_map/ppermute | solution.py:184
  52.3 4.7 %collective-permute-start.26 = (bf16[72,128]{1,0:T(8,128)(2,1)S(1)}, bf16[72,128]{1,0:T(8,128)(2,1)S(1)}, u32[]{:S(2)}, u32[]{:S(2)}) collective-permute-start(bf16[72,128]{1,0:T(8,128)(2,1)S(1)} %get-tuple-element.81), channel_id=1, source_target_pairs={{0,22},{2,20},{4,18},{6,16},{8,30},{10,28},{12,26},{14,24},{16,6},... | collective-permute-start | bytes 55304 | tf_op jit(solution)/shard_map/ppermute | solution.py:184
  57.3 3.5 %collective-permute-start.28 = (bf16[72,128]{1,0:T(8,128)(2,1)S(1)}, bf16[72,128]{1,0:T(8,128)(2,1)S(1)}, u32[]{:S(2)}, u32[]{:S(2)}) collective-permute-start(bf16[72,128]{1,0:T(8,128)(2,1)S(1)} %get-tuple-element.83), channel_id=1, source_target_pairs={{0,26},{2,24},{4,30},{6,28},{8,18},{10,16},{12,22},{14,20},{16,10}... | collective-permute-start | bytes 55304 | tf_op jit(solution)/shard_map/ppermute | solution.py:184
  61.1 5.4 %collective-permute-start.30 = (bf16[72,128]{1,0:T(8,128)(2,1)S(1)}, bf16[72,128]{1,0:T(8,128)(2,1)S(1)}, u32[]{:S(2)}, u32[]{:S(2)}) collective-permute-start(bf16[72,128]{1,0:T(8,128)(2,1)S(1)} %get-tuple-element.85), channel_id=1, source_target_pairs={{0,30},{2,28},{4,26},{6,24},{8,22},{10,20},{12,18},{14,16},{16,14}... | collective-permute-start | bytes 55304 | tf_op jit(solution)/shard_map/ppermute | solution.py:184
  68.4 4.1 %triangle.1 = (bf16[72,128]{1,0:T(8,128)(2,1)S(1)}, bf16[72,128]{1,0:T(8,128)(2,1)S(1)}, bf16[72,128]{1,0:T(8,128)(2,1)S(1)}, bf16[72,128]{1,0:T(8,128)(2,1)S(1)...) custom-call(bf16[16,72,128]{2,1,0:T(8,128)(2,1)S(1)} %collect.1.left, ...), custom_call_target="tpu_custom_call" | custom-call | tf_op jit(solution)/shard_map/triangle/pallas_call | solution.py:227
  72.6 1.6 %collective-permute-start.31 = (bf16[72,128]{1,0:T(8,128)(2,1)S(1)}, bf16[72,128]{1,0:T(8,128)(2,1)S(1)}, u32[]{:S(2)}, u32[]{:S(2)}) collective-permute-start(bf16[72,128]{1,0:T(8,128)(2,1)S(1)} %get-tuple-element.87), channel_id=1, source_target_pairs={{0,2},{2,0},{4,6},{6,4},{8,10},{10,8},{12,14},{14,12},{16,18},{18,... | collective-permute-start | bytes 55304 | tf_op jit(solution)/shard_map/ppermute | solution.py:184
  74.2 1.5 %collective-permute-start.32 = (bf16[72,128]{1,0:T(8,128)(2,1)S(1)}, bf16[72,128]{1,0:T(8,128)(2,1)S(1)}, u32[]{:S(2)}, u32[]{:S(2)}) collective-permute-start(bf16[72,128]{1,0:T(8,128)(2,1)S(1)} %get-tuple-element.88), channel_id=1, source_target_pairs={{0,4},{2,6},{4,0},{6,2},{8,12},{10,14},{12,8},{14,10},{16,20},{18,... | collective-permute-start | bytes 55304 | tf_op jit(solution)/shard_map/ppermute | solution.py:184
  76.1 3.0 %collective-permute-start.35 = (bf16[72,128]{1,0:T(8,128)(2,1)S(1)}, bf16[72,128]{1,0:T(8,128)(2,1)S(1)}, u32[]{:S(2)}, u32[]{:S(2)}) collective-permute-start(bf16[72,128]{1,0:T(8,128)(2,1)S(1)} %get-tuple-element.91), channel_id=1, source_target_pairs={{0,10},{2,8},{4,14},{6,12},{8,2},{10,0},{12,6},{14,4},{16,26},{18,... | collective-permute-start | bytes 55304 | tf_op jit(solution)/shard_map/ppermute | solution.py:184
  80.1 1.9 %collective-permute-start.37 = (bf16[72,128]{1,0:T(8,128)(2,1)S(1)}, bf16[72,128]{1,0:T(8,128)(2,1)S(1)}, u32[]{:S(2)}, u32[]{:S(2)}) collective-permute-start(bf16[72,128]{1,0:T(8,128)(2,1)S(1)} %get-tuple-element.93), channel_id=1, source_target_pairs={{0,14},{2,12},{4,10},{6,8},{8,6},{10,4},{12,2},{14,0},{16,30},{18,... | collective-permute-start | bytes 55304 | tf_op jit(solution)/shard_map/ppermute | solution.py:184
  82.0 2.2 %collective-permute-start.38 = (bf16[72,128]{1,0:T(8,128)(2,1)S(1)}, bf16[72,128]{1,0:T(8,128)(2,1)S(1)}, u32[]{:S(2)}, u32[]{:S(2)}) collective-permute-start(bf16[72,128]{1,0:T(8,128)(2,1)S(1)} %get-tuple-element.94), channel_id=1, source_target_pairs={{0,16},{2,18},{4,20},{6,22},{8,24},{10,26},{12,28},{14,30},{16,0},... | collective-permute-start | bytes 55304 | tf_op jit(solution)/shard_map/ppermute | solution.py:184
  84.2 1.7 %collective-permute-start.39 = (bf16[72,128]{1,0:T(8,128)(2,1)S(1)}, bf16[72,128]{1,0:T(8,128)(2,1)S(1)}, u32[]{:S(2)}, u32[]{:S(2)}) collective-permute-start(bf16[72,128]{1,0:T(8,128)(2,1)S(1)} %get-tuple-element.95), channel_id=1, source_target_pairs={{0,18},{2,16},{4,22},{6,20},{8,26},{10,24},{12,30},{14,28},{16,2},... | collective-permute-start | bytes 55304 | tf_op jit(solution)/shard_map/ppermute | solution.py:184
  85.9 3.0 %collective-permute-start.40 = (bf16[72,128]{1,0:T(8,128)(2,1)S(1)}, bf16[72,128]{1,0:T(8,128)(2,1)S(1)}, u32[]{:S(2)}, u32[]{:S(2)}) collective-permute-start(bf16[72,128]{1,0:T(8,128)(2,1)S(1)} %get-tuple-element.96), channel_id=1, source_target_pairs={{0,20},{2,22},{4,16},{6,18},{8,28},{10,30},{12,24},{14,26},{16,4},... | collective-permute-start | bytes 55304 | tf_op jit(solution)/shard_map/ppermute | solution.py:184
  89.7 3.5 %collective-permute-start.42 = (bf16[72,128]{1,0:T(8,128)(2,1)S(1)}, bf16[72,128]{1,0:T(8,128)(2,1)S(1)}, u32[]{:S(2)}, u32[]{:S(2)}) collective-permute-start(bf16[72,128]{1,0:T(8,128)(2,1)S(1)} %get-tuple-element.98), channel_id=1, source_target_pairs={{0,24},{2,26},{4,28},{6,30},{8,16},{10,18},{12,20},{14,22},{16,8},... | collective-permute-start | bytes 55304 | tf_op jit(solution)/shard_map/ppermute | solution.py:184
  94.4 4.5 %collective-permute-start.44 = (bf16[72,128]{1,0:T(8,128)(2,1)S(1)}, bf16[72,128]{1,0:T(8,128)(2,1)S(1)}, u32[]{:S(2)}, u32[]{:S(2)}) collective-permute-start(bf16[72,128]{1,0:T(8,128)(2,1)S(1)} %get-tuple-element.100), channel_id=1, source_target_pairs={{0,28},{2,30},{4,24},{6,26},{8,20},{10,22},{12,16},{14,18},{16,12}... | collective-permute-start | bytes 55304 | tf_op jit(solution)/shard_map/ppermute | solution.py:184
  99.6 1.3 %collective-permute-done.44.refs_14_ = bf16[72,128]{1,0:T(8,128)(2,1)S(1)} collective-permute-done((bf16[72,128]{1,0:T(8,128)(2,1)S(1)}, bf16[72,128]{1,0:T(8,128)(2,1)S(1)}, u32[]{:S(2)}, u32[]{:S(2)}) %collective-permute-start.44) | collective-permute-done | bytes 18464 | tf_op jit(solution)/shard_map/ppermute | solution.py:184
  100.9 5.4 %collective-permute-done.45.refs_15_ = bf16[72,128]{1,0:T(8,128)(2,1)S(1)} collective-permute-done((bf16[72,128]{1,0:T(8,128)(2,1)S(1)}, bf16[72,128]{1,0:T(8,128)(2,1)S(1)}, u32[]{:S(2)}, u32[]{:S(2)}) %collective-permute-start.45) | collective-permute-done | bytes 18464 | tf_op jit(solution)/shard_map/ppermute | solution.py:184
  106.9 1.3 %output.1 = bf16[1152,128]{1,0:T(8,128)(2,1)} custom-call(bf16[72,128]{1,0:T(8,128)(2,1)S(1)} %get-tuple-element.86.refs_0_, bf16[72,128]{1,0:T(8,128)(2,1)S(1)} %collective-permute-done.31.refs_1_, bf16[72,128]{1,0:T(8,128)(2,1)S(1)} %collective-permute-done.32.refs_2_, bf16[72,128]{1,0:T(8,128)(2,1)S(1)} %collective-permute-done.33.refs_3_, ...), custom_call_target="tpu_custom_call" | custom-call | tf_op jit(solution)/shard_map/output/pallas_call | solution.py:242
  (78 shorter events, 15.0 us)
Async XLA Ops:
  4.6 8.0 %collective-permute-start = (bf16[72,128]{1,0:T(8,128)(2,1)S(1)}, bf16[72,128]{1,0:T(8,128)(2,1)S(1)}, u32[]{:S(2)}, u32[]{:S(2)}) collective-permute-start(bf16[72,128]{1,0:T(8,128)(2,1)S(1)} %get-tuple-element.55), channel_id=1, source_target_pairs={{0,2},{2,0},{4,6},{6,4},{8,10},{10,8},{12,14},{14,12},{16,18},{18,... | collective-permute-start | bytes 55304 | tf_op jit(solution)/shard_map/ppermute | solution.py:184
  7.6 7.5 %collective-permute-start.1 = (bf16[72,128]{1,0:T(8,128)(2,1)S(1)}, bf16[72,128]{1,0:T(8,128)(2,1)S(1)}, u32[]{:S(2)}, u32[]{:S(2)}) collective-permute-start(bf16[72,128]{1,0:T(8,128)(2,1)S(1)} %get-tuple-element.56), channel_id=1, source_target_pairs={{0,4},{2,6},{4,0},{6,2},{8,12},{10,14},{12,8},{14,10},{16,20},{18,... | collective-permute-start | bytes 55304 | tf_op jit(solution)/shard_map/ppermute | solution.py:184
  9.2 8.9 %collective-permute-start.3 = (bf16[72,128]{1,0:T(8,128)(2,1)S(1)}, bf16[72,128]{1,0:T(8,128)(2,1)S(1)}, u32[]{:S(2)}, u32[]{:S(2)}) collective-permute-start(bf16[72,128]{1,0:T(8,128)(2,1)S(1)} %get-tuple-element.58), channel_id=1, source_target_pairs={{0,8},{2,10},{4,12},{6,14},{8,0},{10,2},{12,4},{14,6},{16,24},{18,... | collective-permute-start | bytes 55304 | tf_op jit(solution)/shard_map/ppermute | solution.py:184
  11.2 8.2 %collective-permute-start.4 = (bf16[72,128]{1,0:T(8,128)(2,1)S(1)}, bf16[72,128]{1,0:T(8,128)(2,1)S(1)}, u32[]{:S(2)}, u32[]{:S(2)}) collective-permute-start(bf16[72,128]{1,0:T(8,128)(2,1)S(1)} %get-tuple-element.59), channel_id=1, source_target_pairs={{0,10},{2,8},{4,14},{6,12},{8,2},{10,0},{12,6},{14,4},{16,26},{18,... | collective-permute-start | bytes 55304 | tf_op jit(solution)/shard_map/ppermute | solution.py:184
  12.6 10.3 %collective-permute-start.5 = (bf16[72,128]{1,0:T(8,128)(2,1)S(1)}, bf16[72,128]{1,0:T(8,128)(2,1)S(1)}, u32[]{:S(2)}, u32[]{:S(2)}) collective-permute-start(bf16[72,128]{1,0:T(8,128)(2,1)S(1)} %get-tuple-element.60), channel_id=1, source_target_pairs={{0,12},{2,14},{4,8},{6,10},{8,4},{10,6},{12,0},{14,2},{16,28},{18,... | collective-permute-start | bytes 55304 | tf_op jit(solution)/shard_map/ppermute | solution.py:184
  15.1 7.8 %collective-permute-start.6 = (bf16[72,128]{1,0:T(8,128)(2,1)S(1)}, bf16[72,128]{1,0:T(8,128)(2,1)S(1)}, u32[]{:S(2)}, u32[]{:S(2)}) collective-permute-start(bf16[72,128]{1,0:T(8,128)(2,1)S(1)} %get-tuple-element.61), channel_id=1, source_target_pairs={{0,14},{2,12},{4,10},{6,8},{8,6},{10,4},{12,2},{14,0},{16,30},{18,... | collective-permute-start | bytes 55304 | tf_op jit(solution)/shard_map/ppermute | solution.py:184
  15.2 11.6 %collective-permute-start.7 = (bf16[72,128]{1,0:T(8,128)(2,1)S(1)}, bf16[72,128]{1,0:T(8,128)(2,1)S(1)}, u32[]{:S(2)}, u32[]{:S(2)}) collective-permute-start(bf16[72,128]{1,0:T(8,128)(2,1)S(1)} %get-tuple-element.62), channel_id=1, source_target_pairs={{0,16},{2,18},{4,20},{6,22},{8,24},{10,26},{12,28},{14,30},{16,0},... | collective-permute-start | bytes 55304 | tf_op jit(solution)/shard_map/ppermute | solution.py:184
  18.1 9.8 %collective-permute-start.8 = (bf16[72,128]{1,0:T(8,128)(2,1)S(1)}, bf16[72,128]{1,0:T(8,128)(2,1)S(1)}, u32[]{:S(2)}, u32[]{:S(2)}) collective-permute-start(bf16[72,128]{1,0:T(8,128)(2,1)S(1)} %get-tuple-element.63), channel_id=1, source_target_pairs={{0,18},{2,16},{4,22},{6,20},{8,26},{10,24},{12,30},{14,28},{16,2},... | collective-permute-start | bytes 55304 | tf_op jit(solution)/shard_map/ppermute | solution.py:184
  19.3 13.1 %collective-permute-start.9 = (bf16[72,128]{1,0:T(8,128)(2,1)S(1)}, bf16[72,128]{1,0:T(8,128)(2,1)S(1)}, u32[]{:S(2)}, u32[]{:S(2)}) collective-permute-start(bf16[72,128]{1,0:T(8,128)(2,1)S(1)} %get-tuple-element.64), channel_id=1, source_target_pairs={{0,20},{2,22},{4,16},{6,18},{8,28},{10,30},{12,24},{14,26},{16,4},... | collective-permute-start | bytes 55304 | tf_op jit(solution)/shard_map/ppermute | solution.py:184
  22.9 9.6 %collective-permute-start.10 = (bf16[72,128]{1,0:T(8,128)(2,1)S(1)}, bf16[72,128]{1,0:T(8,128)(2,1)S(1)}, u32[]{:S(2)}, u32[]{:S(2)}) collective-permute-start(bf16[72,128]{1,0:T(8,128)(2,1)S(1)} %get-tuple-element.65), channel_id=1, source_target_pairs={{0,22},{2,20},{4,18},{6,16},{8,30},{10,28},{12,26},{14,24},{16,6},... | collective-permute-start | bytes 55304 | tf_op jit(solution)/shard_map/ppermute | solution.py:184
  22.9 9.6 %collective-permute-start.11 = (bf16[72,128]{1,0:T(8,128)(2,1)S(1)}, bf16[72,128]{1,0:T(8,128)(2,1)S(1)}, u32[]{:S(2)}, u32[]{:S(2)}) collective-permute-start(bf16[72,128]{1,0:T(8,128)(2,1)S(1)} %get-tuple-element.66), channel_id=1, source_target_pairs={{0,24},{2,26},{4,28},{6,30},{8,16},{10,18},{12,20},{14,22},{16,8},... | collective-permute-start | bytes 55304 | tf_op jit(solution)/shard_map/ppermute | solution.py:184
  32.5 7.4 %collective-permute-start.14 = (bf16[72,128]{1,0:T(8,128)(2,1)S(1)}, bf16[72,128]{1,0:T(8,128)(2,1)S(1)}, u32[]{:S(2)}, u32[]{:S(2)}) collective-permute-start(bf16[72,128]{1,0:T(8,128)(2,1)S(1)} %get-tuple-element.69), channel_id=1, source_target_pairs={{0,30},{2,28},{4,26},{6,24},{8,22},{10,20},{12,18},{14,16},{16,14}... | collective-permute-start | bytes 55304 | tf_op jit(solution)/shard_map/ppermute | solution.py:184
  39.9 28.6 %collective-permute-start.15 = (bf16[16,72,128]{2,1,0:T(8,128)(2,1)S(1)}, bf16[16,72,128]{2,1,0:T(8,128)(2,1)S(1)}, u32[]{:S(2)}, u32[]{:S(2)}) collective-permute-start(bf16[16,72,128]{2,1,0:T(8,128)(2,1)S(1)} %collect.1.left_ref), channel_id=1, source_target_pairs={{0,1},{1,0},{2,3},{3,2},{4,5},{5,4},{6,7},{7,6},{8,9},{9,8},{10,11... | collective-permute-start | bytes 884744 | tf_op jit(solution)/shard_map/ppermute | solution.py:226
  45.5 6.8 %collective-permute-start.21 = (bf16[72,128]{1,0:T(8,128)(2,1)S(1)}, bf16[72,128]{1,0:T(8,128)(2,1)S(1)}, u32[]{:S(2)}, u32[]{:S(2)}) collective-permute-start(bf16[72,128]{1,0:T(8,128)(2,1)S(1)} %get-tuple-element.76), channel_id=1, source_target_pairs={{0,12},{2,14},{4,8},{6,10},{8,4},{10,6},{12,0},{14,2},{16,28},{18,... | collective-permute-start | bytes 55304 | tf_op jit(solution)/shard_map/ppermute | solution.py:184
  45.7 6.6 %collective-permute-start.22 = (bf16[72,128]{1,0:T(8,128)(2,1)S(1)}, bf16[72,128]{1,0:T(8,128)(2,1)S(1)}, u32[]{:S(2)}, u32[]{:S(2)}) collective-permute-start(bf16[72,128]{1,0:T(8,128)(2,1)S(1)} %get-tuple-element.77), channel_id=1, source_target_pairs={{0,14},{2,12},{4,10},{6,8},{8,6},{10,4},{12,2},{14,0},{16,30},{18,... | collective-permute-start | bytes 55304 | tf_op jit(solution)/shard_map/ppermute | solution.py:184
  49.4 7.7 %collective-permute-start.23 = (bf16[72,128]{1,0:T(8,128)(2,1)S(1)}, bf16[72,128]{1,0:T(8,128)(2,1)S(1)}, u32[]{:S(2)}, u32[]{:S(2)}) collective-permute-start(bf16[72,128]{1,0:T(8,128)(2,1)S(1)} %get-tuple-element.78), channel_id=1, source_target_pairs={{0,16},{2,18},{4,20},{6,22},{8,24},{10,26},{12,28},{14,30},{16,0},... | collective-permute-start | bytes 55304 | tf_op jit(solution)/shard_map/ppermute | solution.py:184
  49.4 8.0 %collective-permute-start.24 = (bf16[72,128]{1,0:T(8,128)(2,1)S(1)}, bf16[72,128]{1,0:T(8,128)(2,1)S(1)}, u32[]{:S(2)}, u32[]{:S(2)}) collective-permute-start(bf16[72,128]{1,0:T(8,128)(2,1)S(1)} %get-tuple-element.79), channel_id=1, source_target_pairs={{0,18},{2,16},{4,22},{6,20},{8,26},{10,24},{12,30},{14,28},{16,2},... | collective-permute-start | bytes 55304 | tf_op jit(solution)/shard_map/ppermute | solution.py:184
  52.2 8.6 %collective-permute-start.25 = (bf16[72,128]{1,0:T(8,128)(2,1)S(1)}, bf16[72,128]{1,0:T(8,128)(2,1)S(1)}, u32[]{:S(2)}, u32[]{:S(2)}) collective-permute-start(bf16[72,128]{1,0:T(8,128)(2,1)S(1)} %get-tuple-element.80), channel_id=1, source_target_pairs={{0,20},{2,22},{4,16},{6,18},{8,28},{10,30},{12,24},{14,26},{16,4},... | collective-permute-start | bytes 55304 | tf_op jit(solution)/shard_map/ppermute | solution.py:184
  52.3 8.8 %collective-permute-start.26 = (bf16[72,128]{1,0:T(8,128)(2,1)S(1)}, bf16[72,128]{1,0:T(8,128)(2,1)S(1)}, u32[]{:S(2)}, u32[]{:S(2)}) collective-permute-start(bf16[72,128]{1,0:T(8,128)(2,1)S(1)} %get-tuple-element.81), channel_id=1, source_target_pairs={{0,22},{2,20},{4,18},{6,16},{8,30},{10,28},{12,26},{14,24},{16,6},... | collective-permute-start | bytes 55304 | tf_op jit(solution)/shard_map/ppermute | solution.py:184
  57.0 9.5 %collective-permute-start.27 = (bf16[72,128]{1,0:T(8,128)(2,1)S(1)}, bf16[72,128]{1,0:T(8,128)(2,1)S(1)}, u32[]{:S(2)}, u32[]{:S(2)}) collective-permute-start(bf16[72,128]{1,0:T(8,128)(2,1)S(1)} %get-tuple-element.82), channel_id=1, source_target_pairs={{0,24},{2,26},{4,28},{6,30},{8,16},{10,18},{12,20},{14,22},{16,8},... | collective-permute-start | bytes 55304 | tf_op jit(solution)/shard_map/ppermute | solution.py:184
  57.3 9.1 %collective-permute-start.28 = (bf16[72,128]{1,0:T(8,128)(2,1)S(1)}, bf16[72,128]{1,0:T(8,128)(2,1)S(1)}, u32[]{:S(2)}, u32[]{:S(2)}) collective-permute-start(bf16[72,128]{1,0:T(8,128)(2,1)S(1)} %get-tuple-element.83), channel_id=1, source_target_pairs={{0,26},{2,24},{4,30},{6,28},{8,18},{10,16},{12,22},{14,20},{16,10}... | collective-permute-start | bytes 55304 | tf_op jit(solution)/shard_map/ppermute | solution.py:184
  61.1 7.4 %collective-permute-start.30 = (bf16[72,128]{1,0:T(8,128)(2,1)S(1)}, bf16[72,128]{1,0:T(8,128)(2,1)S(1)}, u32[]{:S(2)}, u32[]{:S(2)}) collective-permute-start(bf16[72,128]{1,0:T(8,128)(2,1)S(1)} %get-tuple-element.85), channel_id=1, source_target_pairs={{0,30},{2,28},{4,26},{6,24},{8,22},{10,20},{12,18},{14,16},{16,14}... | collective-permute-start | bytes 55304 | tf_op jit(solution)/shard_map/ppermute | solution.py:184
  76.1 8.1 %collective-permute-start.34 = (bf16[72,128]{1,0:T(8,128)(2,1)S(1)}, bf16[72,128]{1,0:T(8,128)(2,1)S(1)}, u32[]{:S(2)}, u32[]{:S(2)}) collective-permute-start(bf16[72,128]{1,0:T(8,128)(2,1)S(1)} %get-tuple-element.90), channel_id=1, source_target_pairs={{0,8},{2,10},{4,12},{6,14},{8,0},{10,2},{12,4},{14,6},{16,24},{18,... | collective-permute-start | bytes 55304 | tf_op jit(solution)/shard_map/ppermute | solution.py:184
  76.1 9.7 %collective-permute-start.35 = (bf16[72,128]{1,0:T(8,128)(2,1)S(1)}, bf16[72,128]{1,0:T(8,128)(2,1)S(1)}, u32[]{:S(2)}, u32[]{:S(2)}) collective-permute-start(bf16[72,128]{1,0:T(8,128)(2,1)S(1)} %get-tuple-element.91), channel_id=1, source_target_pairs={{0,10},{2,8},{4,14},{6,12},{8,2},{10,0},{12,6},{14,4},{16,26},{18,... | collective-permute-start | bytes 55304 | tf_op jit(solution)/shard_map/ppermute | solution.py:184
  79.1 9.8 %collective-permute-start.36 = (bf16[72,128]{1,0:T(8,128)(2,1)S(1)}, bf16[72,128]{1,0:T(8,128)(2,1)S(1)}, u32[]{:S(2)}, u32[]{:S(2)}) collective-permute-start(bf16[72,128]{1,0:T(8,128)(2,1)S(1)} %get-tuple-element.92), channel_id=1, source_target_pairs={{0,12},{2,14},{4,8},{6,10},{8,4},{10,6},{12,0},{14,2},{16,28},{18,... | collective-permute-start | bytes 55304 | tf_op jit(solution)/shard_map/ppermute | solution.py:184
  80.1 9.6 %collective-permute-start.37 = (bf16[72,128]{1,0:T(8,128)(2,1)S(1)}, bf16[72,128]{1,0:T(8,128)(2,1)S(1)}, u32[]{:S(2)}, u32[]{:S(2)}) collective-permute-start(bf16[72,128]{1,0:T(8,128)(2,1)S(1)} %get-tuple-element.93), channel_id=1, source_target_pairs={{0,14},{2,12},{4,10},{6,8},{8,6},{10,4},{12,2},{14,0},{16,30},{18,... | collective-permute-start | bytes 55304 | tf_op jit(solution)/shard_map/ppermute | solution.py:184
  82.0 11.2 %collective-permute-start.38 = (bf16[72,128]{1,0:T(8,128)(2,1)S(1)}, bf16[72,128]{1,0:T(8,128)(2,1)S(1)}, u32[]{:S(2)}, u32[]{:S(2)}) collective-permute-start(bf16[72,128]{1,0:T(8,128)(2,1)S(1)} %get-tuple-element.94), channel_id=1, source_target_pairs={{0,16},{2,18},{4,20},{6,22},{8,24},{10,26},{12,28},{14,30},{16,0},... | collective-permute-start | bytes 55304 | tf_op jit(solution)/shard_map/ppermute | solution.py:184
  84.2 10.2 %collective-permute-start.39 = (bf16[72,128]{1,0:T(8,128)(2,1)S(1)}, bf16[72,128]{1,0:T(8,128)(2,1)S(1)}, u32[]{:S(2)}, u32[]{:S(2)}) collective-permute-start(bf16[72,128]{1,0:T(8,128)(2,1)S(1)} %get-tuple-element.95), channel_id=1, source_target_pairs={{0,18},{2,16},{4,22},{6,20},{8,26},{10,24},{12,30},{14,28},{16,2},... | collective-permute-start | bytes 55304 | tf_op jit(solution)/shard_map/ppermute | solution.py:184
  85.9 13.0 %collective-permute-start.40 = (bf16[72,128]{1,0:T(8,128)(2,1)S(1)}, bf16[72,128]{1,0:T(8,128)(2,1)S(1)}, u32[]{:S(2)}, u32[]{:S(2)}) collective-permute-start(bf16[72,128]{1,0:T(8,128)(2,1)S(1)} %get-tuple-element.96), channel_id=1, source_target_pairs={{0,20},{2,22},{4,16},{6,18},{8,28},{10,30},{12,24},{14,26},{16,4},... | collective-permute-start | bytes 55304 | tf_op jit(solution)/shard_map/ppermute | solution.py:184
  88.9 10.2 %collective-permute-start.41 = (bf16[72,128]{1,0:T(8,128)(2,1)S(1)}, bf16[72,128]{1,0:T(8,128)(2,1)S(1)}, u32[]{:S(2)}, u32[]{:S(2)}) collective-permute-start(bf16[72,128]{1,0:T(8,128)(2,1)S(1)} %get-tuple-element.97), channel_id=1, source_target_pairs={{0,22},{2,20},{4,18},{6,16},{8,30},{10,28},{12,26},{14,24},{16,6},... | collective-permute-start | bytes 55304 | tf_op jit(solution)/shard_map/ppermute | solution.py:184
  89.7 9.5 %collective-permute-start.42 = (bf16[72,128]{1,0:T(8,128)(2,1)S(1)}, bf16[72,128]{1,0:T(8,128)(2,1)S(1)}, u32[]{:S(2)}, u32[]{:S(2)}) collective-permute-start(bf16[72,128]{1,0:T(8,128)(2,1)S(1)} %get-tuple-element.98), channel_id=1, source_target_pairs={{0,24},{2,26},{4,28},{6,30},{8,16},{10,18},{12,20},{14,22},{16,8},... | collective-permute-start | bytes 55304 | tf_op jit(solution)/shard_map/ppermute | solution.py:184
  98.9 7.4 %collective-permute-start.45 = (bf16[72,128]{1,0:T(8,128)(2,1)S(1)}, bf16[72,128]{1,0:T(8,128)(2,1)S(1)}, u32[]{:S(2)}, u32[]{:S(2)}) collective-permute-start(bf16[72,128]{1,0:T(8,128)(2,1)S(1)} %get-tuple-element.101), channel_id=1, source_target_pairs={{0,30},{2,28},{4,26},{6,24},{8,22},{10,20},{12,18},{14,16},{16,14}... | collective-permute-start | bytes 55304 | tf_op jit(solution)/shard_map/ppermute | solution.py:184
  (21 other events, 120.3 us)

commit v3 on v1

v3 whole, which is shorter than its diff:
```python
import functools
import math

import jax
import jax.numpy as jnp
from jax import lax
from jax.experimental import pallas as pl
from jax.experimental.pallas import tpu as pltpu
from jax.sharding import PartitionSpec as P

TILE = 96
LANES = 128
EPS = 1e-05
VMEM_BYTES = 32 * 1024 * 1024
WHOLE_VMEM_BYTES = 64 * 1024 * 1024
VMEM = pl.BlockSpec(memory_space=pltpu.VMEM)
HBM = pl.BlockSpec(memory_space=pltpu.HBM)
SMEM = pl.BlockSpec(memory_space=pltpu.SMEM)


def column(row):
    return jnp.broadcast_to(row, (8, row.shape[1])).T[:, :1]


def steps(at, width, count):
    total = jnp.zeros_like(at)
    for edge in range(1, count):
        total += (at >= edge * width).astype(jnp.int32)
    return total


def sigmoid(values):
    return 0.5 * jnp.tanh(0.5 * values) + 0.5


def keep_of(tile_ref, chain_ref, rows, cols):
    tokens = chain_ref.shape[1]
    tiles = tile_ref.shape[1]
    positions = rows * cols
    at = lax.broadcasted_iota(jnp.int32, (1, positions), 1)
    row = steps(at, cols, rows)
    k = lax.axis_index("row") * rows + row
    i = lax.axis_index("col") * cols + at - row * cols
    token = lax.broadcasted_iota(jnp.int32, (tokens, positions), 0)
    pick = (token == k).astype(jnp.float32) - (token == i).astype(jnp.float32)
    chains = jnp.broadcast_to(chain_ref[...].astype(jnp.bfloat16), (8, tokens))
    apart = jnp.dot(chains, pick.astype(jnp.bfloat16), preferred_element_type=jnp.float32)[:1]
    k_tile = steps(k, TILE, tiles)
    i_tile = steps(i, TILE, tiles)
    tile_vals = jnp.zeros((1, positions), jnp.float32)
    for a in range(tiles):
        for b in range(tiles):
            here = (k_tile == a) & (i_tile == b)
            tile_vals = jnp.where(here, tile_ref[a, b].astype(jnp.float32), tile_vals)
    return jnp.where(apart == 0.0, 1.0, tile_vals)


def cycle_of(cols):
    cycle = math.lcm(cols, LANES)
    return cycle // cols, cycle // LANES


def fetch(sems, *pairs):
    copies = [pltpu.make_async_copy(src, dst, sems.at[at]) for at, (src, dst) in enumerate(pairs)]
    for copy in copies:
        copy.start()
    for copy in copies:
        copy.wait()


def project_kernel(
    rows, cols, shares, tile_hbm, chain_hbm, pair_hbm, gain_hbm, w_hbm, message_ref, gate_ref,
    tile_ref, chain_ref, pair_ref, gain_ref, w_ref, message, sems,
):
    fetch(
        sems,
        (w_hbm, w_ref),
        (pair_hbm, pair_ref),
        (gain_hbm, gain_ref),
        (chain_hbm, chain_ref),
        (tile_hbm, tile_ref),
    )
    hidden = (w_ref.shape[1] - w_ref.shape[0]) // 4
    own = hidden // shares
    groups = cycle_of(cols)[1]
    keep = keep_of(tile_ref, chain_ref, rows, cols)
    w_t = w_ref[...].T
    gain = column(gain_ref[...])
    for group in range(rows * cols // LANES):
        block = pair_ref[group * LANES : (group + 1) * LANES, :].astype(jnp.float32).T
        center = block - jnp.mean(block, axis=0, keepdims=True)
        spread = jnp.mean(center * center, axis=0, keepdims=True)
        normed = (center * lax.rsqrt(spread + EPS) * gain).astype(jnp.bfloat16)
        projected = jnp.dot(w_t, normed, preferred_element_type=jnp.float32)
        kept = keep[:, group * LANES : (group + 1) * LANES]
        for side in range(2):
            value = projected[2 * side * hidden : (2 * side + 1) * hidden]
            gate = projected[(2 * side + 1) * hidden : (2 * side + 2) * hidden]
            line = (group // groups * 2 + side) * groups + group % groups
            message[:, line * own : (line + 1) * own, :] = (sigmoid(gate) * value * kept).reshape(
                shares, own, LANES
            )
        gate_ref[group] = sigmoid(projected[4 * hidden :])
    message_ref[...] = message[...].astype(jnp.bfloat16)


def take_channel(ref, side, channel, own, cols):
    tokens, groups = cycle_of(cols)
    count = ref.shape[0] // (own * groups * 2)
    lanes = [
        ref[pl.ds((side * groups + group) * own + channel, count, stride=own * groups * 2), :]
        for group in range(groups)
    ]
    found = []
    for token in range(tokens):
        start, pieces = token * cols, []
        while start < (token + 1) * cols:
            group = start // LANES
            end = min((group + 1) * LANES, (token + 1) * cols)
            pieces.append(lanes[group][:, start - group * LANES : end - group * LANES])
            start = end
        found.append(jnp.concatenate(pieces, axis=1).astype(jnp.bfloat16))
    return jnp.concatenate(found, axis=0)


def put_channel(ref, held, channel, own, cols):
    tokens, groups = cycle_of(cols)
    count = cols // tokens
    lines = [
        jnp.concatenate(
            [held[piece, pl.ds(token, count, stride=tokens), :] for piece in range(held.shape[0])], axis=1
        )
        for token in range(tokens)
    ]
    for group in range(groups):
        start, pieces = group * LANES, []
        while start < (group + 1) * LANES:
            token = start // cols
            end = min((token + 1) * cols, (group + 1) * LANES)
            pieces.append(lines[token][:, start - token * cols : end - token * cols])
            start = end
        ref[pl.ds(group * own + channel, count, stride=own * groups), :] = jnp.concatenate(pieces, axis=1)


def triangle(own, cols, lefts, rights, held, mixed):
    for channel in range(own):
        right = take_channel(rights, 1, channel, own, cols)
        left = take_channel(lefts, 0, channel, own, cols)
        total = lax.dot_general(left, right, (((0,), (0,)), ((), ())), preferred_element_type=jnp.float32)
        at = channel % 2
        for start in range(0, cols, LANES):
            width = min(LANES, cols - start)
            held[at, start // LANES, :, :width] = total[:, start : start + width]
        put_channel(mixed, held.at[at], channel, own, cols)


def first_kernel(own, cols, own_ref, mixed_ref, ours, held, mixed):
    ours[...] = own_ref[...].astype(jnp.float32).reshape(ours.shape)
    triangle(own, cols, ours, ours, held, mixed)
    mixed_ref[...] = mixed[...].astype(jnp.bfloat16).reshape(mixed_ref.shape)


def second_kernel(own, cols, own_ref, other_ref, first_ref, mixed_ref, ours, others, held, mixed):
    half = first_ref.shape[0]
    at = lax.axis_index("col")
    ours[...] = own_ref[...].astype(jnp.float32).reshape(ours.shape)
    others[...] = other_ref[...].astype(jnp.float32).reshape(others.shape)
    mixed_ref[pl.ds(at * half, half)] = first_ref[...]
    triangle(own, cols, others, ours, held, mixed)
    mixed_ref[pl.ds((1 - at) * half, half)] = mixed[...].astype(jnp.bfloat16).reshape(first_ref.shape)


def output_kernel(own, mixed_ref, gate_ref, gain_ref, w_ref, update_ref, mixed):
    shares = mixed_ref.shape[0]
    mixed[...] = mixed_ref[...].astype(jnp.float32)
    w_t = w_ref[...].T
    gain = column(gain_ref[...])
    for group in range(gate_ref.shape[0]):
        block = mixed[:, group * own : (group + 1) * own, :].reshape(shares * own, LANES)
        center = block - jnp.mean(block, axis=0, keepdims=True)
        spread = jnp.mean(center * center, axis=0, keepdims=True)
        normed = (center * lax.rsqrt(spread + EPS) * gain).astype(jnp.bfloat16)
        projected = jnp.dot(w_t, normed, preferred_element_type=jnp.float32)
        update = (gate_ref[group] * projected).T
        update_ref[group * LANES : (group + 1) * LANES, :] = update.astype(jnp.bfloat16)


def on_device(shares, pair, tile_mask, chain_ids, gain_in, w_proj, gain_mid, w_out):
    rows, cols, width = pair.shape
    hidden = w_out.shape[0]
    own = hidden // shares
    positions = rows * cols
    lines = positions // LANES * own
    half = shares // 2
    params = pltpu.CompilerParams(vmem_limit_bytes=VMEM_BYTES)
    tokens = chain_ids.shape[0]
    message, gate = pl.pallas_call(
        functools.partial(project_kernel, rows, cols, shares),
        out_shape=(
            jax.ShapeDtypeStruct((shares, 2 * lines, LANES), jnp.bfloat16),
            jax.ShapeDtypeStruct((positions // LANES, width, LANES), jnp.float32),
        ),
        in_specs=[HBM] * 5,
        out_specs=(VMEM, VMEM),
        scratch_shapes=[
            pltpu.SMEM(tile_mask.shape, jnp.int32),
            pltpu.VMEM((1, tokens), jnp.int32),
            pltpu.VMEM((positions, width), jnp.bfloat16),
            pltpu.VMEM((1, width), jnp.float32),
            pltpu.VMEM(w_proj.shape, jnp.bfloat16),
            pltpu.VMEM((shares, 2 * lines, LANES), jnp.float32),
            pltpu.SemaphoreType.DMA((5,)),
        ],
        compiler_params=pltpu.CompilerParams(vmem_limit_bytes=WHOLE_VMEM_BYTES),
        name="project",
    )(tile_mask, chain_ids[None, :], pair.reshape(positions, width), gain_in[None, :], w_proj)
    message = lax.all_to_all(message, "row", split_axis=0, concat_axis=0, tiled=True)
    other = lax.ppermute(message, "col", [(0, 1), (1, 0)])
    blocks = pltpu.VMEM((shares * 2 * lines, LANES), jnp.float32)
    held = pltpu.VMEM((2, pl.cdiv(cols, LANES), cols, LANES), jnp.float32)
    out = pltpu.VMEM((half * lines, LANES), jnp.float32)
    first = pl.pallas_call(
        functools.partial(first_kernel, own, cols),
        out_shape=jax.ShapeDtypeStruct((half, lines, LANES), jnp.bfloat16),
        in_specs=[VMEM],
        out_specs=VMEM,
        scratch_shapes=[blocks, held, out],
        compiler_params=params,
        cost_estimate=pl.CostEstimate(
            flops=2 * own * cols * cols * tokens, bytes_accessed=8 * shares * lines * LANES, transcendentals=0
        ),
        name="first",
    )(message)
    mixed = pl.pallas_call(
        functools.partial(second_kernel, own, cols),
        out_shape=jax.ShapeDtypeStruct((shares, lines, LANES), jnp.bfloat16),
        in_specs=[VMEM, VMEM, VMEM],
        out_specs=VMEM,
        scratch_shapes=[blocks, blocks, held, out],
        compiler_params=params,
        name="second",
    )(message, other, first)
    mixed = lax.all_to_all(mixed, "row", split_axis=0, concat_axis=0, tiled=True)
    update = pl.pallas_call(
        functools.partial(output_kernel, own),
        out_shape=jax.ShapeDtypeStruct((positions, width), jnp.bfloat16),
        in_specs=[VMEM, VMEM, VMEM, VMEM],
        out_specs=VMEM,
        scratch_shapes=[pltpu.VMEM((shares, lines, LANES), jnp.float32)],
        compiler_params=params,
        name="output",
    )(mixed, gate, gain_mid[None, :], w_out)
    return update.reshape(rows, cols, width)


def solution(mesh):
    in_specs = (P(("grp", "row"), "col", None), P("grp", None), P("grp"), P(), P(), P(), P())
    out_specs = P(("grp", "row"), "col", None)
    return jax.shard_map(
        functools.partial(on_device, mesh.shape["row"]),
        mesh=mesh,
        in_specs=in_specs,
        out_specs=out_specs,
        check_vma=False,
    )
```

time: 57.5 us -> 48.6 us (0.85)
  blocking collectives: 18.8 us -> 39.8 us
  waiting for transfers between devices: 18.8 us -> 0.41 us
  starting transfers between devices: 7.15 us -> 0.01 us
  local copies, waits for them, and re-layouts: 4.09 us -> 0.66 us
  Pallas kernels: 8.15 us -> 7.44 us
    all_to_all x1 -> x2, blocking collectives: 18.8 us -> 39.8 us  [the longest x1 25.8 us: on_device(): lax.all_to_all(message, 'row', split_axis=0, concat_axis=0, tiled=True)]
    all_to_all x2 -> x0, waiting for transfers between devices: 18.8 us -> none  [the longest x1 9.8 us: on_device(): lax.all_to_all(right, 'row', split_axis=0, concat_axis=0, tiled=True)]
    all_to_all x2 -> x0, starting transfers between devices: 7.08 us -> none  [the longest x1 3.54 us: on_device(): lax.all_to_all(right, 'row', split_axis=0, concat_axis=0, tiled=True)]
    unnamed x14 -> x6, local copies, waits for them, and re-layouts: 3.87 us -> 0.66 us
    pallas_call x1 -> x2, Pallas kernels: 4.83 us -> 3.17 us  [the longest x1 1.59 us: on_device(): pl.pallas_call(functools.partial(first_kernel, own, cols), out_shape=jax....]
    pallas_call x1, Pallas kernels: 2.13 us -> 3.02 us  [on_device(): pl.pallas_call(functools.partial(project_kernel, rows, cols, shares), out...]
  transfers between devices with their start and end apart: 3 -> 1, of which waited for: 2 -> 1; matrix products, arithmetic and copies ran while one was open for 0% -> 0% of each run, Pallas kernels for 0% -> 3%
where the time goes in v3:
time: 48.6 us; the launch traced here: 48.3 us
  blocking collectives  39.8 us (82%)
  Pallas kernels  7.44 us (15%)
  local copies, waits for them, and re-layouts  0.66 us (1%)
    all_to_all x1, blocking collectives, on_device(): lax.all_to_all(message, 'row', split_axis=0, concat_axis=0, tiled=True)  25.8 us
    all_to_all x1, blocking collectives, on_device(): lax.all_to_all(mixed, 'row', split_axis=0, concat_axis=0, tiled=True)  14 us
    pallas_call x1, Pallas kernels, on_device(): pl.pallas_call(functools.partial(project_kernel, rows, cols, shares), out...  3.02 us
    pallas_call x1, Pallas kernels, on_device(): pl.pallas_call(functools.partial(first_kernel, own, cols), out_shape=jax....  1.59 us
    pallas_call x1, Pallas kernels, on_device(): pl.pallas_call(functools.partial(second_kernel, own, cols), out_shape=jax...  1.58 us
    pallas_call x1, Pallas kernels, on_device(): pl.pallas_call(functools.partial(output_kernel, own), out_shape=jax.Shape...  1.25 us
  transfers between devices with their start and end apart: 1, of which 1 were waited for; matrix products, arithmetic and copies ran while one was open for 0% of the time, Pallas kernels for 3%

profile of v3, /device:TPU:0, one launch (start us, length us, event | category | flops | bytes accessed | tf_op | source)
XLA Modules:
  0.0 48.3 jit_solution(12588858204409313450)
XLA Ops:
  0.0 3.0 %project.1 = (bf16[16,144,128]{2,1,0:T(8,128)(2,1)}, f32[9,128,128]{2,1,0:T(8,128)}) custom-call(s32[2,2]{1,0:T(2,128)} %tile_hbm.1, s32[1,192]{1,0:T(1,128)} %bitcast.7, bf16[1152,128]{1,0:T(8,128)(2,1)} %bitcast.6, f32[1,128]{1,0:T(1,128)} %bitcast.8, bf16[128,640]{1,0:T(8,128)(2,1)} %w_hbm.1), custom_call_target="tpu_custom_call" | custom-call | tf_op jit(solution)/shard_map/project/pallas_call | solution.py:197
  3.0 25.8 %all_to_all.10.own_ref = bf16[16,144,128]{2,1,0:T(8,128)(2,1)S(1)} all-to-all(bf16[16,144,128]{2,1,0:T(8,128)(2,1)} %get-tuple-element.7), channel_id=1, replica_groups=mesh['grp'=1,'row'=16,'col'=2] {'row'}, dimensions={0} | all-to-all | bytes 1179648 | tf_op jit(solution)/shard_map/all_to_all | solution.py:217
  28.8 0.0 collective-permute-start
  28.8 1.6 %first.1.first_ref = bf16[8,72,128]{2,1,0:T(8,128)(2,1)S(1)} custom-call(bf16[16,144,128]{2,1,0:T(8,128)(2,1)S(1)} %all_to_all.10.own_ref), custom_call_target="tpu_custom_call" | custom-call | flops 28311552 | bytes 1179648 | tf_op jit(solution)/shard_map/first/pallas_call | solution.py:222
  30.4 0.4 collective-permute-done.other_ref
  30.8 0.0 copy-start.1
  30.8 1.6 %second.1 = bf16[16,72,128]{2,1,0:T(8,128)(2,1)S(1)} custom-call(bf16[16,144,128]{2,1,0:T(8,128)(2,1)S(1)} %all_to_all.10.own_ref, bf16[16,144,128]{2,1,0:T(8,128)(2,1)S(1)} %collective-permute-done.other_ref, bf16[8,72,128]{2,1,0:T(8,128)(2,1)S(1)} %first.1.first_ref), custom_call_target="tpu_custom_call" | custom-call | tf_op jit(solution)/shard_map/second/pallas_call | solution.py:234
  32.4 0.0 copy-start
  32.4 14.0 %all_to_all.11.mixed_ref = bf16[16,72,128]{2,1,0:T(8,128)(2,1)S(1)} all-to-all(bf16[16,72,128]{2,1,0:T(8,128)(2,1)S(1)} %second.1), channel_id=1, replica_groups=mesh['grp'=1,'row'=16,'col'=2] {'row'}, dimensions={0} | all-to-all | bytes 589824 | tf_op jit(solution)/shard_map/all_to_all | solution.py:243
  46.4 0.0 copy-start.2
  46.4 0.0 copy-done.1
  46.4 0.0 copy-done
  46.4 0.6 %copy-done.2 = f32[128]{0:T(128)S(1)} copy-done((f32[128]{0:T(128)S(1)}, f32[128]{0:T(128)}, u32[]{:S(2)}) %copy-start.2) | copy-done | bytes 536
  47.1 1.2 %output.1 = bf16[1152,128]{1,0:T(8,128)(2,1)} custom-call(bf16[16,72,128]{2,1,0:T(8,128)(2,1)S(1)} %all_to_all.11.mixed_ref, f32[9,128,128]{2,1,0:T(8,128)S(1)} %copy-done, f32[1,128]{1,0:T(1,128)S(1)} %bitcast.5, bf16[128,128]{1,0:T(8,128)(2,1)S(1)} %copy-done.1), custom_call_target="tpu_custom_call" | custom-call | tf_op jit(solution)/shard_map/output/pallas_call | solution.py:244
Async XLA Ops:
  28.8 2.0 %collective-permute-start = (bf16[16,144,128]{2,1,0:T(8,128)(2,1)S(1)}, bf16[16,144,128]{2,1,0:T(8,128)(2,1)S(1)}, u32[]{:S(2)}, u32[]{:S(2)}) collective-permute-start(bf16[16,144,128]{2,1,0:T(8,128)(2,1)S(1)} %all_to_all.10.own_ref), channel_id=1, source_target_pairs={{0,1},{1,0},{2,3},{3,2},{4,5},{5,4},{6,7},{7,6},{8,9},{9,8},{10,11... | collective-permute-start | bytes 1769480 | tf_op jit(solution)/shard_map/ppermute | solution.py:218
  30.8 15.6 %copy-start.1 = (bf16[128,128]{1,0:T(8,128)(2,1)S(1)}, bf16[128,128]{1,0:T(8,128)(2,1)}, u32[]{:S(2)}) copy-start(bf16[128,128]{1,0:T(8,128)(2,1)} %w_ref.1) | copy-start | bytes 98308
  32.4 14.0 %copy-start = (f32[9,128,128]{2,1,0:T(8,128)S(1)}, f32[9,128,128]{2,1,0:T(8,128)}, u32[]{:S(2)}) copy-start(f32[9,128,128]{2,1,0:T(8,128)} %get-tuple-element.8.gate_ref) | copy-start | bytes 1769476
  46.4 0.7 %copy-start.2 = (f32[128]{0:T(128)S(1)}, f32[128]{0:T(128)}, u32[]{:S(2)}) copy-start(f32[128]{0:T(128)} %param.12) | copy-start | bytes 1540

commit v4 on v3

--- a/solution.py
+++ b/solution.py
@@ -11,6 +11,7 @@
 TILE = 96
 LANES = 128
 EPS = 1e-05
+PARTS = 2
 VMEM_BYTES = 32 * 1024 * 1024
 WHOLE_VMEM_BYTES = 64 * 1024 * 1024
 VMEM = pl.BlockSpec(memory_space=pltpu.VMEM)
@@ -69,8 +70,8 @@
 
 
 def project_kernel(
-    rows, cols, shares, tile_hbm, chain_hbm, pair_hbm, gain_hbm, w_hbm, message_ref, gate_ref,
-    tile_ref, chain_ref, pair_ref, gain_ref, w_ref, message, sems,
+    rows, cols, peers, tile_hbm, chain_hbm, pair_hbm, gain_hbm, w_hbm, message_ref, normed_ref,
+    tile_ref, chain_ref, pair_ref, gain_ref, w_ref, sems,
 ):
     fetch(
         sems,
@@ -81,27 +82,42 @@
         (tile_hbm, tile_ref),
     )
     hidden = (w_ref.shape[1] - w_ref.shape[0]) // 4
-    own = hidden // shares
+    own = hidden // peers
     groups = cycle_of(cols)[1]
     keep = keep_of(tile_ref, chain_ref, rows, cols)
-    w_t = w_ref[...].T
+    w_t = w_ref[:, : 4 * hidden].T
     gain = column(gain_ref[...])
-    for group in range(rows * cols // LANES):
-        block = pair_ref[group * LANES : (group + 1) * LANES, :].astype(jnp.float32).T
+    positions = rows * cols
+    for start in range(0, positions, 2 * LANES):
+        end = min(start + 2 * LANES, positions)
+        block = pair_ref[start:end, :].astype(jnp.float32).T
         center = block - jnp.mean(block, axis=0, keepdims=True)
         spread = jnp.mean(center * center, axis=0, keepdims=True)
         normed = (center * lax.rsqrt(spread + EPS) * gain).astype(jnp.bfloat16)
+        normed_ref[:, start:end] = normed
         projected = jnp.dot(w_t, normed, preferred_element_type=jnp.float32)
-        kept = keep[:, group * LANES : (group + 1) * LANES]
+        kept = keep[:, start:end]
         for side in range(2):
             value = projected[2 * side * hidden : (2 * side + 1) * hidden]
             gate = projected[(2 * side + 1) * hidden : (2 * side + 2) * hidden]
-            line = (group // groups * 2 + side) * groups + group % groups
-            message[:, line * own : (line + 1) * own, :] = (sigmoid(gate) * value * kept).reshape(
-                shares, own, LANES
-            )
-        gate_ref[group] = sigmoid(projected[4 * hidden :])
-    message_ref[...] = message[...].astype(jnp.bfloat16)
+            sent = (sigmoid(gate) * value * kept).astype(jnp.bfloat16)
+            for group in range(start // LANES, end // LANES):
+                line = (group // groups * 2 + side) * groups + group % groups
+                at = group * LANES - start
+                message_ref[:, line * own : (line + 1) * own, :] = sent[:, at : at + LANES].reshape(
+                    peers, own, LANES
+                )
+
+
+def gate_kernel(normed_ref, w_hbm, gain_hbm, w_out_hbm, gate_ref, w_out_ref, gain_ref, w, w_out, gain, sems):
+    width = w_hbm.shape[0]
+    last = w_hbm.shape[1] - width
+    fetch(sems, (w_hbm, w), (w_out_hbm, w_out), (gain_hbm, gain))
+    gate_ref[...] = sigmoid(
+        jnp.dot(w[:, last:].T, normed_ref[...], preferred_element_type=jnp.float32)
+    )
+    w_out_ref[...] = w_out[...].T
+    gain_ref[...] = jnp.broadcast_to(column(gain[...]), gain_ref.shape)
 
 
 def take_channel(ref, side, channel, own, cols):
@@ -119,8 +135,8 @@
             end = min((group + 1) * LANES, (token + 1) * cols)
             pieces.append(lanes[group][:, start - group * LANES : end - group * LANES])
             start = end
-        found.append(jnp.concatenate(pieces, axis=1).astype(jnp.bfloat16))
-    return jnp.concatenate(found, axis=0)
+        found.append(jnp.concatenate(pieces, axis=1))
+    return jnp.concatenate(found, axis=0).astype(jnp.bfloat16)
 
 
 def put_channel(ref, held, channel, own, cols):
@@ -170,35 +186,37 @@
     mixed_ref[pl.ds((1 - at) * half, half)] = mixed[...].astype(jnp.bfloat16).reshape(first_ref.shape)
 
 
-def output_kernel(own, mixed_ref, gate_ref, gain_ref, w_ref, update_ref, mixed):
-    shares = mixed_ref.shape[0]
-    mixed[...] = mixed_ref[...].astype(jnp.float32)
-    w_t = w_ref[...].T
-    gain = column(gain_ref[...])
-    for group in range(gate_ref.shape[0]):
-        block = mixed[:, group * own : (group + 1) * own, :].reshape(shares * own, LANES)
+def output_kernel(own, mixed_ref, gate_ref, gain_ref, w_t_ref, update_ref):
+    shares, hidden = mixed_ref.shape[0], w_t_ref.shape[1]
+    peers = hidden // own
+    for group in range(gate_ref.shape[1] // LANES):
+        block = jnp.zeros((hidden, LANES), jnp.float32)
+        for part in range(shares // peers):
+            sums = mixed_ref[part * peers : (part + 1) * peers, group * own : (group + 1) * own, :]
+            block += sums.astype(jnp.float32).reshape(hidden, LANES)
         center = block - jnp.mean(block, axis=0, keepdims=True)
         spread = jnp.mean(center * center, axis=0, keepdims=True)
-        normed = (center * lax.rsqrt(spread + EPS) * gain).astype(jnp.bfloat16)
-        projected = jnp.dot(w_t, normed, preferred_element_type=jnp.float32)
-        update = (gate_ref[group] * projected).T
-        update_ref[group * LANES : (group + 1) * LANES, :] = update.astype(jnp.bfloat16)
+        normed = (center * lax.rsqrt(spread + EPS) * gain_ref[...]).astype(jnp.bfloat16)
+        projected = jnp.dot(w_t_ref[...], normed, preferred_element_type=jnp.float32)
+        lanes = slice(group * LANES, (group + 1) * LANES)
+        update_ref[lanes, :] = (gate_ref[:, lanes] * projected).T.astype(jnp.bfloat16)
 
 
 def on_device(shares, pair, tile_mask, chain_ids, gain_in, w_proj, gain_mid, w_out):
     rows, cols, width = pair.shape
     hidden = w_out.shape[0]
-    own = hidden // shares
+    peers = shares // PARTS
+    own = hidden // peers
     positions = rows * cols
     lines = positions // LANES * own
     half = shares // 2
     params = pltpu.CompilerParams(vmem_limit_bytes=VMEM_BYTES)
     tokens = chain_ids.shape[0]
-    message, gate = pl.pallas_call(
-        functools.partial(project_kernel, rows, cols, shares),
+    message, normed = pl.pallas_call(
+        functools.partial(project_kernel, rows, cols, peers),
         out_shape=(
-            jax.ShapeDtypeStruct((shares, 2 * lines, LANES), jnp.bfloat16),
-            jax.ShapeDtypeStruct((positions // LANES, width, LANES), jnp.float32),
+            jax.ShapeDtypeStruct((peers, 2 * lines, LANES), jnp.bfloat16),
+            jax.ShapeDtypeStruct((width, positions), jnp.bfloat16),
         ),
         in_specs=[HBM] * 5,
         out_specs=(VMEM, VMEM),
@@ -208,15 +226,42 @@
             pltpu.VMEM((positions, width), jnp.bfloat16),
             pltpu.VMEM((1, width), jnp.float32),
             pltpu.VMEM(w_proj.shape, jnp.bfloat16),
-            pltpu.VMEM((shares, 2 * lines, LANES), jnp.float32),
             pltpu.SemaphoreType.DMA((5,)),
         ],
         compiler_params=pltpu.CompilerParams(vmem_limit_bytes=WHOLE_VMEM_BYTES),
         name="project",
     )(tile_mask, chain_ids[None, :], pair.reshape(positions, width), gain_in[None, :], w_proj)
-    message = lax.all_to_all(message, "row", split_axis=0, concat_axis=0, tiled=True)
+    message = lax.all_to_all(
+        message,
+        "row",
+        split_axis=0,
+        concat_axis=0,
+        axis_index_groups=[list(range(part * peers, (part + 1) * peers)) for part in range(PARTS)],
+        tiled=True,
+    )
+    gate, w_out_t, gain = pl.pallas_call(
+        gate_kernel,
+        out_shape=(
+            jax.ShapeDtypeStruct((width, positions), jnp.float32),
+            jax.ShapeDtypeStruct(w_out.shape[::-1], jnp.bfloat16),
+            jax.ShapeDtypeStruct((hidden, LANES), jnp.float32),
+        ),
+        in_specs=[VMEM] + [HBM] * 3,
+        out_specs=(VMEM, VMEM, VMEM),
+        scratch_shapes=[
+            pltpu.VMEM(w_proj.shape, jnp.bfloat16),
+            pltpu.VMEM(w_out.shape, jnp.bfloat16),
+            pltpu.VMEM((1, hidden), jnp.float32),
+            pltpu.SemaphoreType.DMA((3,)),
+        ],
+        compiler_params=params,
+        cost_estimate=pl.CostEstimate(
+            flops=2 * width * width * positions, bytes_accessed=4 * width * positions, transcendentals=0
+        ),
+        name="gate",
+    )(normed, w_proj, gain_mid[None, :], w_out)
     other = lax.ppermute(message, "col", [(0, 1), (1, 0)])
-    blocks = pltpu.VMEM((shares * 2 * lines, LANES), jnp.float32)
+    blocks = pltpu.VMEM((peers * 2 * lines, LANES), jnp.float32)
     held = pltpu.VMEM((2, pl.cdiv(cols, LANES), cols, LANES), jnp.float32)
     out = pltpu.VMEM((half * lines, LANES), jnp.float32)
     first = pl.pallas_call(
@@ -244,12 +289,11 @@
     update = pl.pallas_call(
         functools.partial(output_kernel, own),
         out_shape=jax.ShapeDtypeStruct((positions, width), jnp.bfloat16),
-        in_specs=[VMEM, VMEM, VMEM, VMEM],
+        in_specs=[VMEM] * 4,
         out_specs=VMEM,
-        scratch_shapes=[pltpu.VMEM((shares, lines, LANES), jnp.float32)],
         compiler_params=params,
         name="output",
-    )(mixed, gate, gain_mid[None, :], w_out)
+    )(mixed, gate, gain, w_out_t)
     return update.reshape(rows, cols, width)
 
 

time: 48.6 us -> 47.2 us (0.971)
  blocking collectives: 39.8 us -> 16.6 us
  waiting for transfers between devices: 0.41 us -> 15.4 us
  starting transfers between devices: 0.01 us -> 4.19 us
  Pallas kernels: 7.44 us -> 10 us
    all_to_all x2 -> x1, blocking collectives: 39.8 us -> 16.6 us  [on_device(): lax.all_to_all(message, 'row', split_axis=0, concat_axis=0, axis_index_gr...]
    all_to_all x0 -> x1, waiting for transfers between devices: none -> 15.4 us  [on_device(): lax.all_to_all(mixed, 'row', split_axis=0, concat_axis=0, tiled=True)]
    all_to_all x0 -> x1, starting transfers between devices: none -> 4.19 us  [on_device(): lax.all_to_all(mixed, 'row', split_axis=0, concat_axis=0, tiled=True)]
    pallas_call x1, Pallas kernels: 1.58 us -> 3.17 us  [on_device(): pl.pallas_call(functools.partial(second_kernel, own, cols), out_shape=jax...]
    pallas_call x1, Pallas kernels: 1.59 us -> 2.33 us  [on_device(): pl.pallas_call(functools.partial(first_kernel, own, cols), out_shape=jax....]
    pallas_call x1 -> x2, Pallas kernels: 3.02 us -> 3.3 us  [the longest x1 2.77 us: on_device(): pl.pallas_call(functools.partial(project_kernel, rows, cols, peers), out_...]
  transfers between devices with their start and end apart: 1 -> 2, of which waited for: 1 -> 1; matrix products, arithmetic and copies ran while one was open for 0% -> 0% of each run, Pallas kernels for 3% -> 6%
where the time goes in v4:
time: 47.2 us; the launch traced here: 46.9 us
  blocking collectives  16.6 us (35%)
  waiting for transfers between devices  15.4 us (33%)
  Pallas kernels  10 us (21%)
  starting transfers between devices  4.19 us (9%)
  local copies, waits for them, and re-layouts  0.63 us (1%)
    all_to_all x1, blocking collectives, on_device(): lax.all_to_all(message, 'row', split_axis=0, concat_axis=0, axis_index_gr...  16.6 us
    all_to_all x1, waiting for transfers between devices, on_device(): lax.all_to_all(mixed, 'row', split_axis=0, concat_axis=0, tiled=True)  15.4 us
    all_to_all x1, starting transfers between devices, on_device(): lax.all_to_all(mixed, 'row', split_axis=0, concat_axis=0, tiled=True)  4.19 us
    pallas_call x1, Pallas kernels, on_device(): pl.pallas_call(functools.partial(second_kernel, own, cols), out_shape=jax...  3.17 us
    pallas_call x1, Pallas kernels, on_device(): pl.pallas_call(functools.partial(project_kernel, rows, cols, peers), out_...  2.77 us
    pallas_call x1, Pallas kernels, on_device(): pl.pallas_call(functools.partial(first_kernel, own, cols), out_shape=jax....  2.33 us
    pallas_call x1, Pallas kernels, on_device(): pl.pallas_call(functools.partial(output_kernel, own), out_shape=jax.Shape...  1.2 us
  transfers between devices with their start and end apart: 2, of which 1 were waited for; matrix products, arithmetic and copies ran while one was open for 0% of the time, Pallas kernels for 6%

profile of v4, /device:TPU:0, one launch (start us, length us, event | category | flops | bytes accessed | tf_op | source)
XLA Modules:
  0.0 46.9 jit_solution(3130619695455973761)
XLA Ops:
  0.0 2.8 %project.1 = (bf16[8,288,128]{2,1,0:T(8,128)(2,1)}, bf16[128,1152]{1,0:T(8,128)(2,1)}) custom-call(s32[2,2]{1,0:T(2,128)} %tile_hbm.1, s32[1,192]{1,0:T(1,128)} %bitcast.7, bf16[1152,128]{1,0:T(8,128)(2,1)} %bitcast.6, f32[1,128]{1,0:T(1,128)} %bitcast.8, bf16[128,640]{1,0:T(8,128)(2,1)} %w_hbm.3), custom_call_target="tpu_custom_call" | custom-call | tf_op jit(solution)/shard_map/project/pallas_call | solution.py:215
  2.8 16.6 %all_to_all.10.own_ref = bf16[8,288,128]{2,1,0:T(8,128)(2,1)S(1)} all-to-all(bf16[8,288,128]{2,1,0:T(8,128)(2,1)} %get-tuple-element.10), channel_id=1, replica_groups={{0,2,4,6,8,10,12,14},{16,18,20,22,24,26,28,30},{1,3,5,7,9,11,13,15},{17..., dimensions={0} | all-to-all | bytes 1179648 | tf_op jit(solution)/shard_map/all_to_all | solution.py:234
  19.4 0.0 collective-permute-start
  19.4 2.3 %first.1.first_ref = bf16[8,144,128]{2,1,0:T(8,128)(2,1)S(1)} custom-call(bf16[8,288,128]{2,1,0:T(8,128)(2,1)S(1)} %all_to_all.10.own_ref), custom_call_target="tpu_custom_call" | custom-call | flops 56623104 | bytes 2359296 | tf_op jit(solution)/shard_map/first/pallas_call | solution.py:267
  21.7 0.0 collective-permute-done.other_ref
  21.7 3.2 %second.1 = bf16[16,144,128]{2,1,0:T(8,128)(2,1)} custom-call(bf16[8,288,128]{2,1,0:T(8,128)(2,1)S(1)} %all_to_all.10.own_ref, bf16[8,288,128]{2,1,0:T(8,128)(2,1)S(1)} %collective-permute-done.other_ref, bf16[8,144,128]{2,1,0:T(8,128)(2,1)S(1)} %first.1.first_ref), custom_call_target="tpu_custom_call" | custom-call | tf_op jit(solution)/shard_map/second/pallas_call | solution.py:279
  24.9 0.0 copy-start
  24.9 0.0 copy-start.1
  24.9 0.0 copy-start.2
  24.9 4.2 %all-to-all-start.1 = ((bf16[16,144,128]{2,1,0:T(8,128)(2,1)}), bf16[16,144,128]{2,1,0:T(8,128)(2,1)S(1)}, u32[]{:S(2)}, u32[]{:S(2)}) async-start(bf16[16,144,128]{2,1,0:T(8,128)(2,1)} %second.1), calls=%async_computation.1 | async-start | bytes 1179648 | tf_op jit(solution)/shard_map/all_to_all | solution.py:288
  29.1 0.0 copy-start.3
  29.1 0.0 copy-done
  29.1 0.0 copy-done.1
  29.1 0.0 copy-done.2
  29.1 0.6 %copy-done.3 = f32[128]{0:T(128)S(1)} copy-done((f32[128]{0:T(128)S(1)}, f32[128]{0:T(128)}, u32[]{:S(2)}) %copy-start.3) | copy-done | bytes 536
  29.7 0.5 %gate.1 = (f32[128,1152]{1,0:T(8,128)S(1)}, bf16[128,128]{1,0:T(8,128)(2,1)S(1)}, f32[128,128]{1,0:T(8,128)S(1)}) custom-call(bf16[128,1152]{1,0:T(8,128)(2,1)S(1)} %copy-done.1, bf16[128,640]{1,0:T(8,128)(2,1)S(1)} %copy-done, f32[1,128]{1,0:T(1,128)S(1)} %bitcast.5, bf16[128,128]{1,0:T(8,128)(2,1)S(1)} %copy-done.2), custom_call_target="tpu_custom_call" | custom-call | flops 37748736 | bytes 589824 | tf_op jit(solution)/shard_map/gate/pallas_call | solution.py:242
  30.3 15.4 %all-to-all-done.1.mixed_ref = bf16[16,144,128]{2,1,0:T(8,128)(2,1)S(1)} async-done(((bf16[16,144,128]{2,1,0:T(8,128)(2,1)}), bf16[16,144,128]{2,1,0:T(8,128)(2,1)S(1)}, u32[]{:S(2)}, u32[]{:S(2)}) %all-to-all-start.1) | async-done | bytes 589856 | tf_op jit(solution)/shard_map/all_to_all | solution.py:288
  45.7 1.2 %output.1 = bf16[1152,128]{1,0:T(8,128)(2,1)} custom-call(bf16[16,144,128]{2,1,0:T(8,128)(2,1)S(1)} %all-to-all-done.1.mixed_ref, f32[128,1152]{1,0:T(8,128)S(1)} %get-tuple-element.12.gate_ref, f32[128,128]{1,0:T(8,128)S(1)} %get-tuple-element.13.gain_ref, bf16[128,128]{1,0:T(8,128)(2,1)S(1)} %get-tuple-element.14.w_t_ref), custom_call_target="tpu_custom_call" | custom-call | tf_op jit(solution)/shard_map/output/pallas_call | solution.py:289
Async XLA Ops:
  19.4 2.3 %collective-permute-start = (bf16[8,288,128]{2,1,0:T(8,128)(2,1)S(1)}, bf16[8,288,128]{2,1,0:T(8,128)(2,1)S(1)}, u32[]{:S(2)}, u32[]{:S(2)}) collective-permute-start(bf16[8,288,128]{2,1,0:T(8,128)(2,1)S(1)} %all_to_all.10.own_ref), channel_id=1, source_target_pairs={{0,1},{1,0},{2,3},{3,2},{4,5},{5,4},{6,7},{7,6},{8,9},{9,8},{10,11... | collective-permute-start | bytes 1769480 | tf_op jit(solution)/shard_map/ppermute | solution.py:263
  24.9 4.2 %copy-start = (bf16[128,640]{1,0:T(8,128)(2,1)S(1)}, bf16[128,640]{1,0:T(8,128)(2,1)}, u32[]{:S(2)}) copy-start(bf16[128,640]{1,0:T(8,128)(2,1)} %w_hbm.3) | copy-start | bytes 491524
  24.9 4.2 %copy-start.1 = (bf16[128,1152]{1,0:T(8,128)(2,1)S(1)}, bf16[128,1152]{1,0:T(8,128)(2,1)}, u32[]{:S(2)}) copy-start(bf16[128,1152]{1,0:T(8,128)(2,1)} %get-tuple-element.11.normed_ref) | copy-start | bytes 884740
  24.9 4.2 %copy-start.2 = (bf16[128,128]{1,0:T(8,128)(2,1)S(1)}, bf16[128,128]{1,0:T(8,128)(2,1)}, u32[]{:S(2)}) copy-start(bf16[128,128]{1,0:T(8,128)(2,1)} %w_out_hbm.1) | copy-start | bytes 98308
  24.9 20.8 %all-to-all-start.1 = ((bf16[16,144,128]{2,1,0:T(8,128)(2,1)}), bf16[16,144,128]{2,1,0:T(8,128)(2,1)S(1)}, u32[]{:S(2)}, u32[]{:S(2)}) async-start(bf16[16,144,128]{2,1,0:T(8,128)(2,1)} %second.1), calls=%async_computation.1 | async-start | bytes 1179648 | tf_op jit(solution)/shard_map/all_to_all | solution.py:288
  29.1 0.7 %copy-start.3 = (f32[128]{0:T(128)S(1)}, f32[128]{0:T(128)}, u32[]{:S(2)}) copy-start(f32[128]{0:T(128)} %param.12) | copy-start | bytes 1540

commit v5 on v4

--- a/solution.py
+++ b/solution.py
@@ -120,70 +120,94 @@
     gain_ref[...] = jnp.broadcast_to(column(gain[...]), gain_ref.shape)
 
 
-def take_channel(ref, side, channel, own, cols):
+def unpack(message_ref, side, spread_ref, own, cols):
     tokens, groups = cycle_of(cols)
-    count = ref.shape[0] // (own * groups * 2)
-    lanes = [
-        ref[pl.ds((side * groups + group) * own + channel, count, stride=own * groups * 2), :]
-        for group in range(groups)
-    ]
-    found = []
-    for token in range(tokens):
-        start, pieces = token * cols, []
-        while start < (token + 1) * cols:
-            group = start // LANES
-            end = min((group + 1) * LANES, (token + 1) * cols)
-            pieces.append(lanes[group][:, start - group * LANES : end - group * LANES])
-            start = end
-        found.append(jnp.concatenate(pieces, axis=1))
-    return jnp.concatenate(found, axis=0).astype(jnp.bfloat16)
-
-
-def put_channel(ref, held, channel, own, cols):
+    lane = lax.broadcasted_iota(jnp.int32, (own, LANES), 1)
+    peers, lines, _ = message_ref.shape
+    cycles = lines // (2 * groups * own)
+    for peer in range(peers):
+        for cycle in range(cycles):
+            base = (cycle * 2 + side) * groups * own
+            held = [
+                message_ref[peer, base + group * own : base + (group + 1) * own, :].astype(jnp.float32)
+                for group in range(groups)
+            ]
+            for token in range(tokens):
+                k = (peer * cycles + cycle) * tokens + token
+                for chunk in range(spread_ref.shape[0]):
+                    group, off = divmod(token * cols + chunk * LANES, LANES)
+                    value = held[group]
+                    if off and group + 1 < groups:
+                        value = jnp.where(lane >= off, value, held[group + 1])
+                    if off:
+                        value = pltpu.roll(value, LANES - off, axis=1)
+                    spread_ref[chunk, k * own : (k + 1) * own, :] = value
+
+
+def pack(spread_ref, mixed_ref, first, own, cols):
     tokens, groups = cycle_of(cols)
-    count = cols // tokens
-    lines = [
-        jnp.concatenate(
-            [held[piece, pl.ds(token, count, stride=tokens), :] for piece in range(held.shape[0])], axis=1
+    lane = lax.broadcasted_iota(jnp.int32, (own, LANES), 1)
+    cycles = mixed_ref.shape[1] // (groups * own)
+    for at in range(cols // tokens):
+        peer, cycle = divmod(at, cycles)
+        rolled = {}
+        lines = []
+        for group in range(groups):
+            value, here = None, 0
+            while here < LANES:
+                token, col = divmod(group * LANES + here, cols)
+                chunk, there = divmod(col, LANES)
+                shift = (here - there) % LANES
+                if (token, chunk, shift) not in rolled:
+                    line = (at * tokens + token) * own
+                    piece = spread_ref[chunk, line : line + own, :]
+                    rolled[token, chunk, shift] = pltpu.roll(piece, shift, axis=1) if shift else piece
+                piece = rolled[token, chunk, shift]
+                value = piece if value is None else jnp.where(lane >= here, piece, value)
+                here += min(LANES - here, LANES - there, cols - col)
+            lines.append(value)
+        base = cycle * groups * own
+        mixed_ref[first + peer, base : base + groups * own, :] = jnp.concatenate(lines, axis=0).astype(
+            jnp.bfloat16
         )
-        for token in range(tokens)
-    ]
-    for group in range(groups):
-        start, pieces = group * LANES, []
-        while start < (group + 1) * LANES:
-            token = start // cols
-            end = min((token + 1) * cols, (group + 1) * LANES)
-            pieces.append(lines[token][:, start - token * cols : end - token * cols])
-            start = end
-        ref[pl.ds(group * own + channel, count, stride=own * groups), :] = jnp.concatenate(pieces, axis=1)
-
-
-def triangle(own, cols, lefts, rights, held, mixed):
+
+
+def channel_of(spread_ref, channel, own):
+    count = spread_ref.shape[1] // own
+    return jnp.concatenate(
+        [spread_ref[chunk, pl.ds(channel, count, stride=own), :] for chunk in range(spread_ref.shape[0])],
+        axis=1,
+    ).astype(jnp.bfloat16)
+
+
+def multiply(lefts, rights, mixed, own, cols):
+    width = lefts.shape[0] * LANES
+    one = lax.broadcasted_iota(jnp.int32, (cols, width), 0) == lax.broadcasted_iota(jnp.int32, (cols, width), 1)
+    one = one.astype(jnp.bfloat16)
     for channel in range(own):
-        right = take_channel(rights, 1, channel, own, cols)
-        left = take_channel(lefts, 0, channel, own, cols)
-        total = lax.dot_general(left, right, (((0,), (0,)), ((), ())), preferred_element_type=jnp.float32)
-        at = channel % 2
-        for start in range(0, cols, LANES):
-            width = min(LANES, cols - start)
-            held[at, start // LANES, :, :width] = total[:, start : start + width]
-        put_channel(mixed, held.at[at], channel, own, cols)
-
-
-def first_kernel(own, cols, own_ref, mixed_ref, ours, held, mixed):
-    ours[...] = own_ref[...].astype(jnp.float32).reshape(ours.shape)
-    triangle(own, cols, ours, ours, held, mixed)
-    mixed_ref[...] = mixed[...].astype(jnp.bfloat16).reshape(mixed_ref.shape)
-
-
-def second_kernel(own, cols, own_ref, other_ref, first_ref, mixed_ref, ours, others, held, mixed):
+        left = channel_of(lefts, channel, own)
+        left_t = lax.dot_general(one, left, (((1,), (1,)), ((), ())), preferred_element_type=jnp.float32)
+        total = jnp.dot(left_t.astype(jnp.bfloat16), rights[channel], preferred_element_type=jnp.float32)
+        for chunk in range(mixed.shape[0]):
+            mixed[chunk, pl.ds(channel, cols, stride=own), :] = total[:, chunk * LANES : (chunk + 1) * LANES]
+
+
+def first_kernel(own, cols, message_ref, mixed_ref, right_ref, lefts, rights, mixed):
+    unpack(message_ref, 0, lefts, own, cols)
+    unpack(message_ref, 1, rights, own, cols)
+    for channel in range(own):
+        right_ref[channel] = channel_of(rights, channel, own)
+    multiply(lefts, right_ref, mixed, own, cols)
+    pack(mixed, mixed_ref, 0, own, cols)
+
+
+def second_kernel(own, cols, other_ref, right_ref, first_ref, mixed_ref, lefts, mixed):
     half = first_ref.shape[0]
     at = lax.axis_index("col")
-    ours[...] = own_ref[...].astype(jnp.float32).reshape(ours.shape)
-    others[...] = other_ref[...].astype(jnp.float32).reshape(others.shape)
     mixed_ref[pl.ds(at * half, half)] = first_ref[...]
-    triangle(own, cols, others, ours, held, mixed)
-    mixed_ref[pl.ds((1 - at) * half, half)] = mixed[...].astype(jnp.bfloat16).reshape(first_ref.shape)
+    unpack(other_ref, 0, lefts, own, cols)
+    multiply(lefts, right_ref, mixed, own, cols)
+    pack(mixed, mixed_ref, (1 - at) * half, own, cols)
 
 
 def output_kernel(own, mixed_ref, gate_ref, gain_ref, w_t_ref, update_ref):
@@ -261,18 +285,22 @@
         name="gate",
     )(normed, w_proj, gain_mid[None, :], w_out)
     other = lax.ppermute(message, "col", [(0, 1), (1, 0)])
-    blocks = pltpu.VMEM((peers * 2 * lines, LANES), jnp.float32)
-    held = pltpu.VMEM((2, pl.cdiv(cols, LANES), cols, LANES), jnp.float32)
-    out = pltpu.VMEM((half * lines, LANES), jnp.float32)
-    first = pl.pallas_call(
+    chunks = pl.cdiv(cols, LANES)
+    depth = peers * rows
+    spread = pltpu.VMEM((chunks, depth * own, LANES), jnp.float32)
+    held = pltpu.VMEM((chunks, cols * own, LANES), jnp.float32)
+    first, right = pl.pallas_call(
         functools.partial(first_kernel, own, cols),
-        out_shape=jax.ShapeDtypeStruct((half, lines, LANES), jnp.bfloat16),
+        out_shape=(
+            jax.ShapeDtypeStruct((half, lines, LANES), jnp.bfloat16),
+            jax.ShapeDtypeStruct((own, depth, chunks * LANES), jnp.bfloat16),
+        ),
         in_specs=[VMEM],
-        out_specs=VMEM,
-        scratch_shapes=[blocks, held, out],
+        out_specs=(VMEM, VMEM),
+        scratch_shapes=[spread, spread, held],
         compiler_params=params,
         cost_estimate=pl.CostEstimate(
-            flops=2 * own * cols * cols * tokens, bytes_accessed=8 * shares * lines * LANES, transcendentals=0
+            flops=4 * own * cols * cols * depth, bytes_accessed=8 * shares * lines * LANES, transcendentals=0
         ),
         name="first",
     )(message)
@@ -281,10 +309,10 @@
         out_shape=jax.ShapeDtypeStruct((shares, lines, LANES), jnp.bfloat16),
         in_specs=[VMEM, VMEM, VMEM],
         out_specs=VMEM,
-        scratch_shapes=[blocks, blocks, held, out],
+        scratch_shapes=[spread, held],
         compiler_params=params,
         name="second",
-    )(message, other, first)
+    )(other, right, first)
     mixed = lax.all_to_all(mixed, "row", split_axis=0, concat_axis=0, tiled=True)
     update = pl.pallas_call(
         functools.partial(output_kernel, own),

time: 47.2 us -> 47.8 us (1.013)
  Pallas kernels: 10 us -> 10.6 us
  transfers between devices with their start and end apart: 2 -> 2, of which waited for: 1 -> 1; matrix products, arithmetic and copies ran while one was open for 0% -> 0% of each run, Pallas kernels for 6% -> 7%
where the time goes in v5:
time: 47.8 us; the launch traced here: 47.5 us
  blocking collectives  16.6 us (35%)
  waiting for transfers between devices  15.4 us (32%)
  Pallas kernels  10.6 us (22%)
  starting transfers between devices  4.19 us (9%)
  local copies, waits for them, and re-layouts  0.63 us (1%)
    all_to_all x1, blocking collectives, on_device(): lax.all_to_all(message, 'row', split_axis=0, concat_axis=0, axis_index_gr...  16.6 us
    all_to_all x1, waiting for transfers between devices, on_device(): lax.all_to_all(mixed, 'row', split_axis=0, concat_axis=0, tiled=True)  15.4 us
    all_to_all x1, starting transfers between devices, on_device(): lax.all_to_all(mixed, 'row', split_axis=0, concat_axis=0, tiled=True)  4.19 us
    pallas_call x1, Pallas kernels, on_device(): pl.pallas_call(functools.partial(second_kernel, own, cols), out_shape=jax...  3.48 us
    pallas_call x1, Pallas kernels, on_device(): pl.pallas_call(functools.partial(project_kernel, rows, cols, peers), out_...  2.76 us
    pallas_call x1, Pallas kernels, on_device(): pl.pallas_call(functools.partial(first_kernel, own, cols), out_shape=(jax...  2.66 us
    pallas_call x1, Pallas kernels, on_device(): pl.pallas_call(functools.partial(output_kernel, own), out_shape=jax.Shape...  1.2 us
  transfers between devices with their start and end apart: 2, of which 1 were waited for; matrix products, arithmetic and copies ran while one was open for 0% of the time, Pallas kernels for 7%

profile of v5, /device:TPU:0, one launch (start us, length us, event | category | flops | bytes accessed | tf_op | source)
XLA Modules:
  0.0 47.5 jit_solution(249948845767335351)
XLA Ops:
  0.0 2.8 %project.1 = (bf16[8,288,128]{2,1,0:T(8,128)(2,1)}, bf16[128,1152]{1,0:T(8,128)(2,1)}) custom-call(s32[2,2]{1,0:T(2,128)} %tile_hbm.1, s32[1,192]{1,0:T(1,128)} %bitcast.7, bf16[1152,128]{1,0:T(8,128)(2,1)} %bitcast.6, f32[1,128]{1,0:T(1,128)} %bitcast.8, bf16[128,640]{1,0:T(8,128)(2,1)} %w_hbm.3), custom_call_target="tpu_custom_call" | custom-call | tf_op jit(solution)/shard_map/project/pallas_call | solution.py:239
  2.8 16.6 %all_to_all.10.message_ref = bf16[8,288,128]{2,1,0:T(8,128)(2,1)S(1)} all-to-all(bf16[8,288,128]{2,1,0:T(8,128)(2,1)} %get-tuple-element.12), channel_id=1, replica_groups={{0,2,4,6,8,10,12,14},{16,18,20,22,24,26,28,30},{1,3,5,7,9,11,13,15},{17..., dimensions={0} | all-to-all | bytes 1179648 | tf_op jit(solution)/shard_map/all_to_all | solution.py:258
  19.3 0.0 collective-permute-start
  19.4 2.7 %first.1 = (bf16[8,144,128]{2,1,0:T(8,128)(2,1)S(1)}, bf16[16,96,128]{2,1,0:T(8,128)(2,1)S(1)}) custom-call(bf16[8,288,128]{2,1,0:T(8,128)(2,1)S(1)} %all_to_all.10.message_ref), custom_call_target="tpu_custom_call" | custom-call | flops 56623104 | bytes 2359296 | tf_op jit(solution)/shard_map/first/pallas_call | solution.py:292
  22.0 0.0 collective-permute-done.other_ref
  22.0 3.5 %second.1 = bf16[16,144,128]{2,1,0:T(8,128)(2,1)} custom-call(bf16[8,288,128]{2,1,0:T(8,128)(2,1)S(1)} %collective-permute-done.other_ref, bf16[16,96,128]{2,1,0:T(8,128)(2,1)S(1)} %get-tuple-element.13.right_ref, bf16[8,144,128]{2,1,0:T(8,128)(2,1)S(1)} %get-tuple-element.14.first_ref), custom_call_target="tpu_custom_call" | custom-call | tf_op jit(solution)/shard_map/second/pallas_call | solution.py:307
  25.5 0.0 copy-start
  25.5 0.0 copy-start.1
  25.5 0.0 copy-start.2
  25.5 4.2 %all-to-all-start.1 = ((bf16[16,144,128]{2,1,0:T(8,128)(2,1)}), bf16[16,144,128]{2,1,0:T(8,128)(2,1)S(1)}, u32[]{:S(2)}, u32[]{:S(2)}) async-start(bf16[16,144,128]{2,1,0:T(8,128)(2,1)} %second.1), calls=%async_computation.1 | async-start | bytes 1179648 | tf_op jit(solution)/shard_map/all_to_all | solution.py:316
  29.7 0.0 copy-start.3
  29.7 0.0 copy-done
  29.7 0.0 copy-done.1
  29.7 0.0 copy-done.2
  29.8 0.6 %copy-done.3 = f32[128]{0:T(128)S(1)} copy-done((f32[128]{0:T(128)S(1)}, f32[128]{0:T(128)}, u32[]{:S(2)}) %copy-start.3) | copy-done | bytes 536
  30.4 0.5 %gate.1 = (f32[128,1152]{1,0:T(8,128)S(1)}, bf16[128,128]{1,0:T(8,128)(2,1)S(1)}, f32[128,128]{1,0:T(8,128)S(1)}) custom-call(bf16[128,1152]{1,0:T(8,128)(2,1)S(1)} %copy-done.1, bf16[128,640]{1,0:T(8,128)(2,1)S(1)} %copy-done, f32[1,128]{1,0:T(1,128)S(1)} %bitcast.5, bf16[128,128]{1,0:T(8,128)(2,1)S(1)} %copy-done.2), custom_call_target="tpu_custom_call" | custom-call | flops 37748736 | bytes 589824 | tf_op jit(solution)/shard_map/gate/pallas_call | solution.py:266
  30.9 15.4 %all-to-all-done.1.mixed_ref = bf16[16,144,128]{2,1,0:T(8,128)(2,1)S(1)} async-done(((bf16[16,144,128]{2,1,0:T(8,128)(2,1)}), bf16[16,144,128]{2,1,0:T(8,128)(2,1)S(1)}, u32[]{:S(2)}, u32[]{:S(2)}) %all-to-all-start.1) | async-done | bytes 589856 | tf_op jit(solution)/shard_map/all_to_all | solution.py:316
  46.3 1.2 %output.1 = bf16[1152,128]{1,0:T(8,128)(2,1)} custom-call(bf16[16,144,128]{2,1,0:T(8,128)(2,1)S(1)} %all-to-all-done.1.mixed_ref, f32[128,1152]{1,0:T(8,128)S(1)} %get-tuple-element.16.gate_ref, f32[128,128]{1,0:T(8,128)S(1)} %get-tuple-element.17.gain_ref, bf16[128,128]{1,0:T(8,128)(2,1)S(1)} %get-tuple-element.18.w_t_ref), custom_call_target="tpu_custom_call" | custom-call | tf_op jit(solution)/shard_map/output/pallas_call | solution.py:317
Async XLA Ops:
  19.3 2.7 %collective-permute-start = (bf16[8,288,128]{2,1,0:T(8,128)(2,1)S(1)}, bf16[8,288,128]{2,1,0:T(8,128)(2,1)S(1)}, u32[]{:S(2)}, u32[]{:S(2)}) collective-permute-start(bf16[8,288,128]{2,1,0:T(8,128)(2,1)S(1)} %all_to_all.10.message_ref), channel_id=1, source_target_pairs={{0,1},{1,0},{2,3},{3,2},{4,5},{5,4},{6,7},{7,6},{8,9},{9,8},{10,11... | collective-permute-start | bytes 1769480 | tf_op jit(solution)/shard_map/ppermute | solution.py:287
  25.5 4.2 %copy-start = (bf16[128,640]{1,0:T(8,128)(2,1)S(1)}, bf16[128,640]{1,0:T(8,128)(2,1)}, u32[]{:S(2)}) copy-start(bf16[128,640]{1,0:T(8,128)(2,1)} %w_hbm.3) | copy-start | bytes 491524
  25.5 4.2 %copy-start.1 = (bf16[128,1152]{1,0:T(8,128)(2,1)S(1)}, bf16[128,1152]{1,0:T(8,128)(2,1)}, u32[]{:S(2)}) copy-start(bf16[128,1152]{1,0:T(8,128)(2,1)} %get-tuple-element.15.normed_ref) | copy-start | bytes 884740
  25.5 4.2 %copy-start.2 = (bf16[128,128]{1,0:T(8,128)(2,1)S(1)}, bf16[128,128]{1,0:T(8,128)(2,1)}, u32[]{:S(2)}) copy-start(bf16[128,128]{1,0:T(8,128)(2,1)} %w_out_hbm.1) | copy-start | bytes 98308
  25.5 20.8 %all-to-all-start.1 = ((bf16[16,144,128]{2,1,0:T(8,128)(2,1)}), bf16[16,144,128]{2,1,0:T(8,128)(2,1)S(1)}, u32[]{:S(2)}, u32[]{:S(2)}) async-start(bf16[16,144,128]{2,1,0:T(8,128)(2,1)} %second.1), calls=%async_computation.1 | async-start | bytes 1179648 | tf_op jit(solution)/shard_map/all_to_all | solution.py:316
  29.7 0.7 %copy-start.3 = (f32[128]{0:T(128)S(1)}, f32[128]{0:T(128)}, u32[]{:S(2)}) copy-start(f32[128]{0:T(128)} %param.12) | copy-start | bytes 1540

commit v6 on v5

--- a/solution.py
+++ b/solution.py
@@ -15,6 +15,7 @@
 VMEM_BYTES = 32 * 1024 * 1024
 WHOLE_VMEM_BYTES = 64 * 1024 * 1024
 VMEM = pl.BlockSpec(memory_space=pltpu.VMEM)
+ANY = pl.BlockSpec(memory_space=pl.ANY)
 HBM = pl.BlockSpec(memory_space=pltpu.HBM)
 SMEM = pl.BlockSpec(memory_space=pltpu.SMEM)
 
@@ -109,13 +110,17 @@
                 )
 
 
-def gate_kernel(normed_ref, w_hbm, gain_hbm, w_out_hbm, gate_ref, w_out_ref, gain_ref, w, w_out, gain, sems):
-    width = w_hbm.shape[0]
-    last = w_hbm.shape[1] - width
-    fetch(sems, (w_hbm, w), (w_out_hbm, w_out), (gain_hbm, gain))
+def gate_kernel(normed_ref, w_hbm, gate_ref, done_ref, w, sems):
+    last = w_hbm.shape[1] - w_hbm.shape[0]
+    fetch(sems, (w_hbm, w))
     gate_ref[...] = sigmoid(
         jnp.dot(w[:, last:].T, normed_ref[...], preferred_element_type=jnp.float32)
     )
+    done_ref[...] = jnp.zeros_like(done_ref)
+
+
+def weights_kernel(_, gain_hbm, w_out_hbm, w_out_ref, gain_ref, w_out, gain, sems):
+    fetch(sems, (w_out_hbm, w_out), (gain_hbm, gain))
     w_out_ref[...] = w_out[...].T
     gain_ref[...] = jnp.broadcast_to(column(gain[...]), gain_ref.shape)
 
@@ -180,33 +185,56 @@
     ).astype(jnp.bfloat16)
 
 
-def multiply(lefts, rights, mixed, own, cols):
-    width = lefts.shape[0] * LANES
+def multiply(lefts, rights, left, left_t, mixed, own, cols):
+    _, deep, width = rights.shape
+    depth = lefts.shape[1] // own
     one = lax.broadcasted_iota(jnp.int32, (cols, width), 0) == lax.broadcasted_iota(jnp.int32, (cols, width), 1)
     one = one.astype(jnp.bfloat16)
+    if depth < deep:
+        left[:, depth:, :] = jnp.zeros((own, deep - depth, width), jnp.bfloat16)
     for channel in range(own):
-        left = channel_of(lefts, channel, own)
-        left_t = lax.dot_general(one, left, (((1,), (1,)), ((), ())), preferred_element_type=jnp.float32)
-        total = jnp.dot(left_t.astype(jnp.bfloat16), rights[channel], preferred_element_type=jnp.float32)
-        for chunk in range(mixed.shape[0]):
-            mixed[chunk, pl.ds(channel, cols, stride=own), :] = total[:, chunk * LANES : (chunk + 1) * LANES]
-
-
-def first_kernel(own, cols, message_ref, mixed_ref, right_ref, lefts, rights, mixed):
+        left[channel, :depth, :] = channel_of(lefts, channel, own)
+    for pair in range(0, own, 2):
+        both = lax.dot_general(
+            one,
+            left[pair : pair + 2].reshape(2 * deep, width),
+            (((1,), (1,)), ((), ())),
+            preferred_element_type=jnp.float32,
+        ).astype(jnp.bfloat16)
+        left_t[pair] = both[:, :deep]
+        left_t[pair + 1] = both[:, deep:]
+    for pair in range(0, own, 2):
+        both = jnp.dot(
+            left_t[pair : pair + 2].reshape(2 * cols, deep),
+            jnp.concatenate([rights[pair], rights[pair + 1]], axis=1),
+            preferred_element_type=jnp.float32,
+        )
+        for at in range(2):
+            for chunk in range(mixed.shape[0]):
+                start = at * width + chunk * LANES
+                mixed[chunk, pl.ds(pair + at, cols, stride=own), :] = both[
+                    at * cols : (at + 1) * cols, start : start + LANES
+                ]
+
+
+def first_kernel(own, cols, message_ref, _, mixed_ref, right_ref, lefts, rights, left, left_t, mixed):
+    unpack(message_ref, 1, rights, own, cols)
+    depth = rights.shape[1] // own
+    if depth < right_ref.shape[1]:
+        right_ref[:, depth:, :] = jnp.zeros((own, right_ref.shape[1] - depth, right_ref.shape[2]), jnp.bfloat16)
+    for channel in range(own):
+        right_ref[channel, :depth, :] = channel_of(rights, channel, own)
     unpack(message_ref, 0, lefts, own, cols)
-    unpack(message_ref, 1, rights, own, cols)
-    for channel in range(own):
-        right_ref[channel] = channel_of(rights, channel, own)
-    multiply(lefts, right_ref, mixed, own, cols)
+    multiply(lefts, right_ref, left, left_t, mixed, own, cols)
     pack(mixed, mixed_ref, 0, own, cols)
 
 
-def second_kernel(own, cols, other_ref, right_ref, first_ref, mixed_ref, lefts, mixed):
+def second_kernel(own, cols, other_ref, right_ref, first_ref, mixed_ref, lefts, left, left_t, mixed):
     half = first_ref.shape[0]
     at = lax.axis_index("col")
     mixed_ref[pl.ds(at * half, half)] = first_ref[...]
     unpack(other_ref, 0, lefts, own, cols)
-    multiply(lefts, right_ref, mixed, own, cols)
+    multiply(lefts, right_ref, left, left_t, mixed, own, cols)
     pack(mixed, mixed_ref, (1 - at) * half, own, cols)
 
 
@@ -263,56 +291,75 @@
         axis_index_groups=[list(range(part * peers, (part + 1) * peers)) for part in range(PARTS)],
         tiled=True,
     )
-    gate, w_out_t, gain = pl.pallas_call(
+    gate, done = pl.pallas_call(
         gate_kernel,
         out_shape=(
             jax.ShapeDtypeStruct((width, positions), jnp.float32),
-            jax.ShapeDtypeStruct(w_out.shape[::-1], jnp.bfloat16),
-            jax.ShapeDtypeStruct((hidden, LANES), jnp.float32),
-        ),
-        in_specs=[VMEM] + [HBM] * 3,
-        out_specs=(VMEM, VMEM, VMEM),
-        scratch_shapes=[
-            pltpu.VMEM(w_proj.shape, jnp.bfloat16),
-            pltpu.VMEM(w_out.shape, jnp.bfloat16),
-            pltpu.VMEM((1, hidden), jnp.float32),
-            pltpu.SemaphoreType.DMA((3,)),
-        ],
+            jax.ShapeDtypeStruct((8, LANES), jnp.float32),
+        ),
+        in_specs=[VMEM, HBM],
+        out_specs=(VMEM, VMEM),
+        scratch_shapes=[pltpu.VMEM(w_proj.shape, jnp.bfloat16), pltpu.SemaphoreType.DMA((1,))],
         compiler_params=params,
         cost_estimate=pl.CostEstimate(
             flops=2 * width * width * positions, bytes_accessed=4 * width * positions, transcendentals=0
         ),
         name="gate",
-    )(normed, w_proj, gain_mid[None, :], w_out)
+    )(normed, w_proj)
+    message, done = lax.optimization_barrier((message, done))
     other = lax.ppermute(message, "col", [(0, 1), (1, 0)])
     chunks = pl.cdiv(cols, LANES)
     depth = peers * rows
+    deep = pl.cdiv(depth, LANES) * LANES
     spread = pltpu.VMEM((chunks, depth * own, LANES), jnp.float32)
-    held = pltpu.VMEM((chunks, cols * own, LANES), jnp.float32)
+    held = [
+        pltpu.VMEM((own, deep, chunks * LANES), jnp.bfloat16),
+        pltpu.VMEM((own, cols, deep), jnp.bfloat16),
+        pltpu.VMEM((chunks, cols * own, LANES), jnp.float32),
+    ]
+    cost = pl.CostEstimate(
+        flops=4 * own * cols * cols * depth, bytes_accessed=8 * shares * lines * LANES, transcendentals=0
+    )
     first, right = pl.pallas_call(
         functools.partial(first_kernel, own, cols),
         out_shape=(
             jax.ShapeDtypeStruct((half, lines, LANES), jnp.bfloat16),
-            jax.ShapeDtypeStruct((own, depth, chunks * LANES), jnp.bfloat16),
-        ),
-        in_specs=[VMEM],
+            jax.ShapeDtypeStruct((own, deep, chunks * LANES), jnp.bfloat16),
+        ),
+        in_specs=[VMEM, VMEM],
         out_specs=(VMEM, VMEM),
-        scratch_shapes=[spread, spread, held],
-        compiler_params=params,
-        cost_estimate=pl.CostEstimate(
-            flops=4 * own * cols * cols * depth, bytes_accessed=8 * shares * lines * LANES, transcendentals=0
-        ),
+        scratch_shapes=[spread, spread, *held],
+        compiler_params=params,
+        cost_estimate=cost,
         name="first",
-    )(message)
+    )(message, done)
     mixed = pl.pallas_call(
         functools.partial(second_kernel, own, cols),
         out_shape=jax.ShapeDtypeStruct((shares, lines, LANES), jnp.bfloat16),
         in_specs=[VMEM, VMEM, VMEM],
         out_specs=VMEM,
-        scratch_shapes=[spread, held],
-        compiler_params=params,
+        scratch_shapes=[spread, *held],
+        compiler_params=params,
+        cost_estimate=cost,
         name="second",
     )(other, right, first)
+    w_out_t, gain = pl.pallas_call(
+        weights_kernel,
+        out_shape=(
+            jax.ShapeDtypeStruct(w_out.shape[::-1], jnp.bfloat16),
+            jax.ShapeDtypeStruct((hidden, LANES), jnp.float32),
+        ),
+        in_specs=[ANY, HBM, HBM],
+        out_specs=(VMEM, VMEM),
+        scratch_shapes=[
+            pltpu.VMEM(w_out.shape, jnp.bfloat16),
+            pltpu.VMEM((1, hidden), jnp.float32),
+            pltpu.SemaphoreType.DMA((2,)),
+        ],
+        compiler_params=params,
+        cost_estimate=pl.CostEstimate(flops=hidden * width, bytes_accessed=8 * hidden * width, transcendentals=0),
+        name="weights",
+    )(right, gain_mid[None, :], w_out)
     mixed = lax.all_to_all(mixed, "row", split_axis=0, concat_axis=0, tiled=True)
     update = pl.pallas_call(
         functools.partial(output_kernel, own),

time: 47.8 us -> 45.8 us (0.958)
  blocking collectives: 16.6 us -> 0 us
  waiting for transfers between devices: 15.4 us -> 25.7 us
  starting transfers between devices: 4.19 us -> 11.2 us
  Pallas kernels: 10.6 us -> 7.75 us
    all_to_all x1 -> x0, blocking collectives: 16.6 us -> none  [on_device(): lax.all_to_all(message, 'row', split_axis=0, concat_axis=0, axis_index_gr...]
    all_to_all x0 -> x1, waiting for transfers between devices: none -> 9.21 us  [on_device(): lax.all_to_all(message, 'row', split_axis=0, concat_axis=0, axis_index_gr...]
    all_to_all x0 -> x1, starting transfers between devices: none -> 6.33 us  [on_device(): lax.all_to_all(message, 'row', split_axis=0, concat_axis=0, axis_index_gr...]
    pallas_call x1, Pallas kernels: 3.48 us -> 1.87 us  [on_device(): pl.pallas_call(functools.partial(second_kernel, own, cols), out_shape=jax...]
    pallas_call x1, Pallas kernels: 2.66 us -> 1.22 us  [on_device(): pl.pallas_call(functools.partial(first_kernel, own, cols), out_shape=(jax...]
    ppermute x1, waiting for transfers between devices: 0.01 us -> 0.77 us  [on_device(): other = lax.ppermute(message, 'col', [(0, 1), (1, 0)])]
    all_to_all x1, starting transfers between devices: 4.19 us -> 4.89 us  [on_device(): lax.all_to_all(mixed, 'row', split_axis=0, concat_axis=0, tiled=True)]
  transfers between devices with their start and end apart: 2 -> 3, of which waited for: 1 -> 3; matrix products, arithmetic and copies ran while one was open for 0% -> 0% of each run, Pallas kernels for 7% -> 4%
where the time goes in v6:
time: 45.8 us; the launch traced here: 45.4 us
  waiting for transfers between devices  25.7 us (56%)
  starting transfers between devices  11.2 us (24%)
  Pallas kernels  7.75 us (17%)
  local copies, waits for them, and re-layouts  0.66 us (1%)
    all_to_all x1, waiting for transfers between devices, on_device(): lax.all_to_all(mixed, 'row', split_axis=0, concat_axis=0, tiled=True)  15.7 us
    all_to_all x1, waiting for transfers between devices, on_device(): lax.all_to_all(message, 'row', split_axis=0, concat_axis=0, axis_index_gr...  9.21 us
    all_to_all x1, starting transfers between devices, on_device(): lax.all_to_all(message, 'row', split_axis=0, concat_axis=0, axis_index_gr...  6.33 us
    all_to_all x1, starting transfers between devices, on_device(): lax.all_to_all(mixed, 'row', split_axis=0, concat_axis=0, tiled=True)  4.89 us
    pallas_call x1, Pallas kernels, on_device(): pl.pallas_call(functools.partial(project_kernel, rows, cols, peers), out_...  2.77 us
    pallas_call x1, Pallas kernels, on_device(): pl.pallas_call(functools.partial(second_kernel, own, cols), out_shape=jax...  1.87 us
    pallas_call x1, Pallas kernels, on_device(): pl.pallas_call(functools.partial(first_kernel, own, cols), out_shape=(jax...  1.22 us
    pallas_call x1, Pallas kernels, on_device(): pl.pallas_call(functools.partial(output_kernel, own), out_shape=jax.Shape...  1.2 us
  transfers between devices with their start and end apart: 3, of which 3 were waited for; matrix products, arithmetic and copies ran while one was open for 0% of the time, Pallas kernels for 4%

profile of v6, /device:TPU:0, one launch (start us, length us, event | category | flops | bytes accessed | tf_op | source)
XLA Modules:
  0.0 45.4 jit_solution(4484744650696516387)
XLA Ops:
  0.0 2.8 %project.1 = (bf16[8,288,128]{2,1,0:T(8,128)(2,1)}, bf16[128,1152]{1,0:T(8,128)(2,1)}) custom-call(s32[2,2]{1,0:T(2,128)} %tile_hbm.1, s32[1,192]{1,0:T(1,128)} %bitcast.7, bf16[1152,128]{1,0:T(8,128)(2,1)} %bitcast.6, f32[1,128]{1,0:T(1,128)} %bitcast.8, bf16[128,640]{1,0:T(8,128)(2,1)} %w_hbm.3), custom_call_target="tpu_custom_call" | custom-call | tf_op jit(solution)/shard_map/project/pallas_call | solution.py:267
  2.8 0.0 copy-start
  2.8 0.0 copy-start.1
  2.8 6.3 %all-to-all-start = ((bf16[8,288,128]{2,1,0:T(8,128)(2,1)}), bf16[8,288,128]{2,1,0:T(8,128)(2,1)S(1)}, u32[]{:S(2)}, u32[]{:S(2)}) async-start(bf16[8,288,128]{2,1,0:T(8,128)(2,1)} %get-tuple-element.15), calls=%async_computation | async-start | bytes 1179648 | tf_op jit(solution)/shard_map/all_to_all | solution.py:286
  9.1 0.0 copy-done
  9.1 0.0 copy-done.1
  9.1 0.5 %gate.1 = (f32[128,1152]{1,0:T(8,128)S(1)}, f32[8,128]{1,0:T(8,128)S(1)}) custom-call(bf16[128,1152]{1,0:T(8,128)(2,1)S(1)} %copy-done.1, bf16[128,640]{1,0:T(8,128)(2,1)S(1)} %copy-done), custom_call_target="tpu_custom_call" | custom-call | flops 37748736 | bytes 589824 | tf_op jit(solution)/shard_map/gate/pallas_call | solution.py:294
  9.6 9.2 %all-to-all-done.message_ref = bf16[8,288,128]{2,1,0:T(8,128)(2,1)S(1)} async-done(((bf16[8,288,128]{2,1,0:T(8,128)(2,1)}), bf16[8,288,128]{2,1,0:T(8,128)(2,1)S(1)}, u32[]{:S(2)}, u32[]{:S(2)}) %all-to-all-start) | async-done | bytes 589856 | tf_op jit(solution)/shard_map/all_to_all | solution.py:286
  18.9 0.0 collective-permute-start
  18.9 1.2 %first.1 = (bf16[8,144,128]{2,1,0:T(8,128)(2,1)S(1)}, bf16[16,128,128]{2,1,0:T(8,128)(2,1)S(1)}) custom-call(bf16[8,288,128]{2,1,0:T(8,128)(2,1)S(1)} %all-to-all-done.message_ref, f32[8,128]{1,0:T(8,128)S(1)} %get-tuple-element.19._), custom_call_target="tpu_custom_call" | custom-call | flops 56623104 | bytes 2359296 | tf_op jit(solution)/shard_map/first/pallas_call | solution.py:323
  20.1 0.8 %collective-permute-done.other_ref = bf16[8,288,128]{2,1,0:T(8,128)(2,1)S(1)} collective-permute-done((bf16[8,288,128]{2,1,0:T(8,128)(2,1)S(1)}, bf16[8,288,128]{2,1,0:T(8,128)(2,1)S(1)}, u32[]{:S(2)}, u32[]{:S(2)}) %collective-permute-start) | collective-permute-done | bytes 589856 | tf_op jit(solution)/shard_map/ppermute | solution.py:310
  20.9 1.9 %second.1 = bf16[16,144,128]{2,1,0:T(8,128)(2,1)} custom-call(bf16[8,288,128]{2,1,0:T(8,128)(2,1)S(1)} %collective-permute-done.other_ref, bf16[16,128,128]{2,1,0:T(8,128)(2,1)S(1)} %get-tuple-element.20.right_ref._, bf16[8,144,128]{2,1,0:T(8,128)(2,1)S(1)} %get-tuple-element.21.first_ref), custom_call_target="tpu_custom_call" | custom-call | flops 56623104 | bytes 2359296 | tf_op jit(solution)/shard_map/second/pallas_call | solution.py:336
  22.7 0.0 copy-start.2
  22.7 4.9 %all-to-all-start.1 = ((bf16[16,144,128]{2,1,0:T(8,128)(2,1)}), bf16[16,144,128]{2,1,0:T(8,128)(2,1)S(1)}, u32[]{:S(2)}, u32[]{:S(2)}) async-start(bf16[16,144,128]{2,1,0:T(8,128)(2,1)} %second.1), calls=%async_computation.1 | async-start | bytes 1179648 | tf_op jit(solution)/shard_map/all_to_all | solution.py:363
  27.6 0.0 copy-start.3
  27.6 0.0 copy-done.2
  27.7 0.6 %copy-done.3 = f32[128]{0:T(128)S(1)} copy-done((f32[128]{0:T(128)S(1)}, f32[128]{0:T(128)}, u32[]{:S(2)}) %copy-start.3) | copy-done | bytes 536
  28.3 0.2 weights.1
  28.5 15.7 %all-to-all-done.1.mixed_ref = bf16[16,144,128]{2,1,0:T(8,128)(2,1)S(1)} async-done(((bf16[16,144,128]{2,1,0:T(8,128)(2,1)}), bf16[16,144,128]{2,1,0:T(8,128)(2,1)S(1)}, u32[]{:S(2)}, u32[]{:S(2)}) %all-to-all-start.1) | async-done | bytes 589856 | tf_op jit(solution)/shard_map/all_to_all | solution.py:363
  44.2 1.2 %output.1 = bf16[1152,128]{1,0:T(8,128)(2,1)} custom-call(bf16[16,144,128]{2,1,0:T(8,128)(2,1)S(1)} %all-to-all-done.1.mixed_ref, f32[128,1152]{1,0:T(8,128)S(1)} %get-tuple-element.22.gate_ref, f32[128,128]{1,0:T(8,128)S(1)} %get-tuple-element.23.gain_ref, bf16[128,128]{1,0:T(8,128)(2,1)S(1)} %get-tuple-element.24.w_t_ref), custom_call_target="tpu_custom_call" | custom-call | tf_op jit(solution)/shard_map/output/pallas_call | solution.py:364
Async XLA Ops:
  2.8 6.4 %copy-start = (bf16[128,640]{1,0:T(8,128)(2,1)S(1)}, bf16[128,640]{1,0:T(8,128)(2,1)}, u32[]{:S(2)}) copy-start(bf16[128,640]{1,0:T(8,128)(2,1)} %w_hbm.3) | copy-start | bytes 491524
  2.8 6.3 %copy-start.1 = (bf16[128,1152]{1,0:T(8,128)(2,1)S(1)}, bf16[128,1152]{1,0:T(8,128)(2,1)}, u32[]{:S(2)}) copy-start(bf16[128,1152]{1,0:T(8,128)(2,1)} %get-tuple-element.16.normed_ref) | copy-start | bytes 884740
  2.8 16.1 %all-to-all-start = ((bf16[8,288,128]{2,1,0:T(8,128)(2,1)}), bf16[8,288,128]{2,1,0:T(8,128)(2,1)S(1)}, u32[]{:S(2)}, u32[]{:S(2)}) async-start(bf16[8,288,128]{2,1,0:T(8,128)(2,1)} %get-tuple-element.15), calls=%async_computation | async-start | bytes 1179648 | tf_op jit(solution)/shard_map/all_to_all | solution.py:286
  18.9 2.0 %collective-permute-start = (bf16[8,288,128]{2,1,0:T(8,128)(2,1)S(1)}, bf16[8,288,128]{2,1,0:T(8,128)(2,1)S(1)}, u32[]{:S(2)}, u32[]{:S(2)}) collective-permute-start(bf16[8,288,128]{2,1,0:T(8,128)(2,1)S(1)} %all-to-all-done.message_ref), channel_id=1, source_target_pairs={{0,1},{1,0},{2,3},{3,2},{4,5},{5,4},{6,7},{7,6},{8,9},{9,8},{10,11... | collective-permute-start | bytes 1769480 | tf_op jit(solution)/shard_map/ppermute | solution.py:310
  22.7 4.9 %copy-start.2 = (bf16[128,128]{1,0:T(8,128)(2,1)S(1)}, bf16[128,128]{1,0:T(8,128)(2,1)}, u32[]{:S(2)}) copy-start(bf16[128,128]{1,0:T(8,128)(2,1)} %w_out_hbm.1) | copy-start | bytes 98308
  22.7 21.4 %all-to-all-start.1 = ((bf16[16,144,128]{2,1,0:T(8,128)(2,1)}), bf16[16,144,128]{2,1,0:T(8,128)(2,1)S(1)}, u32[]{:S(2)}, u32[]{:S(2)}) async-start(bf16[16,144,128]{2,1,0:T(8,128)(2,1)} %second.1), calls=%async_computation.1 | async-start | bytes 1179648 | tf_op jit(solution)/shard_map/all_to_all | solution.py:363
  27.6 0.7 %copy-start.3 = (f32[128]{0:T(128)S(1)}, f32[128]{0:T(128)}, u32[]{:S(2)}) copy-start(f32[128]{0:T(128)} %param.12) | copy-start | bytes 1540

commit v7 on v6

v7 whole, which is shorter than its diff:
```python
import functools
import math

import jax
import jax.numpy as jnp
from jax import lax
from jax.experimental import pallas as pl
from jax.experimental.pallas import tpu as pltpu
from jax.sharding import PartitionSpec as P

TILE = 96
LANES = 128
EPS = 1e-05
PARTS = 2
VMEM_BYTES = 32 * 1024 * 1024
WHOLE_VMEM_BYTES = 64 * 1024 * 1024
VMEM = pl.BlockSpec(memory_space=pltpu.VMEM)
ANY = pl.BlockSpec(memory_space=pl.ANY)
HBM = pl.BlockSpec(memory_space=pltpu.HBM)
SMEM = pl.BlockSpec(memory_space=pltpu.SMEM)


def column(row):
    return jnp.broadcast_to(row, (8, row.shape[1])).T[:, :1]


def steps(at, width, count):
    total = jnp.zeros_like(at)
    for edge in range(1, count):
        total += (at >= edge * width).astype(jnp.int32)
    return total


def sigmoid(values):
    return 0.5 * jnp.tanh(0.5 * values) + 0.5


def keep_of(tile_ref, chain_ref, rows, cols):
    tokens = chain_ref.shape[1]
    tiles = tile_ref.shape[1]
    positions = rows * cols
    at = lax.broadcasted_iota(jnp.int32, (1, positions), 1)
    row = steps(at, cols, rows)
    k = lax.axis_index("row") * rows + row
    i = lax.axis_index("col") * cols + at - row * cols
    token = lax.broadcasted_iota(jnp.int32, (tokens, positions), 0)
    pick = (token == k).astype(jnp.float32) - (token == i).astype(jnp.float32)
    chains = jnp.broadcast_to(chain_ref[...].astype(jnp.bfloat16), (8, tokens))
    apart = jnp.dot(chains, pick.astype(jnp.bfloat16), preferred_element_type=jnp.float32)[:1]
    k_tile = steps(k, TILE, tiles)
    i_tile = steps(i, TILE, tiles)
    tile_vals = jnp.zeros((1, positions), jnp.float32)
    for a in range(tiles):
        for b in range(tiles):
            here = (k_tile == a) & (i_tile == b)
            tile_vals = jnp.where(here, tile_ref[a, b].astype(jnp.float32), tile_vals)
    return jnp.where(apart == 0.0, 1.0, tile_vals)


def cycle_of(cols):
    cycle = math.lcm(cols, LANES)
    return cycle // cols, cycle // LANES


def start_copies(sems, *pairs):
    copies = [pltpu.make_async_copy(src, dst, sems.at[at]) for at, (src, dst) in enumerate(pairs)]
    for copy in copies:
        copy.start()
    return copies


def fetch(sems, *pairs):
    for copy in start_copies(sems, *pairs):
        copy.wait()


def project_kernel(
    rows, cols, tile_hbm, chain_hbm, pair_hbm, gain_hbm, w_hbm, message_hbm, normed_hbm,
    tile_ref, chain_ref, pair_ref, gain_ref, w_ref, message_ref, normed_ref, sems, out_sems,
):
    *small, last = start_copies(
        sems,
        (w_hbm, w_ref),
        (gain_hbm, gain_ref),
        (chain_hbm, chain_ref),
        (tile_hbm, tile_ref),
        (pair_hbm, pair_ref),
    )
    hidden = (w_ref.shape[1] - w_ref.shape[0]) // 4
    peers = message_ref.shape[0]
    own = hidden // peers
    groups = cycle_of(cols)[1]
    for copy in small:
        copy.wait()
    keep = keep_of(tile_ref, chain_ref, rows, cols)
    w_t = w_ref[:, : 4 * hidden].T
    gain = column(gain_ref[...])
    last.wait()
    leaving = []
    for cycle in range(rows * cols // (groups * LANES)):
        lanes = slice(cycle * groups * LANES, (cycle + 1) * groups * LANES)
        block = pair_ref[lanes, :].astype(jnp.float32).T
        center = block - jnp.mean(block, axis=0, keepdims=True)
        spread = jnp.mean(center * center, axis=0, keepdims=True)
        normed = (center * lax.rsqrt(spread + EPS) * gain).astype(jnp.bfloat16)
        normed_ref[:, lanes] = normed
        projected = jnp.dot(w_t, normed, preferred_element_type=jnp.float32)
        sides = []
        for side in range(2):
            value = projected[2 * side * hidden : (2 * side + 1) * hidden]
            gate = projected[(2 * side + 1) * hidden : (2 * side + 2) * hidden]
            sides.append((sigmoid(gate) * value * keep[:, lanes]).reshape(peers, own, groups * LANES))
        both = jnp.concatenate(sides, axis=1).astype(jnp.bfloat16)
        for group in range(groups):
            line = (cycle * groups + group) * 2 * own
            message_ref[:, line : line + 2 * own, :] = both[:, :, group * LANES : (group + 1) * LANES]
        lines = slice(cycle * groups * 2 * own, (cycle + 1) * groups * 2 * own)
        leaving += start_copies(
            out_sems.at[cycle],
            (message_ref.at[:, lines, :], message_hbm.at[:, lines, :]),
            (normed_ref.at[:, lanes], normed_hbm.at[:, lanes]),
        )
    for copy in leaving:
        copy.wait()


def gate_kernel(normed_ref, w_hbm, gate_ref, w, sems):
    last = w_hbm.shape[1] - w_hbm.shape[0]
    fetch(sems, (w_hbm, w))
    gate_ref[...] = sigmoid(
        jnp.dot(w[:, last:].T, normed_ref[...], preferred_element_type=jnp.float32)
    )


def weights_kernel(_, gain_hbm, w_out_hbm, w_out_ref, gain_ref, w_out, gain, sems):
    fetch(sems, (w_out_hbm, w_out), (gain_hbm, gain))
    w_out_ref[...] = w_out[...].T
    gain_ref[...] = jnp.broadcast_to(column(gain[...]), gain_ref.shape)


def unpack(message_ref, spread_ref, own, cols):
    tokens, groups = cycle_of(cols)
    peers, lines, _ = message_ref.shape
    lane = lax.broadcasted_iota(jnp.int32, (2 * own, LANES), 1)
    cycles = lines // (2 * groups * own)
    for peer in range(peers):
        for cycle in range(cycles):
            base = cycle * groups
            held = [
                message_ref[peer, (base + group) * 2 * own : (base + group + 1) * 2 * own, :].astype(jnp.float32)
                for group in range(groups)
            ]
            for token in range(tokens):
                k = (peer * cycles + cycle) * tokens + token
                for chunk in range(spread_ref.shape[0]):
                    group, off = divmod(token * cols + chunk * LANES, LANES)
                    value = held[group]
                    if off and group + 1 < groups:
                        value = jnp.where(lane >= off, value, held[group + 1])
                    if off:
                        value = pltpu.roll(value, LANES - off, axis=1)
                    spread_ref[chunk, k * 2 * own : (k + 1) * 2 * own, :] = value


def pack(spread_ref, mixed_ref, first, own, cols):
    tokens, groups = cycle_of(cols)
    lane = lax.broadcasted_iota(jnp.int32, (own, LANES), 1)
    batch = 16 // math.gcd(groups * own, 16)
    for start in range(0, cols // tokens, batch):
        lines = []
        for at in range(start, start + batch):
            rolled = {}
            for group in range(groups):
                value, here = None, 0
                while here < LANES:
                    token, col = divmod(group * LANES + here, cols)
                    chunk, there = divmod(col, LANES)
                    shift = (here - there) % LANES
                    if (token, chunk, shift) not in rolled:
                        line = (at * tokens + token) * own
                        piece = spread_ref[chunk, line : line + own, :]
                        rolled[token, chunk, shift] = pltpu.roll(piece, shift, axis=1) if shift else piece
                    piece = rolled[token, chunk, shift]
                    value = piece if value is None else jnp.where(lane >= here, piece, value)
                    here += min(LANES - here, LANES - there, cols - col)
                lines.append(value)
        at = first + start * groups * own
        mixed_ref[at : at + batch * groups * own, :] = jnp.concatenate(lines, axis=0).astype(jnp.bfloat16)


def channel_of(spread_ref, line, stride):
    count = spread_ref.shape[1] // stride
    return jnp.concatenate(
        [spread_ref[chunk, pl.ds(line, count, stride=stride), :] for chunk in range(spread_ref.shape[0])],
        axis=1,
    ).astype(jnp.bfloat16)


def triangle_kernel(own, cols, shares, message_ref, mixed_hbm, done_ref, spread, left, left_t, right, mixed, out, sems):
    halves, chunks = spread.shape[:2]
    width = chunks * LANES
    deep = right.shape[1]
    depth = spread.shape[2] // (2 * own)
    done_ref[...] = jnp.zeros_like(done_ref)
    one = lax.broadcasted_iota(jnp.int32, (cols, width), 0) == lax.broadcasted_iota(jnp.int32, (cols, width), 1)
    one = one.astype(jnp.bfloat16)
    if depth < deep:
        right[:, depth:, :] = jnp.zeros((own, deep - depth, halves * width), jnp.bfloat16)
    peers = message_ref.shape[0] // halves
    for half in range(halves):
        unpack(message_ref.at[half * peers : (half + 1) * peers], spread.at[half], own, cols)
        if depth < deep:
            left[:, half * deep + depth : (half + 1) * deep, :] = jnp.zeros((own, deep - depth, width), jnp.bfloat16)
        for channel in range(own):
            left[channel, half * deep : half * deep + depth, :] = channel_of(spread.at[half], channel, 2 * own)
            right[channel, :depth, half * width : (half + 1) * width] = channel_of(
                spread.at[half], own + channel, 2 * own
            )
    for channel in range(own):
        both = lax.dot_general(
            one, left[channel], (((1,), (1,)), ((), ())), preferred_element_type=jnp.float32
        ).astype(jnp.bfloat16)
        for half in range(halves):
            left_t[channel, half * cols : (half + 1) * cols, :] = both[:, half * deep : (half + 1) * deep]
    for channel in range(own):
        total = jnp.dot(left_t[channel], right[channel], preferred_element_type=jnp.float32)
        for i_half in range(halves):
            for j_half in range(halves):
                for chunk in range(chunks):
                    start = j_half * width + chunk * LANES
                    mixed[i_half, j_half, chunk, pl.ds(channel, cols, stride=own), :] = total[
                        i_half * cols : (i_half + 1) * cols, start : start + LANES
                    ]
    each = out.shape[0] // (halves * halves)
    leaving = []
    for j_half in range(halves):
        for i_half in range(halves):
            at = j_half * halves + i_half
            pack(mixed.at[i_half, j_half], out, at * each, own, cols)
            lines = slice(at * each, (at + 1) * each)
            leaving += start_copies(sems.at[at], (out.at[lines, :], mixed_hbm.at[lines, :]))
    for copy in leaving:
        copy.wait()


def output_kernel(own, shares, halves, mixed_ref, gate_ref, gain_ref, w_t_ref, update_ref, mixed):
    lines = mixed.shape[1]
    peers = shares // PARTS
    mixed[...] = mixed_ref[...].astype(jnp.float32).reshape(mixed.shape)
    for group in range(lines // own):
        blocks = []
        for half in range(halves):
            first = half * shares
            block = mixed[first : first + peers, group * own : (group + 1) * own, :]
            for part in range(1, PARTS):
                start = first + part * peers
                block += mixed[start : start + peers, group * own : (group + 1) * own, :]
            blocks.append(block.reshape(peers * own, LANES))
        block = jnp.concatenate(blocks, axis=0)
        center = block - jnp.mean(block, axis=0, keepdims=True)
        spread = jnp.mean(center * center, axis=0, keepdims=True)
        normed = (center * lax.rsqrt(spread + EPS) * gain_ref[...]).astype(jnp.bfloat16)
        projected = jnp.dot(w_t_ref[...], normed, preferred_element_type=jnp.float32)
        lanes = slice(group * LANES, (group + 1) * LANES)
        update_ref[lanes, :] = (gate_ref[:, lanes] * projected).T.astype(jnp.bfloat16)


def on_device(shares, halves, pair, tile_mask, chain_ids, gain_in, w_proj, gain_mid, w_out):
    rows, cols, width = pair.shape
    hidden = w_out.shape[0]
    peers = shares // PARTS
    own = hidden // (peers * halves)
    positions = rows * cols
    groups = positions // LANES
    lines = groups * own
    cycles = groups // cycle_of(cols)[1]
    params = pltpu.CompilerParams(vmem_limit_bytes=VMEM_BYTES)
    whole_params = pltpu.CompilerParams(vmem_limit_bytes=WHOLE_VMEM_BYTES)
    tokens = chain_ids.shape[0]
    message = jax.ShapeDtypeStruct((peers * halves, 2 * lines, LANES), jnp.bfloat16)
    message, normed = pl.pallas_call(
        functools.partial(project_kernel, rows, cols),
        out_shape=(message, jax.ShapeDtypeStruct((width, positions), jnp.bfloat16)),
        in_specs=[HBM] * 5,
        out_specs=(HBM, HBM),
        scratch_shapes=[
            pltpu.SMEM(tile_mask.shape, jnp.int32),
            pltpu.VMEM((1, tokens), jnp.int32),
            pltpu.VMEM((positions, width), jnp.bfloat16),
            pltpu.VMEM((1, width), jnp.float32),
            pltpu.VMEM(w_proj.shape, jnp.bfloat16),
            pltpu.VMEM(message.shape, jnp.bfloat16),
            pltpu.VMEM((width, positions), jnp.bfloat16),
            pltpu.SemaphoreType.DMA((5,)),
            pltpu.SemaphoreType.DMA((cycles, 2)),
        ],
        compiler_params=whole_params,
        name="project",
    )(tile_mask, chain_ids[None, :], pair.reshape(positions, width), gain_in[None, :], w_proj)
    message = lax.all_to_all(
        message,
        ("col", "row"),
        split_axis=0,
        concat_axis=0,
        axis_index_groups=[
            [half * shares + part * peers + at for half in range(halves) for at in range(peers)]
            for part in range(PARTS)
        ],
        tiled=True,
    )
    gate = pl.pallas_call(
        gate_kernel,
        out_shape=jax.ShapeDtypeStruct((width, positions), jnp.float32),
        in_specs=[VMEM, HBM],
        out_specs=VMEM,
        scratch_shapes=[pltpu.VMEM(w_proj.shape, jnp.bfloat16), pltpu.SemaphoreType.DMA((1,))],
        compiler_params=params,
        cost_estimate=pl.CostEstimate(
            flops=2 * width * width * positions, bytes_accessed=4 * width * positions, transcendentals=0
        ),
        name="gate",
    )(normed, w_proj)
    chunks = pl.cdiv(cols, LANES)
    depth = peers * rows
    deep = pl.cdiv(depth, LANES) * LANES
    mixed, done = pl.pallas_call(
        functools.partial(triangle_kernel, own, cols, shares),
        out_shape=(
            jax.ShapeDtypeStruct((halves * shares * lines, LANES), jnp.bfloat16),
            jax.ShapeDtypeStruct((8, LANES), jnp.float32),
        ),
        in_specs=[VMEM],
        out_specs=(HBM, VMEM),
        scratch_shapes=[
            pltpu.VMEM((halves, chunks, depth * 2 * own, LANES), jnp.float32),
            pltpu.VMEM((own, halves * deep, chunks * LANES), jnp.bfloat16),
            pltpu.VMEM((own, halves * cols, deep), jnp.bfloat16),
            pltpu.VMEM((own, deep, halves * chunks * LANES), jnp.bfloat16),
            pltpu.VMEM((halves, halves, chunks, cols * own, LANES), jnp.float32),
            pltpu.VMEM((halves * shares * lines, LANES), jnp.bfloat16),
            pltpu.SemaphoreType.DMA((halves * halves, 1)),
        ],
        compiler_params=params,
        name="triangle",
    )(message)
    mixed = lax.all_to_all(
        mixed.reshape(halves * shares, lines, LANES),
        ("col", "row"),
        split_axis=0,
        concat_axis=0,
        tiled=True,
    ).reshape(halves * shares * lines, LANES)
    w_out_t, gain = pl.pallas_call(
        weights_kernel,
        out_shape=(
            jax.ShapeDtypeStruct(w_out.shape[::-1], jnp.bfloat16),
            jax.ShapeDtypeStruct((hidden, LANES), jnp.float32),
        ),
        in_specs=[ANY, HBM, HBM],
        out_specs=(VMEM, VMEM),
        scratch_shapes=[
            pltpu.VMEM(w_out.shape, jnp.bfloat16),
            pltpu.VMEM((1, hidden), jnp.float32),
            pltpu.SemaphoreType.DMA((2,)),
        ],
        compiler_params=params,
        cost_estimate=pl.CostEstimate(flops=hidden * width, bytes_accessed=8 * hidden * width, transcendentals=0),
        name="weights",
    )(done, gain_mid[None, :], w_out)
    update = pl.pallas_call(
        functools.partial(output_kernel, own, shares, halves),
        out_shape=jax.ShapeDtypeStruct((positions, width), jnp.bfloat16),
        in_specs=[VMEM] * 4,
        out_specs=VMEM,
        scratch_shapes=[pltpu.VMEM((halves * shares, lines, LANES), jnp.float32)],
        compiler_params=params,
        name="output",
    )(mixed, gate, gain, w_out_t)
    return update.reshape(rows, cols, width)


def solution(mesh):
    in_specs = (P(("grp", "row"), "col", None), P("grp", None), P("grp"), P(), P(), P(), P())
    out_specs = P(("grp", "row"), "col", None)
    return jax.shard_map(
        functools.partial(on_device, mesh.shape["row"], mesh.shape["col"]),
        mesh=mesh,
        in_specs=in_specs,
        out_specs=out_specs,
        check_vma=False,
    )
```

time: 45.8 us -> 45.3 us (0.989)
  blocking collectives: 0 us -> 17.5 us
  waiting for transfers between devices: 25.7 us -> 16.8 us
  starting transfers between devices: 11.2 us -> 3.23 us
  Pallas kernels: 7.75 us -> 6.66 us
    all_to_all x0 -> x1, blocking collectives: none -> 17.5 us  [on_device(): lax.all_to_all(message, ('col', 'row'), split_axis=0, concat_axis=0, axis...]
    all_to_all x2 -> x1, waiting for transfers between devices: 24.9 us -> 16.8 us  [on_device(): lax.all_to_all(mixed.reshape(halves * shares, lines, LANES), ('col', 'row...]
    all_to_all x2 -> x1, starting transfers between devices: 11.2 us -> 3.23 us  [on_device(): lax.all_to_all(mixed.reshape(halves * shares, lines, LANES), ('col', 'row...]
    pallas_call x5 -> x4, Pallas kernels: 7.55 us -> 6.46 us  [the longest x1 2.7 us: on_device(): pl.pallas_call(functools.partial(project_kernel, rows, cols), out_shape=(...]
    ppermute x1 -> x0, waiting for transfers between devices: 0.77 us -> none  [on_device(): other = lax.ppermute(message, 'col', [(0, 1), (1, 0)])]
  transfers between devices with their start and end apart: 3 -> 1, of which waited for: 3 -> 1; matrix products, arithmetic and copies ran while one was open for 0% -> 0% of each run, Pallas kernels for 4% -> 2%
where the time goes in v7:
time: 45.3 us; the launch traced here: 45 us
  blocking collectives  17.5 us (39%)
  waiting for transfers between devices  16.8 us (37%)
  Pallas kernels  6.66 us (15%)
  starting transfers between devices  3.23 us (7%)
  local copies, waits for them, and re-layouts  0.67 us (1%)
    all_to_all x1, blocking collectives, on_device(): lax.all_to_all(message, ('col', 'row'), split_axis=0, concat_axis=0, axis...  17.5 us
    all_to_all x1, waiting for transfers between devices, on_device(): lax.all_to_all(mixed.reshape(halves * shares, lines, LANES), ('col', 'row...  16.8 us
    all_to_all x1, starting transfers between devices, on_device(): lax.all_to_all(mixed.reshape(halves * shares, lines, LANES), ('col', 'row...  3.23 us
    pallas_call x1, Pallas kernels, on_device(): pl.pallas_call(functools.partial(project_kernel, rows, cols), out_shape=(...  2.7 us
    pallas_call x1, Pallas kernels, on_device(): pl.pallas_call(functools.partial(triangle_kernel, own, cols, shares), out...  2.08 us
    pallas_call x1, Pallas kernels, on_device(): pl.pallas_call(functools.partial(output_kernel, own, shares, halves), out...  1.19 us
  transfers between devices with their start and end apart: 1, of which 1 were waited for; matrix products, arithmetic and copies ran while one was open for 0% of the time, Pallas kernels for 2%

profile of v7, /device:TPU:0, one launch (start us, length us, event | category | flops | bytes accessed | tf_op | source)
XLA Modules:
  0.0 45.0 jit_solution(1131289314225258733)
XLA Ops:
  0.0 2.7 %project.1 = (bf16[16,144,128]{2,1,0:T(8,128)(2,1)}, bf16[128,1152]{1,0:T(8,128)(2,1)}) custom-call(s32[2,2]{1,0:T(2,128)} %tile_hbm.1, s32[1,192]{1,0:T(1,128)} %bitcast.10, bf16[1152,128]{1,0:T(8,128)(2,1)} %bitcast.9, f32[1,128]{1,0:T(1,128)} %bitcast.11, bf16[128,640]{1,0:T(8,128)(2,1)} %w_hbm.3), custom_call_target="tpu_custom_call" | custom-call | tf_op jit(solution)/shard_map/project/pallas_call | solution.py:281
  2.7 17.5 %all_to_all.10.message_ref = bf16[16,144,128]{2,1,0:T(8,128)(2,1)S(1)} all-to-all(bf16[16,144,128]{2,1,0:T(8,128)(2,1)} %get-tuple-element.11), channel_id=1, replica_groups={{0,2,4,6,8,10,12,14,1,3,5,7,9,11,13,15},{16,18,20,22,24,26,28,30,17,19,..., dimensions={0} | all-to-all | bytes 1179648 | tf_op jit(solution)/shard_map/all_to_all | solution.py:300
  20.2 2.1 %triangle.1 = (bf16[2304,128]{1,0:T(8,128)(2,1)}, f32[8,128]{1,0:T(8,128)S(1)}) custom-call(bf16[16,144,128]{2,1,0:T(8,128)(2,1)S(1)} %all_to_all.10.message_ref), custom_call_target="tpu_custom_call" | custom-call | tf_op jit(solution)/shard_map/triangle/pallas_call | solution.py:326
  22.3 0.0 copy-start
  22.3 0.0 copy-start.1
  22.3 3.2 %all-to-all-start.1 = ((bf16[32,72,128]{2,1,0:T(8,128)(2,1)}), bf16[32,72,128]{2,1,0:T(8,128)(2,1)S(1)}, u32[]{:S(2)}, u32[]{:S(2)}) async-start(bf16[32,72,128]{2,1,0:T(8,128)(2,1)} %bitcast.3), calls=%async_computation.1 | async-start | bytes 1179648 | tf_op jit(solution)/shard_map/all_to_all | solution.py:346
  25.6 0.0 copy-done
  25.6 0.0 copy-done.1
  25.6 0.0 copy-start.2
  25.6 0.5 %gate.1.gate_ref = f32[128,1152]{1,0:T(8,128)S(1)} custom-call(bf16[128,1152]{1,0:T(8,128)(2,1)S(1)} %copy-done.1, bf16[128,640]{1,0:T(8,128)(2,1)S(1)} %copy-done), custom_call_target="tpu_custom_call" | custom-call | flops 37748736 | bytes 589824 | tf_op jit(solution)/shard_map/gate/pallas_call | solution.py:311
  26.1 0.0 copy-start.3
  26.1 0.2 copy-done.2
  26.3 0.4 copy-done.3
  26.8 0.2 weights.1
  27.0 16.8 %all-to-all-done.1 = bf16[32,72,128]{2,1,0:T(8,128)(2,1)S(1)} async-done(((bf16[32,72,128]{2,1,0:T(8,128)(2,1)}), bf16[32,72,128]{2,1,0:T(8,128)(2,1)S(1)}, u32[]{:S(2)}, u32[]{:S(2)}) %all-to-all-start.1) | async-done | bytes 589856 | tf_op jit(solution)/shard_map/all_to_all | solution.py:346
  43.8 1.2 %output.1 = bf16[1152,128]{1,0:T(8,128)(2,1)} custom-call(bf16[2304,128]{1,0:T(8,128)(2,1)S(1)} %bitcast.7, f32[128,1152]{1,0:T(8,128)S(1)} %gate.1.gate_ref, f32[128,128]{1,0:T(8,128)S(1)} %get-tuple-element.15.gain_ref, bf16[128,128]{1,0:T(8,128)(2,1)S(1)} %get-tuple-element.16.w_t_ref), custom_call_target="tpu_custom_call" | custom-call | tf_op jit(solution)/shard_map/output/pallas_call | solution.py:370
Async XLA Ops:
  22.3 3.3 %copy-start = (bf16[128,640]{1,0:T(8,128)(2,1)S(1)}, bf16[128,640]{1,0:T(8,128)(2,1)}, u32[]{:S(2)}) copy-start(bf16[128,640]{1,0:T(8,128)(2,1)} %w_hbm.3) | copy-start | bytes 491524
  22.3 3.3 %copy-start.1 = (bf16[128,1152]{1,0:T(8,128)(2,1)S(1)}, bf16[128,1152]{1,0:T(8,128)(2,1)}, u32[]{:S(2)}) copy-start(bf16[128,1152]{1,0:T(8,128)(2,1)} %get-tuple-element.13.normed_ref) | copy-start | bytes 884740
  22.3 21.5 %all-to-all-start.1 = ((bf16[32,72,128]{2,1,0:T(8,128)(2,1)}), bf16[32,72,128]{2,1,0:T(8,128)(2,1)S(1)}, u32[]{:S(2)}, u32[]{:S(2)}) async-start(bf16[32,72,128]{2,1,0:T(8,128)(2,1)} %bitcast.3), calls=%async_computation.1 | async-start | bytes 1179648 | tf_op jit(solution)/shard_map/all_to_all | solution.py:346
  25.6 0.8 %copy-start.2 = (bf16[128,128]{1,0:T(8,128)(2,1)S(1)}, bf16[128,128]{1,0:T(8,128)(2,1)}, u32[]{:S(2)}) copy-start(bf16[128,128]{1,0:T(8,128)(2,1)} %w_out_hbm.1) | copy-start | bytes 98308
  26.1 0.7 %copy-start.3 = (f32[128]{0:T(128)S(1)}, f32[128]{0:T(128)}, u32[]{:S(2)}) copy-start(f32[128]{0:T(128)} %param.12) | copy-start | bytes 1540

commit v8 on v7

--- a/solution.py
+++ b/solution.py
@@ -78,28 +78,32 @@
     rows, cols, tile_hbm, chain_hbm, pair_hbm, gain_hbm, w_hbm, message_hbm, normed_hbm,
     tile_ref, chain_ref, pair_ref, gain_ref, w_ref, message_ref, normed_ref, sems, out_sems,
 ):
-    *small, last = start_copies(
+    hidden = (w_ref.shape[1] - w_ref.shape[0]) // 4
+    peers = message_ref.shape[0]
+    own = hidden // peers
+    groups = cycle_of(cols)[1]
+    size = groups * LANES
+    copies = start_copies(
         sems,
         (w_hbm, w_ref),
         (gain_hbm, gain_ref),
         (chain_hbm, chain_ref),
         (tile_hbm, tile_ref),
-        (pair_hbm, pair_ref),
+        *[
+            (pair_hbm.at[start : start + size, :], pair_ref.at[start : start + size, :])
+            for start in range(0, rows * cols, size)
+        ],
     )
-    hidden = (w_ref.shape[1] - w_ref.shape[0]) // 4
-    peers = message_ref.shape[0]
-    own = hidden // peers
-    groups = cycle_of(cols)[1]
-    for copy in small:
+    for copy in copies[:4]:
         copy.wait()
     keep = keep_of(tile_ref, chain_ref, rows, cols)
     w_t = w_ref[:, : 4 * hidden].T
     gain = column(gain_ref[...])
-    last.wait()
     leaving = []
-    for cycle in range(rows * cols // (groups * LANES)):
-        lanes = slice(cycle * groups * LANES, (cycle + 1) * groups * LANES)
-        block = pair_ref[lanes, :].astype(jnp.float32).T
+    for cycle in range(rows * cols // size):
+        lanes = slice(cycle * size, (cycle + 1) * size)
+        copies[4 + cycle].wait()
+        block = pair_ref[lanes, :].T.astype(jnp.float32)
         center = block - jnp.mean(block, axis=0, keepdims=True)
         spread = jnp.mean(center * center, axis=0, keepdims=True)
         normed = (center * lax.rsqrt(spread + EPS) * gain).astype(jnp.bfloat16)
@@ -109,7 +113,7 @@
         for side in range(2):
             value = projected[2 * side * hidden : (2 * side + 1) * hidden]
             gate = projected[(2 * side + 1) * hidden : (2 * side + 2) * hidden]
-            sides.append((sigmoid(gate) * value * keep[:, lanes]).reshape(peers, own, groups * LANES))
+            sides.append((sigmoid(gate) * value * keep[:, lanes]).reshape(peers, own, size))
         both = jnp.concatenate(sides, axis=1).astype(jnp.bfloat16)
         for group in range(groups):
             line = (cycle * groups + group) * 2 * own
@@ -124,18 +128,15 @@
         copy.wait()
 
 
-def gate_kernel(normed_ref, w_hbm, gate_ref, w, sems):
+def gate_kernel(normed_ref, w_hbm, gain_hbm, w_out_hbm, gate_ref, w_out_ref, gain_ref, done_ref, w, w_out, gain, sems):
+    fetch(sems, (w_hbm, w), (w_out_hbm, w_out), (gain_hbm, gain))
     last = w_hbm.shape[1] - w_hbm.shape[0]
-    fetch(sems, (w_hbm, w))
     gate_ref[...] = sigmoid(
         jnp.dot(w[:, last:].T, normed_ref[...], preferred_element_type=jnp.float32)
     )
-
-
-def weights_kernel(_, gain_hbm, w_out_hbm, w_out_ref, gain_ref, w_out, gain, sems):
-    fetch(sems, (w_out_hbm, w_out), (gain_hbm, gain))
     w_out_ref[...] = w_out[...].T
     gain_ref[...] = jnp.broadcast_to(column(gain[...]), gain_ref.shape)
+    done_ref[...] = jnp.zeros_like(done_ref)
 
 
 def unpack(message_ref, spread_ref, own, cols):
@@ -196,12 +197,11 @@
     ).astype(jnp.bfloat16)
 
 
-def triangle_kernel(own, cols, shares, message_ref, mixed_hbm, done_ref, spread, left, left_t, right, mixed, out, sems):
+def triangle_kernel(own, cols, message_ref, _, mixed_ref, spread, left, left_t, right, mixed):
     halves, chunks = spread.shape[:2]
     width = chunks * LANES
     deep = right.shape[1]
     depth = spread.shape[2] // (2 * own)
-    done_ref[...] = jnp.zeros_like(done_ref)
     one = lax.broadcasted_iota(jnp.int32, (cols, width), 0) == lax.broadcasted_iota(jnp.int32, (cols, width), 1)
     one = one.astype(jnp.bfloat16)
     if depth < deep:
@@ -231,16 +231,11 @@
                     mixed[i_half, j_half, chunk, pl.ds(channel, cols, stride=own), :] = total[
                         i_half * cols : (i_half + 1) * cols, start : start + LANES
                     ]
-    each = out.shape[0] // (halves * halves)
-    leaving = []
+    each = mixed_ref.shape[0] // (halves * halves)
     for j_half in range(halves):
         for i_half in range(halves):
             at = j_half * halves + i_half
-            pack(mixed.at[i_half, j_half], out, at * each, own, cols)
-            lines = slice(at * each, (at + 1) * each)
-            leaving += start_copies(sems.at[at], (out.at[lines, :], mixed_hbm.at[lines, :]))
-    for copy in leaving:
-        copy.wait()
+            pack(mixed.at[i_half, j_half], mixed_ref, at * each, own, cols)
 
 
 def output_kernel(own, shares, halves, mixed_ref, gate_ref, gain_ref, w_t_ref, update_ref, mixed):
@@ -262,7 +257,7 @@
         normed = (center * lax.rsqrt(spread + EPS) * gain_ref[...]).astype(jnp.bfloat16)
         projected = jnp.dot(w_t_ref[...], normed, preferred_element_type=jnp.float32)
         lanes = slice(group * LANES, (group + 1) * LANES)
-        update_ref[lanes, :] = (gate_ref[:, lanes] * projected).T.astype(jnp.bfloat16)
+        update_ref[lanes, :] = (gate_ref[:, lanes] * projected).astype(jnp.bfloat16).T
 
 
 def on_device(shares, halves, pair, tile_mask, chain_ids, gain_in, w_proj, gain_mid, w_out):
@@ -291,7 +286,7 @@
             pltpu.VMEM(w_proj.shape, jnp.bfloat16),
             pltpu.VMEM(message.shape, jnp.bfloat16),
             pltpu.VMEM((width, positions), jnp.bfloat16),
-            pltpu.SemaphoreType.DMA((5,)),
+            pltpu.SemaphoreType.DMA((4 + cycles,)),
             pltpu.SemaphoreType.DMA((cycles, 2)),
         ],
         compiler_params=whole_params,
@@ -308,41 +303,47 @@
         ],
         tiled=True,
     )
-    gate = pl.pallas_call(
+    gate, w_out_t, gain, done = pl.pallas_call(
         gate_kernel,
-        out_shape=jax.ShapeDtypeStruct((width, positions), jnp.float32),
-        in_specs=[VMEM, HBM],
-        out_specs=VMEM,
-        scratch_shapes=[pltpu.VMEM(w_proj.shape, jnp.bfloat16), pltpu.SemaphoreType.DMA((1,))],
+        out_shape=(
+            jax.ShapeDtypeStruct((width, positions), jnp.float32),
+            jax.ShapeDtypeStruct(w_out.shape[::-1], jnp.bfloat16),
+            jax.ShapeDtypeStruct((hidden, LANES), jnp.float32),
+            jax.ShapeDtypeStruct((8, LANES), jnp.float32),
+        ),
+        in_specs=[VMEM, HBM, HBM, HBM],
+        out_specs=(VMEM, VMEM, VMEM, VMEM),
+        scratch_shapes=[
+            pltpu.VMEM(w_proj.shape, jnp.bfloat16),
+            pltpu.VMEM(w_out.shape, jnp.bfloat16),
+            pltpu.VMEM((1, hidden), jnp.float32),
+            pltpu.SemaphoreType.DMA((3,)),
+        ],
         compiler_params=params,
         cost_estimate=pl.CostEstimate(
             flops=2 * width * width * positions, bytes_accessed=4 * width * positions, transcendentals=0
         ),
         name="gate",
-    )(normed, w_proj)
+    )(normed, w_proj, gain_mid[None, :], w_out)
+    message, done = lax.optimization_barrier((message, done))
     chunks = pl.cdiv(cols, LANES)
     depth = peers * rows
     deep = pl.cdiv(depth, LANES) * LANES
-    mixed, done = pl.pallas_call(
-        functools.partial(triangle_kernel, own, cols, shares),
-        out_shape=(
-            jax.ShapeDtypeStruct((halves * shares * lines, LANES), jnp.bfloat16),
-            jax.ShapeDtypeStruct((8, LANES), jnp.float32),
-        ),
-        in_specs=[VMEM],
-        out_specs=(HBM, VMEM),
+    mixed = pl.pallas_call(
+        functools.partial(triangle_kernel, own, cols),
+        out_shape=jax.ShapeDtypeStruct((halves * shares * lines, LANES), jnp.bfloat16),
+        in_specs=[VMEM, ANY],
+        out_specs=VMEM,
         scratch_shapes=[
             pltpu.VMEM((halves, chunks, depth * 2 * own, LANES), jnp.float32),
             pltpu.VMEM((own, halves * deep, chunks * LANES), jnp.bfloat16),
             pltpu.VMEM((own, halves * cols, deep), jnp.bfloat16),
             pltpu.VMEM((own, deep, halves * chunks * LANES), jnp.bfloat16),
             pltpu.VMEM((halves, halves, chunks, cols * own, LANES), jnp.float32),
-            pltpu.VMEM((halves * shares * lines, LANES), jnp.bfloat16),
-            pltpu.SemaphoreType.DMA((halves * halves, 1)),
         ],
         compiler_params=params,
         name="triangle",
-    )(message)
+    )(message, done)
     mixed = lax.all_to_all(
         mixed.reshape(halves * shares, lines, LANES),
         ("col", "row"),
@@ -350,23 +351,6 @@
         concat_axis=0,
         tiled=True,
     ).reshape(halves * shares * lines, LANES)
-    w_out_t, gain = pl.pallas_call(
-        weights_kernel,
-        out_shape=(
-            jax.ShapeDtypeStruct(w_out.shape[::-1], jnp.bfloat16),
-            jax.ShapeDtypeStruct((hidden, LANES), jnp.float32),
-        ),
-        in_specs=[ANY, HBM, HBM],
-        out_specs=(VMEM, VMEM),
-        scratch_shapes=[
-            pltpu.VMEM(w_out.shape, jnp.bfloat16),
-            pltpu.VMEM((1, hidden), jnp.float32),
-            pltpu.SemaphoreType.DMA((2,)),
-        ],
-        compiler_params=params,
-        cost_estimate=pl.CostEstimate(flops=hidden * width, bytes_accessed=8 * hidden * width, transcendentals=0),
-        name="weights",
-    )(done, gain_mid[None, :], w_out)
     update = pl.pallas_call(
         functools.partial(output_kernel, own, shares, halves),
         out_shape=jax.ShapeDtypeStruct((positions, width), jnp.bfloat16),

time: 45.3 us -> 45.1 us (level)
  waiting for transfers between devices: 16.8 us -> 9.03 us
  blocking collectives: 17.5 us -> 22.4 us
  starting transfers between devices: 3.23 us -> 6.43 us
    all_to_all x1, waiting for transfers between devices: 16.8 us -> 9.03 us  [on_device(): lax.all_to_all(message, ('col', 'row'), split_axis=0, concat_axis=0, axis...]
    all_to_all x1, blocking collectives: 17.5 us -> 22.4 us  [on_device(): lax.all_to_all(mixed.reshape(halves * shares, lines, LANES), ('col', 'row...]
    all_to_all x1, starting transfers between devices: 3.23 us -> 6.43 us  [on_device(): lax.all_to_all(message, ('col', 'row'), split_axis=0, concat_axis=0, axis...]
    pallas_call x3 -> x2, Pallas kernels: 2.77 us -> 1.8 us  [the longest x1 1.27 us: on_device(): pl.pallas_call(functools.partial(triangle_kernel, own, cols), out_shape=j...]
    pallas_call x1, Pallas kernels: 2.7 us -> 3.29 us  [on_device(): pl.pallas_call(functools.partial(project_kernel, rows, cols), out_shape=(...]
  transfers between devices with their start and end apart: 1 -> 1, of which waited for: 1 -> 1; matrix products, arithmetic and copies ran while one was open for 0% -> 0% of each run, Pallas kernels for 2% -> 1%
where the time goes in v8:
time: 45.1 us; the launch traced here: 44.8 us
  blocking collectives  22.4 us (50%)
  waiting for transfers between devices  9.03 us (20%)
  starting transfers between devices  6.43 us (14%)
  Pallas kernels  6.25 us (14%)
  local copies, waits for them, and re-layouts  0.64 us (1%)
    all_to_all x1, blocking collectives, on_device(): lax.all_to_all(mixed.reshape(halves * shares, lines, LANES), ('col', 'row...  22.4 us
    all_to_all x1, waiting for transfers between devices, on_device(): lax.all_to_all(message, ('col', 'row'), split_axis=0, concat_axis=0, axis...  9.03 us
    all_to_all x1, starting transfers between devices, on_device(): lax.all_to_all(message, ('col', 'row'), split_axis=0, concat_axis=0, axis...  6.43 us
    pallas_call x1, Pallas kernels, on_device(): pl.pallas_call(functools.partial(project_kernel, rows, cols), out_shape=(...  3.29 us
    pallas_call x1, Pallas kernels, on_device(): pl.pallas_call(functools.partial(triangle_kernel, own, cols), out_shape=j...  1.27 us
    pallas_call x1, Pallas kernels, on_device(): pl.pallas_call(functools.partial(output_kernel, own, shares, halves), out...  1.16 us
  transfers between devices with their start and end apart: 1, of which 1 were waited for; matrix products, arithmetic and copies ran while one was open for 0% of the time, Pallas kernels for 1%

profile of v8, /device:TPU:0, one launch (start us, length us, event | category | flops | bytes accessed | tf_op | source)
XLA Modules:
  0.0 44.8 jit_solution(14793263947974201081)
XLA Ops:
  0.0 3.3 %project.1 = (bf16[16,144,128]{2,1,0:T(8,128)(2,1)}, bf16[128,1152]{1,0:T(8,128)(2,1)}) custom-call(s32[2,2]{1,0:T(2,128)} %tile_hbm.1, s32[1,192]{1,0:T(1,128)} %bitcast.11, bf16[1152,128]{1,0:T(8,128)(2,1)} %bitcast.10, f32[1,128]{1,0:T(1,128)} %bitcast.12, bf16[128,640]{1,0:T(8,128)(2,1)} %w_hbm.3), custom_call_target="tpu_custom_call" | custom-call | tf_op jit(solution)/shard_map/project/pallas_call | solution.py:276
  3.3 0.0 copy-start
  3.3 0.0 copy-start.1
  3.3 0.0 copy-start.2
  3.3 6.4 %all-to-all-start = ((bf16[16,144,128]{2,1,0:T(8,128)(2,1)}), bf16[16,144,128]{2,1,0:T(8,128)(2,1)S(1)}, u32[]{:S(2)}, u32[]{:S(2)}) async-start(bf16[16,144,128]{2,1,0:T(8,128)(2,1)} %get-tuple-element.13), calls=%async_computation | async-start | bytes 1179648 | tf_op jit(solution)/shard_map/all_to_all | solution.py:295
  9.8 0.0 copy-start.3
  9.8 0.0 copy-done
  9.8 0.0 copy-done.1
  9.8 0.0 copy-done.2
  9.8 0.6 %copy-done.3 = f32[128]{0:T(128)S(1)} copy-done((f32[128]{0:T(128)S(1)}, f32[128]{0:T(128)}, u32[]{:S(2)}) %copy-start.3) | copy-done | bytes 536
  10.4 0.5 %gate.1 = (f32[128,1152]{1,0:T(8,128)S(1)}, bf16[128,128]{1,0:T(8,128)(2,1)S(1)}, f32[128,128]{1,0:T(8,128)S(1)}, f32[8,128]{1,0:T(8,128)S(1)}) custom-call(bf16[128,1152]{1,0:T(8,128)(2,1)S(1)} %copy-done.1, bf16[128,640]{1,0:T(8,128)(2,1)S(1)} %copy-done, f32[1,128]{1,0:T(1,128)S(1)} %bitcast.9, bf16[128,128]{1,0:T(8,128)(2,1)S(1)} %copy-done.2), custom_call_target="tpu_custom_call" | custom-call | flops 37748736 | bytes 589824 | tf_op jit(solution)/shard_map/gate/pallas_call | solution.py:306
  11.0 9.0 %all-to-all-done.message_ref = bf16[16,144,128]{2,1,0:T(8,128)(2,1)S(1)} async-done(((bf16[16,144,128]{2,1,0:T(8,128)(2,1)}), bf16[16,144,128]{2,1,0:T(8,128)(2,1)S(1)}, u32[]{:S(2)}, u32[]{:S(2)}) %all-to-all-start) | async-done | bytes 589856 | tf_op jit(solution)/shard_map/all_to_all | solution.py:295
  20.0 1.3 %triangle.1 = bf16[2304,128]{1,0:T(8,128)(2,1)S(1)} custom-call(bf16[16,144,128]{2,1,0:T(8,128)(2,1)S(1)} %all-to-all-done.message_ref, f32[8,128]{1,0:T(8,128)S(1)} %get-tuple-element.17._), custom_call_target="tpu_custom_call" | custom-call | tf_op jit(solution)/shard_map/triangle/pallas_call | solution.py:332
  21.3 22.4 %all_to_all.10 = bf16[32,72,128]{2,1,0:T(8,128)(2,1)S(1)} all-to-all(bf16[32,72,128]{2,1,0:T(8,128)(2,1)S(1)} %bitcast.8), channel_id=1, replica_groups=mesh['grp'=1,'row'=16,'col'=2] {'col','row'}, dimensions={0} | all-to-all | bytes 1179648 | tf_op jit(solution)/shard_map/all_to_all | solution.py:347
  43.7 1.2 %output.1 = bf16[1152,128]{1,0:T(8,128)(2,1)} custom-call(bf16[2304,128]{1,0:T(8,128)(2,1)S(1)} %bitcast.7, f32[128,1152]{1,0:T(8,128)S(1)} %get-tuple-element.18.gate_ref, f32[128,128]{1,0:T(8,128)S(1)} %get-tuple-element.19.gain_ref, bf16[128,128]{1,0:T(8,128)(2,1)S(1)} %get-tuple-element.20.w_t_ref), custom_call_target="tpu_custom_call" | custom-call | tf_op jit(solution)/shard_map/output/pallas_call | solution.py:354
Async XLA Ops:
  3.3 6.5 %copy-start = (bf16[128,640]{1,0:T(8,128)(2,1)S(1)}, bf16[128,640]{1,0:T(8,128)(2,1)}, u32[]{:S(2)}) copy-start(bf16[128,640]{1,0:T(8,128)(2,1)} %w_hbm.3) | copy-start | bytes 491524
  3.3 6.5 %copy-start.1 = (bf16[128,1152]{1,0:T(8,128)(2,1)S(1)}, bf16[128,1152]{1,0:T(8,128)(2,1)}, u32[]{:S(2)}) copy-start(bf16[128,1152]{1,0:T(8,128)(2,1)} %get-tuple-element.14.normed_ref) | copy-start | bytes 884740
  3.3 6.5 %copy-start.2 = (bf16[128,128]{1,0:T(8,128)(2,1)S(1)}, bf16[128,128]{1,0:T(8,128)(2,1)}, u32[]{:S(2)}) copy-start(bf16[128,128]{1,0:T(8,128)(2,1)} %w_out_hbm.1) | copy-start | bytes 98308
  3.3 16.7 %all-to-all-start = ((bf16[16,144,128]{2,1,0:T(8,128)(2,1)}), bf16[16,144,128]{2,1,0:T(8,128)(2,1)S(1)}, u32[]{:S(2)}, u32[]{:S(2)}) async-start(bf16[16,144,128]{2,1,0:T(8,128)(2,1)} %get-tuple-element.13), calls=%async_computation | async-start | bytes 1179648 | tf_op jit(solution)/shard_map/all_to_all | solution.py:295
  9.8 0.7 %copy-start.3 = (f32[128]{0:T(128)S(1)}, f32[128]{0:T(128)}, u32[]{:S(2)}) copy-start(f32[128]{0:T(128)} %param.12) | copy-start | bytes 1540

commit v9 on v8

--- a/solution.py
+++ b/solution.py
@@ -29,6 +29,20 @@
     for edge in range(1, count):
         total += (at >= edge * width).astype(jnp.int32)
     return total
+
+
+def identity(rows, cols):
+    same = lax.broadcasted_iota(jnp.int32, (rows, cols), 0) == lax.broadcasted_iota(jnp.int32, (rows, cols), 1)
+    return same.astype(jnp.bfloat16)
+
+
+def transpose(block):
+    return lax.dot_general(
+        identity(block.shape[1], block.shape[1]),
+        block,
+        (((1,), (1,)), ((), ())),
+        preferred_element_type=jnp.float32,
+    )
 
 
 def sigmoid(values):
@@ -89,26 +103,23 @@
         (gain_hbm, gain_ref),
         (chain_hbm, chain_ref),
         (tile_hbm, tile_ref),
-        *[
-            (pair_hbm.at[start : start + size, :], pair_ref.at[start : start + size, :])
-            for start in range(0, rows * cols, size)
-        ],
+        (pair_hbm, pair_ref),
     )
     for copy in copies[:4]:
         copy.wait()
     keep = keep_of(tile_ref, chain_ref, rows, cols)
     w_t = w_ref[:, : 4 * hidden].T
     gain = column(gain_ref[...])
-    leaving = []
-    for cycle in range(rows * cols // size):
-        lanes = slice(cycle * size, (cycle + 1) * size)
-        copies[4 + cycle].wait()
-        block = pair_ref[lanes, :].T.astype(jnp.float32)
+    copies[4].wait()
+    cycles = [slice(start, start + size) for start in range(0, rows * cols, size)]
+    for lanes in cycles:
+        block = transpose(pair_ref[lanes, :])
         center = block - jnp.mean(block, axis=0, keepdims=True)
         spread = jnp.mean(center * center, axis=0, keepdims=True)
-        normed = (center * lax.rsqrt(spread + EPS) * gain).astype(jnp.bfloat16)
-        normed_ref[:, lanes] = normed
-        projected = jnp.dot(w_t, normed, preferred_element_type=jnp.float32)
+        normed_ref[:, lanes] = (center * lax.rsqrt(spread + EPS) * gain).astype(jnp.bfloat16)
+    leaving = []
+    for cycle, lanes in enumerate(cycles):
+        projected = jnp.dot(w_t, normed_ref[:, lanes], preferred_element_type=jnp.float32)
         sides = []
         for side in range(2):
             value = projected[2 * side * hidden : (2 * side + 1) * hidden]
@@ -202,8 +213,7 @@
     width = chunks * LANES
     deep = right.shape[1]
     depth = spread.shape[2] // (2 * own)
-    one = lax.broadcasted_iota(jnp.int32, (cols, width), 0) == lax.broadcasted_iota(jnp.int32, (cols, width), 1)
-    one = one.astype(jnp.bfloat16)
+    one = identity(cols, width)
     if depth < deep:
         right[:, depth:, :] = jnp.zeros((own, deep - depth, halves * width), jnp.bfloat16)
     peers = message_ref.shape[0] // halves
@@ -238,7 +248,7 @@
             pack(mixed.at[i_half, j_half], mixed_ref, at * each, own, cols)
 
 
-def output_kernel(own, shares, halves, mixed_ref, gate_ref, gain_ref, w_t_ref, update_ref, mixed):
+def output_kernel(own, shares, halves, mixed_ref, gate_ref, gain_ref, w_t_ref, update_ref, mixed, normed):
     lines = mixed.shape[1]
     peers = shares // PARTS
     mixed[...] = mixed_ref[...].astype(jnp.float32).reshape(mixed.shape)
@@ -254,10 +264,14 @@
         block = jnp.concatenate(blocks, axis=0)
         center = block - jnp.mean(block, axis=0, keepdims=True)
         spread = jnp.mean(center * center, axis=0, keepdims=True)
-        normed = (center * lax.rsqrt(spread + EPS) * gain_ref[...]).astype(jnp.bfloat16)
-        projected = jnp.dot(w_t_ref[...], normed, preferred_element_type=jnp.float32)
+        normed[:, group * LANES : (group + 1) * LANES] = (
+            center * lax.rsqrt(spread + EPS) * gain_ref[...]
+        ).astype(jnp.bfloat16)
+    projected = jnp.dot(w_t_ref[...], normed[...], preferred_element_type=jnp.float32)
+    update = (gate_ref[...] * projected).astype(jnp.bfloat16)
+    for group in range(lines // own):
         lanes = slice(group * LANES, (group + 1) * LANES)
-        update_ref[lanes, :] = (gate_ref[:, lanes] * projected).astype(jnp.bfloat16).T
+        update_ref[lanes, :] = transpose(update[:, lanes]).astype(jnp.bfloat16)
 
 
 def on_device(shares, halves, pair, tile_mask, chain_ids, gain_in, w_proj, gain_mid, w_out):
@@ -286,7 +300,7 @@
             pltpu.VMEM(w_proj.shape, jnp.bfloat16),
             pltpu.VMEM(message.shape, jnp.bfloat16),
             pltpu.VMEM((width, positions), jnp.bfloat16),
-            pltpu.SemaphoreType.DMA((4 + cycles,)),
+            pltpu.SemaphoreType.DMA((5,)),
             pltpu.SemaphoreType.DMA((cycles, 2)),
         ],
         compiler_params=whole_params,
@@ -356,7 +370,10 @@
         out_shape=jax.ShapeDtypeStruct((positions, width), jnp.bfloat16),
         in_specs=[VMEM] * 4,
         out_specs=VMEM,
-        scratch_shapes=[pltpu.VMEM((halves * shares, lines, LANES), jnp.float32)],
+        scratch_shapes=[
+            pltpu.VMEM((halves * shares, lines, LANES), jnp.float32),
+            pltpu.VMEM((hidden, positions), jnp.bfloat16),
+        ],
         compiler_params=params,
         name="output",
     )(mixed, gate, gain, w_out_t)

time: 45.1 us -> 44.8 us (level)
    pallas_call x1, Pallas kernels: 3.29 us -> 2.81 us  [on_device(): pl.pallas_call(functools.partial(project_kernel, rows, cols), out_shape=(...]
where the time goes in v9:
time: 44.8 us; the launch traced here: 44.5 us
  blocking collectives  22.4 us (50%)
  waiting for transfers between devices  9.03 us (20%)
  starting transfers between devices  6.43 us (14%)
  Pallas kernels  5.93 us (13%)
  local copies, waits for them, and re-layouts  0.64 us (1%)
    all_to_all x1, blocking collectives, on_device(): lax.all_to_all(mixed.reshape(halves * shares, lines, LANES), ('col', 'row...  22.4 us
    all_to_all x1, waiting for transfers between devices, on_device(): lax.all_to_all(message, ('col', 'row'), split_axis=0, concat_axis=0, axis...  9.03 us
    all_to_all x1, starting transfers between devices, on_device(): lax.all_to_all(message, ('col', 'row'), split_axis=0, concat_axis=0, axis...  6.43 us
    pallas_call x1, Pallas kernels, on_device(): pl.pallas_call(functools.partial(project_kernel, rows, cols), out_shape=(...  2.81 us
    pallas_call x1, Pallas kernels, on_device(): pl.pallas_call(functools.partial(output_kernel, own, shares, halves), out...  1.32 us
    pallas_call x1, Pallas kernels, on_device(): pl.pallas_call(functools.partial(triangle_kernel, own, cols), out_shape=j...  1.27 us
  transfers between devices with their start and end apart: 1, of which 1 were waited for; matrix products, arithmetic and copies ran while one was open for 0% of the time, Pallas kernels for 1%

profile of v9, /device:TPU:0, one launch (start us, length us, event | category | flops | bytes accessed | tf_op | source)
XLA Modules:
  0.0 44.5 jit_solution(17281198305796328476)
XLA Ops:
  0.0 2.8 %project.1 = (bf16[16,144,128]{2,1,0:T(8,128)(2,1)}, bf16[128,1152]{1,0:T(8,128)(2,1)}) custom-call(s32[2,2]{1,0:T(2,128)} %tile_hbm.1, s32[1,192]{1,0:T(1,128)} %bitcast.11, bf16[1152,128]{1,0:T(8,128)(2,1)} %bitcast.10, f32[1,128]{1,0:T(1,128)} %bitcast.12, bf16[128,640]{1,0:T(8,128)(2,1)} %w_hbm.3), custom_call_target="tpu_custom_call" | custom-call | tf_op jit(solution)/shard_map/project/pallas_call | solution.py:290
  2.8 0.0 copy-start
  2.8 0.0 copy-start.1
  2.8 0.0 copy-start.2
  2.9 6.4 %all-to-all-start = ((bf16[16,144,128]{2,1,0:T(8,128)(2,1)}), bf16[16,144,128]{2,1,0:T(8,128)(2,1)S(1)}, u32[]{:S(2)}, u32[]{:S(2)}) async-start(bf16[16,144,128]{2,1,0:T(8,128)(2,1)} %get-tuple-element.13), calls=%async_computation | async-start | bytes 1179648 | tf_op jit(solution)/shard_map/all_to_all | solution.py:309
  9.3 0.0 copy-start.3
  9.3 0.0 copy-done
  9.3 0.0 copy-done.1
  9.3 0.0 copy-done.2
  9.3 0.6 %copy-done.3 = f32[128]{0:T(128)S(1)} copy-done((f32[128]{0:T(128)S(1)}, f32[128]{0:T(128)}, u32[]{:S(2)}) %copy-start.3) | copy-done | bytes 536
  10.0 0.5 %gate.1 = (f32[128,1152]{1,0:T(8,128)S(1)}, bf16[128,128]{1,0:T(8,128)(2,1)S(1)}, f32[128,128]{1,0:T(8,128)S(1)}, f32[8,128]{1,0:T(8,128)S(1)}) custom-call(bf16[128,1152]{1,0:T(8,128)(2,1)S(1)} %copy-done.1, bf16[128,640]{1,0:T(8,128)(2,1)S(1)} %copy-done, f32[1,128]{1,0:T(1,128)S(1)} %bitcast.9, bf16[128,128]{1,0:T(8,128)(2,1)S(1)} %copy-done.2), custom_call_target="tpu_custom_call" | custom-call | flops 37748736 | bytes 589824 | tf_op jit(solution)/shard_map/gate/pallas_call | solution.py:320
  10.5 9.0 %all-to-all-done.message_ref = bf16[16,144,128]{2,1,0:T(8,128)(2,1)S(1)} async-done(((bf16[16,144,128]{2,1,0:T(8,128)(2,1)}), bf16[16,144,128]{2,1,0:T(8,128)(2,1)S(1)}, u32[]{:S(2)}, u32[]{:S(2)}) %all-to-all-start) | async-done | bytes 589856 | tf_op jit(solution)/shard_map/all_to_all | solution.py:309
  19.5 1.3 %triangle.1 = bf16[2304,128]{1,0:T(8,128)(2,1)S(1)} custom-call(bf16[16,144,128]{2,1,0:T(8,128)(2,1)S(1)} %all-to-all-done.message_ref, f32[8,128]{1,0:T(8,128)S(1)} %get-tuple-element.17._), custom_call_target="tpu_custom_call" | custom-call | tf_op jit(solution)/shard_map/triangle/pallas_call | solution.py:346
  20.8 22.4 %all_to_all.10 = bf16[32,72,128]{2,1,0:T(8,128)(2,1)S(1)} all-to-all(bf16[32,72,128]{2,1,0:T(8,128)(2,1)S(1)} %bitcast.8), channel_id=1, replica_groups=mesh['grp'=1,'row'=16,'col'=2] {'col','row'}, dimensions={0} | all-to-all | bytes 1179648 | tf_op jit(solution)/shard_map/all_to_all | solution.py:361
  43.2 1.3 %output.1 = bf16[1152,128]{1,0:T(8,128)(2,1)} custom-call(bf16[2304,128]{1,0:T(8,128)(2,1)S(1)} %bitcast.7, f32[128,1152]{1,0:T(8,128)S(1)} %get-tuple-element.18.gate_ref, f32[128,128]{1,0:T(8,128)S(1)} %get-tuple-element.19.gain_ref, bf16[128,128]{1,0:T(8,128)(2,1)S(1)} %get-tuple-element.20.w_t_ref), custom_call_target="tpu_custom_call" | custom-call | tf_op jit(solution)/shard_map/output/pallas_call | solution.py:368
Async XLA Ops:
  2.8 6.5 %copy-start = (bf16[128,640]{1,0:T(8,128)(2,1)S(1)}, bf16[128,640]{1,0:T(8,128)(2,1)}, u32[]{:S(2)}) copy-start(bf16[128,640]{1,0:T(8,128)(2,1)} %w_hbm.3) | copy-start | bytes 491524
  2.8 6.5 %copy-start.1 = (bf16[128,1152]{1,0:T(8,128)(2,1)S(1)}, bf16[128,1152]{1,0:T(8,128)(2,1)}, u32[]{:S(2)}) copy-start(bf16[128,1152]{1,0:T(8,128)(2,1)} %get-tuple-element.14.normed_ref) | copy-start | bytes 884740
  2.8 6.5 %copy-start.2 = (bf16[128,128]{1,0:T(8,128)(2,1)S(1)}, bf16[128,128]{1,0:T(8,128)(2,1)}, u32[]{:S(2)}) copy-start(bf16[128,128]{1,0:T(8,128)(2,1)} %w_out_hbm.1) | copy-start | bytes 98308
  2.9 16.7 %all-to-all-start = ((bf16[16,144,128]{2,1,0:T(8,128)(2,1)}), bf16[16,144,128]{2,1,0:T(8,128)(2,1)S(1)}, u32[]{:S(2)}, u32[]{:S(2)}) async-start(bf16[16,144,128]{2,1,0:T(8,128)(2,1)} %get-tuple-element.13), calls=%async_computation | async-start | bytes 1179648 | tf_op jit(solution)/shard_map/all_to_all | solution.py:309
  9.3 0.7 %copy-start.3 = (f32[128]{0:T(128)S(1)}, f32[128]{0:T(128)}, u32[]{:S(2)}) copy-start(f32[128]{0:T(128)} %param.12) | copy-start | bytes 1540

commit v10 on v9

--- a/solution.py
+++ b/solution.py
@@ -150,16 +150,19 @@
     done_ref[...] = jnp.zeros_like(done_ref)
 
 
-def unpack(message_ref, spread_ref, own, cols):
+def unpack(message_ref, half, halves, spread_ref, own, cols):
     tokens, groups = cycle_of(cols)
-    peers, lines, _ = message_ref.shape
+    members, lines, _ = message_ref.shape
+    peers = members // halves
     lane = lax.broadcasted_iota(jnp.int32, (2 * own, LANES), 1)
     cycles = lines // (2 * groups * own)
     for peer in range(peers):
         for cycle in range(cycles):
             base = cycle * groups
             held = [
-                message_ref[peer, (base + group) * 2 * own : (base + group + 1) * 2 * own, :].astype(jnp.float32)
+                message_ref[
+                    peer * halves + half, (base + group) * 2 * own : (base + group + 1) * 2 * own, :
+                ].astype(jnp.float32)
                 for group in range(groups)
             ]
             for token in range(tokens):
@@ -174,30 +177,25 @@
                     spread_ref[chunk, k * 2 * own : (k + 1) * 2 * own, :] = value
 
 
-def pack(spread_ref, mixed_ref, first, own, cols):
+def pack(spread_ref, at, own, cols):
     tokens, groups = cycle_of(cols)
     lane = lax.broadcasted_iota(jnp.int32, (own, LANES), 1)
-    batch = 16 // math.gcd(groups * own, 16)
-    for start in range(0, cols // tokens, batch):
-        lines = []
-        for at in range(start, start + batch):
-            rolled = {}
-            for group in range(groups):
-                value, here = None, 0
-                while here < LANES:
-                    token, col = divmod(group * LANES + here, cols)
-                    chunk, there = divmod(col, LANES)
-                    shift = (here - there) % LANES
-                    if (token, chunk, shift) not in rolled:
-                        line = (at * tokens + token) * own
-                        piece = spread_ref[chunk, line : line + own, :]
-                        rolled[token, chunk, shift] = pltpu.roll(piece, shift, axis=1) if shift else piece
-                    piece = rolled[token, chunk, shift]
-                    value = piece if value is None else jnp.where(lane >= here, piece, value)
-                    here += min(LANES - here, LANES - there, cols - col)
-                lines.append(value)
-        at = first + start * groups * own
-        mixed_ref[at : at + batch * groups * own, :] = jnp.concatenate(lines, axis=0).astype(jnp.bfloat16)
+    rolled, lines = {}, []
+    for group in range(groups):
+        value, here = None, 0
+        while here < LANES:
+            token, col = divmod(group * LANES + here, cols)
+            chunk, there = divmod(col, LANES)
+            shift = (here - there) % LANES
+            if (token, chunk, shift) not in rolled:
+                line = (at * tokens + token) * own
+                piece = spread_ref[chunk, line : line + own, :]
+                rolled[token, chunk, shift] = pltpu.roll(piece, shift, axis=1) if shift else piece
+            piece = rolled[token, chunk, shift]
+            value = piece if value is None else jnp.where(lane >= here, piece, value)
+            here += min(LANES - here, LANES - there, cols - col)
+        lines.append(value)
+    return lines
 
 
 def channel_of(spread_ref, line, stride):
@@ -208,7 +206,7 @@
     ).astype(jnp.bfloat16)
 
 
-def triangle_kernel(own, cols, message_ref, _, mixed_ref, spread, left, left_t, right, mixed):
+def triangle_kernel(own, cols, shares, message_ref, _, mixed_ref, spread, left, left_t, right, mixed):
     halves, chunks = spread.shape[:2]
     width = chunks * LANES
     deep = right.shape[1]
@@ -216,9 +214,8 @@
     one = identity(cols, width)
     if depth < deep:
         right[:, depth:, :] = jnp.zeros((own, deep - depth, halves * width), jnp.bfloat16)
-    peers = message_ref.shape[0] // halves
     for half in range(halves):
-        unpack(message_ref.at[half * peers : (half + 1) * peers], spread.at[half], own, cols)
+        unpack(message_ref, half, halves, spread.at[half], own, cols)
         if depth < deep:
             left[:, half * deep + depth : (half + 1) * deep, :] = jnp.zeros((own, deep - depth, width), jnp.bfloat16)
         for channel in range(own):
@@ -241,37 +238,42 @@
                     mixed[i_half, j_half, chunk, pl.ds(channel, cols, stride=own), :] = total[
                         i_half * cols : (i_half + 1) * cols, start : start + LANES
                     ]
-    each = mixed_ref.shape[0] // (halves * halves)
-    for j_half in range(halves):
-        for i_half in range(halves):
-            at = j_half * halves + i_half
-            pack(mixed.at[i_half, j_half], mixed_ref, at * each, own, cols)
-
-
-def output_kernel(own, shares, halves, mixed_ref, gate_ref, gain_ref, w_t_ref, update_ref, mixed, normed):
-    lines = mixed.shape[1]
-    peers = shares // PARTS
+    groups = cycle_of(cols)[1]
+    each = mixed_ref.shape[0] // shares
+    cycles = each // (halves * groups * own)
+    for share in range(shares):
+        i_half, peer = divmod(share, shares // halves)
+        lines = []
+        for j_half in range(halves):
+            for cycle in range(cycles):
+                lines += pack(mixed.at[i_half, j_half], peer * cycles + cycle, own, cols)
+        mixed_ref[share * each : (share + 1) * each, :] = jnp.concatenate(lines, axis=0).astype(jnp.bfloat16)
+
+
+def output_kernel(own, parts, mixed_ref, gate_ref, gain_ref, w_t_ref, update_hbm, mixed, update, sems):
+    members, lines, _ = mixed.shape
+    members = members // parts
     mixed[...] = mixed_ref[...].astype(jnp.float32).reshape(mixed.shape)
-    for group in range(lines // own):
-        blocks = []
-        for half in range(halves):
-            first = half * shares
-            block = mixed[first : first + peers, group * own : (group + 1) * own, :]
-            for part in range(1, PARTS):
-                start = first + part * peers
-                block += mixed[start : start + peers, group * own : (group + 1) * own, :]
-            blocks.append(block.reshape(peers * own, LANES))
-        block = jnp.concatenate(blocks, axis=0)
+    groups = lines // own
+    steps = math.gcd(groups, 3)
+    leaving = []
+    for group in range(groups):
+        sums = mixed[:members, group * own : (group + 1) * own, :]
+        for part in range(1, parts):
+            sums += mixed[part * members : (part + 1) * members, group * own : (group + 1) * own, :]
+        block = sums.reshape(members * own, LANES)
         center = block - jnp.mean(block, axis=0, keepdims=True)
         spread = jnp.mean(center * center, axis=0, keepdims=True)
-        normed[:, group * LANES : (group + 1) * LANES] = (
-            center * lax.rsqrt(spread + EPS) * gain_ref[...]
-        ).astype(jnp.bfloat16)
-    projected = jnp.dot(w_t_ref[...], normed[...], preferred_element_type=jnp.float32)
-    update = (gate_ref[...] * projected).astype(jnp.bfloat16)
-    for group in range(lines // own):
+        normed = (center * lax.rsqrt(spread + EPS) * gain_ref[...]).astype(jnp.bfloat16)
+        projected = jnp.dot(w_t_ref[...], normed, preferred_element_type=jnp.float32)
         lanes = slice(group * LANES, (group + 1) * LANES)
-        update_ref[lanes, :] = transpose(update[:, lanes]).astype(jnp.bfloat16)
+        update[lanes, :] = (gate_ref[:, lanes] * projected).T.astype(jnp.bfloat16)
+        step, last = divmod((group + 1) * steps, groups)
+        if last == 0:
+            done = slice((step - 1) * (groups // steps) * LANES, (group + 1) * LANES)
+            leaving += start_copies(sems.at[step - 1], (update.at[done, :], update_hbm.at[done, :]))
+    for copy in leaving:
+        copy.wait()
 
 
 def on_device(shares, halves, pair, tile_mask, chain_ids, gain_in, w_proj, gain_mid, w_out):
@@ -308,11 +310,11 @@
     )(tile_mask, chain_ids[None, :], pair.reshape(positions, width), gain_in[None, :], w_proj)
     message = lax.all_to_all(
         message,
-        ("col", "row"),
+        ("row", "col"),
         split_axis=0,
         concat_axis=0,
         axis_index_groups=[
-            [half * shares + part * peers + at for half in range(halves) for at in range(peers)]
+            list(range(part * peers * halves, (part + 1) * peers * halves))
             for part in range(PARTS)
         ],
         tiled=True,
@@ -344,7 +346,7 @@
     depth = peers * rows
     deep = pl.cdiv(depth, LANES) * LANES
     mixed = pl.pallas_call(
-        functools.partial(triangle_kernel, own, cols),
+        functools.partial(triangle_kernel, own, cols, shares),
         out_shape=jax.ShapeDtypeStruct((halves * shares * lines, LANES), jnp.bfloat16),
         in_specs=[VMEM, ANY],
         out_specs=VMEM,
@@ -360,19 +362,20 @@
     )(message, done)
     mixed = lax.all_to_all(
         mixed.reshape(halves * shares, lines, LANES),
-        ("col", "row"),
+        ("row", "col"),
         split_axis=0,
         concat_axis=0,
         tiled=True,
     ).reshape(halves * shares * lines, LANES)
     update = pl.pallas_call(
-        functools.partial(output_kernel, own, shares, halves),
+        functools.partial(output_kernel, own, PARTS),
         out_shape=jax.ShapeDtypeStruct((positions, width), jnp.bfloat16),
         in_specs=[VMEM] * 4,
-        out_specs=VMEM,
+        out_specs=HBM,
         scratch_shapes=[
-            pltpu.VMEM((halves * shares, lines, LANES), jnp.float32),
-            pltpu.VMEM((hidden, positions), jnp.bfloat16),
+            pltpu.VMEM((shares * halves, lines, LANES), jnp.float32),
+            pltpu.VMEM((positions, width), jnp.bfloat16),
+            pltpu.SemaphoreType.DMA((math.gcd(groups, 3), 1)),
         ],
         compiler_params=params,
         name="output",

time: 44.8 us -> 42.8 us (0.955)
  blocking collectives: 22.4 us -> 19.6 us
  waiting for transfers between devices: 9.03 us -> 10.1 us
    all_to_all x1, blocking collectives: 22.4 us -> 19.6 us  [on_device(): lax.all_to_all(mixed.reshape(halves * shares, lines, LANES), ('row', 'col...]
    all_to_all x1, waiting for transfers between devices: 9.03 us -> 10.1 us  [on_device(): lax.all_to_all(message, ('row', 'col'), split_axis=0, concat_axis=0, axis...]
where the time goes in v10:
time: 42.8 us; the launch traced here: 42.6 us
  blocking collectives  19.6 us (46%)
  waiting for transfers between devices  10.1 us (24%)
  starting transfers between devices  6.43 us (15%)
  Pallas kernels  5.75 us (13%)
  local copies, waits for them, and re-layouts  0.64 us (1%)
    all_to_all x1, blocking collectives, on_device(): lax.all_to_all(mixed.reshape(halves * shares, lines, LANES), ('row', 'col...  19.6 us
    all_to_all x1, waiting for transfers between devices, on_device(): lax.all_to_all(message, ('row', 'col'), split_axis=0, concat_axis=0, axis...  10.1 us
    all_to_all x1, starting transfers between devices, on_device(): lax.all_to_all(message, ('row', 'col'), split_axis=0, concat_axis=0, axis...  6.43 us
    pallas_call x1, Pallas kernels, on_device(): pl.pallas_call(functools.partial(project_kernel, rows, cols), out_shape=(...  2.81 us
    pallas_call x1, Pallas kernels, on_device(): pl.pallas_call(functools.partial(triangle_kernel, own, cols, shares), out...  1.27 us
    pallas_call x1, Pallas kernels, on_device(): pl.pallas_call(functools.partial(output_kernel, own, PARTS), out_shape=ja...  1.14 us
  transfers between devices with their start and end apart: 1, of which 1 were waited for; matrix products, arithmetic and copies ran while one was open for 0% of the time, Pallas kernels for 1%

profile of v10, /device:TPU:0, one launch (start us, length us, event | category | flops | bytes accessed | tf_op | source)
XLA Modules:
  0.0 42.6 jit_solution(14126717773717248818)
XLA Ops:
  0.0 2.8 %project.1 = (bf16[16,144,128]{2,1,0:T(8,128)(2,1)}, bf16[128,1152]{1,0:T(8,128)(2,1)}) custom-call(s32[2,2]{1,0:T(2,128)} %tile_hbm.1, s32[1,192]{1,0:T(1,128)} %bitcast.11, bf16[1152,128]{1,0:T(8,128)(2,1)} %bitcast.10, f32[1,128]{1,0:T(1,128)} %bitcast.12, bf16[128,640]{1,0:T(8,128)(2,1)} %w_hbm.3), custom_call_target="tpu_custom_call" | custom-call | tf_op jit(solution)/shard_map/project/pallas_call | solution.py:292
  2.8 0.0 copy-start
  2.8 0.0 copy-start.1
  2.8 0.0 copy-start.2
  2.9 6.4 %all-to-all-start = ((bf16[16,144,128]{2,1,0:T(8,128)(2,1)}), bf16[16,144,128]{2,1,0:T(8,128)(2,1)S(1)}, u32[]{:S(2)}, u32[]{:S(2)}) async-start(bf16[16,144,128]{2,1,0:T(8,128)(2,1)} %get-tuple-element.13), calls=%async_computation | async-start | bytes 1179648 | tf_op jit(solution)/shard_map/all_to_all | solution.py:311
  9.3 0.0 copy-start.3
  9.3 0.0 copy-done
  9.3 0.0 copy-done.1
  9.3 0.0 copy-done.2
  9.3 0.6 %copy-done.3 = f32[128]{0:T(128)S(1)} copy-done((f32[128]{0:T(128)S(1)}, f32[128]{0:T(128)}, u32[]{:S(2)}) %copy-start.3) | copy-done | bytes 536
  10.0 0.5 %gate.1 = (f32[128,1152]{1,0:T(8,128)S(1)}, bf16[128,128]{1,0:T(8,128)(2,1)S(1)}, f32[128,128]{1,0:T(8,128)S(1)}, f32[8,128]{1,0:T(8,128)S(1)}) custom-call(bf16[128,1152]{1,0:T(8,128)(2,1)S(1)} %copy-done.1, bf16[128,640]{1,0:T(8,128)(2,1)S(1)} %copy-done, f32[1,128]{1,0:T(1,128)S(1)} %bitcast.9, bf16[128,128]{1,0:T(8,128)(2,1)S(1)} %copy-done.2), custom_call_target="tpu_custom_call" | custom-call | flops 37748736 | bytes 589824 | tf_op jit(solution)/shard_map/gate/pallas_call | solution.py:322
  10.5 10.1 %all-to-all-done.message_ref = bf16[16,144,128]{2,1,0:T(8,128)(2,1)S(1)} async-done(((bf16[16,144,128]{2,1,0:T(8,128)(2,1)}), bf16[16,144,128]{2,1,0:T(8,128)(2,1)S(1)}, u32[]{:S(2)}, u32[]{:S(2)}) %all-to-all-start) | async-done | bytes 589856 | tf_op jit(solution)/shard_map/all_to_all | solution.py:311
  20.5 1.3 %triangle.1 = bf16[2304,128]{1,0:T(8,128)(2,1)S(1)} custom-call(bf16[16,144,128]{2,1,0:T(8,128)(2,1)S(1)} %all-to-all-done.message_ref, f32[8,128]{1,0:T(8,128)S(1)} %get-tuple-element.17._), custom_call_target="tpu_custom_call" | custom-call | tf_op jit(solution)/shard_map/triangle/pallas_call | solution.py:348
  21.8 19.6 %all_to_all.10 = bf16[32,72,128]{2,1,0:T(8,128)(2,1)S(1)} all-to-all(bf16[32,72,128]{2,1,0:T(8,128)(2,1)S(1)} %bitcast.8), channel_id=1, replica_groups=mesh['grp'=1,'row'=16,'col'=2] {'row','col'}, dimensions={0} | all-to-all | bytes 1179648 | tf_op jit(solution)/shard_map/all_to_all | solution.py:363
  41.4 1.1 %output.1 = bf16[1152,128]{1,0:T(8,128)(2,1)} custom-call(bf16[2304,128]{1,0:T(8,128)(2,1)S(1)} %bitcast.7, f32[128,1152]{1,0:T(8,128)S(1)} %get-tuple-element.18.gate_ref, f32[128,128]{1,0:T(8,128)S(1)} %get-tuple-element.19.gain_ref, bf16[128,128]{1,0:T(8,128)(2,1)S(1)} %get-tuple-element.20.w_t_ref), custom_call_target="tpu_custom_call" | custom-call | tf_op jit(solution)/shard_map/output/pallas_call | solution.py:370
Async XLA Ops:
  2.8 6.5 %copy-start = (bf16[128,640]{1,0:T(8,128)(2,1)S(1)}, bf16[128,640]{1,0:T(8,128)(2,1)}, u32[]{:S(2)}) copy-start(bf16[128,640]{1,0:T(8,128)(2,1)} %w_hbm.3) | copy-start | bytes 491524
  2.8 6.5 %copy-start.1 = (bf16[128,1152]{1,0:T(8,128)(2,1)S(1)}, bf16[128,1152]{1,0:T(8,128)(2,1)}, u32[]{:S(2)}) copy-start(bf16[128,1152]{1,0:T(8,128)(2,1)} %get-tuple-element.14.normed_ref) | copy-start | bytes 884740
  2.8 6.5 %copy-start.2 = (bf16[128,128]{1,0:T(8,128)(2,1)S(1)}, bf16[128,128]{1,0:T(8,128)(2,1)}, u32[]{:S(2)}) copy-start(bf16[128,128]{1,0:T(8,128)(2,1)} %w_out_hbm.1) | copy-start | bytes 98308
  2.9 17.7 %all-to-all-start = ((bf16[16,144,128]{2,1,0:T(8,128)(2,1)}), bf16[16,144,128]{2,1,0:T(8,128)(2,1)S(1)}, u32[]{:S(2)}, u32[]{:S(2)}) async-start(bf16[16,144,128]{2,1,0:T(8,128)(2,1)} %get-tuple-element.13), calls=%async_computation | async-start | bytes 1179648 | tf_op jit(solution)/shard_map/all_to_all | solution.py:311
  9.3 0.7 %copy-start.3 = (f32[128]{0:T(128)S(1)}, f32[128]{0:T(128)}, u32[]{:S(2)}) copy-start(f32[128]{0:T(128)} %param.12) | copy-start | bytes 1540

commit v11 on v10

--- a/solution.py
+++ b/solution.py
@@ -18,6 +18,16 @@
 ANY = pl.BlockSpec(memory_space=pl.ANY)
 HBM = pl.BlockSpec(memory_space=pltpu.HBM)
 SMEM = pl.BlockSpec(memory_space=pltpu.SMEM)
+
+
+def forward_order(peers, halves):
+    bits = (peers - 1).bit_length()
+    turned = sorted(range(peers), key=lambda at: sum((at >> bit & 1) << (bits - 1 - bit) for bit in range(bits)))
+    return [(at, half) for half in range(halves) for at in turned]
+
+
+def return_order(peers, halves, parts):
+    return [(part, at, half) for at in range(peers) for half in range(halves) for part in range(parts)]
 
 
 def column(row):
@@ -154,14 +164,16 @@
     tokens, groups = cycle_of(cols)
     members, lines, _ = message_ref.shape
     peers = members // halves
+    order = forward_order(peers, halves)
     lane = lax.broadcasted_iota(jnp.int32, (2 * own, LANES), 1)
     cycles = lines // (2 * groups * own)
     for peer in range(peers):
+        member = order.index((peer, half))
         for cycle in range(cycles):
             base = cycle * groups
             held = [
                 message_ref[
-                    peer * halves + half, (base + group) * 2 * own : (base + group + 1) * 2 * own, :
+                    member, (base + group) * 2 * own : (base + group + 1) * 2 * own, :
                 ].astype(jnp.float32)
                 for group in range(groups)
             ]
@@ -206,7 +218,7 @@
     ).astype(jnp.bfloat16)
 
 
-def triangle_kernel(own, cols, shares, message_ref, _, mixed_ref, spread, left, left_t, right, mixed):
+def triangle_kernel(own, cols, shares, parts, message_ref, _, mixed_ref, spread, left, left_t, right, mixed):
     halves, chunks = spread.shape[:2]
     width = chunks * LANES
     deep = right.shape[1]
@@ -239,29 +251,36 @@
                         i_half * cols : (i_half + 1) * cols, start : start + LANES
                     ]
     groups = cycle_of(cols)[1]
-    each = mixed_ref.shape[0] // shares
-    cycles = each // (halves * groups * own)
-    for share in range(shares):
-        i_half, peer = divmod(share, shares // halves)
+    peers = shares // parts
+    order = return_order(peers, halves, parts)
+    each = mixed_ref.shape[0] // len(order)
+    cycles = each // (groups * own)
+    batch = 16 // math.gcd(each, 16)
+    for start in range(0, len(order), batch):
         lines = []
-        for j_half in range(halves):
+        for part, at, j_half in order[start : start + batch]:
+            i_half, peer = divmod(part * peers + at, shares // halves)
             for cycle in range(cycles):
                 lines += pack(mixed.at[i_half, j_half], peer * cycles + cycle, own, cols)
-        mixed_ref[share * each : (share + 1) * each, :] = jnp.concatenate(lines, axis=0).astype(jnp.bfloat16)
-
-
-def output_kernel(own, parts, mixed_ref, gate_ref, gain_ref, w_t_ref, update_hbm, mixed, update, sems):
+        mixed_ref[start * each : (start + batch) * each, :] = jnp.concatenate(lines, axis=0).astype(jnp.bfloat16)
+
+
+def output_kernel(own, halves, parts, mixed_ref, gate_ref, gain_ref, w_t_ref, update_hbm, mixed, update, sems):
     members, lines, _ = mixed.shape
-    members = members // parts
+    peers = members // (halves * parts)
+    order = return_order(peers, halves, parts)
     mixed[...] = mixed_ref[...].astype(jnp.float32).reshape(mixed.shape)
     groups = lines // own
     steps = math.gcd(groups, 3)
     leaving = []
     for group in range(groups):
-        sums = mixed[:members, group * own : (group + 1) * own, :]
-        for part in range(1, parts):
-            sums += mixed[part * members : (part + 1) * members, group * own : (group + 1) * own, :]
-        block = sums.reshape(members * own, LANES)
+        blocks = []
+        for at, half in forward_order(peers, halves):
+            pieces = [
+                mixed[order.index((part, at, half)), group * own : (group + 1) * own, :] for part in range(parts)
+            ]
+            blocks.append(functools.reduce(jnp.add, pieces))
+        block = jnp.concatenate(blocks, axis=0)
         center = block - jnp.mean(block, axis=0, keepdims=True)
         spread = jnp.mean(center * center, axis=0, keepdims=True)
         normed = (center * lax.rsqrt(spread + EPS) * gain_ref[...]).astype(jnp.bfloat16)
@@ -314,7 +333,7 @@
         split_axis=0,
         concat_axis=0,
         axis_index_groups=[
-            list(range(part * peers * halves, (part + 1) * peers * halves))
+            [(part * peers + at) * halves + half for at, half in forward_order(peers, halves)]
             for part in range(PARTS)
         ],
         tiled=True,
@@ -346,7 +365,7 @@
     depth = peers * rows
     deep = pl.cdiv(depth, LANES) * LANES
     mixed = pl.pallas_call(
-        functools.partial(triangle_kernel, own, cols, shares),
+        functools.partial(triangle_kernel, own, cols, shares, PARTS),
         out_shape=jax.ShapeDtypeStruct((halves * shares * lines, LANES), jnp.bfloat16),
         in_specs=[VMEM, ANY],
         out_specs=VMEM,
@@ -365,10 +384,13 @@
         ("row", "col"),
         split_axis=0,
         concat_axis=0,
+        axis_index_groups=[
+            [(part * peers + at) * halves + half for part, at, half in return_order(peers, halves, PARTS)]
+        ],
         tiled=True,
     ).reshape(halves * shares * lines, LANES)
     update = pl.pallas_call(
-        functools.partial(output_kernel, own, PARTS),
+        functools.partial(output_kernel, own, halves, PARTS),
         out_shape=jax.ShapeDtypeStruct((positions, width), jnp.bfloat16),
         in_specs=[VMEM] * 4,
         out_specs=HBM,

time: 42.8 us -> 43.8 us (1.023)
  the two profiles are of different devices: /device:TPU:0 before, /device:TPU:1 now
where the time goes in v11:
time: 43.8 us; the launch traced here: 43.5 us
  blocking collectives  22.1 us (50%)
  waiting for transfers between devices  8.56 us (20%)
  starting transfers between devices  6.4 us (15%)
  Pallas kernels  5.74 us (13%)
  local copies, waits for them, and re-layouts  0.64 us (1%)
    all_to_all x1, blocking collectives, on_device(): lax.all_to_all(mixed.reshape(halves * shares, lines, LANES), ('row', 'col...  22.1 us
    all_to_all x1, waiting for transfers between devices, on_device(): lax.all_to_all(message, ('row', 'col'), split_axis=0, concat_axis=0, axis...  8.56 us
    all_to_all x1, starting transfers between devices, on_device(): lax.all_to_all(message, ('row', 'col'), split_axis=0, concat_axis=0, axis...  6.4 us
    pallas_call x1, Pallas kernels, on_device(): pl.pallas_call(functools.partial(project_kernel, rows, cols), out_shape=(...  2.81 us
    pallas_call x1, Pallas kernels, on_device(): pl.pallas_call(functools.partial(triangle_kernel, own, cols, shares, PART...  1.27 us
    pallas_call x1, Pallas kernels, on_device(): pl.pallas_call(functools.partial(output_kernel, own, halves, PARTS), out_...  1.14 us
  transfers between devices with their start and end apart: 1, of which 1 were waited for; matrix products, arithmetic and copies ran while one was open for 0% of the time, Pallas kernels for 1%

profile of v11, /device:TPU:1, one launch (start us, length us, event | category | flops | bytes accessed | tf_op | source)
XLA Modules:
  0.0 43.5 jit_solution(16793663404208671902)
XLA Ops:
  0.0 2.8 %project.1 = (bf16[16,144,128]{2,1,0:T(8,128)(2,1)}, bf16[128,1152]{1,0:T(8,128)(2,1)}) custom-call(s32[2,2]{1,0:T(2,128)} %tile_hbm.1, s32[1,192]{1,0:T(1,128)} %bitcast.11, bf16[1152,128]{1,0:T(8,128)(2,1)} %bitcast.10, f32[1,128]{1,0:T(1,128)} %bitcast.12, bf16[128,640]{1,0:T(8,128)(2,1)} %w_hbm.3), custom_call_target="tpu_custom_call" | custom-call | tf_op jit(solution)/shard_map/project/pallas_call | solution.py:311
  2.8 0.0 copy-start
  2.8 0.0 copy-start.1
  2.8 0.0 copy-start.2
  2.9 6.4 %all-to-all-start = ((bf16[16,144,128]{2,1,0:T(8,128)(2,1)}), bf16[16,144,128]{2,1,0:T(8,128)(2,1)S(1)}, u32[]{:S(2)}, u32[]{:S(2)}) async-start(bf16[16,144,128]{2,1,0:T(8,128)(2,1)} %get-tuple-element.13), calls=%async_computation | async-start | bytes 1179648 | tf_op jit(solution)/shard_map/all_to_all | solution.py:330
  9.3 0.0 copy-start.3
  9.3 0.0 copy-done
  9.3 0.0 copy-done.1
  9.3 0.0 copy-done.2
  9.3 0.6 %copy-done.3 = f32[128]{0:T(128)S(1)} copy-done((f32[128]{0:T(128)S(1)}, f32[128]{0:T(128)}, u32[]{:S(2)}) %copy-start.3) | copy-done | bytes 536
  9.9 0.5 %gate.1 = (f32[128,1152]{1,0:T(8,128)S(1)}, bf16[128,128]{1,0:T(8,128)(2,1)S(1)}, f32[128,128]{1,0:T(8,128)S(1)}, f32[8,128]{1,0:T(8,128)S(1)}) custom-call(bf16[128,1152]{1,0:T(8,128)(2,1)S(1)} %copy-done.1, bf16[128,640]{1,0:T(8,128)(2,1)S(1)} %copy-done, f32[1,128]{1,0:T(1,128)S(1)} %bitcast.9, bf16[128,128]{1,0:T(8,128)(2,1)S(1)} %copy-done.2), custom_call_target="tpu_custom_call" | custom-call | flops 37748736 | bytes 589824 | tf_op jit(solution)/shard_map/gate/pallas_call | solution.py:341
  10.4 8.6 %all-to-all-done.message_ref = bf16[16,144,128]{2,1,0:T(8,128)(2,1)S(1)} async-done(((bf16[16,144,128]{2,1,0:T(8,128)(2,1)}), bf16[16,144,128]{2,1,0:T(8,128)(2,1)S(1)}, u32[]{:S(2)}, u32[]{:S(2)}) %all-to-all-start) | async-done | bytes 589856 | tf_op jit(solution)/shard_map/all_to_all | solution.py:330
  19.0 1.3 %triangle.1 = bf16[2304,128]{1,0:T(8,128)(2,1)S(1)} custom-call(bf16[16,144,128]{2,1,0:T(8,128)(2,1)S(1)} %all-to-all-done.message_ref, f32[8,128]{1,0:T(8,128)S(1)} %get-tuple-element.17._), custom_call_target="tpu_custom_call" | custom-call | tf_op jit(solution)/shard_map/triangle/pallas_call | solution.py:367
  20.3 22.1 %all_to_all.10 = bf16[32,72,128]{2,1,0:T(8,128)(2,1)S(1)} all-to-all(bf16[32,72,128]{2,1,0:T(8,128)(2,1)S(1)} %bitcast.8), channel_id=1, replica_groups={{0,16,1,17,2,18,3,19,4,20,5,21,6,22,7,23,8,24,9,25,10,26,11,27,12,28,13..., dimensions={0} | all-to-all | bytes 1179648 | tf_op jit(solution)/shard_map/all_to_all | solution.py:382
  42.4 1.1 %output.1 = bf16[1152,128]{1,0:T(8,128)(2,1)} custom-call(bf16[2304,128]{1,0:T(8,128)(2,1)S(1)} %bitcast.7, f32[128,1152]{1,0:T(8,128)S(1)} %get-tuple-element.18.gate_ref, f32[128,128]{1,0:T(8,128)S(1)} %get-tuple-element.19.gain_ref, bf16[128,128]{1,0:T(8,128)(2,1)S(1)} %get-tuple-element.20.w_t_ref), custom_call_target="tpu_custom_call" | custom-call | tf_op jit(solution)/shard_map/output/pallas_call | solution.py:392
Async XLA Ops:
  2.8 6.4 %copy-start = (bf16[128,640]{1,0:T(8,128)(2,1)S(1)}, bf16[128,640]{1,0:T(8,128)(2,1)}, u32[]{:S(2)}) copy-start(bf16[128,640]{1,0:T(8,128)(2,1)} %w_hbm.3) | copy-start | bytes 491524
  2.8 6.4 %copy-start.1 = (bf16[128,1152]{1,0:T(8,128)(2,1)S(1)}, bf16[128,1152]{1,0:T(8,128)(2,1)}, u32[]{:S(2)}) copy-start(bf16[128,1152]{1,0:T(8,128)(2,1)} %get-tuple-element.14.normed_ref) | copy-start | bytes 884740
  2.8 6.4 %copy-start.2 = (bf16[128,128]{1,0:T(8,128)(2,1)S(1)}, bf16[128,128]{1,0:T(8,128)(2,1)}, u32[]{:S(2)}) copy-start(bf16[128,128]{1,0:T(8,128)(2,1)} %w_out_hbm.1) | copy-start | bytes 98308
  2.9 16.2 %all-to-all-start = ((bf16[16,144,128]{2,1,0:T(8,128)(2,1)}), bf16[16,144,128]{2,1,0:T(8,128)(2,1)S(1)}, u32[]{:S(2)}, u32[]{:S(2)}) async-start(bf16[16,144,128]{2,1,0:T(8,128)(2,1)} %get-tuple-element.13), calls=%async_computation | async-start | bytes 1179648 | tf_op jit(solution)/shard_map/all_to_all | solution.py:330
  9.3 0.7 %copy-start.3 = (f32[128]{0:T(128)S(1)}, f32[128]{0:T(128)}, u32[]{:S(2)}) copy-start(f32[128]{0:T(128)} %param.12) | copy-start | bytes 1540

commit v12 on v10

--- a/solution.py
+++ b/solution.py
@@ -11,9 +11,10 @@
 TILE = 96
 LANES = 128
 EPS = 1e-05
-PARTS = 2
+OWN = 4
 VMEM_BYTES = 32 * 1024 * 1024
 WHOLE_VMEM_BYTES = 64 * 1024 * 1024
+ROWS = 8
 VMEM = pl.BlockSpec(memory_space=pltpu.VMEM)
 ANY = pl.BlockSpec(memory_space=pl.ANY)
 HBM = pl.BlockSpec(memory_space=pltpu.HBM)
@@ -88,15 +89,28 @@
         copy.wait()
 
 
+def turn_pairs(first, second):
+    axis = first.ndim - 2
+    upper = lax.broadcasted_iota(jnp.int32, first.shape, axis) < OWN
+    return (
+        jnp.where(upper, first, pltpu.roll(second, OWN, axis=axis)),
+        jnp.where(upper, pltpu.roll(first, OWN, axis=axis), second),
+    )
+
+
+def sides_by_member(left, right):
+    lines, width = left.shape
+    pairs = turn_pairs(left.reshape(-1, ROWS, width), right.reshape(-1, ROWS, width))
+    return jnp.stack(pairs, axis=1).reshape(2 * lines, width).astype(jnp.bfloat16)
+
+
 def project_kernel(
     rows, cols, tile_hbm, chain_hbm, pair_hbm, gain_hbm, w_hbm, message_hbm, normed_hbm,
-    tile_ref, chain_ref, pair_ref, gain_ref, w_ref, message_ref, normed_ref, sems, out_sems,
+    tile_ref, chain_ref, pair_ref, gain_ref, w_ref, held, message_ref, normed_ref, sems, out_sems,
 ):
     hidden = (w_ref.shape[1] - w_ref.shape[0]) // 4
-    peers = message_ref.shape[0]
-    own = hidden // peers
-    groups = cycle_of(cols)[1]
-    size = groups * LANES
+    members = held.shape[0]
+    size = cycle_of(cols)[1] * LANES
     copies = start_copies(
         sems,
         (w_hbm, w_ref),
@@ -108,7 +122,9 @@
     for copy in copies[:4]:
         copy.wait()
     keep = keep_of(tile_ref, chain_ref, rows, cols)
-    w_t = w_ref[:, : 4 * hidden].T
+    w_t = w_ref[:, : 4 * hidden].astype(jnp.float32).T
+    w_value = sides_by_member(w_t[:hidden], w_t[2 * hidden : 3 * hidden])
+    w_gate = sides_by_member(w_t[hidden : 2 * hidden], w_t[3 * hidden :])
     gain = column(gain_ref[...])
     copies[4].wait()
     cycles = [slice(start, start + size) for start in range(0, rows * cols, size)]
@@ -117,24 +133,23 @@
         center = block - jnp.mean(block, axis=0, keepdims=True)
         spread = jnp.mean(center * center, axis=0, keepdims=True)
         normed_ref[:, lanes] = (center * lax.rsqrt(spread + EPS) * gain).astype(jnp.bfloat16)
-    leaving = []
-    for cycle, lanes in enumerate(cycles):
-        projected = jnp.dot(w_t, normed_ref[:, lanes], preferred_element_type=jnp.float32)
-        sides = []
-        for side in range(2):
-            value = projected[2 * side * hidden : (2 * side + 1) * hidden]
-            gate = projected[(2 * side + 1) * hidden : (2 * side + 2) * hidden]
-            sides.append((sigmoid(gate) * value * keep[:, lanes]).reshape(peers, own, size))
-        both = jnp.concatenate(sides, axis=1).astype(jnp.bfloat16)
-        for group in range(groups):
-            line = (cycle * groups + group) * 2 * own
-            message_ref[:, line : line + 2 * own, :] = both[:, :, group * LANES : (group + 1) * LANES]
-        lines = slice(cycle * groups * 2 * own, (cycle + 1) * groups * 2 * own)
-        leaving += start_copies(
-            out_sems.at[cycle],
-            (message_ref.at[:, lines, :], message_hbm.at[:, lines, :]),
-            (normed_ref.at[:, lanes], normed_hbm.at[:, lanes]),
+    leaving = start_copies(out_sems.at[0], (normed_ref, normed_hbm))
+    for lanes in cycles:
+        normed = normed_ref[:, lanes]
+        value = jnp.dot(w_value, normed, preferred_element_type=jnp.float32)
+        gate = jnp.dot(w_gate, normed, preferred_element_type=jnp.float32)
+        sent = (sigmoid(gate) * value * keep[:, lanes]).reshape(members, ROWS, size)
+        for start in range(0, size, LANES):
+            line = (lanes.start + start) // LANES * ROWS
+            held[:, line : line + ROWS, :] = sent[:, :, start : start + LANES]
+    steps = out_sems.shape[0] - 1
+    some = members // steps
+    for step in range(steps):
+        lines = slice(step * some * held.shape[1], (step + 1) * some * held.shape[1])
+        message_ref[lines, :] = (
+            held[step * some : (step + 1) * some].reshape(-1, LANES).astype(jnp.bfloat16)
         )
+        leaving += start_copies(out_sems.at[step + 1], (message_ref.at[lines, :], message_hbm.at[lines, :]))
     for copy in leaving:
         copy.wait()
 
@@ -150,19 +165,16 @@
     done_ref[...] = jnp.zeros_like(done_ref)
 
 
-def unpack(message_ref, half, halves, spread_ref, own, cols):
+def unpack(message, half, halves, spread_ref, cols):
     tokens, groups = cycle_of(cols)
-    members, lines, _ = message_ref.shape
-    peers = members // halves
-    lane = lax.broadcasted_iota(jnp.int32, (2 * own, LANES), 1)
-    cycles = lines // (2 * groups * own)
-    for peer in range(peers):
+    members, lines, _ = message.shape
+    lane = lax.broadcasted_iota(jnp.int32, (ROWS, LANES), 1)
+    cycles = lines // (ROWS * groups)
+    for peer in range(members // halves):
         for cycle in range(cycles):
-            base = cycle * groups
+            base = cycle * groups * ROWS
             held = [
-                message_ref[
-                    peer * halves + half, (base + group) * 2 * own : (base + group + 1) * 2 * own, :
-                ].astype(jnp.float32)
+                message[peer * halves + half, base + group * ROWS : base + (group + 1) * ROWS, :]
                 for group in range(groups)
             ]
             for token in range(tokens):
@@ -174,12 +186,12 @@
                         value = jnp.where(lane >= off, value, held[group + 1])
                     if off:
                         value = pltpu.roll(value, LANES - off, axis=1)
-                    spread_ref[chunk, k * 2 * own : (k + 1) * 2 * own, :] = value
-
-
-def pack(spread_ref, at, own, cols):
+                    spread_ref[chunk, k * ROWS : (k + 1) * ROWS, :] = value
+
+
+def pack(spread_ref, at, cols):
     tokens, groups = cycle_of(cols)
-    lane = lax.broadcasted_iota(jnp.int32, (own, LANES), 1)
+    lane = lax.broadcasted_iota(jnp.int32, (ROWS, LANES), 1)
     rolled, lines = {}, []
     for group in range(groups):
         value, here = None, 0
@@ -188,8 +200,8 @@
             chunk, there = divmod(col, LANES)
             shift = (here - there) % LANES
             if (token, chunk, shift) not in rolled:
-                line = (at * tokens + token) * own
-                piece = spread_ref[chunk, line : line + own, :]
+                line = (at * tokens + token) * ROWS
+                piece = spread_ref[chunk, line : line + ROWS, :]
                 rolled[token, chunk, shift] = pltpu.roll(piece, shift, axis=1) if shift else piece
             piece = rolled[token, chunk, shift]
             value = piece if value is None else jnp.where(lane >= here, piece, value)
@@ -206,62 +218,67 @@
     ).astype(jnp.bfloat16)
 
 
-def triangle_kernel(own, cols, shares, message_ref, _, mixed_ref, spread, left, left_t, right, mixed):
+def triangle_kernel(cols, shares, message_ref, _, mixed_ref, message, spread, left, left_t, right, mixed):
     halves, chunks = spread.shape[:2]
     width = chunks * LANES
     deep = right.shape[1]
-    depth = spread.shape[2] // (2 * own)
+    depth = spread.shape[2] // ROWS
     one = identity(cols, width)
+    message[...] = message_ref[...].astype(jnp.float32).reshape(message.shape)
     if depth < deep:
-        right[:, depth:, :] = jnp.zeros((own, deep - depth, halves * width), jnp.bfloat16)
+        right[:, depth:, :] = jnp.zeros((OWN, deep - depth, halves * width), jnp.bfloat16)
     for half in range(halves):
-        unpack(message_ref, half, halves, spread.at[half], own, cols)
+        unpack(message, half, halves, spread.at[half], cols)
         if depth < deep:
-            left[:, half * deep + depth : (half + 1) * deep, :] = jnp.zeros((own, deep - depth, width), jnp.bfloat16)
-        for channel in range(own):
-            left[channel, half * deep : half * deep + depth, :] = channel_of(spread.at[half], channel, 2 * own)
+            left[:, half * deep + depth : (half + 1) * deep, :] = jnp.zeros((OWN, deep - depth, width), jnp.bfloat16)
+        for channel in range(OWN):
+            left[channel, half * deep : half * deep + depth, :] = channel_of(spread.at[half], channel, ROWS)
             right[channel, :depth, half * width : (half + 1) * width] = channel_of(
-                spread.at[half], own + channel, 2 * own
+                spread.at[half], OWN + channel, ROWS
             )
-    for channel in range(own):
+    for channel in range(OWN):
         both = lax.dot_general(
             one, left[channel], (((1,), (1,)), ((), ())), preferred_element_type=jnp.float32
         ).astype(jnp.bfloat16)
         for half in range(halves):
             left_t[channel, half * cols : (half + 1) * cols, :] = both[:, half * deep : (half + 1) * deep]
-    for channel in range(own):
+    for channel in range(OWN):
         total = jnp.dot(left_t[channel], right[channel], preferred_element_type=jnp.float32)
         for i_half in range(halves):
             for j_half in range(halves):
                 for chunk in range(chunks):
                     start = j_half * width + chunk * LANES
-                    mixed[i_half, j_half, chunk, pl.ds(channel, cols, stride=own), :] = total[
+                    mixed[i_half, chunk, pl.ds(j_half * OWN + channel, cols, stride=ROWS), :] = total[
                         i_half * cols : (i_half + 1) * cols, start : start + LANES
                     ]
-    groups = cycle_of(cols)[1]
     each = mixed_ref.shape[0] // shares
-    cycles = each // (halves * groups * own)
+    cycles = message.shape[1] // (ROWS * cycle_of(cols)[1])
     for share in range(shares):
         i_half, peer = divmod(share, shares // halves)
         lines = []
-        for j_half in range(halves):
-            for cycle in range(cycles):
-                lines += pack(mixed.at[i_half, j_half], peer * cycles + cycle, own, cols)
+        for cycle in range(cycles):
+            lines += pack(mixed.at[i_half], peer * cycles + cycle, cols)
+        lines += lines[-1:] * (len(lines) % 2)
+        turned = [turn_pairs(lines[at], lines[at + 1]) for at in range(0, len(lines), 2)]
+        lines = [pair[j_half] for j_half in range(halves) for pair in turned]
         mixed_ref[share * each : (share + 1) * each, :] = jnp.concatenate(lines, axis=0).astype(jnp.bfloat16)
 
 
-def output_kernel(own, parts, mixed_ref, gate_ref, gain_ref, w_t_ref, update_hbm, mixed, update, sems):
-    members, lines, _ = mixed.shape
-    members = members // parts
+def output_kernel(parts, mixed_ref, gate_ref, gain_ref, w_t_ref, update_hbm, mixed, update, sems):
+    members = mixed.shape[0] // parts
     mixed[...] = mixed_ref[...].astype(jnp.float32).reshape(mixed.shape)
-    groups = lines // own
+    groups = update.shape[0] // LANES
     steps = math.gcd(groups, 3)
     leaving = []
     for group in range(groups):
-        sums = mixed[:members, group * own : (group + 1) * own, :]
-        for part in range(1, parts):
-            sums += mixed[part * members : (part + 1) * members, group * own : (group + 1) * own, :]
-        block = sums.reshape(members * own, LANES)
+        if group % 2 == 0:
+            lines = slice(group // 2 * ROWS, (group // 2 + 1) * ROWS)
+            sums = mixed[:members, lines, :]
+            for part in range(1, parts):
+                sums += mixed[part * members : (part + 1) * members, lines, :]
+            sums = sums.reshape(members // 2, 2, ROWS, LANES)
+            blocks = turn_pairs(sums[:, 0], sums[:, 1])
+        block = blocks[group % 2].reshape(members * OWN, LANES)
         center = block - jnp.mean(block, axis=0, keepdims=True)
         spread = jnp.mean(center * center, axis=0, keepdims=True)
         normed = (center * lax.rsqrt(spread + EPS) * gain_ref[...]).astype(jnp.bfloat16)
@@ -279,19 +296,21 @@
 def on_device(shares, halves, pair, tile_mask, chain_ids, gain_in, w_proj, gain_mid, w_out):
     rows, cols, width = pair.shape
     hidden = w_out.shape[0]
-    peers = shares // PARTS
-    own = hidden // (peers * halves)
+    devices = shares * halves
+    members = hidden // OWN
+    parts = devices // members
     positions = rows * cols
     groups = positions // LANES
-    lines = groups * own
-    cycles = groups // cycle_of(cols)[1]
+    sent, back = groups * ROWS, pl.cdiv(groups, 2) * ROWS
     params = pltpu.CompilerParams(vmem_limit_bytes=VMEM_BYTES)
     whole_params = pltpu.CompilerParams(vmem_limit_bytes=WHOLE_VMEM_BYTES)
     tokens = chain_ids.shape[0]
-    message = jax.ShapeDtypeStruct((peers * halves, 2 * lines, LANES), jnp.bfloat16)
     message, normed = pl.pallas_call(
         functools.partial(project_kernel, rows, cols),
-        out_shape=(message, jax.ShapeDtypeStruct((width, positions), jnp.bfloat16)),
+        out_shape=(
+            jax.ShapeDtypeStruct((members * sent, LANES), jnp.bfloat16),
+            jax.ShapeDtypeStruct((width, positions), jnp.bfloat16),
+        ),
         in_specs=[HBM] * 5,
         out_specs=(HBM, HBM),
         scratch_shapes=[
@@ -300,25 +319,23 @@
             pltpu.VMEM((positions, width), jnp.bfloat16),
             pltpu.VMEM((1, width), jnp.float32),
             pltpu.VMEM(w_proj.shape, jnp.bfloat16),
-            pltpu.VMEM(message.shape, jnp.bfloat16),
+            pltpu.VMEM((members, sent, LANES), jnp.float32),
+            pltpu.VMEM((members * sent, LANES), jnp.bfloat16),
             pltpu.VMEM((width, positions), jnp.bfloat16),
             pltpu.SemaphoreType.DMA((5,)),
-            pltpu.SemaphoreType.DMA((cycles, 2)),
+            pltpu.SemaphoreType.DMA((5, 1)),
         ],
         compiler_params=whole_params,
         name="project",
     )(tile_mask, chain_ids[None, :], pair.reshape(positions, width), gain_in[None, :], w_proj)
     message = lax.all_to_all(
-        message,
+        message.reshape(members, sent, LANES),
         ("row", "col"),
         split_axis=0,
         concat_axis=0,
-        axis_index_groups=[
-            list(range(part * peers * halves, (part + 1) * peers * halves))
-            for part in range(PARTS)
-        ],
+        axis_index_groups=[list(range(part * members, (part + 1) * members)) for part in range(parts)],
         tiled=True,
-    )
+    ).reshape(members * sent, LANES)
     gate, w_out_t, gain, done = pl.pallas_call(
         gate_kernel,
         out_shape=(
@@ -343,37 +360,34 @@
     )(normed, w_proj, gain_mid[None, :], w_out)
     message, done = lax.optimization_barrier((message, done))
     chunks = pl.cdiv(cols, LANES)
-    depth = peers * rows
+    depth = members // halves * rows
     deep = pl.cdiv(depth, LANES) * LANES
     mixed = pl.pallas_call(
-        functools.partial(triangle_kernel, own, cols, shares),
-        out_shape=jax.ShapeDtypeStruct((halves * shares * lines, LANES), jnp.bfloat16),
+        functools.partial(triangle_kernel, cols, shares),
+        out_shape=jax.ShapeDtypeStruct((devices * back, LANES), jnp.bfloat16),
         in_specs=[VMEM, ANY],
         out_specs=VMEM,
         scratch_shapes=[
-            pltpu.VMEM((halves, chunks, depth * 2 * own, LANES), jnp.float32),
-            pltpu.VMEM((own, halves * deep, chunks * LANES), jnp.bfloat16),
-            pltpu.VMEM((own, halves * cols, deep), jnp.bfloat16),
-            pltpu.VMEM((own, deep, halves * chunks * LANES), jnp.bfloat16),
-            pltpu.VMEM((halves, halves, chunks, cols * own, LANES), jnp.float32),
+            pltpu.VMEM((members, sent, LANES), jnp.float32),
+            pltpu.VMEM((halves, chunks, depth * ROWS, LANES), jnp.float32),
+            pltpu.VMEM((OWN, halves * deep, chunks * LANES), jnp.bfloat16),
+            pltpu.VMEM((OWN, halves * cols, deep), jnp.bfloat16),
+            pltpu.VMEM((OWN, deep, halves * chunks * LANES), jnp.bfloat16),
+            pltpu.VMEM((halves, chunks, cols * ROWS, LANES), jnp.float32),
         ],
         compiler_params=params,
         name="triangle",
     )(message, done)
     mixed = lax.all_to_all(
-        mixed.reshape(halves * shares, lines, LANES),
-        ("row", "col"),
-        split_axis=0,
-        concat_axis=0,
-        tiled=True,
-    ).reshape(halves * shares * lines, LANES)
+        mixed.reshape(devices, back, LANES), ("row", "col"), split_axis=0, concat_axis=0, tiled=True
+    ).reshape(devices * back, LANES)
     update = pl.pallas_call(
-        functools.partial(output_kernel, own, PARTS),
+        functools.partial(output_kernel, parts),
         out_shape=jax.ShapeDtypeStruct((positions, width), jnp.bfloat16),
         in_specs=[VMEM] * 4,
         out_specs=HBM,
         scratch_shapes=[
-            pltpu.VMEM((shares * halves, lines, LANES), jnp.float32),
+            pltpu.VMEM((devices, back, LANES), jnp.float32),
             pltpu.VMEM((positions, width), jnp.bfloat16),
             pltpu.SemaphoreType.DMA((math.gcd(groups, 3), 1)),
         ],

time: 42.8 us -> 44.3 us (1.035)
  waiting for transfers between devices: 10.1 us -> 15.5 us
  blocking collectives: 19.6 us -> 15.1 us
  starting transfers between devices: 6.43 us -> 7.31 us
    all_to_all x1, waiting for transfers between devices: 10.1 us -> 15.5 us  [on_device(): lax.all_to_all(message.reshape(members, sent, LANES), ('row', 'col'), spl...]
    all_to_all x1, blocking collectives: 19.6 us -> 15.1 us  [on_device(): lax.all_to_all(mixed.reshape(devices, back, LANES), ('row', 'col'), split...]
    all_to_all x1, starting transfers between devices: 6.43 us -> 7.31 us  [on_device(): lax.all_to_all(message.reshape(members, sent, LANES), ('row', 'col'), spl...]
where the time goes in v12:
time: 44.3 us; the launch traced here: 44.1 us
  waiting for transfers between devices  15.5 us (35%)
  blocking collectives  15.1 us (34%)
  starting transfers between devices  7.31 us (17%)
  Pallas kernels  5.42 us (12%)
  local copies, waits for them, and re-layouts  0.64 us (1%)
    all_to_all x1, waiting for transfers between devices, on_device(): lax.all_to_all(message.reshape(members, sent, LANES), ('row', 'col'), spl...  15.5 us
    all_to_all x1, blocking collectives, on_device(): lax.all_to_all(mixed.reshape(devices, back, LANES), ('row', 'col'), split...  15.1 us
    all_to_all x1, starting transfers between devices, on_device(): lax.all_to_all(message.reshape(members, sent, LANES), ('row', 'col'), spl...  7.31 us
    pallas_call x1, Pallas kernels, on_device(): pl.pallas_call(functools.partial(project_kernel, rows, cols), out_shape=(...  2.81 us
    pallas_call x1, Pallas kernels, on_device(): pl.pallas_call(functools.partial(output_kernel, parts), out_shape=jax.Sha...  1.19 us
    pallas_call x1, Pallas kernels, on_device(): pl.pallas_call(functools.partial(triangle_kernel, cols, shares), out_shap...  0.9 us
  transfers between devices with their start and end apart: 1, of which 1 were waited for; matrix products, arithmetic and copies ran while one was open for 0% of the time, Pallas kernels for 1%

profile of v12, /device:TPU:0, one launch (start us, length us, event | category | flops | bytes accessed | tf_op | source)
XLA Modules:
  0.0 44.1 jit_solution(16123777697995468911)
XLA Ops:
  0.0 2.8 %project.1 = (bf16[2304,128]{1,0:T(8,128)(2,1)}, bf16[128,1152]{1,0:T(8,128)(2,1)}) custom-call(s32[2,2]{1,0:T(2,128)} %tile_hbm.1, s32[1,192]{1,0:T(1,128)} %bitcast.15, bf16[1152,128]{1,0:T(8,128)(2,1)} %bitcast.14, f32[1,128]{1,0:T(1,128)} %bitcast.16, bf16[128,640]{1,0:T(8,128)(2,1)} %w_hbm.3), custom_call_target="tpu_custom_call" | custom-call | tf_op jit(solution)/shard_map/project/pallas_call | solution.py:308
  2.8 0.0 copy-start
  2.8 0.0 copy-start.1
  2.8 0.0 copy-start.2
  2.9 7.3 %all-to-all-start = ((bf16[32,72,128]{2,1,0:T(8,128)(2,1)}), bf16[32,72,128]{2,1,0:T(8,128)(2,1)S(1)}, u32[]{:S(2)}, u32[]{:S(2)}) async-start(bf16[32,72,128]{2,1,0:T(8,128)(2,1)} %bitcast.13), calls=%async_computation | async-start | bytes 1179648 | tf_op jit(solution)/shard_map/all_to_all | solution.py:331
  10.2 0.0 copy-start.3
  10.2 0.0 copy-done
  10.2 0.0 copy-done.1
  10.2 0.0 copy-done.2
  10.2 0.6 %copy-done.3 = f32[128]{0:T(128)S(1)} copy-done((f32[128]{0:T(128)S(1)}, f32[128]{0:T(128)}, u32[]{:S(2)}) %copy-start.3) | copy-done | bytes 536
  10.8 0.5 %gate.1 = (f32[128,1152]{1,0:T(8,128)S(1)}, bf16[128,128]{1,0:T(8,128)(2,1)S(1)}, f32[128,128]{1,0:T(8,128)S(1)}, f32[8,128]{1,0:T(8,128)S(1)}) custom-call(bf16[128,1152]{1,0:T(8,128)(2,1)S(1)} %copy-done.1, bf16[128,640]{1,0:T(8,128)(2,1)S(1)} %copy-done, f32[1,128]{1,0:T(1,128)S(1)} %bitcast.12, bf16[128,128]{1,0:T(8,128)(2,1)S(1)} %copy-done.2), custom_call_target="tpu_custom_call" | custom-call | flops 37748736 | bytes 589824 | tf_op jit(solution)/shard_map/gate/pallas_call | solution.py:339
  11.4 15.5 %all-to-all-done = bf16[32,72,128]{2,1,0:T(8,128)(2,1)S(1)} async-done(((bf16[32,72,128]{2,1,0:T(8,128)(2,1)}), bf16[32,72,128]{2,1,0:T(8,128)(2,1)S(1)}, u32[]{:S(2)}, u32[]{:S(2)}) %all-to-all-start) | async-done | bytes 589856 | tf_op jit(solution)/shard_map/all_to_all | solution.py:331
  26.9 0.9 %triangle.1 = bf16[1280,128]{1,0:T(8,128)(2,1)S(1)} custom-call(bf16[2304,128]{1,0:T(8,128)(2,1)S(1)} %bitcast.9, f32[8,128]{1,0:T(8,128)S(1)} %get-tuple-element.17._), custom_call_target="tpu_custom_call" | custom-call | tf_op jit(solution)/shard_map/triangle/pallas_call | solution.py:365
  27.8 15.1 %all_to_all.10 = bf16[32,40,128]{2,1,0:T(8,128)(2,1)S(1)} all-to-all(bf16[32,40,128]{2,1,0:T(8,128)(2,1)S(1)} %bitcast.11), channel_id=1, replica_groups=mesh['grp'=1,'row'=16,'col'=2] {'row','col'}, dimensions={0} | all-to-all | bytes 655360 | tf_op jit(solution)/shard_map/all_to_all | solution.py:381
  42.9 1.2 %output.1 = bf16[1152,128]{1,0:T(8,128)(2,1)} custom-call(bf16[1280,128]{1,0:T(8,128)(2,1)S(1)} %bitcast.10, f32[128,1152]{1,0:T(8,128)S(1)} %get-tuple-element.18.gate_ref, f32[128,128]{1,0:T(8,128)S(1)} %get-tuple-element.19.gain_ref, bf16[128,128]{1,0:T(8,128)(2,1)S(1)} %get-tuple-element.20.w_t_ref), custom_call_target="tpu_custom_call" | custom-call | tf_op jit(solution)/shard_map/output/pallas_call | solution.py:384
Async XLA Ops:
  2.8 7.4 %copy-start = (bf16[128,640]{1,0:T(8,128)(2,1)S(1)}, bf16[128,640]{1,0:T(8,128)(2,1)}, u32[]{:S(2)}) copy-start(bf16[128,640]{1,0:T(8,128)(2,1)} %w_hbm.3) | copy-start | bytes 491524
  2.8 7.4 %copy-start.1 = (bf16[128,1152]{1,0:T(8,128)(2,1)S(1)}, bf16[128,1152]{1,0:T(8,128)(2,1)}, u32[]{:S(2)}) copy-start(bf16[128,1152]{1,0:T(8,128)(2,1)} %get-tuple-element.14.normed_ref) | copy-start | bytes 884740
  2.8 7.4 %copy-start.2 = (bf16[128,128]{1,0:T(8,128)(2,1)S(1)}, bf16[128,128]{1,0:T(8,128)(2,1)}, u32[]{:S(2)}) copy-start(bf16[128,128]{1,0:T(8,128)(2,1)} %w_out_hbm.1) | copy-start | bytes 98308
  2.9 24.0 %all-to-all-start = ((bf16[32,72,128]{2,1,0:T(8,128)(2,1)}), bf16[32,72,128]{2,1,0:T(8,128)(2,1)S(1)}, u32[]{:S(2)}, u32[]{:S(2)}) async-start(bf16[32,72,128]{2,1,0:T(8,128)(2,1)} %bitcast.13), calls=%async_computation | async-start | bytes 1179648 | tf_op jit(solution)/shard_map/all_to_all | solution.py:331
  10.2 0.7 %copy-start.3 = (f32[128]{0:T(128)S(1)}, f32[128]{0:T(128)}, u32[]{:S(2)}) copy-start(f32[128]{0:T(128)} %param.12) | copy-start | bytes 1540

commit v13 on v11

--- a/solution.py
+++ b/solution.py
@@ -21,13 +21,13 @@
 
 
 def forward_order(peers, halves):
-    bits = (peers - 1).bit_length()
-    turned = sorted(range(peers), key=lambda at: sum((at >> bit & 1) << (bits - 1 - bit) for bit in range(bits)))
-    return [(at, half) for half in range(halves) for at in turned]
+    return [(at, half) for at in reversed(range(peers)) for half in reversed(range(halves))]
 
 
 def return_order(peers, halves, parts):
-    return [(part, at, half) for at in range(peers) for half in range(halves) for part in range(parts)]
+    order = [(part, at, half) for part in range(parts) for at in range(peers) for half in range(halves)]
+    start = peers * halves // 2
+    return order[start:] + order[:start]
 
 
 def column(row):

time: 43.8 us -> 43.7 us (level)
  the two profiles are of different devices: /device:TPU:1 before, /device:TPU:0 now
where the time goes in v13:
time: 43.7 us; the launch traced here: 43.5 us
  blocking collectives  22.1 us (51%)
  starting transfers between devices  7.98 us (18%)
  waiting for transfers between devices  6.87 us (16%)
  Pallas kernels  5.75 us (13%)
  local copies, waits for them, and re-layouts  0.64 us (1%)
    all_to_all x1, blocking collectives, on_device(): lax.all_to_all(mixed.reshape(halves * shares, lines, LANES), ('row', 'col...  22.1 us
    all_to_all x1, starting transfers between devices, on_device(): lax.all_to_all(message, ('row', 'col'), split_axis=0, concat_axis=0, axis...  7.98 us
    all_to_all x1, waiting for transfers between devices, on_device(): lax.all_to_all(message, ('row', 'col'), split_axis=0, concat_axis=0, axis...  6.87 us
    pallas_call x1, Pallas kernels, on_device(): pl.pallas_call(functools.partial(project_kernel, rows, cols), out_shape=(...  2.81 us
    pallas_call x1, Pallas kernels, on_device(): pl.pallas_call(functools.partial(triangle_kernel, own, cols, shares, PART...  1.27 us
    pallas_call x1, Pallas kernels, on_device(): pl.pallas_call(functools.partial(output_kernel, own, halves, PARTS), out_...  1.14 us
  transfers between devices with their start and end apart: 1, of which 1 were waited for; matrix products, arithmetic and copies ran while one was open for 0% of the time, Pallas kernels for 1%

profile of v13, /device:TPU:0, one launch (start us, length us, event | category | flops | bytes accessed | tf_op | source)
XLA Modules:
  0.0 43.5 jit_solution(5879878416349156066)
XLA Ops:
  0.0 2.8 %project.1 = (bf16[16,144,128]{2,1,0:T(8,128)(2,1)}, bf16[128,1152]{1,0:T(8,128)(2,1)}) custom-call(s32[2,2]{1,0:T(2,128)} %tile_hbm.1, s32[1,192]{1,0:T(1,128)} %bitcast.11, bf16[1152,128]{1,0:T(8,128)(2,1)} %bitcast.10, f32[1,128]{1,0:T(1,128)} %bitcast.12, bf16[128,640]{1,0:T(8,128)(2,1)} %w_hbm.3), custom_call_target="tpu_custom_call" | custom-call | tf_op jit(solution)/shard_map/project/pallas_call | solution.py:311
  2.8 0.0 copy-start
  2.8 0.0 copy-start.1
  2.8 0.0 copy-start.2
  2.9 8.0 %all-to-all-start = ((bf16[16,144,128]{2,1,0:T(8,128)(2,1)}), bf16[16,144,128]{2,1,0:T(8,128)(2,1)S(1)}, u32[]{:S(2)}, u32[]{:S(2)}) async-start(bf16[16,144,128]{2,1,0:T(8,128)(2,1)} %get-tuple-element.13), calls=%async_computation | async-start | bytes 1179648 | tf_op jit(solution)/shard_map/all_to_all | solution.py:330
  10.8 0.0 copy-start.3
  10.8 0.0 copy-done
  10.9 0.0 copy-done.1
  10.9 0.0 copy-done.2
  10.9 0.6 %copy-done.3 = f32[128]{0:T(128)S(1)} copy-done((f32[128]{0:T(128)S(1)}, f32[128]{0:T(128)}, u32[]{:S(2)}) %copy-start.3) | copy-done | bytes 536
  11.5 0.5 %gate.1 = (f32[128,1152]{1,0:T(8,128)S(1)}, bf16[128,128]{1,0:T(8,128)(2,1)S(1)}, f32[128,128]{1,0:T(8,128)S(1)}, f32[8,128]{1,0:T(8,128)S(1)}) custom-call(bf16[128,1152]{1,0:T(8,128)(2,1)S(1)} %copy-done.1, bf16[128,640]{1,0:T(8,128)(2,1)S(1)} %copy-done, f32[1,128]{1,0:T(1,128)S(1)} %bitcast.9, bf16[128,128]{1,0:T(8,128)(2,1)S(1)} %copy-done.2), custom_call_target="tpu_custom_call" | custom-call | flops 37748736 | bytes 589824 | tf_op jit(solution)/shard_map/gate/pallas_call | solution.py:341
  12.0 6.9 %all-to-all-done.message_ref = bf16[16,144,128]{2,1,0:T(8,128)(2,1)S(1)} async-done(((bf16[16,144,128]{2,1,0:T(8,128)(2,1)}), bf16[16,144,128]{2,1,0:T(8,128)(2,1)S(1)}, u32[]{:S(2)}, u32[]{:S(2)}) %all-to-all-start) | async-done | bytes 589856 | tf_op jit(solution)/shard_map/all_to_all | solution.py:330
  18.9 1.3 %triangle.1 = bf16[2304,128]{1,0:T(8,128)(2,1)S(1)} custom-call(bf16[16,144,128]{2,1,0:T(8,128)(2,1)S(1)} %all-to-all-done.message_ref, f32[8,128]{1,0:T(8,128)S(1)} %get-tuple-element.17._), custom_call_target="tpu_custom_call" | custom-call | tf_op jit(solution)/shard_map/triangle/pallas_call | solution.py:367
  20.2 22.1 %all_to_all.10 = bf16[32,72,128]{2,1,0:T(8,128)(2,1)S(1)} all-to-all(bf16[32,72,128]{2,1,0:T(8,128)(2,1)S(1)} %bitcast.8), channel_id=1, replica_groups={{8,9,10,11,12,13,14,15,16,17,18,19,20,21,22,23,24,25,26,27,28,29,30,31,..., dimensions={0} | all-to-all | bytes 1179648 | tf_op jit(solution)/shard_map/all_to_all | solution.py:382
  42.3 1.1 %output.1 = bf16[1152,128]{1,0:T(8,128)(2,1)} custom-call(bf16[2304,128]{1,0:T(8,128)(2,1)S(1)} %bitcast.7, f32[128,1152]{1,0:T(8,128)S(1)} %get-tuple-element.18.gate_ref, f32[128,128]{1,0:T(8,128)S(1)} %get-tuple-element.19.gain_ref, bf16[128,128]{1,0:T(8,128)(2,1)S(1)} %get-tuple-element.20.w_t_ref), custom_call_target="tpu_custom_call" | custom-call | tf_op jit(solution)/shard_map/output/pallas_call | solution.py:392
Async XLA Ops:
  2.8 8.0 %copy-start = (bf16[128,640]{1,0:T(8,128)(2,1)S(1)}, bf16[128,640]{1,0:T(8,128)(2,1)}, u32[]{:S(2)}) copy-start(bf16[128,640]{1,0:T(8,128)(2,1)} %w_hbm.3) | copy-start | bytes 491524
  2.8 8.0 %copy-start.1 = (bf16[128,1152]{1,0:T(8,128)(2,1)S(1)}, bf16[128,1152]{1,0:T(8,128)(2,1)}, u32[]{:S(2)}) copy-start(bf16[128,1152]{1,0:T(8,128)(2,1)} %get-tuple-element.14.normed_ref) | copy-start | bytes 884740
  2.8 8.0 %copy-start.2 = (bf16[128,128]{1,0:T(8,128)(2,1)S(1)}, bf16[128,128]{1,0:T(8,128)(2,1)}, u32[]{:S(2)}) copy-start(bf16[128,128]{1,0:T(8,128)(2,1)} %w_out_hbm.1) | copy-start | bytes 98308
  2.9 16.0 %all-to-all-start = ((bf16[16,144,128]{2,1,0:T(8,128)(2,1)}), bf16[16,144,128]{2,1,0:T(8,128)(2,1)S(1)}, u32[]{:S(2)}, u32[]{:S(2)}) async-start(bf16[16,144,128]{2,1,0:T(8,128)(2,1)} %get-tuple-element.13), calls=%async_computation | async-start | bytes 1179648 | tf_op jit(solution)/shard_map/all_to_all | solution.py:330
  10.8 0.7 %copy-start.3 = (f32[128]{0:T(128)S(1)}, f32[128]{0:T(128)}, u32[]{:S(2)}) copy-start(f32[128]{0:T(128)} %param.12) | copy-start | bytes 1540

commit v14 on v10

--- a/solution.py
+++ b/solution.py
@@ -6,6 +6,7 @@
 from jax import lax
 from jax.experimental import pallas as pl
 from jax.experimental.pallas import tpu as pltpu
+from jax.sharding import Mesh
 from jax.sharding import PartitionSpec as P
 
 TILE = 96
@@ -55,7 +56,7 @@
     positions = rows * cols
     at = lax.broadcasted_iota(jnp.int32, (1, positions), 1)
     row = steps(at, cols, rows)
-    k = lax.axis_index("row") * rows + row
+    k = (lax.axis_index("part") * lax.axis_size("row") + lax.axis_index("row")) * rows + row
     i = lax.axis_index("col") * cols + at - row * cols
     token = lax.broadcasted_iota(jnp.int32, (tokens, positions), 0)
     pick = (token == k).astype(jnp.float32) - (token == i).astype(jnp.float32)
@@ -99,18 +100,19 @@
     size = groups * LANES
     copies = start_copies(
         sems,
-        (w_hbm, w_ref),
-        (gain_hbm, gain_ref),
         (chain_hbm, chain_ref),
         (tile_hbm, tile_ref),
+        (gain_hbm, gain_ref),
         (pair_hbm, pair_ref),
-    )
-    for copy in copies[:4]:
+        (w_hbm, w_ref),
+    )
+    for copy in copies[:3]:
         copy.wait()
     keep = keep_of(tile_ref, chain_ref, rows, cols)
-    w_t = w_ref[:, : 4 * hidden].T
     gain = column(gain_ref[...])
     copies[4].wait()
+    w_t = w_ref[:, : 4 * hidden].T
+    copies[3].wait()
     cycles = [slice(start, start + size) for start in range(0, rows * cols, size)]
     for lanes in cycles:
         block = transpose(pair_ref[lanes, :])
@@ -309,15 +311,7 @@
         name="project",
     )(tile_mask, chain_ids[None, :], pair.reshape(positions, width), gain_in[None, :], w_proj)
     message = lax.all_to_all(
-        message,
-        ("row", "col"),
-        split_axis=0,
-        concat_axis=0,
-        axis_index_groups=[
-            list(range(part * peers * halves, (part + 1) * peers * halves))
-            for part in range(PARTS)
-        ],
-        tiled=True,
+        message, ("row", "col"), split_axis=0, concat_axis=0, tiled=True
     )
     gate, w_out_t, gain, done = pl.pallas_call(
         gate_kernel,
@@ -362,7 +356,7 @@
     )(message, done)
     mixed = lax.all_to_all(
         mixed.reshape(halves * shares, lines, LANES),
-        ("row", "col"),
+        ("part", "row", "col"),
         split_axis=0,
         concat_axis=0,
         tiled=True,
@@ -384,12 +378,14 @@
 
 
 def solution(mesh):
-    in_specs = (P(("grp", "row"), "col", None), P("grp", None), P("grp"), P(), P(), P(), P())
-    out_specs = P(("grp", "row"), "col", None)
+    grp, shares, halves = (mesh.shape[axis] for axis in ("grp", "row", "col"))
+    mesh = Mesh(mesh.devices.reshape(grp, PARTS, shares // PARTS, halves), ("grp", "part", "row", "col"))
+    pairs = P(("grp", "part", "row"), "col", None)
+    in_specs = (pairs, P("grp", None), P("grp"), P(), P(), P(), P())
     return jax.shard_map(
-        functools.partial(on_device, mesh.shape["row"], mesh.shape["col"]),
+        functools.partial(on_device, shares, halves),
         mesh=mesh,
         in_specs=in_specs,
-        out_specs=out_specs,
+        out_specs=pairs,
         check_vma=False,
     )

time: 42.8 us -> 42.8 us (level)
  no operation moved by 1% of the time
where the time goes in v14:
time: 42.8 us; the launch traced here: 42.5 us
  blocking collectives  19.6 us (46%)
  waiting for transfers between devices  10.1 us (24%)
  starting transfers between devices  6.43 us (15%)
  Pallas kernels  5.74 us (13%)
  local copies, waits for them, and re-layouts  0.64 us (1%)
    all_to_all x1, blocking collectives, on_device(): lax.all_to_all(mixed.reshape(halves * shares, lines, LANES), ('part', 'ro...  19.6 us
    all_to_all x1, waiting for transfers between devices, on_device(): lax.all_to_all(message, ('row', 'col'), split_axis=0, concat_axis=0, tile...  10.1 us
    all_to_all x1, starting transfers between devices, on_device(): lax.all_to_all(message, ('row', 'col'), split_axis=0, concat_axis=0, tile...  6.43 us
    pallas_call x1, Pallas kernels, on_device(): pl.pallas_call(functools.partial(project_kernel, rows, cols), out_shape=(...  2.79 us
    pallas_call x1, Pallas kernels, on_device(): pl.pallas_call(functools.partial(triangle_kernel, own, cols, shares), out...  1.27 us
    pallas_call x1, Pallas kernels, on_device(): pl.pallas_call(functools.partial(output_kernel, own, PARTS), out_shape=ja...  1.14 us
  transfers between devices with their start and end apart: 1, of which 1 were waited for; matrix products, arithmetic and copies ran while one was open for 0% of the time, Pallas kernels for 1%

profile of v14, /device:TPU:0, one launch (start us, length us, event | category | flops | bytes accessed | tf_op | source)
XLA Modules:
  0.0 42.5 jit_solution(17810144190096292408)
XLA Ops:
  0.0 2.8 %project.1 = (bf16[16,144,128]{2,1,0:T(8,128)(2,1)}, bf16[128,1152]{1,0:T(8,128)(2,1)}) custom-call(s32[2,2]{1,0:T(2,128)} %tile_hbm.1, s32[1,192]{1,0:T(1,128)} %bitcast.11, bf16[1152,128]{1,0:T(8,128)(2,1)} %bitcast.10, f32[1,128]{1,0:T(1,128)} %bitcast.12, bf16[128,640]{1,0:T(8,128)(2,1)} %w_hbm.3), custom_call_target="tpu_custom_call" | custom-call | tf_op jit(solution)/shard_map/project/pallas_call | solution.py:294
  2.8 0.0 copy-start
  2.8 0.0 copy-start.1
  2.8 0.0 copy-start.2
  2.8 6.4 %all-to-all-start = ((bf16[16,144,128]{2,1,0:T(8,128)(2,1)}), bf16[16,144,128]{2,1,0:T(8,128)(2,1)S(1)}, u32[]{:S(2)}, u32[]{:S(2)}) async-start(bf16[16,144,128]{2,1,0:T(8,128)(2,1)} %get-tuple-element.13), calls=%async_computation | async-start | bytes 1179648 | tf_op jit(solution)/shard_map/all_to_all | solution.py:313
  9.3 0.0 copy-start.3
  9.3 0.0 copy-done
  9.3 0.0 copy-done.1
  9.3 0.0 copy-done.2
  9.3 0.6 %copy-done.3 = f32[128]{0:T(128)S(1)} copy-done((f32[128]{0:T(128)S(1)}, f32[128]{0:T(128)}, u32[]{:S(2)}) %copy-start.3) | copy-done | bytes 536
  9.9 0.5 %gate.1 = (f32[128,1152]{1,0:T(8,128)S(1)}, bf16[128,128]{1,0:T(8,128)(2,1)S(1)}, f32[128,128]{1,0:T(8,128)S(1)}, f32[8,128]{1,0:T(8,128)S(1)}) custom-call(bf16[128,1152]{1,0:T(8,128)(2,1)S(1)} %copy-done.1, bf16[128,640]{1,0:T(8,128)(2,1)S(1)} %copy-done, f32[1,128]{1,0:T(1,128)S(1)} %bitcast.9, bf16[128,128]{1,0:T(8,128)(2,1)S(1)} %copy-done.2), custom_call_target="tpu_custom_call" | custom-call | flops 37748736 | bytes 589824 | tf_op jit(solution)/shard_map/gate/pallas_call | solution.py:316
  10.5 10.1 %all-to-all-done.message_ref = bf16[16,144,128]{2,1,0:T(8,128)(2,1)S(1)} async-done(((bf16[16,144,128]{2,1,0:T(8,128)(2,1)}), bf16[16,144,128]{2,1,0:T(8,128)(2,1)S(1)}, u32[]{:S(2)}, u32[]{:S(2)}) %all-to-all-start) | async-done | bytes 589856 | tf_op jit(solution)/shard_map/all_to_all | solution.py:313
  20.5 1.3 %triangle.1 = bf16[2304,128]{1,0:T(8,128)(2,1)S(1)} custom-call(bf16[16,144,128]{2,1,0:T(8,128)(2,1)S(1)} %all-to-all-done.message_ref, f32[8,128]{1,0:T(8,128)S(1)} %get-tuple-element.17._), custom_call_target="tpu_custom_call" | custom-call | tf_op jit(solution)/shard_map/triangle/pallas_call | solution.py:342
  21.8 19.6 %all_to_all.10 = bf16[32,72,128]{2,1,0:T(8,128)(2,1)S(1)} all-to-all(bf16[32,72,128]{2,1,0:T(8,128)(2,1)S(1)} %bitcast.8), channel_id=1, replica_groups=mesh['grp'=1,'part'=2,'row'=8,'col'=2] {'part','row','col'}, dimensions={0} | all-to-all | bytes 1179648 | tf_op jit(solution)/shard_map/all_to_all | solution.py:357
  41.4 1.1 %output.1 = bf16[1152,128]{1,0:T(8,128)(2,1)} custom-call(bf16[2304,128]{1,0:T(8,128)(2,1)S(1)} %bitcast.7, f32[128,1152]{1,0:T(8,128)S(1)} %get-tuple-element.18.gate_ref, f32[128,128]{1,0:T(8,128)S(1)} %get-tuple-element.19.gain_ref, bf16[128,128]{1,0:T(8,128)(2,1)S(1)} %get-tuple-element.20.w_t_ref), custom_call_target="tpu_custom_call" | custom-call | tf_op jit(solution)/shard_map/output/pallas_call | solution.py:364
Async XLA Ops:
  2.8 6.5 %copy-start = (bf16[128,640]{1,0:T(8,128)(2,1)S(1)}, bf16[128,640]{1,0:T(8,128)(2,1)}, u32[]{:S(2)}) copy-start(bf16[128,640]{1,0:T(8,128)(2,1)} %w_hbm.3) | copy-start | bytes 491524
  2.8 6.5 %copy-start.1 = (bf16[128,1152]{1,0:T(8,128)(2,1)S(1)}, bf16[128,1152]{1,0:T(8,128)(2,1)}, u32[]{:S(2)}) copy-start(bf16[128,1152]{1,0:T(8,128)(2,1)} %get-tuple-element.14.normed_ref) | copy-start | bytes 884740
  2.8 6.5 %copy-start.2 = (bf16[128,128]{1,0:T(8,128)(2,1)S(1)}, bf16[128,128]{1,0:T(8,128)(2,1)}, u32[]{:S(2)}) copy-start(bf16[128,128]{1,0:T(8,128)(2,1)} %w_out_hbm.1) | copy-start | bytes 98308
  2.8 17.7 %all-to-all-start = ((bf16[16,144,128]{2,1,0:T(8,128)(2,1)}), bf16[16,144,128]{2,1,0:T(8,128)(2,1)S(1)}, u32[]{:S(2)}, u32[]{:S(2)}) async-start(bf16[16,144,128]{2,1,0:T(8,128)(2,1)} %get-tuple-element.13), calls=%async_computation | async-start | bytes 1179648 | tf_op jit(solution)/shard_map/all_to_all | solution.py:313
  9.3 0.7 %copy-start.3 = (f32[128]{0:T(128)S(1)}, f32[128]{0:T(128)}, u32[]{:S(2)}) copy-start(f32[128]{0:T(128)} %param.12) | copy-start | bytes 1540

commit v15 on v10

--- a/solution.py
+++ b/solution.py
@@ -13,9 +13,7 @@
 EPS = 1e-05
 PARTS = 2
 VMEM_BYTES = 32 * 1024 * 1024
-WHOLE_VMEM_BYTES = 64 * 1024 * 1024
 VMEM = pl.BlockSpec(memory_space=pltpu.VMEM)
-ANY = pl.BlockSpec(memory_space=pl.ANY)
 HBM = pl.BlockSpec(memory_space=pltpu.HBM)
 SMEM = pl.BlockSpec(memory_space=pltpu.SMEM)
 
@@ -89,8 +87,9 @@
 
 
 def project_kernel(
-    rows, cols, tile_hbm, chain_hbm, pair_hbm, gain_hbm, w_hbm, message_hbm, normed_hbm,
-    tile_ref, chain_ref, pair_ref, gain_ref, w_ref, message_ref, normed_ref, sems, out_sems,
+    rows, cols, tile_hbm, chain_hbm, pair_hbm, gain_hbm, w_hbm, gain_mid_hbm, w_out_hbm,
+    message_ref, gate_ref, w_out_ref, gain_mid_ref,
+    tile_ref, chain_ref, pair_ref, gain_ref, w_ref, gain_mid, w_out, normed_ref, sems,
 ):
     hidden = (w_ref.shape[1] - w_ref.shape[0]) // 4
     peers = message_ref.shape[0]
@@ -99,25 +98,27 @@
     size = groups * LANES
     copies = start_copies(
         sems,
-        (w_hbm, w_ref),
-        (gain_hbm, gain_ref),
         (chain_hbm, chain_ref),
         (tile_hbm, tile_ref),
+        (gain_hbm, gain_ref),
         (pair_hbm, pair_ref),
-    )
-    for copy in copies[:4]:
+        (w_hbm, w_ref),
+        (gain_mid_hbm, gain_mid),
+        (w_out_hbm, w_out),
+    )
+    for copy in copies[:3]:
         copy.wait()
     keep = keep_of(tile_ref, chain_ref, rows, cols)
-    w_t = w_ref[:, : 4 * hidden].T
     gain = column(gain_ref[...])
     copies[4].wait()
+    w_t = w_ref[...].T
+    copies[3].wait()
     cycles = [slice(start, start + size) for start in range(0, rows * cols, size)]
     for lanes in cycles:
         block = transpose(pair_ref[lanes, :])
         center = block - jnp.mean(block, axis=0, keepdims=True)
         spread = jnp.mean(center * center, axis=0, keepdims=True)
         normed_ref[:, lanes] = (center * lax.rsqrt(spread + EPS) * gain).astype(jnp.bfloat16)
-    leaving = []
     for cycle, lanes in enumerate(cycles):
         projected = jnp.dot(w_t, normed_ref[:, lanes], preferred_element_type=jnp.float32)
         sides = []
@@ -129,25 +130,11 @@
         for group in range(groups):
             line = (cycle * groups + group) * 2 * own
             message_ref[:, line : line + 2 * own, :] = both[:, :, group * LANES : (group + 1) * LANES]
-        lines = slice(cycle * groups * 2 * own, (cycle + 1) * groups * 2 * own)
-        leaving += start_copies(
-            out_sems.at[cycle],
-            (message_ref.at[:, lines, :], message_hbm.at[:, lines, :]),
-            (normed_ref.at[:, lanes], normed_hbm.at[:, lanes]),
-        )
-    for copy in leaving:
+        gate_ref[:, lanes] = sigmoid(projected[4 * hidden :])
+    for copy in copies[5:]:
         copy.wait()
-
-
-def gate_kernel(normed_ref, w_hbm, gain_hbm, w_out_hbm, gate_ref, w_out_ref, gain_ref, done_ref, w, w_out, gain, sems):
-    fetch(sems, (w_hbm, w), (w_out_hbm, w_out), (gain_hbm, gain))
-    last = w_hbm.shape[1] - w_hbm.shape[0]
-    gate_ref[...] = sigmoid(
-        jnp.dot(w[:, last:].T, normed_ref[...], preferred_element_type=jnp.float32)
-    )
     w_out_ref[...] = w_out[...].T
-    gain_ref[...] = jnp.broadcast_to(column(gain[...]), gain_ref.shape)
-    done_ref[...] = jnp.zeros_like(done_ref)
+    gain_mid_ref[...] = jnp.broadcast_to(column(gain_mid[...]), gain_mid_ref.shape)
 
 
 def unpack(message_ref, half, halves, spread_ref, own, cols):
@@ -206,7 +193,7 @@
     ).astype(jnp.bfloat16)
 
 
-def triangle_kernel(own, cols, shares, message_ref, _, mixed_ref, spread, left, left_t, right, mixed):
+def triangle_kernel(own, cols, shares, message_ref, mixed_ref, spread, left, left_t, right, mixed):
     halves, chunks = spread.shape[:2]
     width = chunks * LANES
     deep = right.shape[1]
@@ -286,28 +273,45 @@
     lines = groups * own
     cycles = groups // cycle_of(cols)[1]
     params = pltpu.CompilerParams(vmem_limit_bytes=VMEM_BYTES)
-    whole_params = pltpu.CompilerParams(vmem_limit_bytes=WHOLE_VMEM_BYTES)
     tokens = chain_ids.shape[0]
     message = jax.ShapeDtypeStruct((peers * halves, 2 * lines, LANES), jnp.bfloat16)
-    message, normed = pl.pallas_call(
+    message, gate, w_out_t, gain = pl.pallas_call(
         functools.partial(project_kernel, rows, cols),
-        out_shape=(message, jax.ShapeDtypeStruct((width, positions), jnp.bfloat16)),
-        in_specs=[HBM] * 5,
-        out_specs=(HBM, HBM),
+        out_shape=(
+            message,
+            jax.ShapeDtypeStruct((width, positions), jnp.float32),
+            jax.ShapeDtypeStruct(w_out.shape[::-1], jnp.bfloat16),
+            jax.ShapeDtypeStruct((hidden, LANES), jnp.float32),
+        ),
+        in_specs=[HBM] * 7,
+        out_specs=[VMEM] * 4,
         scratch_shapes=[
             pltpu.SMEM(tile_mask.shape, jnp.int32),
             pltpu.VMEM((1, tokens), jnp.int32),
             pltpu.VMEM((positions, width), jnp.bfloat16),
             pltpu.VMEM((1, width), jnp.float32),
             pltpu.VMEM(w_proj.shape, jnp.bfloat16),
-            pltpu.VMEM(message.shape, jnp.bfloat16),
+            pltpu.VMEM((1, hidden), jnp.float32),
+            pltpu.VMEM(w_out.shape, jnp.bfloat16),
             pltpu.VMEM((width, positions), jnp.bfloat16),
-            pltpu.SemaphoreType.DMA((5,)),
-            pltpu.SemaphoreType.DMA((cycles, 2)),
+            pltpu.SemaphoreType.DMA((7,)),
         ],
-        compiler_params=whole_params,
+        compiler_params=params,
         name="project",
-    )(tile_mask, chain_ids[None, :], pair.reshape(positions, width), gain_in[None, :], w_proj)
+    )(
+        *[
+            pltpu.with_memory_space_constraint(value, pltpu.HBM)
+            for value in (
+                tile_mask,
+                chain_ids[None, :],
+                pair.reshape(positions, width),
+                gain_in[None, :],
+                w_proj,
+                gain_mid[None, :],
+                w_out,
+            )
+        ]
+    )
     message = lax.all_to_all(
         message,
         ("row", "col"),
@@ -319,36 +323,13 @@
         ],
         tiled=True,
     )
-    gate, w_out_t, gain, done = pl.pallas_call(
-        gate_kernel,
-        out_shape=(
-            jax.ShapeDtypeStruct((width, positions), jnp.float32),
-            jax.ShapeDtypeStruct(w_out.shape[::-1], jnp.bfloat16),
-            jax.ShapeDtypeStruct((hidden, LANES), jnp.float32),
-            jax.ShapeDtypeStruct((8, LANES), jnp.float32),
-        ),
-        in_specs=[VMEM, HBM, HBM, HBM],
-        out_specs=(VMEM, VMEM, VMEM, VMEM),
-        scratch_shapes=[
-            pltpu.VMEM(w_proj.shape, jnp.bfloat16),
-            pltpu.VMEM(w_out.shape, jnp.bfloat16),
-            pltpu.VMEM((1, hidden), jnp.float32),
-            pltpu.SemaphoreType.DMA((3,)),
-        ],
-        compiler_params=params,
-        cost_estimate=pl.CostEstimate(
-            flops=2 * width * width * positions, bytes_accessed=4 * width * positions, transcendentals=0
-        ),
-        name="gate",
-    )(normed, w_proj, gain_mid[None, :], w_out)
-    message, done = lax.optimization_barrier((message, done))
     chunks = pl.cdiv(cols, LANES)
     depth = peers * rows
     deep = pl.cdiv(depth, LANES) * LANES
     mixed = pl.pallas_call(
         functools.partial(triangle_kernel, own, cols, shares),
         out_shape=jax.ShapeDtypeStruct((halves * shares * lines, LANES), jnp.bfloat16),
-        in_specs=[VMEM, ANY],
+        in_specs=[VMEM],
         out_specs=VMEM,
         scratch_shapes=[
             pltpu.VMEM((halves, chunks, depth * 2 * own, LANES), jnp.float32),
@@ -359,7 +340,7 @@
         ],
         compiler_params=params,
         name="triangle",
-    )(message, done)
+    )(message)
     mixed = lax.all_to_all(
         mixed.reshape(halves * shares, lines, LANES),
         ("row", "col"),

time: 42.8 us -> 41.8 us (0.977)
  blocking collectives: 19.6 us -> 36.9 us
  waiting for transfers between devices: 10.1 us -> 0 us
  starting transfers between devices: 6.43 us -> 0 us
  Pallas kernels: 5.75 us -> 4.71 us
  local copies, waits for them, and re-layouts: 0.64 us -> 0 us
    all_to_all x0 -> x1, blocking collectives: none -> 17.3 us  [on_device(): lax.all_to_all(message, ('row', 'col'), split_axis=0, concat_axis=0, axis...]
    all_to_all x1 -> x0, waiting for transfers between devices: 10.1 us -> none  [on_device(): lax.all_to_all(message, ('row', 'col'), split_axis=0, concat_axis=0, axis...]
    all_to_all x1 -> x0, starting transfers between devices: 6.43 us -> none  [on_device(): lax.all_to_all(message, ('row', 'col'), split_axis=0, concat_axis=0, axis...]
    unnamed x8 -> x0, local copies, waits for them, and re-layouts: 0.64 us -> none
    pallas_call x1 -> x0, Pallas kernels: 0.53 us -> none  [on_device(): pl.pallas_call(gate_kernel, out_shape=(jax.ShapeDtypeStruct((width, posit...]
    pallas_call x1, Pallas kernels: 2.81 us -> 2.29 us  [on_device(): pl.pallas_call(functools.partial(project_kernel, rows, cols), out_shape=(...]
  transfers between devices with their start and end apart: 1 -> 0, of which waited for: 1 -> 0; matrix products, arithmetic and copies ran while one was open for 0% -> 0% of each run, Pallas kernels for 1% -> 0%
where the time goes in v15:
time: 41.8 us; the launch traced here: 41.6 us
  blocking collectives  36.9 us (88%)
  Pallas kernels  4.71 us (11%)
    all_to_all x1, blocking collectives, on_device(): lax.all_to_all(mixed.reshape(halves * shares, lines, LANES), ('row', 'col...  19.5 us
    all_to_all x1, blocking collectives, on_device(): lax.all_to_all(message, ('row', 'col'), split_axis=0, concat_axis=0, axis...  17.3 us
    pallas_call x1, Pallas kernels, on_device(): pl.pallas_call(functools.partial(project_kernel, rows, cols), out_shape=(...  2.29 us
    pallas_call x1, Pallas kernels, on_device(): pl.pallas_call(functools.partial(triangle_kernel, own, cols, shares), out...  1.27 us
    pallas_call x1, Pallas kernels, on_device(): pl.pallas_call(functools.partial(output_kernel, own, PARTS), out_shape=ja...  1.14 us

profile of v15, /device:TPU:0, one launch (start us, length us, event | category | flops | bytes accessed | tf_op | source)
XLA Modules:
  0.0 41.6 jit_solution(11558223555421437144)
XLA Ops:
  0.0 2.3 %project.1 = (bf16[16,144,128]{2,1,0:T(8,128)(2,1)S(1)}, f32[128,1152]{1,0:T(8,128)S(1)}, bf16[128,128]{1,0:T(8,128)(2,1)S(1)}, f32[128,128]{1,0:T(8,128)S(1)}) custom-call(s32[2,2]{1,0:T(2,128)} %tile_hbm.1, s32[1,192]{1,0:T(1,128)} %bitcast.10, bf16[1152,128]{1,0:T(8,128)(2,1)} %bitcast.9, f32[1,128]{1,0:T(1,128)} %bitcast.11, bf16[128,640]{1,0:T(8,128)(2,1)} %w_hbm.1, ...), custom_call_target="tpu_custom_call" | custom-call | tf_op jit(solution)/shard_map/project/pallas_call | solution.py:278
  2.3 17.3 %all_to_all.10.message_ref = bf16[16,144,128]{2,1,0:T(8,128)(2,1)S(1)} all-to-all(bf16[16,144,128]{2,1,0:T(8,128)(2,1)S(1)} %get-tuple-element.9), channel_id=1, replica_groups={{0,1,2,3,4,5,6,7,8,9,10,11,12,13,14,15},{16,17,18,19,20,21,22,23,24,25,..., dimensions={0} | all-to-all | bytes 1179648 | tf_op jit(solution)/shard_map/all_to_all | solution.py:315
  19.6 1.3 %triangle.1 = bf16[2304,128]{1,0:T(8,128)(2,1)S(1)} custom-call(bf16[16,144,128]{2,1,0:T(8,128)(2,1)S(1)} %all_to_all.10.message_ref), custom_call_target="tpu_custom_call" | custom-call | tf_op jit(solution)/shard_map/triangle/pallas_call | solution.py:329
  20.9 19.5 %all_to_all.11 = bf16[32,72,128]{2,1,0:T(8,128)(2,1)S(1)} all-to-all(bf16[32,72,128]{2,1,0:T(8,128)(2,1)S(1)} %bitcast.8), channel_id=1, replica_groups=mesh['grp'=1,'row'=16,'col'=2] {'row','col'}, dimensions={0} | all-to-all | bytes 1179648 | tf_op jit(solution)/shard_map/all_to_all | solution.py:344
  40.5 1.1 %output.1 = bf16[1152,128]{1,0:T(8,128)(2,1)} custom-call(bf16[2304,128]{1,0:T(8,128)(2,1)S(1)} %bitcast.7, f32[128,1152]{1,0:T(8,128)S(1)} %get-tuple-element.10.gate_ref, f32[128,128]{1,0:T(8,128)S(1)} %get-tuple-element.11.gain_ref, bf16[128,128]{1,0:T(8,128)(2,1)S(1)} %get-tuple-element.12.w_t_ref), custom_call_target="tpu_custom_call" | custom-call | tf_op jit(solution)/shard_map/output/pallas_call | solution.py:351

commit v16 on v15

v16 whole, which is shorter than its diff:
```python
import functools
import math

import jax
import jax.numpy as jnp
from jax import lax
from jax.experimental import pallas as pl
from jax.experimental.pallas import tpu as pltpu
from jax.sharding import PartitionSpec as P

TILE = 96
LANES = 128
EPS = 1e-05
OWN = 4
VMEM_BYTES = 32 * 1024 * 1024
ROWS = 8
VMEM = pl.BlockSpec(memory_space=pltpu.VMEM)
HBM = pl.BlockSpec(memory_space=pltpu.HBM)
SMEM = pl.BlockSpec(memory_space=pltpu.SMEM)


def column(row):
    return jnp.broadcast_to(row, (8, row.shape[1])).T[:, :1]


def steps(at, width, count):
    total = jnp.zeros_like(at)
    for edge in range(1, count):
        total += (at >= edge * width).astype(jnp.int32)
    return total


def identity(rows, cols):
    same = lax.broadcasted_iota(jnp.int32, (rows, cols), 0) == lax.broadcasted_iota(jnp.int32, (rows, cols), 1)
    return same.astype(jnp.bfloat16)


def transpose(block):
    return lax.dot_general(
        identity(block.shape[1], block.shape[1]),
        block,
        (((1,), (1,)), ((), ())),
        preferred_element_type=jnp.float32,
    )


def sigmoid(values):
    return 0.5 * jnp.tanh(0.5 * values) + 0.5


def keep_of(tile_ref, chain_ref, rows, cols):
    tokens = chain_ref.shape[1]
    tiles = tile_ref.shape[1]
    positions = rows * cols
    at = lax.broadcasted_iota(jnp.int32, (1, positions), 1)
    row = steps(at, cols, rows)
    k = lax.axis_index("row") * rows + row
    i = lax.axis_index("col") * cols + at - row * cols
    token = lax.broadcasted_iota(jnp.int32, (tokens, positions), 0)
    pick = (token == k).astype(jnp.float32) - (token == i).astype(jnp.float32)
    chains = jnp.broadcast_to(chain_ref[...].astype(jnp.bfloat16), (8, tokens))
    apart = jnp.dot(chains, pick.astype(jnp.bfloat16), preferred_element_type=jnp.float32)[:1]
    k_tile = steps(k, TILE, tiles)
    i_tile = steps(i, TILE, tiles)
    tile_vals = jnp.zeros((1, positions), jnp.float32)
    for a in range(tiles):
        for b in range(tiles):
            here = (k_tile == a) & (i_tile == b)
            tile_vals = jnp.where(here, tile_ref[a, b].astype(jnp.float32), tile_vals)
    return jnp.where(apart == 0.0, 1.0, tile_vals)


def cycle_of(cols):
    cycle = math.lcm(cols, LANES)
    return cycle // cols, cycle // LANES


def start_copies(sems, *pairs):
    copies = [pltpu.make_async_copy(src, dst, sems.at[at]) for at, (src, dst) in enumerate(pairs)]
    for copy in copies:
        copy.start()
    return copies


def fetch(sems, *pairs):
    for copy in start_copies(sems, *pairs):
        copy.wait()


def turn_pairs(first, second):
    axis = first.ndim - 2
    upper = lax.broadcasted_iota(jnp.int32, first.shape, axis) < OWN
    return (
        jnp.where(upper, first, pltpu.roll(second, OWN, axis=axis)),
        jnp.where(upper, pltpu.roll(first, OWN, axis=axis), second),
    )


def sides_by_member(left, right):
    lines, width = left.shape
    pairs = turn_pairs(left.reshape(-1, ROWS, width), right.reshape(-1, ROWS, width))
    return jnp.stack(pairs, axis=1).reshape(2 * lines, width).astype(jnp.bfloat16)


def project_kernel(
    rows, cols, tile_hbm, chain_hbm, pair_hbm, gain_hbm, w_hbm, gain_mid_hbm, w_out_hbm,
    message_ref, gate_ref, w_out_ref, gain_mid_ref,
    tile_ref, chain_ref, pair_ref, gain_ref, w_ref, gain_mid, w_out, normed_ref, sems,
):
    hidden = (w_ref.shape[1] - w_ref.shape[0]) // 4
    members = message_ref.shape[0]
    size = cycle_of(cols)[1] * LANES
    copies = start_copies(
        sems,
        (chain_hbm, chain_ref),
        (tile_hbm, tile_ref),
        (gain_hbm, gain_ref),
        (pair_hbm, pair_ref),
        (w_hbm, w_ref),
        (gain_mid_hbm, gain_mid),
        (w_out_hbm, w_out),
    )
    for copy in copies[:3]:
        copy.wait()
    keep = keep_of(tile_ref, chain_ref, rows, cols)
    gain = column(gain_ref[...])
    copies[4].wait()
    w_t = w_ref[...].astype(jnp.float32).T
    w_value = sides_by_member(w_t[:hidden], w_t[2 * hidden : 3 * hidden])
    w_gate = sides_by_member(w_t[hidden : 2 * hidden], w_t[3 * hidden : 4 * hidden])
    w_out_gate = w_t[4 * hidden :].astype(jnp.bfloat16)
    copies[3].wait()
    cycles = [slice(start, start + size) for start in range(0, rows * cols, size)]
    for lanes in cycles:
        block = transpose(pair_ref[lanes, :])
        center = block - jnp.mean(block, axis=0, keepdims=True)
        spread = jnp.mean(center * center, axis=0, keepdims=True)
        normed_ref[:, lanes] = (center * lax.rsqrt(spread + EPS) * gain).astype(jnp.bfloat16)
    for lanes in cycles:
        normed = normed_ref[:, lanes]
        value = jnp.dot(w_value, normed, preferred_element_type=jnp.float32)
        gate = jnp.dot(w_gate, normed, preferred_element_type=jnp.float32)
        sent = (sigmoid(gate) * value * keep[:, lanes]).reshape(members, ROWS, size)
        message_ref[:, :, lanes] = sent.astype(jnp.bfloat16)
        gate_ref[:, lanes] = sigmoid(jnp.dot(w_out_gate, normed, preferred_element_type=jnp.float32))
    for copy in copies[5:]:
        copy.wait()
    w_out_ref[...] = w_out[...].T
    gain_mid_ref[...] = jnp.broadcast_to(column(gain_mid[...]), gain_mid_ref.shape)


def unpack(message, half, halves, spread_ref, cols):
    tokens, groups = cycle_of(cols)
    members, _, positions = message.shape
    lane = lax.broadcasted_iota(jnp.int32, (ROWS, LANES), 1)
    cycles = positions // (LANES * groups)
    for peer in range(members // halves):
        for cycle in range(cycles):
            base = cycle * groups
            held = [
                message[peer * halves + half, :, (base + group) * LANES : (base + group + 1) * LANES].astype(
                    jnp.float32
                )
                for group in range(groups)
            ]
            for token in range(tokens):
                k = (peer * cycles + cycle) * tokens + token
                for chunk in range(spread_ref.shape[0]):
                    group, off = divmod(token * cols + chunk * LANES, LANES)
                    value = held[group]
                    if off and group + 1 < groups:
                        value = jnp.where(lane >= off, value, held[group + 1])
                    if off:
                        value = pltpu.roll(value, LANES - off, axis=1)
                    spread_ref[chunk, k * ROWS : (k + 1) * ROWS, :] = value


def pack(spread_ref, at, cols):
    tokens, groups = cycle_of(cols)
    lane = lax.broadcasted_iota(jnp.int32, (ROWS, LANES), 1)
    rolled, lines = {}, []
    for group in range(groups):
        value, here = None, 0
        while here < LANES:
            token, col = divmod(group * LANES + here, cols)
            chunk, there = divmod(col, LANES)
            shift = (here - there) % LANES
            if (token, chunk, shift) not in rolled:
                line = (at * tokens + token) * ROWS
                piece = spread_ref[chunk, line : line + ROWS, :]
                rolled[token, chunk, shift] = pltpu.roll(piece, shift, axis=1) if shift else piece
            piece = rolled[token, chunk, shift]
            value = piece if value is None else jnp.where(lane >= here, piece, value)
            here += min(LANES - here, LANES - there, cols - col)
        lines.append(value)
    return lines


def channel_of(spread_ref, line, stride):
    count = spread_ref.shape[1] // stride
    return jnp.concatenate(
        [spread_ref[chunk, pl.ds(line, count, stride=stride), :] for chunk in range(spread_ref.shape[0])],
        axis=1,
    ).astype(jnp.bfloat16)


def triangle_kernel(cols, shares, message_ref, mixed_ref, spread, left, left_t, right, mixed):
    halves, chunks = spread.shape[:2]
    width = chunks * LANES
    deep = right.shape[1]
    depth = spread.shape[2] // ROWS
    one = identity(cols, width)
    if depth < deep:
        right[:, depth:, :] = jnp.zeros((OWN, deep - depth, halves * width), jnp.bfloat16)
    for half in range(halves):
        unpack(message_ref, half, halves, spread.at[half], cols)
        if depth < deep:
            left[:, half * deep + depth : (half + 1) * deep, :] = jnp.zeros((OWN, deep - depth, width), jnp.bfloat16)
        for channel in range(OWN):
            left[channel, half * deep : half * deep + depth, :] = channel_of(spread.at[half], channel, ROWS)
            right[channel, :depth, half * width : (half + 1) * width] = channel_of(
                spread.at[half], OWN + channel, ROWS
            )
    for channel in range(OWN):
        both = lax.dot_general(
            one, left[channel], (((1,), (1,)), ((), ())), preferred_element_type=jnp.float32
        ).astype(jnp.bfloat16)
        for half in range(halves):
            left_t[channel, half * cols : (half + 1) * cols, :] = both[:, half * deep : (half + 1) * deep]
    for channel in range(OWN):
        total = jnp.dot(left_t[channel], right[channel], preferred_element_type=jnp.float32)
        for i_half in range(halves):
            for j_half in range(halves):
                for chunk in range(chunks):
                    start = j_half * width + chunk * LANES
                    mixed[i_half, chunk, pl.ds(j_half * OWN + channel, cols, stride=ROWS), :] = total[
                        i_half * cols : (i_half + 1) * cols, start : start + LANES
                    ]
    groups = cycle_of(cols)[1]
    cycles = mixed_ref.shape[2] // (LANES * groups)
    for share in range(shares):
        i_half, peer = divmod(share, shares // halves)
        for cycle in range(cycles):
            for group, line in enumerate(pack(mixed.at[i_half], peer * cycles + cycle, cols)):
                start = (cycle * groups + group) * LANES
                for j_half in range(halves):
                    mixed_ref[share * halves + j_half, :, start : start + LANES] = line[
                        j_half * OWN : (j_half + 1) * OWN
                    ].astype(jnp.bfloat16)


def output_kernel(parts, mixed_ref, gate_ref, gain_ref, w_t_ref, update_hbm, mixed, update, sems):
    members = mixed_ref.shape[0] // parts
    groups = update.shape[0] // LANES
    steps = math.gcd(groups, 3)
    for member in range(members):
        sums = mixed_ref[member].astype(jnp.float32)
        for part in range(1, parts):
            sums += mixed_ref[part * members + member].astype(jnp.float32)
        mixed[member * OWN : (member + 1) * OWN, :] = sums
    leaving = []
    for group in range(groups):
        lanes = slice(group * LANES, (group + 1) * LANES)
        block = mixed[:, lanes]
        center = block - jnp.mean(block, axis=0, keepdims=True)
        spread = jnp.mean(center * center, axis=0, keepdims=True)
        normed = (center * lax.rsqrt(spread + EPS) * gain_ref[...]).astype(jnp.bfloat16)
        projected = jnp.dot(w_t_ref[...], normed, preferred_element_type=jnp.float32)
        update[lanes, :] = (gate_ref[:, lanes] * projected).T.astype(jnp.bfloat16)
        step, last = divmod((group + 1) * steps, groups)
        if last == 0:
            done = slice((step - 1) * (groups // steps) * LANES, (group + 1) * LANES)
            leaving += start_copies(sems.at[step - 1], (update.at[done, :], update_hbm.at[done, :]))
    for copy in leaving:
        copy.wait()


def on_device(shares, halves, pair, tile_mask, chain_ids, gain_in, w_proj, gain_mid, w_out):
    rows, cols, width = pair.shape
    hidden = w_out.shape[0]
    devices = shares * halves
    members = hidden // OWN
    parts = devices // members
    positions = rows * cols
    params = pltpu.CompilerParams(vmem_limit_bytes=VMEM_BYTES)
    tokens = chain_ids.shape[0]
    message, gate, w_out_t, gain = pl.pallas_call(
        functools.partial(project_kernel, rows, cols),
        out_shape=(
            jax.ShapeDtypeStruct((members, ROWS, positions), jnp.bfloat16),
            jax.ShapeDtypeStruct((width, positions), jnp.float32),
            jax.ShapeDtypeStruct(w_out.shape[::-1], jnp.bfloat16),
            jax.ShapeDtypeStruct((hidden, LANES), jnp.float32),
        ),
        in_specs=[HBM] * 7,
        out_specs=[VMEM] * 4,
        scratch_shapes=[
            pltpu.SMEM(tile_mask.shape, jnp.int32),
            pltpu.VMEM((1, tokens), jnp.int32),
            pltpu.VMEM((positions, width), jnp.bfloat16),
            pltpu.VMEM((1, width), jnp.float32),
            pltpu.VMEM(w_proj.shape, jnp.bfloat16),
            pltpu.VMEM((1, hidden), jnp.float32),
            pltpu.VMEM(w_out.shape, jnp.bfloat16),
            pltpu.VMEM((width, positions), jnp.bfloat16),
            pltpu.SemaphoreType.DMA((7,)),
        ],
        compiler_params=params,
        name="project",
    )(
        *[
            pltpu.with_memory_space_constraint(value, pltpu.HBM)
            for value in (
                tile_mask,
                chain_ids[None, :],
                pair.reshape(positions, width),
                gain_in[None, :],
                w_proj,
                gain_mid[None, :],
                w_out,
            )
        ]
    )
    message = lax.all_to_all(
        message,
        ("row", "col"),
        split_axis=0,
        concat_axis=0,
        axis_index_groups=None
        if parts == 1
        else [list(range(part * members, (part + 1) * members)) for part in range(parts)],
        tiled=True,
    )
    chunks = pl.cdiv(cols, LANES)
    depth = members // halves * rows
    deep = pl.cdiv(depth, LANES) * LANES
    mixed = pl.pallas_call(
        functools.partial(triangle_kernel, cols, shares),
        out_shape=jax.ShapeDtypeStruct((devices, OWN, positions), jnp.bfloat16),
        in_specs=[VMEM],
        out_specs=VMEM,
        scratch_shapes=[
            pltpu.VMEM((halves, chunks, depth * ROWS, LANES), jnp.float32),
            pltpu.VMEM((OWN, halves * deep, chunks * LANES), jnp.bfloat16),
            pltpu.VMEM((OWN, halves * cols, deep), jnp.bfloat16),
            pltpu.VMEM((OWN, deep, halves * chunks * LANES), jnp.bfloat16),
            pltpu.VMEM((halves, chunks, cols * ROWS, LANES), jnp.float32),
        ],
        compiler_params=params,
        name="triangle",
    )(message)
    mixed = lax.all_to_all(mixed, ("row", "col"), split_axis=0, concat_axis=0, tiled=True)
    groups = positions // LANES
    update = pl.pallas_call(
        functools.partial(output_kernel, parts),
        out_shape=jax.ShapeDtypeStruct((positions, width), jnp.bfloat16),
        in_specs=[VMEM] * 4,
        out_specs=HBM,
        scratch_shapes=[
            pltpu.VMEM((hidden, positions), jnp.float32),
            pltpu.VMEM((positions, width), jnp.bfloat16),
            pltpu.SemaphoreType.DMA((math.gcd(groups, 3), 1)),
        ],
        compiler_params=params,
        name="output",
    )(mixed, gate, gain, w_out_t)
    return update.reshape(rows, cols, width)


def solution(mesh):
    in_specs = (P(("grp", "row"), "col", None), P("grp", None), P("grp"), P(), P(), P(), P())
    out_specs = P(("grp", "row"), "col", None)
    return jax.shard_map(
        functools.partial(on_device, mesh.shape["row"], mesh.shape["col"]),
        mesh=mesh,
        in_specs=in_specs,
        out_specs=out_specs,
        check_vma=False,
    )
```

time: 41.8 us -> 43 us (1.029)
  blocking collectives: 36.9 us -> 38.3 us
    all_to_all x1, blocking collectives: 17.3 us -> 23.8 us  [on_device(): lax.all_to_all(message, ('row', 'col'), split_axis=0, concat_axis=0, axis...]
    all_to_all x1, blocking collectives: 19.5 us -> 14.5 us  [on_device(): lax.all_to_all(mixed, ('row', 'col'), split_axis=0, concat_axis=0, tiled=...]
where the time goes in v16:
time: 43 us; the launch traced here: 42.8 us
  blocking collectives  38.3 us (89%)
  Pallas kernels  4.42 us (10%)
    all_to_all x1, blocking collectives, on_device(): lax.all_to_all(message, ('row', 'col'), split_axis=0, concat_axis=0, axis...  23.8 us
    all_to_all x1, blocking collectives, on_device(): lax.all_to_all(mixed, ('row', 'col'), split_axis=0, concat_axis=0, tiled=...  14.5 us
    pallas_call x1, Pallas kernels, on_device(): pl.pallas_call(functools.partial(project_kernel, rows, cols), out_shape=(...  2.34 us
    pallas_call x1, Pallas kernels, on_device(): pl.pallas_call(functools.partial(output_kernel, parts), out_shape=jax.Sha...  1.17 us
    pallas_call x1, Pallas kernels, on_device(): pl.pallas_call(functools.partial(triangle_kernel, cols, shares), out_shap...  0.91 us

profile of v16, /device:TPU:0, one launch (start us, length us, event | category | flops | bytes accessed | tf_op | source)
XLA Modules:
  0.0 42.8 jit_solution(15859168972021915804)
XLA Ops:
  0.0 2.3 %project.1 = (bf16[32,8,1152]{2,1,0:T(8,128)(2,1)S(1)}, f32[128,1152]{1,0:T(8,128)S(1)}, bf16[128,128]{1,0:T(8,128)(2,1)S(1)}, f32[128,128]{1,0:T(8,128)S(1)}) custom-call(s32[2,2]{1,0:T(2,128)} %tile_hbm.1, s32[1,192]{1,0:T(1,128)} %bitcast.6, bf16[1152,128]{1,0:T(8,128)(2,1)} %bitcast.5, f32[1,128]{1,0:T(1,128)} %bitcast.7, bf16[128,640]{1,0:T(8,128)(2,1)} %w_hbm.1, ...), custom_call_target="tpu_custom_call" | custom-call | tf_op jit(solution)/shard_map/project/pallas_call | solution.py:287
  2.3 23.8 %all_to_all.10.message_ref = bf16[32,8,1152]{2,1,0:T(8,128)(2,1)S(1)} all-to-all(bf16[32,8,1152]{2,1,0:T(8,128)(2,1)S(1)} %get-tuple-element.9), channel_id=1, replica_groups=mesh['grp'=1,'row'=16,'col'=2] {'row','col'}, dimensions={0} | all-to-all | bytes 1179648 | tf_op jit(solution)/shard_map/all_to_all | solution.py:324
  26.2 0.9 %triangle.1 = bf16[32,4,1152]{2,1,0:T(4,128)(2,1)S(1)} custom-call(bf16[32,8,1152]{2,1,0:T(8,128)(2,1)S(1)} %all_to_all.10.message_ref), custom_call_target="tpu_custom_call" | custom-call | tf_op jit(solution)/shard_map/triangle/pallas_call | solution.py:337
  27.1 14.5 %all_to_all.11.mixed_ref = bf16[32,4,1152]{2,1,0:T(4,128)(2,1)S(1)} all-to-all(bf16[32,4,1152]{2,1,0:T(4,128)(2,1)S(1)} %triangle.1), channel_id=1, replica_groups=mesh['grp'=1,'row'=16,'col'=2] {'row','col'}, dimensions={0} | all-to-all | bytes 589824 | tf_op jit(solution)/shard_map/all_to_all | solution.py:352
  41.6 1.2 %output.1 = bf16[1152,128]{1,0:T(8,128)(2,1)} custom-call(bf16[32,4,1152]{2,1,0:T(4,128)(2,1)S(1)} %all_to_all.11.mixed_ref, f32[128,1152]{1,0:T(8,128)S(1)} %get-tuple-element.10.gate_ref, f32[128,128]{1,0:T(8,128)S(1)} %get-tuple-element.11.gain_ref, bf16[128,128]{1,0:T(8,128)(2,1)S(1)} %get-tuple-element.12.w_t_ref), custom_call_target="tpu_custom_call" | custom-call | tf_op jit(solution)/shard_map/output/pallas_call | solution.py:354

commit v17 on v15

--- a/solution.py
+++ b/solution.py
@@ -41,10 +41,6 @@
         (((1,), (1,)), ((), ())),
         preferred_element_type=jnp.float32,
     )
-
-
-def sigmoid(values):
-    return 0.5 * jnp.tanh(0.5 * values) + 0.5
 
 
 def keep_of(tile_ref, chain_ref, rows, cols):
@@ -96,25 +92,31 @@
     own = hidden // peers
     groups = cycle_of(cols)[1]
     size = groups * LANES
+    cycles = [slice(start, start + size) for start in range(0, rows * cols, size)]
     copies = start_copies(
         sems,
         (chain_hbm, chain_ref),
         (tile_hbm, tile_ref),
         (gain_hbm, gain_ref),
-        (pair_hbm, pair_ref),
         (w_hbm, w_ref),
         (gain_mid_hbm, gain_mid),
         (w_out_hbm, w_out),
+        *[(pair_hbm.at[lanes, :], pair_ref.at[lanes, :]) for lanes in cycles],
     )
     for copy in copies[:3]:
         copy.wait()
     keep = keep_of(tile_ref, chain_ref, rows, cols)
     gain = column(gain_ref[...])
-    copies[4].wait()
-    w_t = w_ref[...].T
     copies[3].wait()
-    cycles = [slice(start, start + size) for start in range(0, rows * cols, size)]
-    for lanes in cycles:
+    w_t = jnp.concatenate(
+        [
+            0.5 * transpose(w_ref[:, start : start + LANES])
+            for start in range(0, w_ref.shape[1], LANES)
+        ],
+        axis=0,
+    ).astype(jnp.bfloat16)
+    for copy, lanes in zip(copies[6:], cycles):
+        copy.wait()
         block = transpose(pair_ref[lanes, :])
         center = block - jnp.mean(block, axis=0, keepdims=True)
         spread = jnp.mean(center * center, axis=0, keepdims=True)
@@ -125,15 +127,15 @@
         for side in range(2):
             value = projected[2 * side * hidden : (2 * side + 1) * hidden]
             gate = projected[(2 * side + 1) * hidden : (2 * side + 2) * hidden]
-            sides.append((sigmoid(gate) * value * keep[:, lanes]).reshape(peers, own, size))
+            sides.append(((jnp.tanh(gate) + 1.0) * value * keep[:, lanes]).reshape(peers, own, size))
         both = jnp.concatenate(sides, axis=1).astype(jnp.bfloat16)
         for group in range(groups):
             line = (cycle * groups + group) * 2 * own
             message_ref[:, line : line + 2 * own, :] = both[:, :, group * LANES : (group + 1) * LANES]
-        gate_ref[:, lanes] = sigmoid(projected[4 * hidden :])
-    for copy in copies[5:]:
-        copy.wait()
-    w_out_ref[...] = w_out[...].T
+        gate_ref[:, lanes] = 0.5 * jnp.tanh(projected[4 * hidden :]) + 0.5
+    for copy in copies[4:6]:
+        copy.wait()
+    w_out_ref[...] = transpose(w_out[...]).astype(jnp.bfloat16)
     gain_mid_ref[...] = jnp.broadcast_to(column(gain_mid[...]), gain_mid_ref.shape)
 
 
@@ -147,9 +149,7 @@
         for cycle in range(cycles):
             base = cycle * groups
             held = [
-                message_ref[
-                    peer * halves + half, (base + group) * 2 * own : (base + group + 1) * 2 * own, :
-                ].astype(jnp.float32)
+                message_ref[peer * halves + half, (base + group) * 2 * own : (base + group + 1) * 2 * own, :]
                 for group in range(groups)
             ]
             for token in range(tokens):
@@ -161,7 +161,7 @@
                         value = jnp.where(lane >= off, value, held[group + 1])
                     if off:
                         value = pltpu.roll(value, LANES - off, axis=1)
-                    spread_ref[chunk, k * 2 * own : (k + 1) * 2 * own, :] = value
+                    spread_ref[chunk, k * 2 * own : (k + 1) * 2 * own, :] = value.astype(jnp.float32)
 
 
 def pack(spread_ref, at, own, cols):
@@ -294,7 +294,7 @@
             pltpu.VMEM((1, hidden), jnp.float32),
             pltpu.VMEM(w_out.shape, jnp.bfloat16),
             pltpu.VMEM((width, positions), jnp.bfloat16),
-            pltpu.SemaphoreType.DMA((7,)),
+            pltpu.SemaphoreType.DMA((6 + groups // cycle_of(cols)[1],)),
         ],
         compiler_params=params,
         name="project",

time: 41.8 us -> 42.3 us (1.012)
  Pallas kernels: 4.71 us -> 5.18 us
    pallas_call x1, Pallas kernels: 2.29 us -> 2.72 us  [on_device(): pl.pallas_call(functools.partial(project_kernel, rows, cols), out_shape=(...]
where the time goes in v17:
time: 42.3 us; the launch traced here: 42.1 us
  blocking collectives  36.9 us (87%)
  Pallas kernels  5.18 us (12%)
    all_to_all x1, blocking collectives, on_device(): lax.all_to_all(mixed.reshape(halves * shares, lines, LANES), ('row', 'col...  19.5 us
    all_to_all x1, blocking collectives, on_device(): lax.all_to_all(message, ('row', 'col'), split_axis=0, concat_axis=0, axis...  17.3 us
    pallas_call x1, Pallas kernels, on_device(): pl.pallas_call(functools.partial(project_kernel, rows, cols), out_shape=(...  2.72 us
    pallas_call x1, Pallas kernels, on_device(): pl.pallas_call(functools.partial(triangle_kernel, own, cols, shares), out...  1.32 us
    pallas_call x1, Pallas kernels, on_device(): pl.pallas_call(functools.partial(output_kernel, own, PARTS), out_shape=ja...  1.14 us

profile of v17, /device:TPU:0, one launch (start us, length us, event | category | flops | bytes accessed | tf_op | source)
XLA Modules:
  0.0 42.1 jit_solution(1765989736798729865)
XLA Ops:
  0.0 2.7 %project.1 = (bf16[16,144,128]{2,1,0:T(8,128)(2,1)S(1)}, f32[128,1152]{1,0:T(8,128)S(1)}, bf16[128,128]{1,0:T(8,128)(2,1)S(1)}, f32[128,128]{1,0:T(8,128)S(1)}) custom-call(s32[2,2]{1,0:T(2,128)} %tile_hbm.1, s32[1,192]{1,0:T(1,128)} %bitcast.10, bf16[1152,128]{1,0:T(8,128)(2,1)} %bitcast.9, f32[1,128]{1,0:T(1,128)} %bitcast.11, bf16[128,640]{1,0:T(8,128)(2,1)} %w_hbm.1, ...), custom_call_target="tpu_custom_call" | custom-call | tf_op jit(solution)/shard_map/project/pallas_call | solution.py:278
  2.7 17.3 %all_to_all.10.message_ref = bf16[16,144,128]{2,1,0:T(8,128)(2,1)S(1)} all-to-all(bf16[16,144,128]{2,1,0:T(8,128)(2,1)S(1)} %get-tuple-element.9), channel_id=1, replica_groups={{0,1,2,3,4,5,6,7,8,9,10,11,12,13,14,15},{16,17,18,19,20,21,22,23,24,25,..., dimensions={0} | all-to-all | bytes 1179648 | tf_op jit(solution)/shard_map/all_to_all | solution.py:315
  20.1 1.3 %triangle.1 = bf16[2304,128]{1,0:T(8,128)(2,1)S(1)} custom-call(bf16[16,144,128]{2,1,0:T(8,128)(2,1)S(1)} %all_to_all.10.message_ref), custom_call_target="tpu_custom_call" | custom-call | tf_op jit(solution)/shard_map/triangle/pallas_call | solution.py:329
  21.4 19.5 %all_to_all.11 = bf16[32,72,128]{2,1,0:T(8,128)(2,1)S(1)} all-to-all(bf16[32,72,128]{2,1,0:T(8,128)(2,1)S(1)} %bitcast.8), channel_id=1, replica_groups=mesh['grp'=1,'row'=16,'col'=2] {'row','col'}, dimensions={0} | all-to-all | bytes 1179648 | tf_op jit(solution)/shard_map/all_to_all | solution.py:344
  40.9 1.1 %output.1 = bf16[1152,128]{1,0:T(8,128)(2,1)} custom-call(bf16[2304,128]{1,0:T(8,128)(2,1)S(1)} %bitcast.7, f32[128,1152]{1,0:T(8,128)S(1)} %get-tuple-element.10.gate_ref, f32[128,128]{1,0:T(8,128)S(1)} %get-tuple-element.11.gain_ref, bf16[128,128]{1,0:T(8,128)(2,1)S(1)} %get-tuple-element.12.w_t_ref), custom_call_target="tpu_custom_call" | custom-call | tf_op jit(solution)/shard_map/output/pallas_call | solution.py:351

commit v18 on v17

--- a/solution.py
+++ b/solution.py
@@ -83,9 +83,8 @@
 
 
 def project_kernel(
-    rows, cols, tile_hbm, chain_hbm, pair_hbm, gain_hbm, w_hbm, gain_mid_hbm, w_out_hbm,
-    message_ref, gate_ref, w_out_ref, gain_mid_ref,
-    tile_ref, chain_ref, pair_ref, gain_ref, w_ref, gain_mid, w_out, normed_ref, sems,
+    rows, cols, tile_hbm, chain_hbm, pair_hbm, gain_hbm, w_hbm, message_ref, gate_ref,
+    tile_ref, chain_ref, pair_ref, gain_ref, w_ref, normed_ref, sems,
 ):
     hidden = (w_ref.shape[1] - w_ref.shape[0]) // 4
     peers = message_ref.shape[0]
@@ -98,16 +97,14 @@
         (chain_hbm, chain_ref),
         (tile_hbm, tile_ref),
         (gain_hbm, gain_ref),
+        (pair_hbm, pair_ref),
         (w_hbm, w_ref),
-        (gain_mid_hbm, gain_mid),
-        (w_out_hbm, w_out),
-        *[(pair_hbm.at[lanes, :], pair_ref.at[lanes, :]) for lanes in cycles],
     )
     for copy in copies[:3]:
         copy.wait()
     keep = keep_of(tile_ref, chain_ref, rows, cols)
     gain = column(gain_ref[...])
-    copies[3].wait()
+    copies[4].wait()
     w_t = jnp.concatenate(
         [
             0.5 * transpose(w_ref[:, start : start + LANES])
@@ -115,8 +112,8 @@
         ],
         axis=0,
     ).astype(jnp.bfloat16)
-    for copy, lanes in zip(copies[6:], cycles):
-        copy.wait()
+    copies[3].wait()
+    for lanes in cycles:
         block = transpose(pair_ref[lanes, :])
         center = block - jnp.mean(block, axis=0, keepdims=True)
         spread = jnp.mean(center * center, axis=0, keepdims=True)
@@ -133,10 +130,6 @@
             line = (cycle * groups + group) * 2 * own
             message_ref[:, line : line + 2 * own, :] = both[:, :, group * LANES : (group + 1) * LANES]
         gate_ref[:, lanes] = 0.5 * jnp.tanh(projected[4 * hidden :]) + 0.5
-    for copy in copies[4:6]:
-        copy.wait()
-    w_out_ref[...] = transpose(w_out[...]).astype(jnp.bfloat16)
-    gain_mid_ref[...] = jnp.broadcast_to(column(gain_mid[...]), gain_mid_ref.shape)
 
 
 def unpack(message_ref, half, halves, spread_ref, own, cols):
@@ -149,7 +142,9 @@
         for cycle in range(cycles):
             base = cycle * groups
             held = [
-                message_ref[peer * halves + half, (base + group) * 2 * own : (base + group + 1) * 2 * own, :]
+                message_ref[
+                    peer * halves + half, (base + group) * 2 * own : (base + group + 1) * 2 * own, :
+                ].astype(jnp.float32)
                 for group in range(groups)
             ]
             for token in range(tokens):
@@ -161,7 +156,7 @@
                         value = jnp.where(lane >= off, value, held[group + 1])
                     if off:
                         value = pltpu.roll(value, LANES - off, axis=1)
-                    spread_ref[chunk, k * 2 * own : (k + 1) * 2 * own, :] = value.astype(jnp.float32)
+                    spread_ref[chunk, k * 2 * own : (k + 1) * 2 * own, :] = value
 
 
 def pack(spread_ref, at, own, cols):
@@ -193,7 +188,11 @@
     ).astype(jnp.bfloat16)
 
 
-def triangle_kernel(own, cols, shares, message_ref, mixed_ref, spread, left, left_t, right, mixed):
+def triangle_kernel(
+    own, cols, shares, message_ref, gain_hbm, w_out_hbm, mixed_ref, gain_ref, w_out_ref,
+    spread, left, left_t, right, mixed, gain, w_out, sems,
+):
+    copies = start_copies(sems, (gain_hbm, gain), (w_out_hbm, w_out))
     halves, chunks = spread.shape[:2]
     width = chunks * LANES
     deep = right.shape[1]
@@ -235,6 +234,10 @@
             for cycle in range(cycles):
                 lines += pack(mixed.at[i_half, j_half], peer * cycles + cycle, own, cols)
         mixed_ref[share * each : (share + 1) * each, :] = jnp.concatenate(lines, axis=0).astype(jnp.bfloat16)
+    for copy in copies:
+        copy.wait()
+    gain_ref[...] = jnp.broadcast_to(column(gain[...]), gain_ref.shape)
+    w_out_ref[...] = transpose(w_out[...]).astype(jnp.bfloat16)
 
 
 def output_kernel(own, parts, mixed_ref, gate_ref, gain_ref, w_t_ref, update_hbm, mixed, update, sems):
@@ -263,6 +266,10 @@
         copy.wait()
 
 
+def in_hbm(value):
+    return pltpu.with_memory_space_constraint(value, pltpu.HBM)
+
+
 def on_device(shares, halves, pair, tile_mask, chain_ids, gain_in, w_proj, gain_mid, w_out):
     rows, cols, width = pair.shape
     hidden = w_out.shape[0]
@@ -275,42 +282,31 @@
     params = pltpu.CompilerParams(vmem_limit_bytes=VMEM_BYTES)
     tokens = chain_ids.shape[0]
     message = jax.ShapeDtypeStruct((peers * halves, 2 * lines, LANES), jnp.bfloat16)
-    message, gate, w_out_t, gain = pl.pallas_call(
+    message, gate = pl.pallas_call(
         functools.partial(project_kernel, rows, cols),
         out_shape=(
             message,
             jax.ShapeDtypeStruct((width, positions), jnp.float32),
-            jax.ShapeDtypeStruct(w_out.shape[::-1], jnp.bfloat16),
-            jax.ShapeDtypeStruct((hidden, LANES), jnp.float32),
         ),
-        in_specs=[HBM] * 7,
-        out_specs=[VMEM] * 4,
+        in_specs=[HBM] * 5,
+        out_specs=[VMEM] * 2,
         scratch_shapes=[
             pltpu.SMEM(tile_mask.shape, jnp.int32),
             pltpu.VMEM((1, tokens), jnp.int32),
             pltpu.VMEM((positions, width), jnp.bfloat16),
             pltpu.VMEM((1, width), jnp.float32),
             pltpu.VMEM(w_proj.shape, jnp.bfloat16),
-            pltpu.VMEM((1, hidden), jnp.float32),
-            pltpu.VMEM(w_out.shape, jnp.bfloat16),
             pltpu.VMEM((width, positions), jnp.bfloat16),
-            pltpu.SemaphoreType.DMA((6 + groups // cycle_of(cols)[1],)),
+            pltpu.SemaphoreType.DMA((5,)),
         ],
         compiler_params=params,
         name="project",
     )(
-        *[
-            pltpu.with_memory_space_constraint(value, pltpu.HBM)
-            for value in (
-                tile_mask,
-                chain_ids[None, :],
-                pair.reshape(positions, width),
-                gain_in[None, :],
-                w_proj,
-                gain_mid[None, :],
-                w_out,
-            )
-        ]
+        in_hbm(tile_mask),
+        in_hbm(chain_ids[None, :]),
+        in_hbm(pair.reshape(positions, width)),
+        in_hbm(gain_in[None, :]),
+        in_hbm(w_proj),
     )
     message = lax.all_to_all(
         message,
@@ -326,21 +322,28 @@
     chunks = pl.cdiv(cols, LANES)
     depth = peers * rows
     deep = pl.cdiv(depth, LANES) * LANES
-    mixed = pl.pallas_call(
+    mixed, gain, w_out_t = pl.pallas_call(
         functools.partial(triangle_kernel, own, cols, shares),
-        out_shape=jax.ShapeDtypeStruct((halves * shares * lines, LANES), jnp.bfloat16),
-        in_specs=[VMEM],
-        out_specs=VMEM,
+        out_shape=(
+            jax.ShapeDtypeStruct((halves * shares * lines, LANES), jnp.bfloat16),
+            jax.ShapeDtypeStruct((hidden, LANES), jnp.float32),
+            jax.ShapeDtypeStruct(w_out.shape[::-1], jnp.bfloat16),
+        ),
+        in_specs=[VMEM, HBM, HBM],
+        out_specs=[VMEM] * 3,
         scratch_shapes=[
             pltpu.VMEM((halves, chunks, depth * 2 * own, LANES), jnp.float32),
             pltpu.VMEM((own, halves * deep, chunks * LANES), jnp.bfloat16),
             pltpu.VMEM((own, halves * cols, deep), jnp.bfloat16),
             pltpu.VMEM((own, deep, halves * chunks * LANES), jnp.bfloat16),
             pltpu.VMEM((halves, halves, chunks, cols * own, LANES), jnp.float32),
+            pltpu.VMEM((1, hidden), jnp.float32),
+            pltpu.VMEM(w_out.shape, jnp.bfloat16),
+            pltpu.SemaphoreType.DMA((2,)),
         ],
         compiler_params=params,
         name="triangle",
-    )(message)
+    )(message, in_hbm(gain_mid[None, :]), in_hbm(w_out))
     mixed = lax.all_to_all(
         mixed.reshape(halves * shares, lines, LANES),
         ("row", "col"),

time: 42.3 us -> 41.9 us (level)
    pallas_call x1, Pallas kernels: 2.72 us -> 2.24 us  [on_device(): pl.pallas_call(functools.partial(project_kernel, rows, cols), out_shape=(...]
where the time goes in v18:
time: 41.9 us; the launch traced here: 41.8 us
  blocking collectives  36.9 us (88%)
  Pallas kernels  4.87 us (12%)
    all_to_all x1, blocking collectives, on_device(): lax.all_to_all(mixed.reshape(halves * shares, lines, LANES), ('row', 'col...  19.5 us
    all_to_all x1, blocking collectives, on_device(): lax.all_to_all(message, ('row', 'col'), split_axis=0, concat_axis=0, axis...  17.3 us
    pallas_call x1, Pallas kernels, on_device(): pl.pallas_call(functools.partial(project_kernel, rows, cols), out_shape=(...  2.24 us
    pallas_call x1, Pallas kernels, on_device(): pl.pallas_call(functools.partial(triangle_kernel, own, cols, shares), out...  1.49 us
    pallas_call x1, Pallas kernels, on_device(): pl.pallas_call(functools.partial(output_kernel, own, PARTS), out_shape=ja...  1.14 us

profile of v18, /device:TPU:0, one launch (start us, length us, event | category | flops | bytes accessed | tf_op | source)
XLA Modules:
  0.0 41.8 jit_solution(689864621143451041)
XLA Ops:
  0.0 2.2 %project.1 = (bf16[16,144,128]{2,1,0:T(8,128)(2,1)S(1)}, f32[128,1152]{1,0:T(8,128)S(1)}) custom-call(s32[2,2]{1,0:T(2,128)} %tile_hbm.1, s32[1,192]{1,0:T(1,128)} %bitcast.10, bf16[1152,128]{1,0:T(8,128)(2,1)} %bitcast.9, f32[1,128]{1,0:T(1,128)} %bitcast.11, bf16[128,640]{1,0:T(8,128)(2,1)} %w_hbm.1), custom_call_target="tpu_custom_call" | custom-call | tf_op jit(solution)/shard_map/project/pallas_call | solution.py:285
  2.2 17.3 %all_to_all.10.message_ref = bf16[16,144,128]{2,1,0:T(8,128)(2,1)S(1)} all-to-all(bf16[16,144,128]{2,1,0:T(8,128)(2,1)S(1)} %get-tuple-element.10), channel_id=1, replica_groups={{0,1,2,3,4,5,6,7,8,9,10,11,12,13,14,15},{16,17,18,19,20,21,22,23,24,25,..., dimensions={0} | all-to-all | bytes 1179648 | tf_op jit(solution)/shard_map/all_to_all | solution.py:311
  19.6 1.5 %triangle.1 = (bf16[2304,128]{1,0:T(8,128)(2,1)S(1)}, f32[128,128]{1,0:T(8,128)S(1)}, bf16[128,128]{1,0:T(8,128)(2,1)S(1)}) custom-call(bf16[16,144,128]{2,1,0:T(8,128)(2,1)S(1)} %all_to_all.10.message_ref, f32[1,128]{1,0:T(1,128)} %bitcast.12, bf16[128,128]{1,0:T(8,128)(2,1)} %w_out_hbm.1), custom_call_target="tpu_custom_call" | custom-call | tf_op jit(solution)/shard_map/triangle/pallas_call | solution.py:325
  21.1 19.5 %all_to_all.11 = bf16[32,72,128]{2,1,0:T(8,128)(2,1)S(1)} all-to-all(bf16[32,72,128]{2,1,0:T(8,128)(2,1)S(1)} %bitcast.8), channel_id=1, replica_groups=mesh['grp'=1,'row'=16,'col'=2] {'row','col'}, dimensions={0} | all-to-all | bytes 1179648 | tf_op jit(solution)/shard_map/all_to_all | solution.py:347
  40.6 1.1 %output.1 = bf16[1152,128]{1,0:T(8,128)(2,1)} custom-call(bf16[2304,128]{1,0:T(8,128)(2,1)S(1)} %bitcast.7, f32[128,1152]{1,0:T(8,128)S(1)} %get-tuple-element.12.gate_ref, f32[128,128]{1,0:T(8,128)S(1)} %get-tuple-element.13.gain_ref, bf16[128,128]{1,0:T(8,128)(2,1)S(1)} %get-tuple-element.14.w_t_ref), custom_call_target="tpu_custom_call" | custom-call | tf_op jit(solution)/shard_map/output/pallas_call | solution.py:354

commit v19 on v17

--- a/solution.py
+++ b/solution.py
@@ -34,9 +34,9 @@
     return same.astype(jnp.bfloat16)
 
 
-def transpose(block):
+def transpose(block, by=None):
     return lax.dot_general(
-        identity(block.shape[1], block.shape[1]),
+        identity(block.shape[1], block.shape[1]) if by is None else by,
         block,
         (((1,), (1,)), ((), ())),
         preferred_element_type=jnp.float32,
@@ -98,16 +98,16 @@
         (chain_hbm, chain_ref),
         (tile_hbm, tile_ref),
         (gain_hbm, gain_ref),
+        (pair_hbm, pair_ref),
         (w_hbm, w_ref),
         (gain_mid_hbm, gain_mid),
         (w_out_hbm, w_out),
-        *[(pair_hbm.at[lanes, :], pair_ref.at[lanes, :]) for lanes in cycles],
     )
     for copy in copies[:3]:
         copy.wait()
     keep = keep_of(tile_ref, chain_ref, rows, cols)
     gain = column(gain_ref[...])
-    copies[3].wait()
+    copies[4].wait()
     w_t = jnp.concatenate(
         [
             0.5 * transpose(w_ref[:, start : start + LANES])
@@ -115,25 +115,23 @@
         ],
         axis=0,
     ).astype(jnp.bfloat16)
-    for copy, lanes in zip(copies[6:], cycles):
-        copy.wait()
-        block = transpose(pair_ref[lanes, :])
-        center = block - jnp.mean(block, axis=0, keepdims=True)
+    copies[3].wait()
+    width = pair_ref.shape[1]
+    centering = (identity(width, width).astype(jnp.float32) - 1.0 / width).astype(jnp.bfloat16)
+    for lanes in cycles:
+        center = transpose(pair_ref[lanes, :], centering)
         spread = jnp.mean(center * center, axis=0, keepdims=True)
         normed_ref[:, lanes] = (center * lax.rsqrt(spread + EPS) * gain).astype(jnp.bfloat16)
-    for cycle, lanes in enumerate(cycles):
+    for lanes in cycles:
         projected = jnp.dot(w_t, normed_ref[:, lanes], preferred_element_type=jnp.float32)
         sides = []
         for side in range(2):
             value = projected[2 * side * hidden : (2 * side + 1) * hidden]
             gate = projected[(2 * side + 1) * hidden : (2 * side + 2) * hidden]
             sides.append(((jnp.tanh(gate) + 1.0) * value * keep[:, lanes]).reshape(peers, own, size))
-        both = jnp.concatenate(sides, axis=1).astype(jnp.bfloat16)
-        for group in range(groups):
-            line = (cycle * groups + group) * 2 * own
-            message_ref[:, line : line + 2 * own, :] = both[:, :, group * LANES : (group + 1) * LANES]
+        message_ref[:, :, lanes] = jnp.concatenate(sides, axis=1).astype(jnp.bfloat16)
         gate_ref[:, lanes] = 0.5 * jnp.tanh(projected[4 * hidden :]) + 0.5
-    for copy in copies[4:6]:
+    for copy in copies[5:]:
         copy.wait()
     w_out_ref[...] = transpose(w_out[...]).astype(jnp.bfloat16)
     gain_mid_ref[...] = jnp.broadcast_to(column(gain_mid[...]), gain_mid_ref.shape)
@@ -141,16 +139,14 @@
 
 def unpack(message_ref, half, halves, spread_ref, own, cols):
     tokens, groups = cycle_of(cols)
-    members, lines, _ = message_ref.shape
-    peers = members // halves
+    members, _, positions = message_ref.shape
     lane = lax.broadcasted_iota(jnp.int32, (2 * own, LANES), 1)
-    cycles = lines // (2 * groups * own)
-    for peer in range(peers):
+    cycles = positions // (LANES * groups)
+    for peer in range(members // halves):
         for cycle in range(cycles):
-            base = cycle * groups
+            starts = [(cycle * groups + group) * LANES for group in range(groups)]
             held = [
-                message_ref[peer * halves + half, (base + group) * 2 * own : (base + group + 1) * 2 * own, :]
-                for group in range(groups)
+                message_ref[peer * halves + half, :, start : start + LANES].astype(jnp.float32) for start in starts
             ]
             for token in range(tokens):
                 k = (peer * cycles + cycle) * tokens + token
@@ -161,7 +157,7 @@
                         value = jnp.where(lane >= off, value, held[group + 1])
                     if off:
                         value = pltpu.roll(value, LANES - off, axis=1)
-                    spread_ref[chunk, k * 2 * own : (k + 1) * 2 * own, :] = value.astype(jnp.float32)
+                    spread_ref[chunk, k * 2 * own : (k + 1) * 2 * own, :] = value
 
 
 def pack(spread_ref, at, own, cols):
@@ -226,34 +222,31 @@
                         i_half * cols : (i_half + 1) * cols, start : start + LANES
                     ]
     groups = cycle_of(cols)[1]
-    each = mixed_ref.shape[0] // shares
-    cycles = each // (halves * groups * own)
+    cycles = mixed_ref.shape[2] // (groups * LANES)
     for share in range(shares):
         i_half, peer = divmod(share, shares // halves)
-        lines = []
         for j_half in range(halves):
             for cycle in range(cycles):
-                lines += pack(mixed.at[i_half, j_half], peer * cycles + cycle, own, cols)
-        mixed_ref[share * each : (share + 1) * each, :] = jnp.concatenate(lines, axis=0).astype(jnp.bfloat16)
-
-
-def output_kernel(own, parts, mixed_ref, gate_ref, gain_ref, w_t_ref, update_hbm, mixed, update, sems):
-    members, lines, _ = mixed.shape
-    members = members // parts
-    mixed[...] = mixed_ref[...].astype(jnp.float32).reshape(mixed.shape)
-    groups = lines // own
-    steps = math.gcd(groups, 3)
+                for group, line in enumerate(pack(mixed.at[i_half, j_half], peer * cycles + cycle, own, cols)):
+                    start = (cycle * groups + group) * LANES
+                    mixed_ref[share * halves + j_half, :, start : start + LANES] = line.astype(jnp.bfloat16)
+
+
+def output_kernel(parts, mixed_ref, gate_ref, gain_ref, w_t_ref, update_hbm, update, sems):
+    members = mixed_ref.shape[0] // parts
+    groups = update.shape[0] // LANES
+    steps = sems.shape[0]
     leaving = []
     for group in range(groups):
-        sums = mixed[:members, group * own : (group + 1) * own, :]
+        lanes = slice(group * LANES, (group + 1) * LANES)
+        sums = mixed_ref[:members, :, lanes].astype(jnp.float32)
         for part in range(1, parts):
-            sums += mixed[part * members : (part + 1) * members, group * own : (group + 1) * own, :]
-        block = sums.reshape(members * own, LANES)
+            sums += mixed_ref[part * members : (part + 1) * members, :, lanes].astype(jnp.float32)
+        block = sums.reshape(-1, LANES)
         center = block - jnp.mean(block, axis=0, keepdims=True)
         spread = jnp.mean(center * center, axis=0, keepdims=True)
         normed = (center * lax.rsqrt(spread + EPS) * gain_ref[...]).astype(jnp.bfloat16)
         projected = jnp.dot(w_t_ref[...], normed, preferred_element_type=jnp.float32)
-        lanes = slice(group * LANES, (group + 1) * LANES)
         update[lanes, :] = (gate_ref[:, lanes] * projected).T.astype(jnp.bfloat16)
         step, last = divmod((group + 1) * steps, groups)
         if last == 0:
@@ -263,6 +256,10 @@
         copy.wait()
 
 
+def in_hbm(value):
+    return pltpu.with_memory_space_constraint(value, pltpu.HBM)
+
+
 def on_device(shares, halves, pair, tile_mask, chain_ids, gain_in, w_proj, gain_mid, w_out):
     rows, cols, width = pair.shape
     hidden = w_out.shape[0]
@@ -270,15 +267,12 @@
     own = hidden // (peers * halves)
     positions = rows * cols
     groups = positions // LANES
-    lines = groups * own
-    cycles = groups // cycle_of(cols)[1]
     params = pltpu.CompilerParams(vmem_limit_bytes=VMEM_BYTES)
     tokens = chain_ids.shape[0]
-    message = jax.ShapeDtypeStruct((peers * halves, 2 * lines, LANES), jnp.bfloat16)
     message, gate, w_out_t, gain = pl.pallas_call(
         functools.partial(project_kernel, rows, cols),
         out_shape=(
-            message,
+            jax.ShapeDtypeStruct((peers * halves, 2 * own, positions), jnp.bfloat16),
             jax.ShapeDtypeStruct((width, positions), jnp.float32),
             jax.ShapeDtypeStruct(w_out.shape[::-1], jnp.bfloat16),
             jax.ShapeDtypeStruct((hidden, LANES), jnp.float32),
@@ -294,33 +288,26 @@
             pltpu.VMEM((1, hidden), jnp.float32),
             pltpu.VMEM(w_out.shape, jnp.bfloat16),
             pltpu.VMEM((width, positions), jnp.bfloat16),
-            pltpu.SemaphoreType.DMA((6 + groups // cycle_of(cols)[1],)),
+            pltpu.SemaphoreType.DMA((7,)),
         ],
         compiler_params=params,
         name="project",
     )(
-        *[
-            pltpu.with_memory_space_constraint(value, pltpu.HBM)
-            for value in (
-                tile_mask,
-                chain_ids[None, :],
-                pair.reshape(positions, width),
-                gain_in[None, :],
-                w_proj,
-                gain_mid[None, :],
-                w_out,
-            )
-        ]
-    )
+        in_hbm(tile_mask),
+        in_hbm(chain_ids[None, :]),
+        in_hbm(pair.reshape(positions, width)),
+        in_hbm(gain_in[None, :]),
+        in_hbm(w_proj),
+        in_hbm(gain_mid[None, :]),
+        in_hbm(w_out),
+    )
+    members = peers * halves
     message = lax.all_to_all(
         message,
         ("row", "col"),
         split_axis=0,
         concat_axis=0,
-        axis_index_groups=[
-            list(range(part * peers * halves, (part + 1) * peers * halves))
-            for part in range(PARTS)
-        ],
+        axis_index_groups=[list(range(part * members, (part + 1) * members)) for part in range(PARTS)],
         tiled=True,
     )
     chunks = pl.cdiv(cols, LANES)
@@ -328,7 +315,7 @@
     deep = pl.cdiv(depth, LANES) * LANES
     mixed = pl.pallas_call(
         functools.partial(triangle_kernel, own, cols, shares),
-        out_shape=jax.ShapeDtypeStruct((halves * shares * lines, LANES), jnp.bfloat16),
+        out_shape=jax.ShapeDtypeStruct((shares * halves, own, positions), jnp.bfloat16),
         in_specs=[VMEM],
         out_specs=VMEM,
         scratch_shapes=[
@@ -341,20 +328,13 @@
         compiler_params=params,
         name="triangle",
     )(message)
-    mixed = lax.all_to_all(
-        mixed.reshape(halves * shares, lines, LANES),
-        ("row", "col"),
-        split_axis=0,
-        concat_axis=0,
-        tiled=True,
-    ).reshape(halves * shares * lines, LANES)
+    mixed = lax.all_to_all(mixed, ("row", "col"), split_axis=0, concat_axis=0, tiled=True)
     update = pl.pallas_call(
-        functools.partial(output_kernel, own, PARTS),
+        functools.partial(output_kernel, PARTS),
         out_shape=jax.ShapeDtypeStruct((positions, width), jnp.bfloat16),
         in_specs=[VMEM] * 4,
         out_specs=HBM,
         scratch_shapes=[
-            pltpu.VMEM((shares * halves, lines, LANES), jnp.float32),
             pltpu.VMEM((positions, width), jnp.bfloat16),
             pltpu.SemaphoreType.DMA((math.gcd(groups, 3), 1)),
         ],

time: 42.3 us -> 41.9 us (level)
  no operation moved by 1% of the time
where the time goes in v19:
time: 41.9 us; the launch traced here: 41.7 us
  blocking collectives  36.9 us (88%)
  Pallas kernels  4.86 us (12%)
    all_to_all x1, blocking collectives, on_device(): lax.all_to_all(mixed, ('row', 'col'), split_axis=0, concat_axis=0, tiled=...  19.5 us
    all_to_all x1, blocking collectives, on_device(): lax.all_to_all(message, ('row', 'col'), split_axis=0, concat_axis=0, axis...  17.3 us
    pallas_call x1, Pallas kernels, on_device(): pl.pallas_call(functools.partial(project_kernel, rows, cols), out_shape=(...  2.43 us
    pallas_call x1, Pallas kernels, on_device(): pl.pallas_call(functools.partial(triangle_kernel, own, cols, shares), out...  1.28 us
    pallas_call x1, Pallas kernels, on_device(): pl.pallas_call(functools.partial(output_kernel, PARTS), out_shape=jax.Sha...  1.15 us

profile of v19, /device:TPU:0, one launch (start us, length us, event | category | flops | bytes accessed | tf_op | source)
XLA Modules:
  0.0 41.7 jit_solution(6901140575119456140)
XLA Ops:
  0.0 2.4 %project.1 = (bf16[16,16,1152]{2,1,0:T(8,128)(2,1)S(1)}, f32[128,1152]{1,0:T(8,128)S(1)}, bf16[128,128]{1,0:T(8,128)(2,1)S(1)}, f32[128,128]{1,0:T(8,128)S(1)}) custom-call(s32[2,2]{1,0:T(2,128)} %tile_hbm.1, s32[1,192]{1,0:T(1,128)} %bitcast.6, bf16[1152,128]{1,0:T(8,128)(2,1)} %bitcast.5, f32[1,128]{1,0:T(1,128)} %bitcast.7, bf16[128,640]{1,0:T(8,128)(2,1)} %w_hbm.1, ...), custom_call_target="tpu_custom_call" | custom-call | tf_op jit(solution)/shard_map/project/pallas_call | solution.py:272
  2.4 17.3 %all_to_all.10.message_ref = bf16[16,16,1152]{2,1,0:T(8,128)(2,1)S(1)} all-to-all(bf16[16,16,1152]{2,1,0:T(8,128)(2,1)S(1)} %get-tuple-element.9), channel_id=1, replica_groups={{0,1,2,3,4,5,6,7,8,9,10,11,12,13,14,15},{16,17,18,19,20,21,22,23,24,25,..., dimensions={0} | all-to-all | bytes 1179648 | tf_op jit(solution)/shard_map/all_to_all | solution.py:305
  19.8 1.3 %triangle.1 = bf16[32,8,1152]{2,1,0:T(8,128)(2,1)S(1)} custom-call(bf16[16,16,1152]{2,1,0:T(8,128)(2,1)S(1)} %all_to_all.10.message_ref), custom_call_target="tpu_custom_call" | custom-call | tf_op jit(solution)/shard_map/triangle/pallas_call | solution.py:316
  21.1 19.5 %all_to_all.11.mixed_ref = bf16[32,8,1152]{2,1,0:T(8,128)(2,1)S(1)} all-to-all(bf16[32,8,1152]{2,1,0:T(8,128)(2,1)S(1)} %triangle.1), channel_id=1, replica_groups=mesh['grp'=1,'row'=16,'col'=2] {'row','col'}, dimensions={0} | all-to-all | bytes 1179648 | tf_op jit(solution)/shard_map/all_to_all | solution.py:331
  40.6 1.2 %output.1 = bf16[1152,128]{1,0:T(8,128)(2,1)} custom-call(bf16[32,8,1152]{2,1,0:T(8,128)(2,1)S(1)} %all_to_all.11.mixed_ref, f32[128,1152]{1,0:T(8,128)S(1)} %get-tuple-element.10.gate_ref, f32[128,128]{1,0:T(8,128)S(1)} %get-tuple-element.11.gain_ref, bf16[128,128]{1,0:T(8,128)(2,1)S(1)} %get-tuple-element.12.w_t_ref), custom_call_target="tpu_custom_call" | custom-call | tf_op jit(solution)/shard_map/output/pallas_call | solution.py:332

commit v20 on v19

--- a/solution.py
+++ b/solution.py
@@ -85,14 +85,13 @@
 def project_kernel(
     rows, cols, tile_hbm, chain_hbm, pair_hbm, gain_hbm, w_hbm, gain_mid_hbm, w_out_hbm,
     message_ref, gate_ref, w_out_ref, gain_mid_ref,
-    tile_ref, chain_ref, pair_ref, gain_ref, w_ref, gain_mid, w_out, normed_ref, sems,
+    tile_ref, chain_ref, pair_ref, gain_ref, w_ref, gain_mid, w_out, w_t_ref, keep_ref, sems,
 ):
     hidden = (w_ref.shape[1] - w_ref.shape[0]) // 4
     peers = message_ref.shape[0]
     own = hidden // peers
     groups = cycle_of(cols)[1]
     size = groups * LANES
-    cycles = [slice(start, start + size) for start in range(0, rows * cols, size)]
     copies = start_copies(
         sems,
         (chain_hbm, chain_ref),
@@ -108,29 +107,30 @@
     keep = keep_of(tile_ref, chain_ref, rows, cols)
     gain = column(gain_ref[...])
     copies[4].wait()
-    w_t = jnp.concatenate(
-        [
-            0.5 * transpose(w_ref[:, start : start + LANES])
-            for start in range(0, w_ref.shape[1], LANES)
-        ],
-        axis=0,
-    ).astype(jnp.bfloat16)
+    for start in range(0, w_ref.shape[1], LANES):
+        lines = slice(start, start + LANES)
+        w_t_ref[lines, :] = (0.5 * transpose(w_ref[:, lines])).astype(jnp.bfloat16)
     copies[3].wait()
     width = pair_ref.shape[1]
     centering = (identity(width, width).astype(jnp.float32) - 1.0 / width).astype(jnp.bfloat16)
-    for lanes in cycles:
+    keep_ref[...] = keep
+
+    @pl.loop(0, rows * cols // size)
+    def _(cycle):
+        start = pl.multiple_of(cycle * size, LANES)
+        lanes = pl.ds(start, size)
         center = transpose(pair_ref[lanes, :], centering)
         spread = jnp.mean(center * center, axis=0, keepdims=True)
-        normed_ref[:, lanes] = (center * lax.rsqrt(spread + EPS) * gain).astype(jnp.bfloat16)
-    for lanes in cycles:
-        projected = jnp.dot(w_t, normed_ref[:, lanes], preferred_element_type=jnp.float32)
+        normed = (center * lax.rsqrt(spread + EPS) * gain).astype(jnp.bfloat16)
+        projected = jnp.dot(w_t_ref[...], normed, preferred_element_type=jnp.float32)
         sides = []
         for side in range(2):
             value = projected[2 * side * hidden : (2 * side + 1) * hidden]
             gate = projected[(2 * side + 1) * hidden : (2 * side + 2) * hidden]
-            sides.append(((jnp.tanh(gate) + 1.0) * value * keep[:, lanes]).reshape(peers, own, size))
+            sides.append(((jnp.tanh(gate) + 1.0) * value * keep_ref[:, lanes]).reshape(peers, own, size))
         message_ref[:, :, lanes] = jnp.concatenate(sides, axis=1).astype(jnp.bfloat16)
         gate_ref[:, lanes] = 0.5 * jnp.tanh(projected[4 * hidden :]) + 0.5
+
     for copy in copies[5:]:
         copy.wait()
     w_out_ref[...] = transpose(w_out[...]).astype(jnp.bfloat16)
@@ -142,14 +142,17 @@
     members, _, positions = message_ref.shape
     lane = lax.broadcasted_iota(jnp.int32, (2 * own, LANES), 1)
     cycles = positions // (LANES * groups)
-    for peer in range(members // halves):
+    lines = cycles * tokens * 2 * own
+
+    @pl.loop(0, members // halves)
+    def _(peer):
         for cycle in range(cycles):
             starts = [(cycle * groups + group) * LANES for group in range(groups)]
             held = [
                 message_ref[peer * halves + half, :, start : start + LANES].astype(jnp.float32) for start in starts
             ]
             for token in range(tokens):
-                k = (peer * cycles + cycle) * tokens + token
+                at = pl.multiple_of(peer * lines, 8) + (cycle * tokens + token) * 2 * own
                 for chunk in range(spread_ref.shape[0]):
                     group, off = divmod(token * cols + chunk * LANES, LANES)
                     value = held[group]
@@ -157,7 +160,7 @@
                         value = jnp.where(lane >= off, value, held[group + 1])
                     if off:
                         value = pltpu.roll(value, LANES - off, axis=1)
-                    spread_ref[chunk, k * 2 * own : (k + 1) * 2 * own, :] = value
+                    spread_ref[chunk, pl.ds(at, 2 * own), :] = value
 
 
 def pack(spread_ref, at, own, cols):
@@ -171,8 +174,8 @@
             chunk, there = divmod(col, LANES)
             shift = (here - there) % LANES
             if (token, chunk, shift) not in rolled:
-                line = (at * tokens + token) * own
-                piece = spread_ref[chunk, line : line + own, :]
+                line = pl.multiple_of(at * tokens * own, 8) + token * own
+                piece = spread_ref[chunk, pl.ds(line, own), :]
                 rolled[token, chunk, shift] = pltpu.roll(piece, shift, axis=1) if shift else piece
             piece = rolled[token, chunk, shift]
             value = piece if value is None else jnp.where(lane >= here, piece, value)
@@ -223,37 +226,46 @@
                     ]
     groups = cycle_of(cols)[1]
     cycles = mixed_ref.shape[2] // (groups * LANES)
-    for share in range(shares):
-        i_half, peer = divmod(share, shares // halves)
-        for j_half in range(halves):
-            for cycle in range(cycles):
-                for group, line in enumerate(pack(mixed.at[i_half, j_half], peer * cycles + cycle, own, cols)):
-                    start = (cycle * groups + group) * LANES
-                    mixed_ref[share * halves + j_half, :, start : start + LANES] = line.astype(jnp.bfloat16)
+
+    @pl.loop(0, shares // halves)
+    def _(peer):
+        for i_half in range(halves):
+            for j_half in range(halves):
+                member = (i_half * (shares // halves) + peer) * halves + j_half
+                for cycle in range(cycles):
+                    at = peer * cycles + cycle
+                    for group, line in enumerate(pack(mixed.at[i_half, j_half], at, own, cols)):
+                        start = (cycle * groups + group) * LANES
+                        mixed_ref[member, :, start : start + LANES] = line.astype(jnp.bfloat16)
 
 
 def output_kernel(parts, mixed_ref, gate_ref, gain_ref, w_t_ref, update_hbm, update, sems):
     members = mixed_ref.shape[0] // parts
     groups = update.shape[0] // LANES
     steps = sems.shape[0]
-    leaving = []
-    for group in range(groups):
-        lanes = slice(group * LANES, (group + 1) * LANES)
-        sums = mixed_ref[:members, :, lanes].astype(jnp.float32)
-        for part in range(1, parts):
-            sums += mixed_ref[part * members : (part + 1) * members, :, lanes].astype(jnp.float32)
-        block = sums.reshape(-1, LANES)
-        center = block - jnp.mean(block, axis=0, keepdims=True)
-        spread = jnp.mean(center * center, axis=0, keepdims=True)
-        normed = (center * lax.rsqrt(spread + EPS) * gain_ref[...]).astype(jnp.bfloat16)
-        projected = jnp.dot(w_t_ref[...], normed, preferred_element_type=jnp.float32)
-        update[lanes, :] = (gate_ref[:, lanes] * projected).T.astype(jnp.bfloat16)
-        step, last = divmod((group + 1) * steps, groups)
-        if last == 0:
-            done = slice((step - 1) * (groups // steps) * LANES, (group + 1) * LANES)
-            leaving += start_copies(sems.at[step - 1], (update.at[done, :], update_hbm.at[done, :]))
-    for copy in leaving:
-        copy.wait()
+    size = groups // steps * LANES
+
+    def leave(step):
+        lines = pl.ds(pl.multiple_of(step * size, LANES), size)
+        return pltpu.make_async_copy(update.at[lines, :], update_hbm.at[lines, :], sems.at[step])
+
+    @pl.loop(0, steps)
+    def _(step):
+        for group in range(groups // steps):
+            lanes = pl.ds(pl.multiple_of(step * size, LANES) + group * LANES, LANES)
+            sums = mixed_ref[:members, :, lanes].astype(jnp.float32)
+            for part in range(1, parts):
+                sums += mixed_ref[part * members : (part + 1) * members, :, lanes].astype(jnp.float32)
+            block = sums.reshape(-1, LANES)
+            center = block - jnp.mean(block, axis=0, keepdims=True)
+            spread = jnp.mean(center * center, axis=0, keepdims=True)
+            normed = (center * lax.rsqrt(spread + EPS) * gain_ref[...]).astype(jnp.bfloat16)
+            projected = jnp.dot(w_t_ref[...], normed, preferred_element_type=jnp.float32)
+            update[lanes, :] = (gate_ref[:, lanes] * projected).T.astype(jnp.bfloat16)
+        leave(step).start()
+
+    for step in range(steps):
+        leave(step).wait()
 
 
 def in_hbm(value):
@@ -287,7 +299,8 @@
             pltpu.VMEM(w_proj.shape, jnp.bfloat16),
             pltpu.VMEM((1, hidden), jnp.float32),
             pltpu.VMEM(w_out.shape, jnp.bfloat16),
-            pltpu.VMEM((width, positions), jnp.bfloat16),
+            pltpu.VMEM(w_proj.shape[::-1], jnp.bfloat16),
+            pltpu.VMEM((1, positions), jnp.float32),
             pltpu.SemaphoreType.DMA((7,)),
         ],
         compiler_params=params,
@@ -336,7 +349,7 @@
         out_specs=HBM,
         scratch_shapes=[
             pltpu.VMEM((positions, width), jnp.bfloat16),
-            pltpu.SemaphoreType.DMA((math.gcd(groups, 3), 1)),
+            pltpu.SemaphoreType.DMA((math.gcd(groups, 3),)),
         ],
         compiler_params=params,
         name="output",

time: 41.9 us -> 45 us (1.074)
  Pallas kernels: 4.86 us -> 7.92 us
    pallas_call x1, Pallas kernels: 1.28 us -> 3.03 us  [on_device(): pl.pallas_call(functools.partial(triangle_kernel, own, cols, shares), out...]
    pallas_call x1, Pallas kernels: 2.43 us -> 3.2 us  [on_device(): pl.pallas_call(functools.partial(project_kernel, rows, cols), out_shape=(...]
    pallas_call x1, Pallas kernels: 1.15 us -> 1.69 us  [on_device(): pl.pallas_call(functools.partial(output_kernel, PARTS), out_shape=jax.Sha...]
where the time goes in v20:
time: 45 us; the launch traced here: 44.8 us
  blocking collectives  36.9 us (82%)
  Pallas kernels  7.92 us (18%)
    all_to_all x1, blocking collectives, on_device(): lax.all_to_all(mixed, ('row', 'col'), split_axis=0, concat_axis=0, tiled=...  19.5 us
    all_to_all x1, blocking collectives, on_device(): lax.all_to_all(message, ('row', 'col'), split_axis=0, concat_axis=0, axis...  17.3 us
    pallas_call x1, Pallas kernels, on_device(): pl.pallas_call(functools.partial(project_kernel, rows, cols), out_shape=(...  3.2 us
    pallas_call x1, Pallas kernels, on_device(): pl.pallas_call(functools.partial(triangle_kernel, own, cols, shares), out...  3.03 us
    pallas_call x1, Pallas kernels, on_device(): pl.pallas_call(functools.partial(output_kernel, PARTS), out_shape=jax.Sha...  1.69 us

profile of v20, /device:TPU:0, one launch (start us, length us, event | category | flops | bytes accessed | tf_op | source)
XLA Modules:
  0.0 44.8 jit_solution(13145180381067258099)
XLA Ops:
  0.0 3.2 %project.1 = (bf16[16,16,1152]{2,1,0:T(8,128)(2,1)S(1)}, f32[128,1152]{1,0:T(8,128)S(1)}, bf16[128,128]{1,0:T(8,128)(2,1)S(1)}, f32[128,128]{1,0:T(8,128)S(1)}) custom-call(s32[2,2]{1,0:T(2,128)} %tile_hbm.1, s32[1,192]{1,0:T(1,128)} %bitcast.6, bf16[1152,128]{1,0:T(8,128)(2,1)} %bitcast.5, f32[1,128]{1,0:T(1,128)} %bitcast.7, bf16[128,640]{1,0:T(8,128)(2,1)} %w_hbm.1, ...), custom_call_target="tpu_custom_call" | custom-call | tf_op jit(solution)/shard_map/project/pallas_call | solution.py:284
  3.2 17.3 %all_to_all.10.message_ref = bf16[16,16,1152]{2,1,0:T(8,128)(2,1)S(1)} all-to-all(bf16[16,16,1152]{2,1,0:T(8,128)(2,1)S(1)} %get-tuple-element.9), channel_id=1, replica_groups={{0,1,2,3,4,5,6,7,8,9,10,11,12,13,14,15},{16,17,18,19,20,21,22,23,24,25,..., dimensions={0} | all-to-all | bytes 1179648 | tf_op jit(solution)/shard_map/all_to_all | solution.py:318
  20.6 3.0 %triangle.1 = bf16[32,8,1152]{2,1,0:T(8,128)(2,1)S(1)} custom-call(bf16[16,16,1152]{2,1,0:T(8,128)(2,1)S(1)} %all_to_all.10.message_ref), custom_call_target="tpu_custom_call" | custom-call | tf_op jit(solution)/shard_map/triangle/pallas_call | solution.py:329
  23.6 19.5 %all_to_all.11.mixed_ref = bf16[32,8,1152]{2,1,0:T(8,128)(2,1)S(1)} all-to-all(bf16[32,8,1152]{2,1,0:T(8,128)(2,1)S(1)} %triangle.1), channel_id=1, replica_groups=mesh['grp'=1,'row'=16,'col'=2] {'row','col'}, dimensions={0} | all-to-all | bytes 1179648 | tf_op jit(solution)/shard_map/all_to_all | solution.py:344
  43.1 1.7 %output.1 = bf16[1152,128]{1,0:T(8,128)(2,1)} custom-call(bf16[32,8,1152]{2,1,0:T(8,128)(2,1)S(1)} %all_to_all.11.mixed_ref, f32[128,1152]{1,0:T(8,128)S(1)} %get-tuple-element.10.gate_ref, f32[128,128]{1,0:T(8,128)S(1)} %get-tuple-element.11.gain_ref, bf16[128,128]{1,0:T(8,128)(2,1)S(1)} %get-tuple-element.12.w_t_ref), custom_call_target="tpu_custom_call" | custom-call | tf_op jit(solution)/shard_map/output/pallas_call | solution.py:345

commit v21 on v17

--- a/solution.py
+++ b/solution.py
@@ -95,19 +95,17 @@
     cycles = [slice(start, start + size) for start in range(0, rows * cols, size)]
     copies = start_copies(
         sems,
+        (pair_hbm, pair_ref),
+        (w_hbm, w_ref),
+        (gain_hbm, gain_ref),
         (chain_hbm, chain_ref),
         (tile_hbm, tile_ref),
-        (gain_hbm, gain_ref),
-        (w_hbm, w_ref),
         (gain_mid_hbm, gain_mid),
         (w_out_hbm, w_out),
-        *[(pair_hbm.at[lanes, :], pair_ref.at[lanes, :]) for lanes in cycles],
-    )
-    for copy in copies[:3]:
-        copy.wait()
-    keep = keep_of(tile_ref, chain_ref, rows, cols)
-    gain = column(gain_ref[...])
-    copies[3].wait()
+    )
+    copies[0].wait()
+    blocks = [transpose(pair_ref[lanes, :]) for lanes in cycles]
+    copies[1].wait()
     w_t = jnp.concatenate(
         [
             0.5 * transpose(w_ref[:, start : start + LANES])
@@ -115,12 +113,15 @@
         ],
         axis=0,
     ).astype(jnp.bfloat16)
-    for copy, lanes in zip(copies[6:], cycles):
-        copy.wait()
-        block = transpose(pair_ref[lanes, :])
+    copies[2].wait()
+    gain = column(gain_ref[...])
+    for lanes, block in zip(cycles, blocks):
         center = block - jnp.mean(block, axis=0, keepdims=True)
         spread = jnp.mean(center * center, axis=0, keepdims=True)
         normed_ref[:, lanes] = (center * lax.rsqrt(spread + EPS) * gain).astype(jnp.bfloat16)
+    copies[3].wait()
+    copies[4].wait()
+    keep = keep_of(tile_ref, chain_ref, rows, cols)
     for cycle, lanes in enumerate(cycles):
         projected = jnp.dot(w_t, normed_ref[:, lanes], preferred_element_type=jnp.float32)
         sides = []
@@ -133,7 +134,7 @@
             line = (cycle * groups + group) * 2 * own
             message_ref[:, line : line + 2 * own, :] = both[:, :, group * LANES : (group + 1) * LANES]
         gate_ref[:, lanes] = 0.5 * jnp.tanh(projected[4 * hidden :]) + 0.5
-    for copy in copies[4:6]:
+    for copy in copies[5:]:
         copy.wait()
     w_out_ref[...] = transpose(w_out[...]).astype(jnp.bfloat16)
     gain_mid_ref[...] = jnp.broadcast_to(column(gain_mid[...]), gain_mid_ref.shape)
@@ -149,7 +150,9 @@
         for cycle in range(cycles):
             base = cycle * groups
             held = [
-                message_ref[peer * halves + half, (base + group) * 2 * own : (base + group + 1) * 2 * own, :]
+                message_ref[
+                    peer * halves + half, (base + group) * 2 * own : (base + group + 1) * 2 * own, :
+                ].astype(jnp.float32)
                 for group in range(groups)
             ]
             for token in range(tokens):
@@ -161,7 +164,7 @@
                         value = jnp.where(lane >= off, value, held[group + 1])
                     if off:
                         value = pltpu.roll(value, LANES - off, axis=1)
-                    spread_ref[chunk, k * 2 * own : (k + 1) * 2 * own, :] = value.astype(jnp.float32)
+                    spread_ref[chunk, k * 2 * own : (k + 1) * 2 * own, :] = value
 
 
 def pack(spread_ref, at, own, cols):
@@ -263,6 +266,10 @@
         copy.wait()
 
 
+def in_hbm(value):
+    return pltpu.with_memory_space_constraint(value, pltpu.HBM)
+
+
 def on_device(shares, halves, pair, tile_mask, chain_ids, gain_in, w_proj, gain_mid, w_out):
     rows, cols, width = pair.shape
     hidden = w_out.shape[0]
@@ -294,23 +301,18 @@
             pltpu.VMEM((1, hidden), jnp.float32),
             pltpu.VMEM(w_out.shape, jnp.bfloat16),
             pltpu.VMEM((width, positions), jnp.bfloat16),
-            pltpu.SemaphoreType.DMA((6 + groups // cycle_of(cols)[1],)),
+            pltpu.SemaphoreType.DMA((7,)),
         ],
         compiler_params=params,
         name="project",
     )(
-        *[
-            pltpu.with_memory_space_constraint(value, pltpu.HBM)
-            for value in (
-                tile_mask,
-                chain_ids[None, :],
-                pair.reshape(positions, width),
-                gain_in[None, :],
-                w_proj,
-                gain_mid[None, :],
-                w_out,
-            )
-        ]
+        in_hbm(tile_mask),
+        in_hbm(chain_ids[None, :]),
+        in_hbm(pair.reshape(positions, width)),
+        in_hbm(gain_in[None, :]),
+        in_hbm(w_proj),
+        in_hbm(gain_mid[None, :]),
+        in_hbm(w_out),
     )
     message = lax.all_to_all(
         message,

time: 42.3 us -> 42.2 us (level)
  no operation moved by 1% of the time
where the time goes in v21:
time: 42.2 us; the launch traced here: 42 us
  blocking collectives  36.9 us (87%)
  Pallas kernels  5.14 us (12%)
    all_to_all x1, blocking collectives, on_device(): lax.all_to_all(mixed.reshape(halves * shares, lines, LANES), ('row', 'col...  19.5 us
    all_to_all x1, blocking collectives, on_device(): lax.all_to_all(message, ('row', 'col'), split_axis=0, concat_axis=0, axis...  17.3 us
    pallas_call x1, Pallas kernels, on_device(): pl.pallas_call(functools.partial(project_kernel, rows, cols), out_shape=(...  2.72 us
    pallas_call x1, Pallas kernels, on_device(): pl.pallas_call(functools.partial(triangle_kernel, own, cols, shares), out...  1.27 us
    pallas_call x1, Pallas kernels, on_device(): pl.pallas_call(functools.partial(output_kernel, own, PARTS), out_shape=ja...  1.14 us

profile of v21, /device:TPU:0, one launch (start us, length us, event | category | flops | bytes accessed | tf_op | source)
XLA Modules:
  0.0 42.0 jit_solution(6926386881378134682)
XLA Ops:
  0.0 2.7 %project.1 = (bf16[16,144,128]{2,1,0:T(8,128)(2,1)S(1)}, f32[128,1152]{1,0:T(8,128)S(1)}, bf16[128,128]{1,0:T(8,128)(2,1)S(1)}, f32[128,128]{1,0:T(8,128)S(1)}) custom-call(s32[2,2]{1,0:T(2,128)} %tile_hbm.1, s32[1,192]{1,0:T(1,128)} %bitcast.10, bf16[1152,128]{1,0:T(8,128)(2,1)} %bitcast.9, f32[1,128]{1,0:T(1,128)} %bitcast.11, bf16[128,640]{1,0:T(8,128)(2,1)} %w_hbm.1, ...), custom_call_target="tpu_custom_call" | custom-call | tf_op jit(solution)/shard_map/project/pallas_call | solution.py:285
  2.7 17.3 %all_to_all.10.message_ref = bf16[16,144,128]{2,1,0:T(8,128)(2,1)S(1)} all-to-all(bf16[16,144,128]{2,1,0:T(8,128)(2,1)S(1)} %get-tuple-element.9), channel_id=1, replica_groups={{0,1,2,3,4,5,6,7,8,9,10,11,12,13,14,15},{16,17,18,19,20,21,22,23,24,25,..., dimensions={0} | all-to-all | bytes 1179648 | tf_op jit(solution)/shard_map/all_to_all | solution.py:317
  20.1 1.3 %triangle.1 = bf16[2304,128]{1,0:T(8,128)(2,1)S(1)} custom-call(bf16[16,144,128]{2,1,0:T(8,128)(2,1)S(1)} %all_to_all.10.message_ref), custom_call_target="tpu_custom_call" | custom-call | tf_op jit(solution)/shard_map/triangle/pallas_call | solution.py:331
  21.4 19.5 %all_to_all.11 = bf16[32,72,128]{2,1,0:T(8,128)(2,1)S(1)} all-to-all(bf16[32,72,128]{2,1,0:T(8,128)(2,1)S(1)} %bitcast.8), channel_id=1, replica_groups=mesh['grp'=1,'row'=16,'col'=2] {'row','col'}, dimensions={0} | all-to-all | bytes 1179648 | tf_op jit(solution)/shard_map/all_to_all | solution.py:346
  40.9 1.1 %output.1 = bf16[1152,128]{1,0:T(8,128)(2,1)} custom-call(bf16[2304,128]{1,0:T(8,128)(2,1)S(1)} %bitcast.7, f32[128,1152]{1,0:T(8,128)S(1)} %get-tuple-element.10.gate_ref, f32[128,128]{1,0:T(8,128)S(1)} %get-tuple-element.11.gain_ref, bf16[128,128]{1,0:T(8,128)(2,1)S(1)} %get-tuple-element.12.w_t_ref), custom_call_target="tpu_custom_call" | custom-call | tf_op jit(solution)/shard_map/output/pallas_call | solution.py:353

commit v22 on v18

--- a/solution.py
+++ b/solution.py
@@ -83,8 +83,8 @@
 
 
 def project_kernel(
-    rows, cols, tile_hbm, chain_hbm, pair_hbm, gain_hbm, w_hbm, message_ref, gate_ref,
-    tile_ref, chain_ref, pair_ref, gain_ref, w_ref, normed_ref, sems,
+    rows, cols, tile_hbm, chain_hbm, pair_hbm, gain_hbm, w_hbm, w_out_hbm, message_ref, gate_ref, w_out_ref,
+    tile_ref, chain_ref, pair_ref, gain_ref, w_ref, w_out, normed_ref, sems,
 ):
     hidden = (w_ref.shape[1] - w_ref.shape[0]) // 4
     peers = message_ref.shape[0]
@@ -99,6 +99,7 @@
         (gain_hbm, gain_ref),
         (pair_hbm, pair_ref),
         (w_hbm, w_ref),
+        (w_out_hbm, w_out),
     )
     for copy in copies[:3]:
         copy.wait()
@@ -130,6 +131,8 @@
             line = (cycle * groups + group) * 2 * own
             message_ref[:, line : line + 2 * own, :] = both[:, :, group * LANES : (group + 1) * LANES]
         gate_ref[:, lanes] = 0.5 * jnp.tanh(projected[4 * hidden :]) + 0.5
+    copies[5].wait()
+    w_out_ref[...] = transpose(w_out[...]).astype(jnp.bfloat16)
 
 
 def unpack(message_ref, half, halves, spread_ref, own, cols):
@@ -189,10 +192,9 @@
 
 
 def triangle_kernel(
-    own, cols, shares, message_ref, gain_hbm, w_out_hbm, mixed_ref, gain_ref, w_out_ref,
-    spread, left, left_t, right, mixed, gain, w_out, sems,
+    own, cols, shares, message_ref, gain_ref, mixed_ref, column_ref, spread, left, left_t, right, mixed
 ):
-    copies = start_copies(sems, (gain_hbm, gain), (w_out_hbm, w_out))
+    column_ref[...] = jnp.broadcast_to(column(gain_ref[...]), column_ref.shape)
     halves, chunks = spread.shape[:2]
     width = chunks * LANES
     deep = right.shape[1]
@@ -234,10 +236,6 @@
             for cycle in range(cycles):
                 lines += pack(mixed.at[i_half, j_half], peer * cycles + cycle, own, cols)
         mixed_ref[share * each : (share + 1) * each, :] = jnp.concatenate(lines, axis=0).astype(jnp.bfloat16)
-    for copy in copies:
-        copy.wait()
-    gain_ref[...] = jnp.broadcast_to(column(gain[...]), gain_ref.shape)
-    w_out_ref[...] = transpose(w_out[...]).astype(jnp.bfloat16)
 
 
 def output_kernel(own, parts, mixed_ref, gate_ref, gain_ref, w_t_ref, update_hbm, mixed, update, sems):
@@ -282,22 +280,25 @@
     params = pltpu.CompilerParams(vmem_limit_bytes=VMEM_BYTES)
     tokens = chain_ids.shape[0]
     message = jax.ShapeDtypeStruct((peers * halves, 2 * lines, LANES), jnp.bfloat16)
-    message, gate = pl.pallas_call(
+    gain_mid = lax.ppermute(gain_mid, "col", [(half, (half + 1) % halves) for half in range(halves)])
+    message, gate, w_out_t = pl.pallas_call(
         functools.partial(project_kernel, rows, cols),
         out_shape=(
             message,
             jax.ShapeDtypeStruct((width, positions), jnp.float32),
+            jax.ShapeDtypeStruct(w_out.shape[::-1], jnp.bfloat16),
         ),
-        in_specs=[HBM] * 5,
-        out_specs=[VMEM] * 2,
+        in_specs=[HBM] * 6,
+        out_specs=[VMEM] * 3,
         scratch_shapes=[
             pltpu.SMEM(tile_mask.shape, jnp.int32),
             pltpu.VMEM((1, tokens), jnp.int32),
             pltpu.VMEM((positions, width), jnp.bfloat16),
             pltpu.VMEM((1, width), jnp.float32),
             pltpu.VMEM(w_proj.shape, jnp.bfloat16),
+            pltpu.VMEM(w_out.shape, jnp.bfloat16),
             pltpu.VMEM((width, positions), jnp.bfloat16),
-            pltpu.SemaphoreType.DMA((5,)),
+            pltpu.SemaphoreType.DMA((6,)),
         ],
         compiler_params=params,
         name="project",
@@ -307,7 +308,9 @@
         in_hbm(pair.reshape(positions, width)),
         in_hbm(gain_in[None, :]),
         in_hbm(w_proj),
-    )
+        in_hbm(w_out),
+    )
+    message, gain_mid = lax.optimization_barrier((message, gain_mid))
     message = lax.all_to_all(
         message,
         ("row", "col"),
@@ -322,28 +325,24 @@
     chunks = pl.cdiv(cols, LANES)
     depth = peers * rows
     deep = pl.cdiv(depth, LANES) * LANES
-    mixed, gain, w_out_t = pl.pallas_call(
+    mixed, gain = pl.pallas_call(
         functools.partial(triangle_kernel, own, cols, shares),
         out_shape=(
             jax.ShapeDtypeStruct((halves * shares * lines, LANES), jnp.bfloat16),
             jax.ShapeDtypeStruct((hidden, LANES), jnp.float32),
-            jax.ShapeDtypeStruct(w_out.shape[::-1], jnp.bfloat16),
         ),
-        in_specs=[VMEM, HBM, HBM],
-        out_specs=[VMEM] * 3,
+        in_specs=[VMEM, VMEM],
+        out_specs=[VMEM, VMEM],
         scratch_shapes=[
             pltpu.VMEM((halves, chunks, depth * 2 * own, LANES), jnp.float32),
             pltpu.VMEM((own, halves * deep, chunks * LANES), jnp.bfloat16),
             pltpu.VMEM((own, halves * cols, deep), jnp.bfloat16),
             pltpu.VMEM((own, deep, halves * chunks * LANES), jnp.bfloat16),
             pltpu.VMEM((halves, halves, chunks, cols * own, LANES), jnp.float32),
-            pltpu.VMEM((1, hidden), jnp.float32),
-            pltpu.VMEM(w_out.shape, jnp.bfloat16),
-            pltpu.SemaphoreType.DMA((2,)),
         ],
         compiler_params=params,
         name="triangle",
-    )(message, in_hbm(gain_mid[None, :]), in_hbm(w_out))
+    )(message, gain_mid[None, :])
     mixed = lax.all_to_all(
         mixed.reshape(halves * shares, lines, LANES),
         ("row", "col"),

time: 41.9 us -> 42.1 us (level)
  starting transfers between devices: 0 us -> 0.45 us
    ppermute x0 -> x1, starting transfers between devices: none -> 0.45 us  [on_device(): lax.ppermute(gain_mid, 'col', [(half, (half + 1) % halves) for half in ra...]
  transfers between devices with their start and end apart: 0 -> 1, of which waited for: 0 -> 0; matrix products, arithmetic and copies ran while one was open for 0% -> 0% of each run, Pallas kernels for 0% -> 6%
where the time goes in v22:
time: 42.1 us; the launch traced here: 41.9 us
  blocking collectives  36.5 us (87%)
  Pallas kernels  4.86 us (12%)
  starting transfers between devices  0.45 us (1%)
    all_to_all x1, blocking collectives, on_device(): lax.all_to_all(mixed.reshape(halves * shares, lines, LANES), ('row', 'col...  19.5 us
    all_to_all x1, blocking collectives, on_device(): lax.all_to_all(message, ('row', 'col'), split_axis=0, concat_axis=0, axis...  17 us
    pallas_call x1, Pallas kernels, on_device(): pl.pallas_call(functools.partial(project_kernel, rows, cols), out_shape=(...  2.42 us
    pallas_call x1, Pallas kernels, on_device(): pl.pallas_call(functools.partial(triangle_kernel, own, cols, shares), out...  1.3 us
    pallas_call x1, Pallas kernels, on_device(): pl.pallas_call(functools.partial(output_kernel, own, PARTS), out_shape=ja...  1.14 us
  transfers between devices with their start and end apart: 1, of which 0 were waited for; matrix products, arithmetic and copies ran while one was open for 0% of the time, Pallas kernels for 6%

profile of v22, /device:TPU:0, one launch (start us, length us, event | category | flops | bytes accessed | tf_op | source)
XLA Modules:
  0.0 41.9 jit_solution(8663168965941574545)
XLA Ops:
  0.0 0.5 %collective-permute-start = (f32[128]{0:T(128)}, f32[128]{0:T(128)S(1)}, u32[]{:S(2)}, u32[]{:S(2)}) collective-permute-start(f32[128]{0:T(128)} %param.12), channel_id=1, source_target_pairs={{0,1},{1,0},{2,3},{3,2},{4,5},{5,4},{6,7},{7,6},{8,9},{9,8},{10,11... | collective-permute-start | bytes 1544 | tf_op jit(solution)/shard_map/ppermute | solution.py:283
  0.5 2.4 %project.1 = (bf16[16,144,128]{2,1,0:T(8,128)(2,1)S(1)}, f32[128,1152]{1,0:T(8,128)S(1)}, bf16[128,128]{1,0:T(8,128)(2,1)S(1)}) custom-call(s32[2,2]{1,0:T(2,128)} %tile_hbm.1, s32[1,192]{1,0:T(1,128)} %bitcast.11, bf16[1152,128]{1,0:T(8,128)(2,1)} %bitcast.10, f32[1,128]{1,0:T(1,128)} %bitcast.12, bf16[128,640]{1,0:T(8,128)(2,1)} %w_hbm.1, ...), custom_call_target="tpu_custom_call" | custom-call | tf_op jit(solution)/shard_map/project/pallas_call | solution.py:284
  2.9 0.0 collective-permute-done
  2.9 17.0 %all_to_all.10.message_ref = bf16[16,144,128]{2,1,0:T(8,128)(2,1)S(1)} all-to-all(bf16[16,144,128]{2,1,0:T(8,128)(2,1)S(1)} %get-tuple-element.13), channel_id=1, replica_groups={{0,1,2,3,4,5,6,7,8,9,10,11,12,13,14,15},{16,17,18,19,20,21,22,23,24,25,..., dimensions={0} | all-to-all | bytes 1179648 | tf_op jit(solution)/shard_map/all_to_all | solution.py:314
  19.9 1.3 %triangle.1 = (bf16[2304,128]{1,0:T(8,128)(2,1)S(1)}, f32[128,128]{1,0:T(8,128)S(1)}) custom-call(bf16[16,144,128]{2,1,0:T(8,128)(2,1)S(1)} %all_to_all.10.message_ref, f32[1,128]{1,0:T(1,128)S(1)} %bitcast.9), custom_call_target="tpu_custom_call" | custom-call | tf_op jit(solution)/shard_map/triangle/pallas_call | solution.py:328
  21.2 19.5 %all_to_all.11 = bf16[32,72,128]{2,1,0:T(8,128)(2,1)S(1)} all-to-all(bf16[32,72,128]{2,1,0:T(8,128)(2,1)S(1)} %bitcast.8), channel_id=1, replica_groups=mesh['grp'=1,'row'=16,'col'=2] {'row','col'}, dimensions={0} | all-to-all | bytes 1179648 | tf_op jit(solution)/shard_map/all_to_all | solution.py:346
  40.7 1.1 %output.1 = bf16[1152,128]{1,0:T(8,128)(2,1)} custom-call(bf16[2304,128]{1,0:T(8,128)(2,1)S(1)} %bitcast.7, f32[128,1152]{1,0:T(8,128)S(1)} %get-tuple-element.16.gate_ref, f32[128,128]{1,0:T(8,128)S(1)} %get-tuple-element.17.gain_ref, bf16[128,128]{1,0:T(8,128)(2,1)S(1)} %get-tuple-element.18.w_t_ref), custom_call_target="tpu_custom_call" | custom-call | tf_op jit(solution)/shard_map/output/pallas_call | solution.py:353
Async XLA Ops:
  0.0 2.9 %collective-permute-start = (f32[128]{0:T(128)}, f32[128]{0:T(128)S(1)}, u32[]{:S(2)}, u32[]{:S(2)}) collective-permute-start(f32[128]{0:T(128)} %param.12), channel_id=1, source_target_pairs={{0,1},{1,0},{2,3},{3,2},{4,5},{5,4},{6,7},{7,6},{8,9},{9,8},{10,11... | collective-permute-start | bytes 1544 | tf_op jit(solution)/shard_map/ppermute | solution.py:283

commit v23 on v21

--- a/solution.py
+++ b/solution.py
@@ -95,17 +95,19 @@
     cycles = [slice(start, start + size) for start in range(0, rows * cols, size)]
     copies = start_copies(
         sems,
+        (chain_hbm, chain_ref),
+        (tile_hbm, tile_ref),
+        (gain_hbm, gain_ref),
         (pair_hbm, pair_ref),
         (w_hbm, w_ref),
-        (gain_hbm, gain_ref),
-        (chain_hbm, chain_ref),
-        (tile_hbm, tile_ref),
         (gain_mid_hbm, gain_mid),
         (w_out_hbm, w_out),
     )
-    copies[0].wait()
-    blocks = [transpose(pair_ref[lanes, :]) for lanes in cycles]
-    copies[1].wait()
+    for copy in copies[:3]:
+        copy.wait()
+    keep = keep_of(tile_ref, chain_ref, rows, cols)
+    gain = column(gain_ref[...])
+    copies[4].wait()
     w_t = jnp.concatenate(
         [
             0.5 * transpose(w_ref[:, start : start + LANES])
@@ -113,15 +115,12 @@
         ],
         axis=0,
     ).astype(jnp.bfloat16)
-    copies[2].wait()
-    gain = column(gain_ref[...])
-    for lanes, block in zip(cycles, blocks):
+    copies[3].wait()
+    for lanes in cycles:
+        block = transpose(pair_ref[lanes, :])
         center = block - jnp.mean(block, axis=0, keepdims=True)
         spread = jnp.mean(center * center, axis=0, keepdims=True)
         normed_ref[:, lanes] = (center * lax.rsqrt(spread + EPS) * gain).astype(jnp.bfloat16)
-    copies[3].wait()
-    copies[4].wait()
-    keep = keep_of(tile_ref, chain_ref, rows, cols)
     for cycle, lanes in enumerate(cycles):
         projected = jnp.dot(w_t, normed_ref[:, lanes], preferred_element_type=jnp.float32)
         sides = []
@@ -136,8 +135,8 @@
         gate_ref[:, lanes] = 0.5 * jnp.tanh(projected[4 * hidden :]) + 0.5
     for copy in copies[5:]:
         copy.wait()
+    gain_mid_ref[...] = jnp.broadcast_to(column(gain_mid[...]), gain_mid_ref.shape)
     w_out_ref[...] = transpose(w_out[...]).astype(jnp.bfloat16)
-    gain_mid_ref[...] = jnp.broadcast_to(column(gain_mid[...]), gain_mid_ref.shape)
 
 
 def unpack(message_ref, half, halves, spread_ref, own, cols):
@@ -196,31 +195,29 @@
     ).astype(jnp.bfloat16)
 
 
-def triangle_kernel(own, cols, shares, message_ref, mixed_ref, spread, left, left_t, right, mixed):
+def triangle_kernel(own, cols, shares, message_ref, mixed_ref, spread, left_t, mixed):
     halves, chunks = spread.shape[:2]
     width = chunks * LANES
-    deep = right.shape[1]
     depth = spread.shape[2] // (2 * own)
+    deep = left_t.shape[2]
     one = identity(cols, width)
-    if depth < deep:
-        right[:, depth:, :] = jnp.zeros((own, deep - depth, halves * width), jnp.bfloat16)
+    padding = [jnp.zeros((deep - depth, width), jnp.bfloat16)] if depth < deep else []
     for half in range(halves):
         unpack(message_ref, half, halves, spread.at[half], own, cols)
-        if depth < deep:
-            left[:, half * deep + depth : (half + 1) * deep, :] = jnp.zeros((own, deep - depth, width), jnp.bfloat16)
-        for channel in range(own):
-            left[channel, half * deep : half * deep + depth, :] = channel_of(spread.at[half], channel, 2 * own)
-            right[channel, :depth, half * width : (half + 1) * width] = channel_of(
-                spread.at[half], own + channel, 2 * own
-            )
+
+    def operand(channel, half):
+        return jnp.concatenate([channel_of(spread.at[half], channel, 2 * own)] + padding, axis=0)
+
     for channel in range(own):
+        left = jnp.concatenate([operand(channel, half) for half in range(halves)], axis=0)
         both = lax.dot_general(
-            one, left[channel], (((1,), (1,)), ((), ())), preferred_element_type=jnp.float32
+            one, left, (((1,), (1,)), ((), ())), preferred_element_type=jnp.float32
         ).astype(jnp.bfloat16)
         for half in range(halves):
             left_t[channel, half * cols : (half + 1) * cols, :] = both[:, half * deep : (half + 1) * deep]
     for channel in range(own):
-        total = jnp.dot(left_t[channel], right[channel], preferred_element_type=jnp.float32)
+        right = jnp.concatenate([operand(own + channel, half) for half in range(halves)], axis=1)
+        total = jnp.dot(left_t[channel], right, preferred_element_type=jnp.float32)
         for i_half in range(halves):
             for j_half in range(halves):
                 for chunk in range(chunks):
@@ -335,9 +332,7 @@
         out_specs=VMEM,
         scratch_shapes=[
             pltpu.VMEM((halves, chunks, depth * 2 * own, LANES), jnp.float32),
-            pltpu.VMEM((own, halves * deep, chunks * LANES), jnp.bfloat16),
             pltpu.VMEM((own, halves * cols, deep), jnp.bfloat16),
-            pltpu.VMEM((own, deep, halves * chunks * LANES), jnp.bfloat16),
             pltpu.VMEM((halves, halves, chunks, cols * own, LANES), jnp.float32),
         ],
         compiler_params=params,

time: 42.2 us -> 41.9 us (level)
  no operation moved by 1% of the time
where the time goes in v23:
time: 41.9 us; the launch traced here: 41.7 us
  blocking collectives  36.9 us (88%)
  Pallas kernels  4.79 us (11%)
    all_to_all x1, blocking collectives, on_device(): lax.all_to_all(mixed.reshape(halves * shares, lines, LANES), ('row', 'col...  19.5 us
    all_to_all x1, blocking collectives, on_device(): lax.all_to_all(message, ('row', 'col'), split_axis=0, concat_axis=0, axis...  17.3 us
    pallas_call x1, Pallas kernels, on_device(): pl.pallas_call(functools.partial(project_kernel, rows, cols), out_shape=(...  2.47 us
    pallas_call x1, Pallas kernels, on_device(): pl.pallas_call(functools.partial(triangle_kernel, own, cols, shares), out...  1.18 us
    pallas_call x1, Pallas kernels, on_device(): pl.pallas_call(functools.partial(output_kernel, own, PARTS), out_shape=ja...  1.14 us

profile of v23, /device:TPU:0, one launch (start us, length us, event | category | flops | bytes accessed | tf_op | source)
XLA Modules:
  0.0 41.7 jit_solution(6725769439911328975)
XLA Ops:
  0.0 2.5 %project.1 = (bf16[16,144,128]{2,1,0:T(8,128)(2,1)S(1)}, f32[128,1152]{1,0:T(8,128)S(1)}, bf16[128,128]{1,0:T(8,128)(2,1)S(1)}, f32[128,128]{1,0:T(8,128)S(1)}) custom-call(s32[2,2]{1,0:T(2,128)} %tile_hbm.1, s32[1,192]{1,0:T(1,128)} %bitcast.10, bf16[1152,128]{1,0:T(8,128)(2,1)} %bitcast.9, f32[1,128]{1,0:T(1,128)} %bitcast.11, bf16[128,640]{1,0:T(8,128)(2,1)} %w_hbm.1, ...), custom_call_target="tpu_custom_call" | custom-call | tf_op jit(solution)/shard_map/project/pallas_call | solution.py:282
  2.5 17.3 %all_to_all.10.message_ref = bf16[16,144,128]{2,1,0:T(8,128)(2,1)S(1)} all-to-all(bf16[16,144,128]{2,1,0:T(8,128)(2,1)S(1)} %get-tuple-element.9), channel_id=1, replica_groups={{0,1,2,3,4,5,6,7,8,9,10,11,12,13,14,15},{16,17,18,19,20,21,22,23,24,25,..., dimensions={0} | all-to-all | bytes 1179648 | tf_op jit(solution)/shard_map/all_to_all | solution.py:314
  19.8 1.2 %triangle.1 = bf16[2304,128]{1,0:T(8,128)(2,1)S(1)} custom-call(bf16[16,144,128]{2,1,0:T(8,128)(2,1)S(1)} %all_to_all.10.message_ref), custom_call_target="tpu_custom_call" | custom-call | tf_op jit(solution)/shard_map/triangle/pallas_call | solution.py:328
  21.0 19.5 %all_to_all.11 = bf16[32,72,128]{2,1,0:T(8,128)(2,1)S(1)} all-to-all(bf16[32,72,128]{2,1,0:T(8,128)(2,1)S(1)} %bitcast.8), channel_id=1, replica_groups=mesh['grp'=1,'row'=16,'col'=2] {'row','col'}, dimensions={0} | all-to-all | bytes 1179648 | tf_op jit(solution)/shard_map/all_to_all | solution.py:341
  40.5 1.1 %output.1 = bf16[1152,128]{1,0:T(8,128)(2,1)} custom-call(bf16[2304,128]{1,0:T(8,128)(2,1)S(1)} %bitcast.7, f32[128,1152]{1,0:T(8,128)S(1)} %get-tuple-element.10.gate_ref, f32[128,128]{1,0:T(8,128)S(1)} %get-tuple-element.11.gain_ref, bf16[128,128]{1,0:T(8,128)(2,1)S(1)} %get-tuple-element.12.w_t_ref), custom_call_target="tpu_custom_call" | custom-call | tf_op jit(solution)/shard_map/output/pallas_call | solution.py:348

commit v24 on v23

--- a/solution.py
+++ b/solution.py
@@ -108,19 +108,17 @@
     keep = keep_of(tile_ref, chain_ref, rows, cols)
     gain = column(gain_ref[...])
     copies[4].wait()
-    w_t = jnp.concatenate(
-        [
-            0.5 * transpose(w_ref[:, start : start + LANES])
-            for start in range(0, w_ref.shape[1], LANES)
-        ],
-        axis=0,
-    ).astype(jnp.bfloat16)
+    w_t = (w_ref[...] * 0.5).T
     copies[3].wait()
     for lanes in cycles:
         block = transpose(pair_ref[lanes, :])
         center = block - jnp.mean(block, axis=0, keepdims=True)
         spread = jnp.mean(center * center, axis=0, keepdims=True)
         normed_ref[:, lanes] = (center * lax.rsqrt(spread + EPS) * gain).astype(jnp.bfloat16)
+    for copy in copies[5:]:
+        copy.wait()
+    gain_mid_ref[...] = jnp.broadcast_to(column(gain_mid[...]), gain_mid_ref.shape)
+    w_out_ref[...] = w_out[...].T
     for cycle, lanes in enumerate(cycles):
         projected = jnp.dot(w_t, normed_ref[:, lanes], preferred_element_type=jnp.float32)
         sides = []
@@ -133,10 +131,6 @@
             line = (cycle * groups + group) * 2 * own
             message_ref[:, line : line + 2 * own, :] = both[:, :, group * LANES : (group + 1) * LANES]
         gate_ref[:, lanes] = 0.5 * jnp.tanh(projected[4 * hidden :]) + 0.5
-    for copy in copies[5:]:
-        copy.wait()
-    gain_mid_ref[...] = jnp.broadcast_to(column(gain_mid[...]), gain_mid_ref.shape)
-    w_out_ref[...] = transpose(w_out[...]).astype(jnp.bfloat16)
 
 
 def unpack(message_ref, half, halves, spread_ref, own, cols):

time: 41.9 us -> 41.7 us (level)
  no operation moved by 1% of the time
where the time goes in v24:
time: 41.7 us; the launch traced here: 41.5 us
  blocking collectives  36.9 us (88%)
  Pallas kernels  4.61 us (11%)
    all_to_all x1, blocking collectives, on_device(): lax.all_to_all(mixed.reshape(halves * shares, lines, LANES), ('row', 'col...  19.5 us
    all_to_all x1, blocking collectives, on_device(): lax.all_to_all(message, ('row', 'col'), split_axis=0, concat_axis=0, axis...  17.3 us
    pallas_call x1, Pallas kernels, on_device(): pl.pallas_call(functools.partial(project_kernel, rows, cols), out_shape=(...  2.29 us
    pallas_call x1, Pallas kernels, on_device(): pl.pallas_call(functools.partial(triangle_kernel, own, cols, shares), out...  1.18 us
    pallas_call x1, Pallas kernels, on_device(): pl.pallas_call(functools.partial(output_kernel, own, PARTS), out_shape=ja...  1.14 us

profile of v24, /device:TPU:0, one launch (start us, length us, event | category | flops | bytes accessed | tf_op | source)
XLA Modules:
  0.0 41.5 jit_solution(16862362790682025158)
XLA Ops:
  0.0 2.3 %project.1 = (bf16[16,144,128]{2,1,0:T(8,128)(2,1)S(1)}, f32[128,1152]{1,0:T(8,128)S(1)}, bf16[128,128]{1,0:T(8,128)(2,1)S(1)}, f32[128,128]{1,0:T(8,128)S(1)}) custom-call(s32[2,2]{1,0:T(2,128)} %tile_hbm.1, s32[1,192]{1,0:T(1,128)} %bitcast.10, bf16[1152,128]{1,0:T(8,128)(2,1)} %bitcast.9, f32[1,128]{1,0:T(1,128)} %bitcast.11, bf16[128,640]{1,0:T(8,128)(2,1)} %w_hbm.1, ...), custom_call_target="tpu_custom_call" | custom-call | tf_op jit(solution)/shard_map/project/pallas_call | solution.py:276
  2.3 17.3 %all_to_all.10.message_ref = bf16[16,144,128]{2,1,0:T(8,128)(2,1)S(1)} all-to-all(bf16[16,144,128]{2,1,0:T(8,128)(2,1)S(1)} %get-tuple-element.9), channel_id=1, replica_groups={{0,1,2,3,4,5,6,7,8,9,10,11,12,13,14,15},{16,17,18,19,20,21,22,23,24,25,..., dimensions={0} | all-to-all | bytes 1179648 | tf_op jit(solution)/shard_map/all_to_all | solution.py:308
  19.6 1.2 %triangle.1 = bf16[2304,128]{1,0:T(8,128)(2,1)S(1)} custom-call(bf16[16,144,128]{2,1,0:T(8,128)(2,1)S(1)} %all_to_all.10.message_ref), custom_call_target="tpu_custom_call" | custom-call | tf_op jit(solution)/shard_map/triangle/pallas_call | solution.py:322
  20.8 19.5 %all_to_all.11 = bf16[32,72,128]{2,1,0:T(8,128)(2,1)S(1)} all-to-all(bf16[32,72,128]{2,1,0:T(8,128)(2,1)S(1)} %bitcast.8), channel_id=1, replica_groups=mesh['grp'=1,'row'=16,'col'=2] {'row','col'}, dimensions={0} | all-to-all | bytes 1179648 | tf_op jit(solution)/shard_map/all_to_all | solution.py:335
  40.4 1.1 %output.1 = bf16[1152,128]{1,0:T(8,128)(2,1)} custom-call(bf16[2304,128]{1,0:T(8,128)(2,1)S(1)} %bitcast.7, f32[128,1152]{1,0:T(8,128)S(1)} %get-tuple-element.10.gate_ref, f32[128,128]{1,0:T(8,128)S(1)} %get-tuple-element.11.gain_ref, bf16[128,128]{1,0:T(8,128)(2,1)S(1)} %get-tuple-element.12.w_t_ref), custom_call_target="tpu_custom_call" | custom-call | tf_op jit(solution)/shard_map/output/pallas_call | solution.py:342

commit v25 on v24

--- a/solution.py
+++ b/solution.py
@@ -237,22 +237,24 @@
     mixed[...] = mixed_ref[...].astype(jnp.float32).reshape(mixed.shape)
     groups = lines // own
     steps = math.gcd(groups, 3)
+    each = groups // steps
     leaving = []
-    for group in range(groups):
-        sums = mixed[:members, group * own : (group + 1) * own, :]
-        for part in range(1, parts):
-            sums += mixed[part * members : (part + 1) * members, group * own : (group + 1) * own, :]
-        block = sums.reshape(members * own, LANES)
+    for step in range(steps):
+        blocks = []
+        for group in range(step * each, (step + 1) * each):
+            sums = mixed[:members, group * own : (group + 1) * own, :]
+            for part in range(1, parts):
+                sums += mixed[part * members : (part + 1) * members, group * own : (group + 1) * own, :]
+            blocks.append(sums.reshape(members * own, LANES))
+        block = jnp.concatenate(blocks, axis=1)
         center = block - jnp.mean(block, axis=0, keepdims=True)
         spread = jnp.mean(center * center, axis=0, keepdims=True)
-        normed = (center * lax.rsqrt(spread + EPS) * gain_ref[...]).astype(jnp.bfloat16)
+        gain = jnp.concatenate([gain_ref[...]] * each, axis=1)
+        normed = (center * lax.rsqrt(spread + EPS) * gain).astype(jnp.bfloat16)
         projected = jnp.dot(w_t_ref[...], normed, preferred_element_type=jnp.float32)
-        lanes = slice(group * LANES, (group + 1) * LANES)
+        lanes = slice(step * each * LANES, (step + 1) * each * LANES)
         update[lanes, :] = (gate_ref[:, lanes] * projected).T.astype(jnp.bfloat16)
-        step, last = divmod((group + 1) * steps, groups)
-        if last == 0:
-            done = slice((step - 1) * (groups // steps) * LANES, (group + 1) * LANES)
-            leaving += start_copies(sems.at[step - 1], (update.at[done, :], update_hbm.at[done, :]))
+        leaving += start_copies(sems.at[step], (update.at[lanes, :], update_hbm.at[lanes, :]))
     for copy in leaving:
         copy.wait()
 

time: 41.7 us -> 41.7 us (level)
  no operation moved by 1% of the time
where the time goes in v25:
time: 41.7 us; the launch traced here: 41.5 us
  blocking collectives  36.9 us (88%)
  Pallas kernels  4.62 us (11%)
    all_to_all x1, blocking collectives, on_device(): lax.all_to_all(mixed.reshape(halves * shares, lines, LANES), ('row', 'col...  19.5 us
    all_to_all x1, blocking collectives, on_device(): lax.all_to_all(message, ('row', 'col'), split_axis=0, concat_axis=0, axis...  17.3 us
    pallas_call x1, Pallas kernels, on_device(): pl.pallas_call(functools.partial(project_kernel, rows, cols), out_shape=(...  2.29 us
    pallas_call x1, Pallas kernels, on_device(): pl.pallas_call(functools.partial(triangle_kernel, own, cols, shares), out...  1.18 us
    pallas_call x1, Pallas kernels, on_device(): pl.pallas_call(functools.partial(output_kernel, own, PARTS), out_shape=ja...  1.15 us

profile of v25, /device:TPU:0, one launch (start us, length us, event | category | flops | bytes accessed | tf_op | source)
XLA Modules:
  0.0 41.5 jit_solution(17601794753112966296)
XLA Ops:
  0.0 2.3 %project.1 = (bf16[16,144,128]{2,1,0:T(8,128)(2,1)S(1)}, f32[128,1152]{1,0:T(8,128)S(1)}, bf16[128,128]{1,0:T(8,128)(2,1)S(1)}, f32[128,128]{1,0:T(8,128)S(1)}) custom-call(s32[2,2]{1,0:T(2,128)} %tile_hbm.1, s32[1,192]{1,0:T(1,128)} %bitcast.10, bf16[1152,128]{1,0:T(8,128)(2,1)} %bitcast.9, f32[1,128]{1,0:T(1,128)} %bitcast.11, bf16[128,640]{1,0:T(8,128)(2,1)} %w_hbm.1, ...), custom_call_target="tpu_custom_call" | custom-call | tf_op jit(solution)/shard_map/project/pallas_call | solution.py:278
  2.3 17.3 %all_to_all.10.message_ref = bf16[16,144,128]{2,1,0:T(8,128)(2,1)S(1)} all-to-all(bf16[16,144,128]{2,1,0:T(8,128)(2,1)S(1)} %get-tuple-element.9), channel_id=1, replica_groups={{0,1,2,3,4,5,6,7,8,9,10,11,12,13,14,15},{16,17,18,19,20,21,22,23,24,25,..., dimensions={0} | all-to-all | bytes 1179648 | tf_op jit(solution)/shard_map/all_to_all | solution.py:310
  19.6 1.2 %triangle.1 = bf16[2304,128]{1,0:T(8,128)(2,1)S(1)} custom-call(bf16[16,144,128]{2,1,0:T(8,128)(2,1)S(1)} %all_to_all.10.message_ref), custom_call_target="tpu_custom_call" | custom-call | tf_op jit(solution)/shard_map/triangle/pallas_call | solution.py:324
  20.8 19.5 %all_to_all.11 = bf16[32,72,128]{2,1,0:T(8,128)(2,1)S(1)} all-to-all(bf16[32,72,128]{2,1,0:T(8,128)(2,1)S(1)} %bitcast.8), channel_id=1, replica_groups=mesh['grp'=1,'row'=16,'col'=2] {'row','col'}, dimensions={0} | all-to-all | bytes 1179648 | tf_op jit(solution)/shard_map/all_to_all | solution.py:337
  40.4 1.2 %output.1 = bf16[1152,128]{1,0:T(8,128)(2,1)} custom-call(bf16[2304,128]{1,0:T(8,128)(2,1)S(1)} %bitcast.7, f32[128,1152]{1,0:T(8,128)S(1)} %get-tuple-element.10.gate_ref, f32[128,128]{1,0:T(8,128)S(1)} %get-tuple-element.11.gain_ref, bf16[128,128]{1,0:T(8,128)(2,1)S(1)} %get-tuple-element.12.w_t_ref), custom_call_target="tpu_custom_call" | custom-call | tf_op jit(solution)/shard_map/output/pallas_call | solution.py:344

commit v26 on v24

--- a/solution.py
+++ b/solution.py
@@ -82,10 +82,24 @@
         copy.wait()
 
 
+def in_first_part():
+    return lax.axis_index("row") < lax.axis_size("row") // PARTS
+
+
+def tail(normed_ref, w_gate_ref, gain_hbm, w_out_hbm, gate_ref, w_out_ref, gain_ref, gain, w_out, sems):
+    copies = start_copies(sems, (gain_hbm, gain), (w_out_hbm, w_out))
+    gate = jnp.dot(w_gate_ref[...], normed_ref[...], preferred_element_type=jnp.float32)
+    gate_ref[...] = 0.5 * jnp.tanh(gate) + 0.5
+    for copy in copies:
+        copy.wait()
+    w_out_ref[...] = w_out[...].T
+    gain_ref[...] = jnp.broadcast_to(column(gain[...]), gain_ref.shape)
+
+
 def project_kernel(
     rows, cols, tile_hbm, chain_hbm, pair_hbm, gain_hbm, w_hbm, gain_mid_hbm, w_out_hbm,
-    message_ref, gate_ref, w_out_ref, gain_mid_ref,
-    tile_ref, chain_ref, pair_ref, gain_ref, w_ref, gain_mid, w_out, normed_ref, sems,
+    message_ref, normed_ref, w_gate_ref, gate_ref, w_out_ref, gain_mid_ref,
+    tile_ref, chain_ref, pair_ref, gain_ref, w_ref, gain_mid, w_out, sems,
 ):
     hidden = (w_ref.shape[1] - w_ref.shape[0]) // 4
     peers = message_ref.shape[0]
@@ -100,8 +114,6 @@
         (gain_hbm, gain_ref),
         (pair_hbm, pair_ref),
         (w_hbm, w_ref),
-        (gain_mid_hbm, gain_mid),
-        (w_out_hbm, w_out),
     )
     for copy in copies[:3]:
         copy.wait()
@@ -109,16 +121,14 @@
     gain = column(gain_ref[...])
     copies[4].wait()
     w_t = (w_ref[...] * 0.5).T
+    w_gate_ref[...] = w_t[4 * hidden :]
+    w_t = w_t[: 4 * hidden]
     copies[3].wait()
     for lanes in cycles:
         block = transpose(pair_ref[lanes, :])
         center = block - jnp.mean(block, axis=0, keepdims=True)
         spread = jnp.mean(center * center, axis=0, keepdims=True)
         normed_ref[:, lanes] = (center * lax.rsqrt(spread + EPS) * gain).astype(jnp.bfloat16)
-    for copy in copies[5:]:
-        copy.wait()
-    gain_mid_ref[...] = jnp.broadcast_to(column(gain_mid[...]), gain_mid_ref.shape)
-    w_out_ref[...] = w_out[...].T
     for cycle, lanes in enumerate(cycles):
         projected = jnp.dot(w_t, normed_ref[:, lanes], preferred_element_type=jnp.float32)
         sides = []
@@ -130,7 +140,10 @@
         for group in range(groups):
             line = (cycle * groups + group) * 2 * own
             message_ref[:, line : line + 2 * own, :] = both[:, :, group * LANES : (group + 1) * LANES]
-        gate_ref[:, lanes] = 0.5 * jnp.tanh(projected[4 * hidden :]) + 0.5
+
+    @pl.when(in_first_part())
+    def _():
+        tail(normed_ref, w_gate_ref, gain_mid_hbm, w_out_hbm, gate_ref, w_out_ref, gain_mid_ref, gain_mid, w_out, sems)
 
 
 def unpack(message_ref, half, halves, spread_ref, own, cols):
@@ -231,7 +244,23 @@
         mixed_ref[share * each : (share + 1) * each, :] = jnp.concatenate(lines, axis=0).astype(jnp.bfloat16)
 
 
-def output_kernel(own, parts, mixed_ref, gate_ref, gain_ref, w_t_ref, update_hbm, mixed, update, sems):
+def output_kernel(
+    own, parts, mixed_ref, gate_ref, gain_ref, w_t_ref, normed_ref, w_gate_ref, gain_hbm, w_out_hbm, update_hbm,
+    mixed, update, sems, gate, w_t, gain_t, gain, w_out, tail_sems,
+):
+    first = in_first_part()
+
+    @pl.when(first)
+    def _():
+        finish(own, parts, mixed_ref, gate_ref, gain_ref, w_t_ref, update_hbm, mixed, update, sems)
+
+    @pl.when(jnp.logical_not(first))
+    def _():
+        tail(normed_ref, w_gate_ref, gain_hbm, w_out_hbm, gate, w_t, gain_t, gain, w_out, tail_sems)
+        finish(own, parts, mixed_ref, gate, gain_t, w_t, update_hbm, mixed, update, sems)
+
+
+def finish(own, parts, mixed_ref, gate_ref, gain_ref, w_t_ref, update_hbm, mixed, update, sems):
     members, lines, _ = mixed.shape
     members = members // parts
     mixed[...] = mixed_ref[...].astype(jnp.float32).reshape(mixed.shape)
@@ -273,16 +302,18 @@
     params = pltpu.CompilerParams(vmem_limit_bytes=VMEM_BYTES)
     tokens = chain_ids.shape[0]
     message = jax.ShapeDtypeStruct((peers * halves, 2 * lines, LANES), jnp.bfloat16)
-    message, gate, w_out_t, gain = pl.pallas_call(
+    message, normed, w_gate, gate, w_out_t, gain = pl.pallas_call(
         functools.partial(project_kernel, rows, cols),
         out_shape=(
             message,
+            jax.ShapeDtypeStruct((width, positions), jnp.bfloat16),
+            jax.ShapeDtypeStruct((width, width), jnp.bfloat16),
             jax.ShapeDtypeStruct((width, positions), jnp.float32),
             jax.ShapeDtypeStruct(w_out.shape[::-1], jnp.bfloat16),
             jax.ShapeDtypeStruct((hidden, LANES), jnp.float32),
         ),
         in_specs=[HBM] * 7,
-        out_specs=[VMEM] * 4,
+        out_specs=[VMEM] * 6,
         scratch_shapes=[
             pltpu.SMEM(tile_mask.shape, jnp.int32),
             pltpu.VMEM((1, tokens), jnp.int32),
@@ -291,8 +322,7 @@
             pltpu.VMEM(w_proj.shape, jnp.bfloat16),
             pltpu.VMEM((1, hidden), jnp.float32),
             pltpu.VMEM(w_out.shape, jnp.bfloat16),
-            pltpu.VMEM((width, positions), jnp.bfloat16),
-            pltpu.SemaphoreType.DMA((7,)),
+            pltpu.SemaphoreType.DMA((5,)),
         ],
         compiler_params=params,
         name="project",
@@ -342,16 +372,22 @@
     update = pl.pallas_call(
         functools.partial(output_kernel, own, PARTS),
         out_shape=jax.ShapeDtypeStruct((positions, width), jnp.bfloat16),
-        in_specs=[VMEM] * 4,
+        in_specs=[VMEM] * 6 + [HBM] * 2,
         out_specs=HBM,
         scratch_shapes=[
-            pltpu.VMEM((shares * halves, lines, LANES), jnp.float32),
+            pltpu.VMEM((halves * shares, lines, LANES), jnp.float32),
             pltpu.VMEM((positions, width), jnp.bfloat16),
             pltpu.SemaphoreType.DMA((math.gcd(groups, 3), 1)),
+            pltpu.VMEM((width, positions), jnp.float32),
+            pltpu.VMEM(w_out.shape[::-1], jnp.bfloat16),
+            pltpu.VMEM((hidden, LANES), jnp.float32),
+            pltpu.VMEM((1, hidden), jnp.float32),
+            pltpu.VMEM(w_out.shape, jnp.bfloat16),
+            pltpu.SemaphoreType.DMA((2,)),
         ],
         compiler_params=params,
         name="output",
-    )(mixed, gate, gain, w_out_t)
+    )(mixed, gate, gain, w_out_t, normed, w_gate, in_hbm(gain_mid[None, :]), in_hbm(w_out))
     return update.reshape(rows, cols, width)
 
 

time: 41.7 us -> 41.5 us (level)
  blocking collectives: 36.9 us -> 35.9 us
  Pallas kernels: 4.61 us -> 5.33 us
    all_to_all x1, blocking collectives: 19.5 us -> 18.6 us  [on_device(): lax.all_to_all(mixed.reshape(halves * shares, lines, LANES), ('row', 'col...]
    pallas_call x1, Pallas kernels: 2.29 us -> 2.97 us  [on_device(): pl.pallas_call(functools.partial(project_kernel, rows, cols), out_shape=(...]
where the time goes in v26:
time: 41.5 us; the launch traced here: 41.3 us
  blocking collectives  35.9 us (87%)
  Pallas kernels  5.33 us (13%)
    all_to_all x1, blocking collectives, on_device(): lax.all_to_all(mixed.reshape(halves * shares, lines, LANES), ('row', 'col...  18.6 us
    all_to_all x1, blocking collectives, on_device(): lax.all_to_all(message, ('row', 'col'), split_axis=0, concat_axis=0, axis...  17.3 us
    pallas_call x1, Pallas kernels, on_device(): pl.pallas_call(functools.partial(project_kernel, rows, cols), out_shape=(...  2.97 us
    pallas_call x1, Pallas kernels, on_device(): pl.pallas_call(functools.partial(triangle_kernel, own, cols, shares), out...  1.19 us
    pallas_call x1, Pallas kernels, on_device(): pl.pallas_call(functools.partial(output_kernel, own, PARTS), out_shape=ja...  1.18 us

profile of v26, /device:TPU:0, one launch (start us, length us, event | category | flops | bytes accessed | tf_op | source)
XLA Modules:
  0.0 41.3 jit_solution(1978182115287363814)
XLA Ops:
  0.0 3.0 %project.1 = (bf16[16,144,128]{2,1,0:T(8,128)(2,1)S(1)}, bf16[128,1152]{1,0:T(8,128)(2,1)S(1)}, bf16[128,128]{1,0:T(8,128)(2,1)S(1)}, f32[128,1152]{1,0:T(8,128)...) custom-call(s32[2,2]{1,0:T(2,128)} %tile_hbm.1, s32[1,192]{1,0:T(1,128)} %bitcast.12, ...), custom_call_target="tpu_custom_call" | custom-call | tf_op jit(solution)/shard_map/project/pallas_call | solution.py:305
  3.0 17.3 %all_to_all.10.message_ref = bf16[16,144,128]{2,1,0:T(8,128)(2,1)S(1)} all-to-all(bf16[16,144,128]{2,1,0:T(8,128)(2,1)S(1)} %get-tuple-element.11), channel_id=1, replica_groups={{0,1,2,3,4,5,6,7,8,9,10,11,12,13,14,15},{16,17,18,19,20,21,22,23,24,25,..., dimensions={0} | all-to-all | bytes 1179648 | tf_op jit(solution)/shard_map/all_to_all | solution.py:338
  20.3 1.2 %triangle.1 = bf16[2304,128]{1,0:T(8,128)(2,1)S(1)} custom-call(bf16[16,144,128]{2,1,0:T(8,128)(2,1)S(1)} %all_to_all.10.message_ref), custom_call_target="tpu_custom_call" | custom-call | tf_op jit(solution)/shard_map/triangle/pallas_call | solution.py:352
  21.5 18.6 %all_to_all.11 = bf16[32,72,128]{2,1,0:T(8,128)(2,1)S(1)} all-to-all(bf16[32,72,128]{2,1,0:T(8,128)(2,1)S(1)} %bitcast.7), channel_id=1, replica_groups=mesh['grp'=1,'row'=16,'col'=2] {'row','col'}, dimensions={0} | all-to-all | bytes 1179648 | tf_op jit(solution)/shard_map/all_to_all | solution.py:365
  40.1 1.2 %output.1 = bf16[1152,128]{1,0:T(8,128)(2,1)} custom-call(bf16[2304,128]{1,0:T(8,128)(2,1)S(1)} %bitcast.8, f32[128,1152]{1,0:T(8,128)S(1)} %get-tuple-element.12.gate_ref, f32[128,128]{1,0:T(8,128)S(1)} %get-tuple-element.13.gain_ref, bf16[128,128]{1,0:T(8,128)(2,1)S(1)} %get-tuple-element.14.w_t_ref, bf16[128,1152]{1,0:T(8,128)(2,1)S(1)} %get-tuple-element.15.normed_ref, ...), custom_call_target="tpu_custom_call" | custom-call | tf_op jit(solution)/shard_map/output/pallas_call | solution.py:372

commit v27 on v26

--- a/solution.py
+++ b/solution.py
@@ -34,9 +34,9 @@
     return same.astype(jnp.bfloat16)
 
 
-def transpose(block):
+def transpose(block, by=None):
     return lax.dot_general(
-        identity(block.shape[1], block.shape[1]),
+        identity(block.shape[1], block.shape[1]) if by is None else by,
         block,
         (((1,), (1,)), ((), ())),
         preferred_element_type=jnp.float32,
@@ -86,8 +86,7 @@
     return lax.axis_index("row") < lax.axis_size("row") // PARTS
 
 
-def tail(normed_ref, w_gate_ref, gain_hbm, w_out_hbm, gate_ref, w_out_ref, gain_ref, gain, w_out, sems):
-    copies = start_copies(sems, (gain_hbm, gain), (w_out_hbm, w_out))
+def tail(normed_ref, w_gate_ref, gate_ref, w_out_ref, gain_ref, gain, w_out, copies):
     gate = jnp.dot(w_gate_ref[...], normed_ref[...], preferred_element_type=jnp.float32)
     gate_ref[...] = 0.5 * jnp.tanh(gate) + 0.5
     for copy in copies:
@@ -115,18 +114,31 @@
         (pair_hbm, pair_ref),
         (w_hbm, w_ref),
     )
+
+    def late_copies():
+        return [
+            pltpu.make_async_copy(gain_mid_hbm, gain_mid, sems.at[5]),
+            pltpu.make_async_copy(w_out_hbm, w_out, sems.at[6]),
+        ]
+
+    @pl.when(in_first_part())
+    def _():
+        for copy in late_copies():
+            copy.start()
+
     for copy in copies[:3]:
         copy.wait()
     keep = keep_of(tile_ref, chain_ref, rows, cols)
     gain = column(gain_ref[...])
+    width = pair_ref.shape[1]
+    centering = (identity(width, width).astype(jnp.float32) - 1.0 / width).astype(jnp.bfloat16)
     copies[4].wait()
     w_t = (w_ref[...] * 0.5).T
     w_gate_ref[...] = w_t[4 * hidden :]
     w_t = w_t[: 4 * hidden]
     copies[3].wait()
     for lanes in cycles:
-        block = transpose(pair_ref[lanes, :])
-        center = block - jnp.mean(block, axis=0, keepdims=True)
+        center = transpose(pair_ref[lanes, :], centering)
         spread = jnp.mean(center * center, axis=0, keepdims=True)
         normed_ref[:, lanes] = (center * lax.rsqrt(spread + EPS) * gain).astype(jnp.bfloat16)
     for cycle, lanes in enumerate(cycles):
@@ -143,7 +155,7 @@
 
     @pl.when(in_first_part())
     def _():
-        tail(normed_ref, w_gate_ref, gain_mid_hbm, w_out_hbm, gate_ref, w_out_ref, gain_mid_ref, gain_mid, w_out, sems)
+        tail(normed_ref, w_gate_ref, gate_ref, w_out_ref, gain_mid_ref, gain_mid, w_out, late_copies())
 
 
 def unpack(message_ref, half, halves, spread_ref, own, cols):
@@ -256,7 +268,8 @@
 
     @pl.when(jnp.logical_not(first))
     def _():
-        tail(normed_ref, w_gate_ref, gain_hbm, w_out_hbm, gate, w_t, gain_t, gain, w_out, tail_sems)
+        copies = start_copies(tail_sems, (gain_hbm, gain), (w_out_hbm, w_out))
+        tail(normed_ref, w_gate_ref, gate, w_t, gain_t, gain, w_out, copies)
         finish(own, parts, mixed_ref, gate, gain_t, w_t, update_hbm, mixed, update, sems)
 
 
@@ -322,7 +335,7 @@
             pltpu.VMEM(w_proj.shape, jnp.bfloat16),
             pltpu.VMEM((1, hidden), jnp.float32),
             pltpu.VMEM(w_out.shape, jnp.bfloat16),
-            pltpu.SemaphoreType.DMA((5,)),
+            pltpu.SemaphoreType.DMA((7,)),
         ],
         compiler_params=params,
         name="project",

time: 41.5 us -> 41.5 us (level)
  blocking collectives: 35.9 us -> 36.5 us
  Pallas kernels: 5.33 us -> 4.77 us
    pallas_call x1, Pallas kernels: 2.97 us -> 2.41 us  [on_device(): pl.pallas_call(functools.partial(project_kernel, rows, cols), out_shape=(...]
    all_to_all x1, blocking collectives: 18.6 us -> 19.1 us  [on_device(): lax.all_to_all(mixed.reshape(halves * shares, lines, LANES), ('row', 'col...]
where the time goes in v27:
time: 41.5 us; the launch traced here: 41.3 us
  blocking collectives  36.5 us (88%)
  Pallas kernels  4.77 us (11%)
    all_to_all x1, blocking collectives, on_device(): lax.all_to_all(mixed.reshape(halves * shares, lines, LANES), ('row', 'col...  19.1 us
    all_to_all x1, blocking collectives, on_device(): lax.all_to_all(message, ('row', 'col'), split_axis=0, concat_axis=0, axis...  17.3 us
    pallas_call x1, Pallas kernels, on_device(): pl.pallas_call(functools.partial(project_kernel, rows, cols), out_shape=(...  2.41 us
    pallas_call x1, Pallas kernels, on_device(): pl.pallas_call(functools.partial(triangle_kernel, own, cols, shares), out...  1.18 us
    pallas_call x1, Pallas kernels, on_device(): pl.pallas_call(functools.partial(output_kernel, own, PARTS), out_shape=ja...  1.18 us

profile of v27, /device:TPU:0, one launch (start us, length us, event | category | flops | bytes accessed | tf_op | source)
XLA Modules:
  0.0 41.3 jit_solution(822390152200371124)
XLA Ops:
  0.0 2.4 %project.1 = (bf16[16,144,128]{2,1,0:T(8,128)(2,1)S(1)}, bf16[128,1152]{1,0:T(8,128)(2,1)S(1)}, bf16[128,128]{1,0:T(8,128)(2,1)S(1)}, f32[128,1152]{1,0:T(8,128)...) custom-call(s32[2,2]{1,0:T(2,128)} %tile_hbm.1, s32[1,192]{1,0:T(1,128)} %bitcast.12, ...), custom_call_target="tpu_custom_call" | custom-call | tf_op jit(solution)/shard_map/project/pallas_call | solution.py:318
  2.4 17.3 %all_to_all.10.message_ref = bf16[16,144,128]{2,1,0:T(8,128)(2,1)S(1)} all-to-all(bf16[16,144,128]{2,1,0:T(8,128)(2,1)S(1)} %get-tuple-element.11), channel_id=1, replica_groups={{0,1,2,3,4,5,6,7,8,9,10,11,12,13,14,15},{16,17,18,19,20,21,22,23,24,25,..., dimensions={0} | all-to-all | bytes 1179648 | tf_op jit(solution)/shard_map/all_to_all | solution.py:351
  19.8 1.2 %triangle.1 = bf16[2304,128]{1,0:T(8,128)(2,1)S(1)} custom-call(bf16[16,144,128]{2,1,0:T(8,128)(2,1)S(1)} %all_to_all.10.message_ref), custom_call_target="tpu_custom_call" | custom-call | tf_op jit(solution)/shard_map/triangle/pallas_call | solution.py:365
  20.9 19.1 %all_to_all.11 = bf16[32,72,128]{2,1,0:T(8,128)(2,1)S(1)} all-to-all(bf16[32,72,128]{2,1,0:T(8,128)(2,1)S(1)} %bitcast.7), channel_id=1, replica_groups=mesh['grp'=1,'row'=16,'col'=2] {'row','col'}, dimensions={0} | all-to-all | bytes 1179648 | tf_op jit(solution)/shard_map/all_to_all | solution.py:378
  40.1 1.2 %output.1 = bf16[1152,128]{1,0:T(8,128)(2,1)} custom-call(bf16[2304,128]{1,0:T(8,128)(2,1)S(1)} %bitcast.8, f32[128,1152]{1,0:T(8,128)S(1)} %get-tuple-element.12.gate_ref, f32[128,128]{1,0:T(8,128)S(1)} %get-tuple-element.13.gain_ref, bf16[128,128]{1,0:T(8,128)(2,1)S(1)} %get-tuple-element.14.w_t_ref, bf16[128,1152]{1,0:T(8,128)(2,1)S(1)} %get-tuple-element.15.normed_ref, ...), custom_call_target="tpu_custom_call" | custom-call | tf_op jit(solution)/shard_map/output/pallas_call | solution.py:385

commit v28 on v27

--- a/solution.py
+++ b/solution.py
@@ -158,7 +158,7 @@
         tail(normed_ref, w_gate_ref, gate_ref, w_out_ref, gain_mid_ref, gain_mid, w_out, late_copies())
 
 
-def unpack(message_ref, half, halves, spread_ref, own, cols):
+def unpack(message_ref, half, halves, spread_ref, own, cols, peers):
     tokens, groups = cycle_of(cols)
     members, lines, _ = message_ref.shape
     peers = members // halves
@@ -221,39 +221,62 @@
     deep = left_t.shape[2]
     one = identity(cols, width)
     padding = [jnp.zeros((deep - depth, width), jnp.bfloat16)] if depth < deep else []
-    for half in range(halves):
-        unpack(message_ref, half, halves, spread.at[half], own, cols)
+    peers = message_ref.shape[0] // halves
 
     def operand(channel, half):
         return jnp.concatenate([channel_of(spread.at[half], channel, 2 * own)] + padding, axis=0)
 
-    for channel in range(own):
-        left = jnp.concatenate([operand(channel, half) for half in range(halves)], axis=0)
-        both = lax.dot_general(
-            one, left, (((1,), (1,)), ((), ())), preferred_element_type=jnp.float32
+    def turn(channel, half):
+        left_t[channel, half * cols : (half + 1) * cols, :] = lax.dot_general(
+            one, operand(channel, half), (((1,), (1,)), ((), ())), preferred_element_type=jnp.float32
         ).astype(jnp.bfloat16)
-        for half in range(halves):
-            left_t[channel, half * cols : (half + 1) * cols, :] = both[:, half * deep : (half + 1) * deep]
-    for channel in range(own):
+
+    def multiply(channel, i_half):
         right = jnp.concatenate([operand(own + channel, half) for half in range(halves)], axis=1)
-        total = jnp.dot(left_t[channel], right, preferred_element_type=jnp.float32)
-        for i_half in range(halves):
-            for j_half in range(halves):
-                for chunk in range(chunks):
-                    start = j_half * width + chunk * LANES
-                    mixed[i_half, j_half, chunk, pl.ds(channel, cols, stride=own), :] = total[
-                        i_half * cols : (i_half + 1) * cols, start : start + LANES
-                    ]
+        lines = slice(i_half * cols, (i_half + 1) * cols)
+        total = jnp.dot(left_t[channel, lines, :], right, preferred_element_type=jnp.float32)
+        for j_half in range(halves):
+            for chunk in range(chunks):
+                start = j_half * width + chunk * LANES
+                mixed[i_half, j_half, chunk, pl.ds(channel, cols, stride=own), :] = total[:, start : start + LANES]
+
     groups = cycle_of(cols)[1]
     each = mixed_ref.shape[0] // shares
     cycles = each // (halves * groups * own)
-    for share in range(shares):
+
+    def send(share):
         i_half, peer = divmod(share, shares // halves)
         lines = []
         for j_half in range(halves):
             for cycle in range(cycles):
                 lines += pack(mixed.at[i_half, j_half], peer * cycles + cycle, own, cols)
         mixed_ref[share * each : (share + 1) * each, :] = jnp.concatenate(lines, axis=0).astype(jnp.bfloat16)
+
+    def between(works, others):
+        for at, work in enumerate(works):
+            work()
+            for other in others[at * len(others) // len(works) : (at + 1) * len(others) // len(works)]:
+                other()
+
+    part = functools.partial
+    waiting = [part(unpack, message_ref, 0, halves, spread.at[0], own, cols, [peer]) for peer in range(peers)]
+    for half in range(halves):
+        for work in waiting:
+            work()
+        waiting = []
+        if half + 1 < halves:
+            waiting = [
+                part(unpack, message_ref, half + 1, halves, spread.at[half + 1], own, cols, [peer])
+                for peer in range(peers)
+            ]
+        between([part(turn, channel, half) for channel in range(own)], waiting)
+        waiting = []
+    for i_half in range(halves):
+        between([part(multiply, channel, i_half) for channel in range(own)], waiting)
+        first = i_half * (shares // halves)
+        waiting = [part(send, share) for share in range(first, first + shares // halves)]
+    for work in waiting:
+        work()
 
 
 def output_kernel(

time: 41.5 us -> 42.6 us (1.027)
  Pallas kernels: 4.77 us -> 5.93 us
    pallas_call x1, Pallas kernels: 1.18 us -> 2.35 us  [on_device(): pl.pallas_call(functools.partial(triangle_kernel, own, cols, shares), out...]
where the time goes in v28:
time: 42.6 us; the launch traced here: 42.4 us
  blocking collectives  36.5 us (86%)
  Pallas kernels  5.93 us (14%)
    all_to_all x1, blocking collectives, on_device(): lax.all_to_all(mixed.reshape(halves * shares, lines, LANES), ('row', 'col...  19.1 us
    all_to_all x1, blocking collectives, on_device(): lax.all_to_all(message, ('row', 'col'), split_axis=0, concat_axis=0, axis...  17.3 us
    pallas_call x1, Pallas kernels, on_device(): pl.pallas_call(functools.partial(project_kernel, rows, cols), out_shape=(...  2.41 us
    pallas_call x1, Pallas kernels, on_device(): pl.pallas_call(functools.partial(triangle_kernel, own, cols, shares), out...  2.35 us
    pallas_call x1, Pallas kernels, on_device(): pl.pallas_call(functools.partial(output_kernel, own, PARTS), out_shape=ja...  1.18 us

profile of v28, /device:TPU:0, one launch (start us, length us, event | category | flops | bytes accessed | tf_op | source)
XLA Modules:
  0.0 42.4 jit_solution(4165710615074762240)
XLA Ops:
  0.0 2.4 %project.1 = (bf16[16,144,128]{2,1,0:T(8,128)(2,1)S(1)}, bf16[128,1152]{1,0:T(8,128)(2,1)S(1)}, bf16[128,128]{1,0:T(8,128)(2,1)S(1)}, f32[128,1152]{1,0:T(8,128)...) custom-call(s32[2,2]{1,0:T(2,128)} %tile_hbm.1, s32[1,192]{1,0:T(1,128)} %bitcast.12, ...), custom_call_target="tpu_custom_call" | custom-call | tf_op jit(solution)/shard_map/project/pallas_call | solution.py:341
  2.4 17.3 %all_to_all.10.message_ref = bf16[16,144,128]{2,1,0:T(8,128)(2,1)S(1)} all-to-all(bf16[16,144,128]{2,1,0:T(8,128)(2,1)S(1)} %get-tuple-element.11), channel_id=1, replica_groups={{0,1,2,3,4,5,6,7,8,9,10,11,12,13,14,15},{16,17,18,19,20,21,22,23,24,25,..., dimensions={0} | all-to-all | bytes 1179648 | tf_op jit(solution)/shard_map/all_to_all | solution.py:374
  19.8 2.3 %triangle.1 = bf16[2304,128]{1,0:T(8,128)(2,1)S(1)} custom-call(bf16[16,144,128]{2,1,0:T(8,128)(2,1)S(1)} %all_to_all.10.message_ref), custom_call_target="tpu_custom_call" | custom-call | tf_op jit(solution)/shard_map/triangle/pallas_call | solution.py:388
  22.1 19.1 %all_to_all.11 = bf16[32,72,128]{2,1,0:T(8,128)(2,1)S(1)} all-to-all(bf16[32,72,128]{2,1,0:T(8,128)(2,1)S(1)} %bitcast.7), channel_id=1, replica_groups=mesh['grp'=1,'row'=16,'col'=2] {'row','col'}, dimensions={0} | all-to-all | bytes 1179648 | tf_op jit(solution)/shard_map/all_to_all | solution.py:401
  41.2 1.2 %output.1 = bf16[1152,128]{1,0:T(8,128)(2,1)} custom-call(bf16[2304,128]{1,0:T(8,128)(2,1)S(1)} %bitcast.8, f32[128,1152]{1,0:T(8,128)S(1)} %get-tuple-element.12.gate_ref, f32[128,128]{1,0:T(8,128)S(1)} %get-tuple-element.13.gain_ref, bf16[128,128]{1,0:T(8,128)(2,1)S(1)} %get-tuple-element.14.w_t_ref, bf16[128,1152]{1,0:T(8,128)(2,1)S(1)} %get-tuple-element.15.normed_ref, ...), custom_call_target="tpu_custom_call" | custom-call | tf_op jit(solution)/shard_map/output/pallas_call | solution.py:408

commit v29 on v26

--- a/solution.py
+++ b/solution.py
@@ -111,19 +111,20 @@
         sems,
         (chain_hbm, chain_ref),
         (tile_hbm, tile_ref),
-        (gain_hbm, gain_ref),
         (pair_hbm, pair_ref),
         (w_hbm, w_ref),
+        (gain_hbm, gain_ref),
     )
-    for copy in copies[:3]:
+    for copy in copies[:2]:
         copy.wait()
     keep = keep_of(tile_ref, chain_ref, rows, cols)
-    gain = column(gain_ref[...])
-    copies[4].wait()
+    copies[3].wait()
     w_t = (w_ref[...] * 0.5).T
     w_gate_ref[...] = w_t[4 * hidden :]
     w_t = w_t[: 4 * hidden]
-    copies[3].wait()
+    copies[4].wait()
+    gain = column(gain_ref[...])
+    copies[2].wait()
     for lanes in cycles:
         block = transpose(pair_ref[lanes, :])
         center = block - jnp.mean(block, axis=0, keepdims=True)

time: 41.5 us -> 41.6 us (level)
  no operation moved by 1% of the time
where the time goes in v29:
time: 41.6 us; the launch traced here: 41.4 us
  blocking collectives  35.9 us (86%)
  Pallas kernels  5.43 us (13%)
    all_to_all x1, blocking collectives, on_device(): lax.all_to_all(mixed.reshape(halves * shares, lines, LANES), ('row', 'col...  18.6 us
    all_to_all x1, blocking collectives, on_device(): lax.all_to_all(message, ('row', 'col'), split_axis=0, concat_axis=0, axis...  17.3 us
    pallas_call x1, Pallas kernels, on_device(): pl.pallas_call(functools.partial(project_kernel, rows, cols), out_shape=(...  3.06 us
    pallas_call x1, Pallas kernels, on_device(): pl.pallas_call(functools.partial(triangle_kernel, own, cols, shares), out...  1.19 us
    pallas_call x1, Pallas kernels, on_device(): pl.pallas_call(functools.partial(output_kernel, own, PARTS), out_shape=ja...  1.18 us

profile of v29, /device:TPU:0, one launch (start us, length us, event | category | flops | bytes accessed | tf_op | source)
XLA Modules:
  0.0 41.4 jit_solution(2935807090612542515)
XLA Ops:
  0.0 3.1 %project.1 = (bf16[16,144,128]{2,1,0:T(8,128)(2,1)S(1)}, bf16[128,1152]{1,0:T(8,128)(2,1)S(1)}, bf16[128,128]{1,0:T(8,128)(2,1)S(1)}, f32[128,1152]{1,0:T(8,128)...) custom-call(s32[2,2]{1,0:T(2,128)} %tile_hbm.1, s32[1,192]{1,0:T(1,128)} %bitcast.12, ...), custom_call_target="tpu_custom_call" | custom-call | tf_op jit(solution)/shard_map/project/pallas_call | solution.py:306
  3.1 17.3 %all_to_all.10.message_ref = bf16[16,144,128]{2,1,0:T(8,128)(2,1)S(1)} all-to-all(bf16[16,144,128]{2,1,0:T(8,128)(2,1)S(1)} %get-tuple-element.11), channel_id=1, replica_groups={{0,1,2,3,4,5,6,7,8,9,10,11,12,13,14,15},{16,17,18,19,20,21,22,23,24,25,..., dimensions={0} | all-to-all | bytes 1179648 | tf_op jit(solution)/shard_map/all_to_all | solution.py:339
  20.4 1.2 %triangle.1 = bf16[2304,128]{1,0:T(8,128)(2,1)S(1)} custom-call(bf16[16,144,128]{2,1,0:T(8,128)(2,1)S(1)} %all_to_all.10.message_ref), custom_call_target="tpu_custom_call" | custom-call | tf_op jit(solution)/shard_map/triangle/pallas_call | solution.py:353
  21.6 18.6 %all_to_all.11 = bf16[32,72,128]{2,1,0:T(8,128)(2,1)S(1)} all-to-all(bf16[32,72,128]{2,1,0:T(8,128)(2,1)S(1)} %bitcast.7), channel_id=1, replica_groups=mesh['grp'=1,'row'=16,'col'=2] {'row','col'}, dimensions={0} | all-to-all | bytes 1179648 | tf_op jit(solution)/shard_map/all_to_all | solution.py:366
  40.2 1.2 %output.1 = bf16[1152,128]{1,0:T(8,128)(2,1)} custom-call(bf16[2304,128]{1,0:T(8,128)(2,1)S(1)} %bitcast.8, f32[128,1152]{1,0:T(8,128)S(1)} %get-tuple-element.12.gate_ref, f32[128,128]{1,0:T(8,128)S(1)} %get-tuple-element.13.gain_ref, bf16[128,128]{1,0:T(8,128)(2,1)S(1)} %get-tuple-element.14.w_t_ref, bf16[128,1152]{1,0:T(8,128)(2,1)S(1)} %get-tuple-element.15.normed_ref, ...), custom_call_target="tpu_custom_call" | custom-call | tf_op jit(solution)/shard_map/output/pallas_call | solution.py:373

commit v30 on v26

--- a/solution.py
+++ b/solution.py
@@ -265,7 +265,7 @@
     members = members // parts
     mixed[...] = mixed_ref[...].astype(jnp.float32).reshape(mixed.shape)
     groups = lines // own
-    steps = math.gcd(groups, 3)
+    ends = [groups // 2, groups - 1, groups]
     leaving = []
     for group in range(groups):
         sums = mixed[:members, group * own : (group + 1) * own, :]
@@ -278,10 +278,10 @@
         projected = jnp.dot(w_t_ref[...], normed, preferred_element_type=jnp.float32)
         lanes = slice(group * LANES, (group + 1) * LANES)
         update[lanes, :] = (gate_ref[:, lanes] * projected).T.astype(jnp.bfloat16)
-        step, last = divmod((group + 1) * steps, groups)
-        if last == 0:
-            done = slice((step - 1) * (groups // steps) * LANES, (group + 1) * LANES)
-            leaving += start_copies(sems.at[step - 1], (update.at[done, :], update_hbm.at[done, :]))
+        if group + 1 in ends:
+            step = ends.index(group + 1)
+            done = slice(([0] + ends)[step] * LANES, (group + 1) * LANES)
+            leaving += start_copies(sems.at[step], (update.at[done, :], update_hbm.at[done, :]))
     for copy in leaving:
         copy.wait()
 
@@ -377,7 +377,7 @@
         scratch_shapes=[
             pltpu.VMEM((halves * shares, lines, LANES), jnp.float32),
             pltpu.VMEM((positions, width), jnp.bfloat16),
-            pltpu.SemaphoreType.DMA((math.gcd(groups, 3), 1)),
+            pltpu.SemaphoreType.DMA((3, 1)),
             pltpu.VMEM((width, positions), jnp.float32),
             pltpu.VMEM(w_out.shape[::-1], jnp.bfloat16),
             pltpu.VMEM((hidden, LANES), jnp.float32),

time: 41.5 us -> 41.5 us (level)
  no operation moved by 1% of the time
where the time goes in v30:
time: 41.5 us; the launch traced here: 41.3 us
  blocking collectives  35.9 us (87%)
  Pallas kernels  5.33 us (13%)
    all_to_all x1, blocking collectives, on_device(): lax.all_to_all(mixed.reshape(halves * shares, lines, LANES), ('row', 'col...  18.6 us
    all_to_all x1, blocking collectives, on_device(): lax.all_to_all(message, ('row', 'col'), split_axis=0, concat_axis=0, axis...  17.3 us
    pallas_call x1, Pallas kernels, on_device(): pl.pallas_call(functools.partial(project_kernel, rows, cols), out_shape=(...  2.97 us
    pallas_call x1, Pallas kernels, on_device(): pl.pallas_call(functools.partial(triangle_kernel, own, cols, shares), out...  1.19 us
    pallas_call x1, Pallas kernels, on_device(): pl.pallas_call(functools.partial(output_kernel, own, PARTS), out_shape=ja...  1.18 us

profile of v30, /device:TPU:0, one launch (start us, length us, event | category | flops | bytes accessed | tf_op | source)
XLA Modules:
  0.0 41.3 jit_solution(8124733425710940907)
XLA Ops:
  0.0 3.0 %project.1 = (bf16[16,144,128]{2,1,0:T(8,128)(2,1)S(1)}, bf16[128,1152]{1,0:T(8,128)(2,1)S(1)}, bf16[128,128]{1,0:T(8,128)(2,1)S(1)}, f32[128,1152]{1,0:T(8,128)...) custom-call(s32[2,2]{1,0:T(2,128)} %tile_hbm.1, s32[1,192]{1,0:T(1,128)} %bitcast.12, ...), custom_call_target="tpu_custom_call" | custom-call | tf_op jit(solution)/shard_map/project/pallas_call | solution.py:305
  3.0 17.3 %all_to_all.10.message_ref = bf16[16,144,128]{2,1,0:T(8,128)(2,1)S(1)} all-to-all(bf16[16,144,128]{2,1,0:T(8,128)(2,1)S(1)} %get-tuple-element.11), channel_id=1, replica_groups={{0,1,2,3,4,5,6,7,8,9,10,11,12,13,14,15},{16,17,18,19,20,21,22,23,24,25,..., dimensions={0} | all-to-all | bytes 1179648 | tf_op jit(solution)/shard_map/all_to_all | solution.py:338
  20.3 1.2 %triangle.1 = bf16[2304,128]{1,0:T(8,128)(2,1)S(1)} custom-call(bf16[16,144,128]{2,1,0:T(8,128)(2,1)S(1)} %all_to_all.10.message_ref), custom_call_target="tpu_custom_call" | custom-call | tf_op jit(solution)/shard_map/triangle/pallas_call | solution.py:352
  21.5 18.6 %all_to_all.11 = bf16[32,72,128]{2,1,0:T(8,128)(2,1)S(1)} all-to-all(bf16[32,72,128]{2,1,0:T(8,128)(2,1)S(1)} %bitcast.7), channel_id=1, replica_groups=mesh['grp'=1,'row'=16,'col'=2] {'row','col'}, dimensions={0} | all-to-all | bytes 1179648 | tf_op jit(solution)/shard_map/all_to_all | solution.py:365
  40.1 1.2 %output.1 = bf16[1152,128]{1,0:T(8,128)(2,1)} custom-call(bf16[2304,128]{1,0:T(8,128)(2,1)S(1)} %bitcast.8, f32[128,1152]{1,0:T(8,128)S(1)} %get-tuple-element.12.gate_ref, f32[128,128]{1,0:T(8,128)S(1)} %get-tuple-element.13.gain_ref, bf16[128,128]{1,0:T(8,128)(2,1)S(1)} %get-tuple-element.14.w_t_ref, bf16[128,1152]{1,0:T(8,128)(2,1)S(1)} %get-tuple-element.15.normed_ref, ...), custom_call_target="tpu_custom_call" | custom-call | tf_op jit(solution)/shard_map/output/pallas_call | solution.py:372

commit v31 on v26

--- a/solution.py
+++ b/solution.py
@@ -215,13 +215,14 @@
     def operand(channel, half):
         return jnp.concatenate([channel_of(spread.at[half], channel, 2 * own)] + padding, axis=0)
 
-    for channel in range(own):
-        left = jnp.concatenate([operand(channel, half) for half in range(halves)], axis=0)
+    for pair in range(0, own, 2):
+        channels = [(channel, half) for channel in (pair, pair + 1) for half in range(halves)]
+        left = jnp.concatenate([operand(channel, half) for channel, half in channels], axis=0)
         both = lax.dot_general(
             one, left, (((1,), (1,)), ((), ())), preferred_element_type=jnp.float32
         ).astype(jnp.bfloat16)
-        for half in range(halves):
-            left_t[channel, half * cols : (half + 1) * cols, :] = both[:, half * deep : (half + 1) * deep]
+        for at, (channel, half) in enumerate(channels):
+            left_t[channel, half * cols : (half + 1) * cols, :] = both[:, at * deep : (at + 1) * deep]
     for channel in range(own):
         right = jnp.concatenate([operand(own + channel, half) for half in range(halves)], axis=1)
         total = jnp.dot(left_t[channel], right, preferred_element_type=jnp.float32)

time: 41.5 us -> 41.5 us (level)
  no operation moved by 1% of the time
where the time goes in v31:
time: 41.5 us; the launch traced here: 41.3 us
  blocking collectives  35.9 us (87%)
  Pallas kernels  5.33 us (13%)
    all_to_all x1, blocking collectives, on_device(): lax.all_to_all(mixed.reshape(halves * shares, lines, LANES), ('row', 'col...  18.6 us
    all_to_all x1, blocking collectives, on_device(): lax.all_to_all(message, ('row', 'col'), split_axis=0, concat_axis=0, axis...  17.3 us
    pallas_call x1, Pallas kernels, on_device(): pl.pallas_call(functools.partial(project_kernel, rows, cols), out_shape=(...  2.97 us
    pallas_call x1, Pallas kernels, on_device(): pl.pallas_call(functools.partial(triangle_kernel, own, cols, shares), out...  1.19 us
    pallas_call x1, Pallas kernels, on_device(): pl.pallas_call(functools.partial(output_kernel, own, PARTS), out_shape=ja...  1.18 us

profile of v31, /device:TPU:0, one launch (start us, length us, event | category | flops | bytes accessed | tf_op | source)
XLA Modules:
  0.0 41.3 jit_solution(1978182115287363814)
XLA Ops:
  0.0 3.0 %project.1 = (bf16[16,144,128]{2,1,0:T(8,128)(2,1)S(1)}, bf16[128,1152]{1,0:T(8,128)(2,1)S(1)}, bf16[128,128]{1,0:T(8,128)(2,1)S(1)}, f32[128,1152]{1,0:T(8,128)...) custom-call(s32[2,2]{1,0:T(2,128)} %tile_hbm.1, s32[1,192]{1,0:T(1,128)} %bitcast.12, ...), custom_call_target="tpu_custom_call" | custom-call | tf_op jit(solution)/shard_map/project/pallas_call | solution.py:306
  3.0 17.3 %all_to_all.10.message_ref = bf16[16,144,128]{2,1,0:T(8,128)(2,1)S(1)} all-to-all(bf16[16,144,128]{2,1,0:T(8,128)(2,1)S(1)} %get-tuple-element.11), channel_id=1, replica_groups={{0,1,2,3,4,5,6,7,8,9,10,11,12,13,14,15},{16,17,18,19,20,21,22,23,24,25,..., dimensions={0} | all-to-all | bytes 1179648 | tf_op jit(solution)/shard_map/all_to_all | solution.py:339
  20.3 1.2 %triangle.1 = bf16[2304,128]{1,0:T(8,128)(2,1)S(1)} custom-call(bf16[16,144,128]{2,1,0:T(8,128)(2,1)S(1)} %all_to_all.10.message_ref), custom_call_target="tpu_custom_call" | custom-call | tf_op jit(solution)/shard_map/triangle/pallas_call | solution.py:353
  21.5 18.6 %all_to_all.11 = bf16[32,72,128]{2,1,0:T(8,128)(2,1)S(1)} all-to-all(bf16[32,72,128]{2,1,0:T(8,128)(2,1)S(1)} %bitcast.7), channel_id=1, replica_groups=mesh['grp'=1,'row'=16,'col'=2] {'row','col'}, dimensions={0} | all-to-all | bytes 1179648 | tf_op jit(solution)/shard_map/all_to_all | solution.py:366
  40.1 1.2 %output.1 = bf16[1152,128]{1,0:T(8,128)(2,1)} custom-call(bf16[2304,128]{1,0:T(8,128)(2,1)S(1)} %bitcast.8, f32[128,1152]{1,0:T(8,128)S(1)} %get-tuple-element.12.gate_ref, f32[128,128]{1,0:T(8,128)S(1)} %get-tuple-element.13.gain_ref, bf16[128,128]{1,0:T(8,128)(2,1)S(1)} %get-tuple-element.14.w_t_ref, bf16[128,1152]{1,0:T(8,128)(2,1)S(1)} %get-tuple-element.15.normed_ref, ...), custom_call_target="tpu_custom_call" | custom-call | tf_op jit(solution)/shard_map/output/pallas_call | solution.py:373
